TPU v7x, 32 devices: a whole 2x2x4 slice. The times are simulated.
32 devices in a mesh: gx: 4 (over y, x), gy: 8 (over z, core).
Axes of the slice: x: 2, y: 2, z: 4, core: 2. Of those that a mesh axis runs over, the one named last changes fastest.
Arguments:
- saved_conc: float32 [3, 2, 64, 64, 512], P(None, None, None, 'gy', 'gx'), may hold values from 0.15 to 0.85
- adjoint_end: float32 [2, 64, 64, 512], P(None, None, 'gy', 'gx'), may hold values from -6 to 6
- rate_field: float32 [64, 64, 512], P(None, 'gy', 'gx'), may hold values from 0.5 to 5
Outputs:
- adjoint_start: float32 [2, 64, 64, 512], P(None, None, 'gy', 'gx')
- rate_grad: float32 [64, 64, 512], P(None, 'gy', 'gx')
All inputs are finite; a program needn't handle non-finite values.
Results may differ from a plain program's by a relative error of at most 0.00023.
Values sent between devices are 32-bit elements; how exact they have to be, the bound alone decides.
No kernel may reach another device: no remote copies, remote signals or barrier semaphores. Data moves between devices by JAX's collectives and lax.ppermute only.
A program may use at most 128 MiB of HBM per device.

v0:
```python
import jax
import jax.numpy as jnp
from jax import lax
from jax.sharding import PartitionSpec as P

mix_energy = 2.5
grad_energy = 1.0
time_step = 0.1
diff_step = 0.03
bath_potential = 0.5


def padded_2(block, sides, width):
    for axis, dim in sides:
        count = lax.axis_size(axis)
        forward = [(i, i + 1) for i in range(count - 1)]
        forward.append((count - 1, 0))
        backward = [(target, source) for source, target in forward]
        low = lax.ppermute(
            lax.slice_in_dim(block, block.shape[dim] - width, None, axis=dim), axis, forward
        )
        high = lax.ppermute(lax.slice_in_dim(block, 0, width, axis=dim), axis, backward)
        block = jnp.concatenate([low, block, high], axis=dim)
    return block


def inner(field, depth):
    rows = field.shape[-2]
    cols = field.shape[-1]
    return field[..., depth : rows - depth, depth : cols - depth]


def laplace_z(field):
    diffs = field[..., 1:, :, :] - field[..., :-1, :, :]
    zeros = jnp.zeros_like(field[..., :1, :, :])
    return jnp.concatenate([diffs, zeros], axis=-3) - jnp.concatenate([zeros, diffs], axis=-3)


def laplace_rim(field):
    center = inner(field, 1)
    sides = (
        field[..., 1:-1, 2:] + field[..., 1:-1, :-2] + field[..., 2:, 1:-1] + field[..., :-2, 1:-1]
    )
    return sides - 4.0 * center + laplace_z(center)


def potential_rim(padded):
    conc = inner(padded, 1)
    return (
        jnp.log(conc / (1.0 - conc))
        + mix_energy * (1.0 - 2.0 * conc)
        - grad_energy * laplace_rim(padded)
    )


def flux_rim(mobility, scaled):
    flux_x = (
        0.5
        * (mobility[..., 1:-1, 1:] + mobility[..., 1:-1, :-1])
        * (scaled[..., 1:-1, 1:] - scaled[..., 1:-1, :-1])
    )
    total = flux_x[..., 1:] - flux_x[..., :-1]
    flux_y = (
        0.5
        * (mobility[..., 1:, 1:-1] + mobility[..., :-1, 1:-1])
        * (scaled[..., 1:, 1:-1] - scaled[..., :-1, 1:-1])
    )
    total = total + flux_y[..., 1:, :] - flux_y[..., :-1, :]
    mob_core = inner(mobility, 1)
    sca_core = inner(scaled, 1)
    flux_z = (
        0.5
        * (mob_core[..., 1:, :, :] + mob_core[..., :-1, :, :])
        * (sca_core[..., 1:, :, :] - sca_core[..., :-1, :, :])
    )
    zeros = jnp.zeros_like(sca_core[..., :1, :, :])
    return (
        total
        + jnp.concatenate([flux_z, zeros], axis=-3)
        - jnp.concatenate([zeros, flux_z], axis=-3)
    )


def face_rim(chem, scaled):
    term_x = (
        -0.5
        * (chem[..., 1:-1, 1:] - chem[..., 1:-1, :-1])
        * (scaled[..., 1:-1, 1:] - scaled[..., 1:-1, :-1])
    )
    total = term_x[..., 1:] + term_x[..., :-1]
    term_y = (
        -0.5
        * (chem[..., 1:, 1:-1] - chem[..., :-1, 1:-1])
        * (scaled[..., 1:, 1:-1] - scaled[..., :-1, 1:-1])
    )
    total = total + term_y[..., 1:, :] + term_y[..., :-1, :]
    chem_core = inner(chem, 1)
    sca_core = inner(scaled, 1)
    term_z = (
        -0.5
        * (chem_core[..., 1:, :, :] - chem_core[..., :-1, :, :])
        * (sca_core[..., 1:, :, :] - sca_core[..., :-1, :, :])
    )
    zeros = jnp.zeros_like(sca_core[..., :1, :, :])
    return (
        total
        + jnp.concatenate([term_z, zeros], axis=-3)
        + jnp.concatenate([zeros, term_z], axis=-3)
    )


def shards(saved_conc, adjoint_end, rate_field):
    steps = saved_conc.shape[0]
    conc_depth = 2
    adjoint = adjoint_end
    rate_grad = jnp.zeros(rate_field.shape, jnp.float32)
    for back in range(steps):
        index = steps - 1 - back
        conc = saved_conc[index]
        conc_pad = padded_2(conc, (("gx", 3), ("gy", 2)), conc_depth)
        chem_rim = potential_rim(conc_pad)
        conc_mid = inner(conc_pad, 1)
        mobility = conc_mid * (1.0 - conc_mid)
        adj_pad = padded_2(adjoint, (("gx", 3), ("gy", 2)), 1)
        scaled = diff_step * adj_pad
        g_core = flux_rim(mobility, scaled) - time_step * rate_field * adjoint
        faces = face_rim(chem_rim, scaled)
        chem_core = inner(chem_rim, 1)
        g_pad = padded_2(g_core, (("gx", 3), ("gy", 2)), 1)
        rate_grad = rate_grad + time_step * jnp.sum(adjoint * (bath_potential - chem_core), axis=0)
        curve = 1.0 / (conc * (1.0 - conc)) - 2.0 * mix_energy
        adjoint = (
            adjoint + (1.0 - 2.0 * conc) * faces + curve * g_core - grad_energy * laplace_rim(g_pad)
        )
    return (adjoint, rate_grad)


def solution(mesh):
    return jax.shard_map(
        shards,
        mesh=mesh,
        in_specs=(P(None, None, None, "gy", "gx"), P(None, None, "gy", "gx"), P(None, "gy", "gx")),
        out_specs=(P(None, None, "gy", "gx"), P(None, "gy", "gx")),
        check_vma=False,
    )
```

profile of v0, /device:TPU:0, one launch (start us, length us, event | category | flops | bytes accessed | tf_op | source)
XLA Modules:
  0.0 279.3 jit_solution(14566509911709346953)
XLA Ops:
  0.6 1.5 fusion.116
  2.4 3.0 %collective-permute-start = (f32[2,64,8,2]{3,1,2,0:T(8,128)S(1)}, f32[2,64,8,2]{3,1,2,0:T(8,128)S(1)}, u32[]{:S(2)}, u32[]{:S(2)}) collective-permute-start(f32[2,64,8,2]{3,1,2,0:T(8,128)S(1)} %get-tuple-element.69), channel_id=1, source_target_pairs={{0,8},{8,16},{16,24},{24,0},{1,9},{9,17},{17,25},{25,1},{2,10},{10... | collective-permute-start | bytes 24584 | tf_op jit(solution)/shard_map/ppermute | solution.py:19
  5.4 1.0 collective-permute-start.1
  6.7 1.1 collective-permute-start.4
  7.8 1.9 collective-permute-start.5
  11.1 30.5 %collective-permute-done.4 = f32[2,64,8,1]{3,1,2,0:T(8,128)S(1)} collective-permute-done((f32[2,64,8,1]{3,1,2,0:T(8,128)S(1)}, f32[2,64,8,1]{3,1,2,0:T(8,128)S(1)}, u32[]{:S(2)}, u32[]{:S(2)}) %collective-permute-start.4) | collective-permute-done | bytes 4128 | tf_op jit(solution)/shard_map/ppermute | solution.py:19
  41.6 2.1 collective-permute-start.13
  43.6 9.7 %collective-permute-done.5 = f32[2,64,8,1]{3,1,2,0:T(8,128)S(1)} collective-permute-done((f32[2,64,8,1]{3,1,2,0:T(8,128)S(1)}, f32[2,64,8,1]{3,1,2,0:T(8,128)S(1)}, u32[]{:S(2)}, u32[]{:S(2)}) %collective-permute-start.5) | collective-permute-done | bytes 4128 | tf_op jit(solution)/shard_map/ppermute | solution.py:22
  53.4 1.5 collective-permute-start.24
  55.1 1.5 collective-permute-start.25
  56.8 7.2 %collective-permute-done.12 = f32[2,64,8,2]{3,1,2,0:T(8,128)S(1)} collective-permute-done((f32[2,64,8,2]{3,1,2,0:T(8,128)S(1)}, f32[2,64,8,2]{3,1,2,0:T(8,128)S(1)}, u32[]{:S(2)}, u32[]{:S(2)}) %collective-permute-start.12) | collective-permute-done | bytes 8224 | tf_op jit(solution)/shard_map/ppermute | solution.py:19
  64.1 1.5 collective-permute-start.7
  65.6 10.3 %collective-permute-done.13 = f32[2,64,8,2]{3,1,2,0:T(8,128)S(1)} collective-permute-done((f32[2,64,8,2]{3,1,2,0:T(8,128)S(1)}, f32[2,64,8,2]{3,1,2,0:T(8,128)S(1)}, u32[]{:S(2)}, u32[]{:S(2)}) %collective-permute-start.13) | collective-permute-done | bytes 8224 | tf_op jit(solution)/shard_map/ppermute | solution.py:22
  76.1 10.4 %collective-permute-done.24 = f32[2,64,8,2]{3,1,2,0:T(8,128)S(1)} collective-permute-done((f32[2,64,8,2]{3,1,2,0:T(8,128)S(1)}, f32[2,64,8,2]{3,1,2,0:T(8,128)S(1)}, u32[]{:S(2)}, u32[]{:S(2)}) %collective-permute-start.24) | collective-permute-done | bytes 8224 | tf_op jit(solution)/shard_map/ppermute | solution.py:19
  86.5 1.5 collective-permute-start.3
  88.1 9.1 %collective-permute-done.25 = f32[2,64,8,2]{3,1,2,0:T(8,128)S(1)} collective-permute-done((f32[2,64,8,2]{3,1,2,0:T(8,128)S(1)}, f32[2,64,8,2]{3,1,2,0:T(8,128)S(1)}, u32[]{:S(2)}, u32[]{:S(2)}) %collective-permute-start.25) | collective-permute-done | bytes 8224 | tf_op jit(solution)/shard_map/ppermute | solution.py:22
  97.5 3.6 %collective-permute-start.15 = (f32[2,64,2,132]{3,1,2,0:T(8,128)S(1)}, f32[2,64,2,132]{3,1,2,0:T(8,128)S(1)}, u32[]{:S(2)}, u32[]{:S(2)}) collective-permute-start(f32[2,64,2,132]{3,1,2,0:T(8,128)S(1)} %get-tuple-element.32), channel_id=1, source_target_pairs={{1,0},{2,1},{3,2},{4,3},{5,4},{6,5},{7,6},{0,7},{9,8},{10,9},{11,1... | collective-permute-start | bytes 405512 | tf_op jit(solution)/shard_map/ppermute | solution.py:22
  101.6 3.6 %collective-permute-start.27 = (f32[2,64,2,132]{3,1,2,0:T(8,128)S(1)}, f32[2,64,2,132]{3,1,2,0:T(8,128)S(1)}, u32[]{:S(2)}, u32[]{:S(2)}) collective-permute-start(f32[2,64,2,132]{3,1,2,0:T(8,128)S(1)} %get-tuple-element.36), channel_id=1, source_target_pairs={{1,0},{2,1},{3,2},{4,3},{5,4},{6,5},{7,6},{0,7},{9,8},{10,9},{11,1... | collective-permute-start | bytes 405512 | tf_op jit(solution)/shard_map/ppermute | solution.py:22
  106.4 2.5 fusion.2
  108.9 0.9 fusion.32
  109.8 1.0 fusion.44
  110.8 0.9 fusion.109
  112.4 1.5 collective-permute-start.8
  115.7 2.5 fusion.5
  118.2 9.1 %collective-permute-done.8 = f32[2,64,8,1]{3,1,2,0:T(8,128)S(1)} collective-permute-done((f32[2,64,8,1]{3,1,2,0:T(8,128)S(1)}, f32[2,64,8,1]{3,1,2,0:T(8,128)S(1)}, u32[]{:S(2)}, u32[]{:S(2)}) %collective-permute-start.8) | collective-permute-done | bytes 4128 | tf_op jit(solution)/shard_map/ppermute | solution.py:22
  127.3 6.9 %collective-permute-done.9 = f32[2,64,8,1]{3,1,2,0:T(8,128)S(1)} collective-permute-done((f32[2,64,8,1]{3,1,2,0:T(8,128)S(1)}, f32[2,64,8,1]{3,1,2,0:T(8,128)S(1)}, u32[]{:S(2)}, u32[]{:S(2)}) %collective-permute-start.9) | collective-permute-done | bytes 4128 | tf_op jit(solution)/shard_map/ppermute | solution.py:19
  134.4 2.5 collective-permute-start.10
  136.9 2.4 collective-permute-done.10
  139.4 3.7 %collective-permute-done.11 = f32[2,64,1,130]{3,1,2,0:T(8,128)S(1)} collective-permute-done((f32[2,64,1,130]{3,1,2,0:T(8,128)S(1)}, f32[2,64,1,130]{3,1,2,0:T(8,128)S(1)}, u32[]{:S(2)}, u32[]{:S(2)}) %collective-permute-start.11) | collective-permute-done | bytes 66592 | tf_op jit(solution)/shard_map/ppermute | solution.py:19
  143.1 1.0 fusion.63
  144.3 2.0 collective-permute-start.16
  146.3 1.0 collective-permute-start.17
  147.8 12.3 %collective-permute-done.16 = f32[2,64,8,1]{3,1,2,0:T(8,128)S(1)} collective-permute-done((f32[2,64,8,1]{3,1,2,0:T(8,128)S(1)}, f32[2,64,8,1]{3,1,2,0:T(8,128)S(1)}, u32[]{:S(2)}, u32[]{:S(2)}) %collective-permute-start.16) | collective-permute-done | bytes 4128 | tf_op jit(solution)/shard_map/ppermute | solution.py:19
  160.1 5.9 %collective-permute-done.17 = f32[2,64,8,1]{3,1,2,0:T(8,128)S(1)} collective-permute-done((f32[2,64,8,1]{3,1,2,0:T(8,128)S(1)}, f32[2,64,8,1]{3,1,2,0:T(8,128)S(1)}, u32[]{:S(2)}, u32[]{:S(2)}) %collective-permute-start.17) | collective-permute-done | bytes 4128 | tf_op jit(solution)/shard_map/ppermute | solution.py:22
  166.2 4.3 %collective-permute-start.19 = (f32[2,64,1,130]{3,1,2,0:T(8,128)S(1)}, f32[2,64,1,130]{3,1,2,0:T(8,128)S(1)}, u32[]{:S(2)}, u32[]{:S(2)}) collective-permute-start(f32[2,64,1,130]{3,1,2,0:T(8,128)S(1)} %get-tuple-element.17), channel_id=1, source_target_pairs={{1,0},{2,1},{3,2},{4,3},{5,4},{6,5},{7,6},{0,7},{9,8},{10,9},{11,1... | collective-permute-start | bytes 199688 | tf_op jit(solution)/shard_map/ppermute | solution.py:22
  171.3 2.0 collective-permute-done.18
  173.7 0.9 fusion.93
  174.6 0.9 fusion.28
  175.6 1.0 fusion.40
  177.1 1.5 collective-permute-start.20
  179.2 2.5 fusion.8
  181.7 10.2 %collective-permute-done.20 = f32[2,64,8,1]{3,1,2,0:T(8,128)S(1)} collective-permute-done((f32[2,64,8,1]{3,1,2,0:T(8,128)S(1)}, f32[2,64,8,1]{3,1,2,0:T(8,128)S(1)}, u32[]{:S(2)}, u32[]{:S(2)}) %collective-permute-start.20) | collective-permute-done | bytes 4128 | tf_op jit(solution)/shard_map/ppermute | solution.py:22
  191.9 10.6 %collective-permute-done.21 = f32[2,64,8,1]{3,1,2,0:T(8,128)S(1)} collective-permute-done((f32[2,64,8,1]{3,1,2,0:T(8,128)S(1)}, f32[2,64,8,1]{3,1,2,0:T(8,128)S(1)}, u32[]{:S(2)}, u32[]{:S(2)}) %collective-permute-start.21) | collective-permute-done | bytes 4128 | tf_op jit(solution)/shard_map/ppermute | solution.py:19
  202.7 1.7 collective-permute-start.22
  204.5 3.0 %collective-permute-done.22 = f32[2,64,1,130]{3,1,2,0:T(8,128)S(1)} collective-permute-done((f32[2,64,1,130]{3,1,2,0:T(8,128)S(1)}, f32[2,64,1,130]{3,1,2,0:T(8,128)S(1)}, u32[]{:S(2)}, u32[]{:S(2)}) %collective-permute-start.22) | collective-permute-done | bytes 66592 | tf_op jit(solution)/shard_map/ppermute | solution.py:22
  207.4 3.2 %collective-permute-done.23 = f32[2,64,1,130]{3,1,2,0:T(8,128)S(1)} collective-permute-done((f32[2,64,1,130]{3,1,2,0:T(8,128)S(1)}, f32[2,64,1,130]{3,1,2,0:T(8,128)S(1)}, u32[]{:S(2)}, u32[]{:S(2)}) %collective-permute-start.23) | collective-permute-done | bytes 66592 | tf_op jit(solution)/shard_map/ppermute | solution.py:19
  210.6 1.0 fusion.61
  211.8 1.8 collective-permute-start.28
  213.6 1.2 collective-permute-start.29
  214.8 12.8 %collective-permute-done.28 = f32[2,64,8,1]{3,1,2,0:T(8,128)S(1)} collective-permute-done((f32[2,64,8,1]{3,1,2,0:T(8,128)S(1)}, f32[2,64,8,1]{3,1,2,0:T(8,128)S(1)}, u32[]{:S(2)}, u32[]{:S(2)}) %collective-permute-start.28) | collective-permute-done | bytes 4128 | tf_op jit(solution)/shard_map/ppermute | solution.py:19
  227.6 6.3 %collective-permute-done.29 = f32[2,64,8,1]{3,1,2,0:T(8,128)S(1)} collective-permute-done((f32[2,64,8,1]{3,1,2,0:T(8,128)S(1)}, f32[2,64,8,1]{3,1,2,0:T(8,128)S(1)}, u32[]{:S(2)}, u32[]{:S(2)}) %collective-permute-start.29) | collective-permute-done | bytes 4128 | tf_op jit(solution)/shard_map/ppermute | solution.py:22
  234.2 3.5 %collective-permute-start.31 = (f32[2,64,1,130]{3,1,2,0:T(8,128)S(1)}, f32[2,64,1,130]{3,1,2,0:T(8,128)S(1)}, u32[]{:S(2)}, u32[]{:S(2)}) collective-permute-start(f32[2,64,1,130]{3,1,2,0:T(8,128)S(1)} %get-tuple-element.13), channel_id=1, source_target_pairs={{1,0},{2,1},{3,2},{4,3},{5,4},{6,5},{7,6},{0,7},{9,8},{10,9},{11,1... | collective-permute-start | bytes 199688 | tf_op jit(solution)/shard_map/ppermute | solution.py:22
  237.7 2.8 %collective-permute-done.30 = f32[2,64,1,130]{3,1,2,0:T(8,128)S(1)} collective-permute-done((f32[2,64,1,130]{3,1,2,0:T(8,128)S(1)}, f32[2,64,1,130]{3,1,2,0:T(8,128)S(1)}, u32[]{:S(2)}, u32[]{:S(2)}) %collective-permute-start.30) | collective-permute-done | bytes 66592 | tf_op jit(solution)/shard_map/ppermute | solution.py:19
  241.0 0.9 fusion.77
  241.9 0.9 fusion.24
  242.8 1.0 fusion.36
  244.4 1.5 collective-permute-start.32
  246.5 0.9 copy.27
  247.3 11.9 %collective-permute-done.32 = f32[2,64,8,1]{3,1,2,0:T(8,128)S(1)} collective-permute-done((f32[2,64,8,1]{3,1,2,0:T(8,128)S(1)}, f32[2,64,8,1]{3,1,2,0:T(8,128)S(1)}, u32[]{:S(2)}, u32[]{:S(2)}) %collective-permute-start.32) | collective-permute-done | bytes 4128 | tf_op jit(solution)/shard_map/ppermute | solution.py:22
  259.2 11.2 %collective-permute-done.33 = f32[2,64,8,1]{3,1,2,0:T(8,128)S(1)} collective-permute-done((f32[2,64,8,1]{3,1,2,0:T(8,128)S(1)}, f32[2,64,8,1]{3,1,2,0:T(8,128)S(1)}, u32[]{:S(2)}, u32[]{:S(2)}) %collective-permute-start.33) | collective-permute-done | bytes 4128 | tf_op jit(solution)/shard_map/ppermute | solution.py:19
  271.2 3.4 %collective-permute-done.34 = f32[2,64,1,130]{3,1,2,0:T(8,128)S(1)} collective-permute-done((f32[2,64,1,130]{3,1,2,0:T(8,128)S(1)}, f32[2,64,1,130]{3,1,2,0:T(8,128)S(1)}, u32[]{:S(2)}, u32[]{:S(2)}) %collective-permute-start.34) | collective-permute-done | bytes 66592 | tf_op jit(solution)/shard_map/ppermute | solution.py:22
  274.6 2.7 collective-permute-done.35
  277.3 0.9 fusion.59
  278.2 1.1 copy.26
  (68 shorter events, 13.9 us)
Async XLA Ops:
  2.2 4.2 %copy-start = (f32[2,64,8,128]{3,2,1,0:T(8,128)S(1)}, f32[2,64,8,128]{3,2,1,0:T(8,128)}, u32[]{:S(2)}) copy-start(f32[2,64,8,128]{3,2,1,0:T(8,128)} %param.4) | copy-start | bytes 1572868
  2.4 52.6 %collective-permute-start = (f32[2,64,8,2]{3,1,2,0:T(8,128)S(1)}, f32[2,64,8,2]{3,1,2,0:T(8,128)S(1)}, u32[]{:S(2)}, u32[]{:S(2)}) collective-permute-start(f32[2,64,8,2]{3,1,2,0:T(8,128)S(1)} %get-tuple-element.69), channel_id=1, source_target_pairs={{0,8},{8,16},{16,24},{24,0},{1,9},{9,17},{17,25},{25,1},{2,10},{10... | collective-permute-start | bytes 24584 | tf_op jit(solution)/shard_map/ppermute | solution.py:19
  5.4 51.1 %collective-permute-start.1 = (f32[2,64,8,2]{3,1,2,0:T(8,128)S(1)}, f32[2,64,8,2]{3,1,2,0:T(8,128)S(1)}, u32[]{:S(2)}, u32[]{:S(2)}) collective-permute-start(f32[2,64,8,2]{3,1,2,0:T(8,128)S(1)} %get-tuple-element.70), channel_id=1, source_target_pairs={{8,0},{16,8},{24,16},{0,24},{9,1},{17,9},{25,17},{1,25},{10,2},{18... | collective-permute-start | bytes 24584 | tf_op jit(solution)/shard_map/ppermute | solution.py:22
  6.7 34.8 %collective-permute-start.4 = (f32[2,64,8,1]{3,1,2,0:T(8,128)S(1)}, f32[2,64,8,1]{3,1,2,0:T(8,128)S(1)}, u32[]{:S(2)}, u32[]{:S(2)}) collective-permute-start(f32[2,64,8,1]{3,1,2,0:T(8,128)S(1)} %get-tuple-element.67), channel_id=1, source_target_pairs={{0,8},{8,16},{16,24},{24,0},{1,9},{9,17},{17,25},{25,1},{2,10},{10... | collective-permute-start | bytes 12296 | tf_op jit(solution)/shard_map/ppermute | solution.py:19
  7.8 45.6 %collective-permute-start.5 = (f32[2,64,8,1]{3,1,2,0:T(8,128)S(1)}, f32[2,64,8,1]{3,1,2,0:T(8,128)S(1)}, u32[]{:S(2)}, u32[]{:S(2)}) collective-permute-start(f32[2,64,8,1]{3,1,2,0:T(8,128)S(1)} %get-tuple-element.68), channel_id=1, source_target_pairs={{8,0},{16,8},{24,16},{0,24},{9,1},{17,9},{25,17},{1,25},{10,2},{18... | collective-permute-start | bytes 12296 | tf_op jit(solution)/shard_map/ppermute | solution.py:22
  10.1 1.0 copy-start.1
  10.1 53.9 %collective-permute-start.12 = (f32[2,64,8,2]{3,1,2,0:T(8,128)S(1)}, f32[2,64,8,2]{3,1,2,0:T(8,128)S(1)}, u32[]{:S(2)}, u32[]{:S(2)}) collective-permute-start(f32[2,64,8,2]{3,1,2,0:T(8,128)S(1)} %get-tuple-element.71), channel_id=1, source_target_pairs={{0,8},{8,16},{16,24},{24,0},{1,9},{9,17},{17,25},{25,1},{2,10},{10... | collective-permute-start | bytes 24584 | tf_op jit(solution)/shard_map/ppermute | solution.py:19
  41.6 34.3 %collective-permute-start.13 = (f32[2,64,8,2]{3,1,2,0:T(8,128)S(1)}, f32[2,64,8,2]{3,1,2,0:T(8,128)S(1)}, u32[]{:S(2)}, u32[]{:S(2)}) collective-permute-start(f32[2,64,8,2]{3,1,2,0:T(8,128)S(1)} %get-tuple-element.72), channel_id=1, source_target_pairs={{8,0},{16,8},{24,16},{0,24},{9,1},{17,9},{25,17},{1,25},{10,2},{18... | collective-permute-start | bytes 24584 | tf_op jit(solution)/shard_map/ppermute | solution.py:22
  53.4 33.1 %collective-permute-start.24 = (f32[2,64,8,2]{3,1,2,0:T(8,128)S(1)}, f32[2,64,8,2]{3,1,2,0:T(8,128)S(1)}, u32[]{:S(2)}, u32[]{:S(2)}) collective-permute-start(f32[2,64,8,2]{3,1,2,0:T(8,128)S(1)} %get-tuple-element.73), channel_id=1, source_target_pairs={{0,8},{8,16},{16,24},{24,0},{1,9},{9,17},{17,25},{25,1},{2,10},{10... | collective-permute-start | bytes 24584 | tf_op jit(solution)/shard_map/ppermute | solution.py:19
  55.1 42.1 %collective-permute-start.25 = (f32[2,64,8,2]{3,1,2,0:T(8,128)S(1)}, f32[2,64,8,2]{3,1,2,0:T(8,128)S(1)}, u32[]{:S(2)}, u32[]{:S(2)}) collective-permute-start(f32[2,64,8,2]{3,1,2,0:T(8,128)S(1)} %get-tuple-element.74), channel_id=1, source_target_pairs={{8,0},{16,8},{24,16},{0,24},{9,1},{17,9},{25,17},{1,25},{10,2},{18... | collective-permute-start | bytes 24584 | tf_op jit(solution)/shard_map/ppermute | solution.py:22
  56.6 40.9 %collective-permute-start.6 = (f32[2,64,1,130]{3,1,2,0:T(8,128)S(1)}, f32[2,64,1,130]{3,1,2,0:T(8,128)S(1)}, u32[]{:S(2)}, u32[]{:S(2)}) collective-permute-start(f32[2,64,1,130]{3,1,2,0:T(8,128)S(1)} %get-tuple-element.22), channel_id=1, source_target_pairs={{0,1},{1,2},{2,3},{3,4},{4,5},{5,6},{6,7},{7,0},{8,9},{9,10},{10,1... | collective-permute-start | bytes 199688 | tf_op jit(solution)/shard_map/ppermute | solution.py:19
  64.1 37.0 %collective-permute-start.7 = (f32[2,64,1,130]{3,1,2,0:T(8,128)S(1)}, f32[2,64,1,130]{3,1,2,0:T(8,128)S(1)}, u32[]{:S(2)}, u32[]{:S(2)}) collective-permute-start(f32[2,64,1,130]{3,1,2,0:T(8,128)S(1)} %get-tuple-element.23), channel_id=1, source_target_pairs={{1,0},{2,1},{3,2},{4,3},{5,4},{6,5},{7,6},{0,7},{9,8},{10,9},{11,1... | collective-permute-start | bytes 199688 | tf_op jit(solution)/shard_map/ppermute | solution.py:22
  75.9 25.7 %collective-permute-start.2 = (f32[2,64,2,132]{3,1,2,0:T(8,128)S(1)}, f32[2,64,2,132]{3,1,2,0:T(8,128)S(1)}, u32[]{:S(2)}, u32[]{:S(2)}) collective-permute-start(f32[2,64,2,132]{3,1,2,0:T(8,128)S(1)} %get-tuple-element.24), channel_id=1, source_target_pairs={{0,1},{1,2},{2,3},{3,4},{4,5},{5,6},{6,7},{7,0},{8,9},{9,10},{10,1... | collective-permute-start | bytes 405512 | tf_op jit(solution)/shard_map/ppermute | solution.py:19
  86.5 18.6 %collective-permute-start.3 = (f32[2,64,2,132]{3,1,2,0:T(8,128)S(1)}, f32[2,64,2,132]{3,1,2,0:T(8,128)S(1)}, u32[]{:S(2)}, u32[]{:S(2)}) collective-permute-start(f32[2,64,2,132]{3,1,2,0:T(8,128)S(1)} %get-tuple-element.25), channel_id=1, source_target_pairs={{1,0},{2,1},{3,2},{4,3},{5,4},{6,5},{7,6},{0,7},{9,8},{10,9},{11,1... | collective-permute-start | bytes 405512 | tf_op jit(solution)/shard_map/ppermute | solution.py:22
  97.2 16.7 %collective-permute-start.14 = (f32[2,64,2,132]{3,1,2,0:T(8,128)S(1)}, f32[2,64,2,132]{3,1,2,0:T(8,128)S(1)}, u32[]{:S(2)}, u32[]{:S(2)}) collective-permute-start(f32[2,64,2,132]{3,1,2,0:T(8,128)S(1)} %get-tuple-element.31), channel_id=1, source_target_pairs={{0,1},{1,2},{2,3},{3,4},{4,5},{5,6},{6,7},{7,0},{8,9},{9,10},{10,1... | collective-permute-start | bytes 405512 | tf_op jit(solution)/shard_map/ppermute | solution.py:19
  97.5 17.0 %collective-permute-start.15 = (f32[2,64,2,132]{3,1,2,0:T(8,128)S(1)}, f32[2,64,2,132]{3,1,2,0:T(8,128)S(1)}, u32[]{:S(2)}, u32[]{:S(2)}) collective-permute-start(f32[2,64,2,132]{3,1,2,0:T(8,128)S(1)} %get-tuple-element.32), channel_id=1, source_target_pairs={{1,0},{2,1},{3,2},{4,3},{5,4},{6,5},{7,6},{0,7},{9,8},{10,9},{11,1... | collective-permute-start | bytes 405512 | tf_op jit(solution)/shard_map/ppermute | solution.py:22
  101.1 46.2 %collective-permute-start.26 = (f32[2,64,2,132]{3,1,2,0:T(8,128)S(1)}, f32[2,64,2,132]{3,1,2,0:T(8,128)S(1)}, u32[]{:S(2)}, u32[]{:S(2)}) collective-permute-start(f32[2,64,2,132]{3,1,2,0:T(8,128)S(1)} %get-tuple-element.35), channel_id=1, source_target_pairs={{0,1},{1,2},{2,3},{3,4},{4,5},{5,6},{6,7},{7,0},{8,9},{9,10},{10,1... | collective-permute-start | bytes 405512 | tf_op jit(solution)/shard_map/ppermute | solution.py:19
  101.6 45.8 %collective-permute-start.27 = (f32[2,64,2,132]{3,1,2,0:T(8,128)S(1)}, f32[2,64,2,132]{3,1,2,0:T(8,128)S(1)}, u32[]{:S(2)}, u32[]{:S(2)}) collective-permute-start(f32[2,64,2,132]{3,1,2,0:T(8,128)S(1)} %get-tuple-element.36), channel_id=1, source_target_pairs={{1,0},{2,1},{3,2},{4,3},{5,4},{6,5},{7,6},{0,7},{9,8},{10,9},{11,1... | collective-permute-start | bytes 405512 | tf_op jit(solution)/shard_map/ppermute | solution.py:22
  112.4 14.9 %collective-permute-start.8 = (f32[2,64,8,1]{3,1,2,0:T(8,128)S(1)}, f32[2,64,8,1]{3,1,2,0:T(8,128)S(1)}, u32[]{:S(2)}, u32[]{:S(2)}) collective-permute-start(f32[2,64,8,1]{3,1,2,0:T(8,128)S(1)} %get-tuple-element.66), channel_id=1, source_target_pairs={{8,0},{16,8},{24,16},{0,24},{9,1},{17,9},{25,17},{1,25},{10,2},{18... | collective-permute-start | bytes 12296 | tf_op jit(solution)/shard_map/ppermute | solution.py:22
  113.8 20.3 %collective-permute-start.9 = (f32[2,64,8,1]{3,1,2,0:T(8,128)S(1)}, f32[2,64,8,1]{3,1,2,0:T(8,128)S(1)}, u32[]{:S(2)}, u32[]{:S(2)}) collective-permute-start(f32[2,64,8,1]{3,1,2,0:T(8,128)S(1)} %get-tuple-element.65), channel_id=1, source_target_pairs={{0,8},{8,16},{16,24},{24,0},{1,9},{9,17},{17,25},{25,1},{2,10},{10... | collective-permute-start | bytes 12296 | tf_op jit(solution)/shard_map/ppermute | solution.py:19
  134.4 5.0 %collective-permute-start.10 = (f32[2,64,1,130]{3,1,2,0:T(8,128)S(1)}, f32[2,64,1,130]{3,1,2,0:T(8,128)S(1)}, u32[]{:S(2)}, u32[]{:S(2)}) collective-permute-start(f32[2,64,1,130]{3,1,2,0:T(8,128)S(1)} %get-tuple-element.20), channel_id=1, source_target_pairs={{1,0},{2,1},{3,2},{4,3},{5,4},{6,5},{7,6},{0,7},{9,8},{10,9},{11,1... | collective-permute-start | bytes 199688 | tf_op jit(solution)/shard_map/ppermute | solution.py:22
  136.9 6.2 %collective-permute-start.11 = (f32[2,64,1,130]{3,1,2,0:T(8,128)S(1)}, f32[2,64,1,130]{3,1,2,0:T(8,128)S(1)}, u32[]{:S(2)}, u32[]{:S(2)}) collective-permute-start(f32[2,64,1,130]{3,1,2,0:T(8,128)S(1)} %get-tuple-element.21), channel_id=1, source_target_pairs={{0,1},{1,2},{2,3},{3,4},{4,5},{5,6},{6,7},{7,0},{8,9},{9,10},{10,1... | collective-permute-start | bytes 199688 | tf_op jit(solution)/shard_map/ppermute | solution.py:19
  144.3 15.8 %collective-permute-start.16 = (f32[2,64,8,1]{3,1,2,0:T(8,128)S(1)}, f32[2,64,8,1]{3,1,2,0:T(8,128)S(1)}, u32[]{:S(2)}, u32[]{:S(2)}) collective-permute-start(f32[2,64,8,1]{3,1,2,0:T(8,128)S(1)} %get-tuple-element.63), channel_id=1, source_target_pairs={{0,8},{8,16},{16,24},{24,0},{1,9},{9,17},{17,25},{25,1},{2,10},{10... | collective-permute-start | bytes 12296 | tf_op jit(solution)/shard_map/ppermute | solution.py:19
  146.3 19.7 %collective-permute-start.17 = (f32[2,64,8,1]{3,1,2,0:T(8,128)S(1)}, f32[2,64,8,1]{3,1,2,0:T(8,128)S(1)}, u32[]{:S(2)}, u32[]{:S(2)}) collective-permute-start(f32[2,64,8,1]{3,1,2,0:T(8,128)S(1)} %get-tuple-element.64), channel_id=1, source_target_pairs={{8,0},{16,8},{24,16},{0,24},{9,1},{17,9},{25,17},{1,25},{10,2},{18... | collective-permute-start | bytes 12296 | tf_op jit(solution)/shard_map/ppermute | solution.py:22
  166.2 7.1 %collective-permute-start.18 = (f32[2,64,1,130]{3,1,2,0:T(8,128)S(1)}, f32[2,64,1,130]{3,1,2,0:T(8,128)S(1)}, u32[]{:S(2)}, u32[]{:S(2)}) collective-permute-start(f32[2,64,1,130]{3,1,2,0:T(8,128)S(1)} %get-tuple-element.16), channel_id=1, source_target_pairs={{0,1},{1,2},{2,3},{3,4},{4,5},{5,6},{6,7},{7,0},{8,9},{9,10},{10,1... | collective-permute-start | bytes 199688 | tf_op jit(solution)/shard_map/ppermute | solution.py:19
  166.2 7.1 %collective-permute-start.19 = (f32[2,64,1,130]{3,1,2,0:T(8,128)S(1)}, f32[2,64,1,130]{3,1,2,0:T(8,128)S(1)}, u32[]{:S(2)}, u32[]{:S(2)}) collective-permute-start(f32[2,64,1,130]{3,1,2,0:T(8,128)S(1)} %get-tuple-element.17), channel_id=1, source_target_pairs={{1,0},{2,1},{3,2},{4,3},{5,4},{6,5},{7,6},{0,7},{9,8},{10,9},{11,1... | collective-permute-start | bytes 199688 | tf_op jit(solution)/shard_map/ppermute | solution.py:22
  177.1 14.8 %collective-permute-start.20 = (f32[2,64,8,1]{3,1,2,0:T(8,128)S(1)}, f32[2,64,8,1]{3,1,2,0:T(8,128)S(1)}, u32[]{:S(2)}, u32[]{:S(2)}) collective-permute-start(f32[2,64,8,1]{3,1,2,0:T(8,128)S(1)} %get-tuple-element.62), channel_id=1, source_target_pairs={{8,0},{16,8},{24,16},{0,24},{9,1},{17,9},{25,17},{1,25},{10,2},{18... | collective-permute-start | bytes 12296 | tf_op jit(solution)/shard_map/ppermute | solution.py:22
  178.6 23.9 %collective-permute-start.21 = (f32[2,64,8,1]{3,1,2,0:T(8,128)S(1)}, f32[2,64,8,1]{3,1,2,0:T(8,128)S(1)}, u32[]{:S(2)}, u32[]{:S(2)}) collective-permute-start(f32[2,64,8,1]{3,1,2,0:T(8,128)S(1)} %get-tuple-element.61), channel_id=1, source_target_pairs={{0,8},{8,16},{16,24},{24,0},{1,9},{9,17},{17,25},{25,1},{2,10},{10... | collective-permute-start | bytes 12296 | tf_op jit(solution)/shard_map/ppermute | solution.py:19
  202.7 4.8 %collective-permute-start.22 = (f32[2,64,1,130]{3,1,2,0:T(8,128)S(1)}, f32[2,64,1,130]{3,1,2,0:T(8,128)S(1)}, u32[]{:S(2)}, u32[]{:S(2)}) collective-permute-start(f32[2,64,1,130]{3,1,2,0:T(8,128)S(1)} %get-tuple-element.14), channel_id=1, source_target_pairs={{1,0},{2,1},{3,2},{4,3},{5,4},{6,5},{7,6},{0,7},{9,8},{10,9},{11,1... | collective-permute-start | bytes 199688 | tf_op jit(solution)/shard_map/ppermute | solution.py:22
  204.4 6.2 %collective-permute-start.23 = (f32[2,64,1,130]{3,1,2,0:T(8,128)S(1)}, f32[2,64,1,130]{3,1,2,0:T(8,128)S(1)}, u32[]{:S(2)}, u32[]{:S(2)}) collective-permute-start(f32[2,64,1,130]{3,1,2,0:T(8,128)S(1)} %get-tuple-element.15), channel_id=1, source_target_pairs={{0,1},{1,2},{2,3},{3,4},{4,5},{5,6},{6,7},{7,0},{8,9},{9,10},{10,1... | collective-permute-start | bytes 199688 | tf_op jit(solution)/shard_map/ppermute | solution.py:19
  211.8 15.8 %collective-permute-start.28 = (f32[2,64,8,1]{3,1,2,0:T(8,128)S(1)}, f32[2,64,8,1]{3,1,2,0:T(8,128)S(1)}, u32[]{:S(2)}, u32[]{:S(2)}) collective-permute-start(f32[2,64,8,1]{3,1,2,0:T(8,128)S(1)} %get-tuple-element.59), channel_id=1, source_target_pairs={{0,8},{8,16},{16,24},{24,0},{1,9},{9,17},{17,25},{25,1},{2,10},{10... | collective-permute-start | bytes 12296 | tf_op jit(solution)/shard_map/ppermute | solution.py:19
  213.6 20.4 %collective-permute-start.29 = (f32[2,64,8,1]{3,1,2,0:T(8,128)S(1)}, f32[2,64,8,1]{3,1,2,0:T(8,128)S(1)}, u32[]{:S(2)}, u32[]{:S(2)}) collective-permute-start(f32[2,64,8,1]{3,1,2,0:T(8,128)S(1)} %get-tuple-element.60), channel_id=1, source_target_pairs={{8,0},{16,8},{24,16},{0,24},{9,1},{17,9},{25,17},{1,25},{10,2},{18... | collective-permute-start | bytes 12296 | tf_op jit(solution)/shard_map/ppermute | solution.py:22
  234.1 6.4 %collective-permute-start.30 = (f32[2,64,1,130]{3,1,2,0:T(8,128)S(1)}, f32[2,64,1,130]{3,1,2,0:T(8,128)S(1)}, u32[]{:S(2)}, u32[]{:S(2)}) collective-permute-start(f32[2,64,1,130]{3,1,2,0:T(8,128)S(1)} %get-tuple-element.12), channel_id=1, source_target_pairs={{0,1},{1,2},{2,3},{3,4},{4,5},{5,6},{6,7},{7,0},{8,9},{9,10},{10,1... | collective-permute-start | bytes 199688 | tf_op jit(solution)/shard_map/ppermute | solution.py:19
  234.2 6.3 %collective-permute-start.31 = (f32[2,64,1,130]{3,1,2,0:T(8,128)S(1)}, f32[2,64,1,130]{3,1,2,0:T(8,128)S(1)}, u32[]{:S(2)}, u32[]{:S(2)}) collective-permute-start(f32[2,64,1,130]{3,1,2,0:T(8,128)S(1)} %get-tuple-element.13), channel_id=1, source_target_pairs={{1,0},{2,1},{3,2},{4,3},{5,4},{6,5},{7,6},{0,7},{9,8},{10,9},{11,1... | collective-permute-start | bytes 199688 | tf_op jit(solution)/shard_map/ppermute | solution.py:22
  244.4 14.8 %collective-permute-start.32 = (f32[2,64,8,1]{3,1,2,0:T(8,128)S(1)}, f32[2,64,8,1]{3,1,2,0:T(8,128)S(1)}, u32[]{:S(2)}, u32[]{:S(2)}) collective-permute-start(f32[2,64,8,1]{3,1,2,0:T(8,128)S(1)} %get-tuple-element.58), channel_id=1, source_target_pairs={{8,0},{16,8},{24,16},{0,24},{9,1},{17,9},{25,17},{1,25},{10,2},{18... | collective-permute-start | bytes 12296 | tf_op jit(solution)/shard_map/ppermute | solution.py:22
  245.8 24.6 %collective-permute-start.33 = (f32[2,64,8,1]{3,1,2,0:T(8,128)S(1)}, f32[2,64,8,1]{3,1,2,0:T(8,128)S(1)}, u32[]{:S(2)}, u32[]{:S(2)}) collective-permute-start(f32[2,64,8,1]{3,1,2,0:T(8,128)S(1)} %get-tuple-element.57), channel_id=1, source_target_pairs={{0,8},{8,16},{16,24},{24,0},{1,9},{9,17},{17,25},{25,1},{2,10},{10... | collective-permute-start | bytes 12296 | tf_op jit(solution)/shard_map/ppermute | solution.py:19
  270.6 4.0 %collective-permute-start.34 = (f32[2,64,1,130]{3,1,2,0:T(8,128)S(1)}, f32[2,64,1,130]{3,1,2,0:T(8,128)S(1)}, u32[]{:S(2)}, u32[]{:S(2)}) collective-permute-start(f32[2,64,1,130]{3,1,2,0:T(8,128)S(1)} %get-tuple-element.10), channel_id=1, source_target_pairs={{1,0},{2,1},{3,2},{4,3},{5,4},{6,5},{7,6},{0,7},{9,8},{10,9},{11,1... | collective-permute-start | bytes 199688 | tf_op jit(solution)/shard_map/ppermute | solution.py:22
  271.1 6.2 %collective-permute-start.35 = (f32[2,64,1,130]{3,1,2,0:T(8,128)S(1)}, f32[2,64,1,130]{3,1,2,0:T(8,128)S(1)}, u32[]{:S(2)}, u32[]{:S(2)}) collective-permute-start(f32[2,64,1,130]{3,1,2,0:T(8,128)S(1)} %get-tuple-element.11), channel_id=1, source_target_pairs={{0,1},{1,2},{2,3},{3,4},{4,5},{5,6},{6,7},{7,0},{8,9},{9,10},{10,1... | collective-permute-start | bytes 199688 | tf_op jit(solution)/shard_map/ppermute | solution.py:19
where the time goes:
time: 279 us
  waiting for transfers between devices  198 us (71%)
  starting transfers between devices  47.8 us (17%)
  other arithmetic  27.1 us (10%)
  local copies, waits for them, and re-layouts  5.9 us (2%)
    ppermute x18, waiting for transfers between devices, padded_2(): lax.ppermute(lax.slice_in_dim(block, block.shape[dim] - width, None, axis...  116 us
    ppermute x18, waiting for transfers between devices, padded_2(): lax.ppermute(lax.slice_in_dim(block, 0, width, axis=dim), axis, backward)  81.2 us
    ppermute x18, starting transfers between devices, padded_2(): lax.ppermute(lax.slice_in_dim(block, 0, width, axis=dim), axis, backward)  36 us
    ppermute x18, starting transfers between devices, padded_2(): lax.ppermute(lax.slice_in_dim(block, block.shape[dim] - width, None, axis...  11.8 us
    sub x3, other arithmetic, potential_rim(): jnp.log(conc / (1.0 - conc)) + mix_energy * (1.0 - 2.0 * conc)  7.46 us
  transfers between devices with their start and end apart: 36, of which 24 were waited for; matrix products, arithmetic and copies ran while one was open for 7% of the time, Pallas kernels for 0%

commit v1 on v0

v1 whole, which is shorter than its diff:
```python
import functools

import jax
import jax.numpy as jnp
from jax import lax
from jax.experimental import pallas as pl
from jax.experimental.pallas import tpu as pltpu
from jax.sharding import PartitionSpec as P

mix_energy = 2.5
grad_energy = 1.0
time_step = 0.1
diff_step = 0.03
bath_potential = 0.5

pad = 16
chunk = 24
depth = 2
vmem_limit = 48 * 1024 * 1024
f32 = jnp.float32


def slots(steps):
    widths = [2 * steps] + [2 * steps - 2 * back for back in range(steps)] + [2 * steps - 1]
    starts = [sum(widths[:i]) for i in range(len(widths))]
    total = -(-sum(widths) // 8) * 8
    return list(zip(starts, widths)), total


def chunks(low, high):
    return [(at, min(chunk, high - at)) for at in range(low, high, chunk)]


def face_mask(shape, depth_z):
    lane = lax.broadcasted_iota(jnp.int32, shape, 1)
    return jnp.where(lane % depth_z == depth_z - 1, 0.0, 1.0).astype(f32)


def up(value):
    return pltpu.roll(value, value.shape[1] - 1, 1)


def down(value):
    return pltpu.roll(value, 1, 1)


def pack_kernel(steps, rows, cols, nz, conc_ref, adj_ref, rate_ref, conc_out, adj_out, rate_out,
                main_up, main_dn, late_up, late_dn, x_right, x_left):
    places, _ = slots(steps)
    lanes = adj_out.shape[2]
    half = cols // 2
    lower = lax.broadcasted_iota(jnp.int32, (half, lanes), 1) < nz

    def to_x(y, value, place):
        start, width = place
        x_right[y, start : start + width, :] = value[cols - width :, :]
        x_left[y, start : start + width, :] = value[:width, :]

    for y in range(rows):
        adj = adj_ref[pl.ds(y, lanes, stride=rows), :].T
        adj_out[y] = adj
        to_x(y, adj, places[0])
        rate = rate_ref[pl.ds(y, nz, stride=rows), :]
        rate = jnp.concatenate([rate] * (lanes // nz), axis=0).T
        rate_out[y] = rate
        to_x(y, rate, places[steps + 1])
        x_right[y, sum(places[-1]) :, :] = jnp.zeros((x_right.shape[1] - sum(places[-1]), lanes), f32)
        x_left[y, sum(places[-1]) :, :] = jnp.zeros((x_left.shape[1] - sum(places[-1]), lanes), f32)
        for side, at in ((main_dn, y), (main_up, y - rows + depth)):
            if 0 <= at < depth:
                side[pl.ds((depth + at) * cols, cols), :] = adj
        for side, edge in ((main_dn, 0), (main_up, rows - 1)):
            if y == edge:
                side[pl.ds(2 * depth * cols, half), :] = jnp.where(lower, rate[:half], rate[half:])
        for back in range(steps):
            conc = conc_ref[steps - 1 - back, pl.ds(y, lanes, stride=rows), :].T
            conc_out[back, y] = conc
            to_x(y, conc, places[1 + back])
            for main, late, at in ((main_dn, late_dn, y), (main_up, late_up, y - rows + depth)):
                if 0 <= at < depth:
                    if back == 0:
                        main[pl.ds(at * cols, cols), :] = conc
                    else:
                        late[pl.ds(((back - 1) * depth + at) * cols, cols), :] = conc


def gather_rows(out, place, rows, cols, own, low, high, x_low, x_high, c_low, c_high, rim):
    start, width = place
    right = pad + cols
    for y in range(rows):
        out[rim + y, pad:right, :] = own(y)
        out[rim + y, pad - width : pad, :] = x_low[y, start : start + width, :]
        out[rim + y, right : right + width, :] = x_high[y, start : start + width, :]
    for at in range(rim):
        for row, halo, corner, from_row in (
            (at, low, c_low, depth - rim + at),
            (rim + rows + at, high, c_high, at),
        ):
            out[row, pad:right, :] = halo(from_row)
            out[row, pad - width : pad, :] = corner[0, from_row, start : start + width, :]
            out[row, right : right + width, :] = corner[1, from_row, start : start + width, :]


def potentials(conc, mob, chem, curve, rows, cols, nz):
    low, high = pad - 8, pad + cols + 8
    lanes = conc.shape[2]

    def mob_row(y, _):
        for at, size in chunks(low - 8, high + 8):
            c = conc[y, at : at + size, :]
            mob[y, at : at + size, :] = c * (1.0 - c)
        return 0

    lax.fori_loop(0, rows + 2 * depth, mob_row, 0)

    def chem_row(y, _):
        for at, size in chunks(low, high):
            mask = face_mask((size, lanes), nz)
            c = conc[y + 1, at : at + size, :]
            inv = 1.0 / mob[y + 1, at : at + size, :]
            step_z = (up(c) - c) * mask
            lap = (
                (conc[y + 1, at + 1 : at + size + 1, :] + conc[y + 1, at - 1 : at + size - 1, :])
                + (conc[y, at : at + size, :] + conc[y + 2, at : at + size, :])
                - 4.0 * c
                + (step_z - down(step_z))
            )
            chem[y, at : at + size, :] = (
                jnp.log(c * c * inv) + mix_energy * (1.0 - 2.0 * c) - grad_energy * lap
            )
            curve[y, at : at + size, :] = inv - 2.0 * mix_energy
        return 0

    lax.fori_loop(0, rows + 2, chem_row, 0)


def advance(conc, mob, chem, curve, adj, rate, pot, part, grad, grad_in, rows, cols, nz):
    low, high = pad - 8, pad + cols + 8
    lanes = conc.shape[2]

    def work(y, at, size, own):
        mask = face_mask((size, lanes), nz)
        span = slice(at, at + size)
        a = adj[y + 1, span, :]
        m = mob[y + 1, span, :]
        total = None
        faces = None
        if own:
            mu = chem[y, span, :]
        sides = (
            (0, slice(at + 1, at + size + 1)),
            (0, slice(at - 1, at + size - 1)),
            (1, span),
            (-1, span),
        )
        for dy, cut in sides:
            diff = adj[y + 1 + dy, cut, :] - a
            flux = (mob[y + 1 + dy, cut, :] + m) * diff
            total = flux if total is None else total + flux
            if own:
                term = (chem[y + dy, cut, :] - mu) * diff
                faces = term if faces is None else faces + term
        diff = (up(a) - a) * mask
        flux = (up(m) + m) * diff
        total = total + (flux - down(flux))
        g = (0.5 * diff_step) * total - time_step * rate[y, span, :] * a
        pot[y, span, :] = g
        if own:
            term = (up(mu) - mu) * diff
            faces = faces + (term + down(term))
            c = conc[y + 1, span, :]
            part[y - 1, span, :] = (
                a + (1.0 - 2.0 * c) * ((-0.5 * diff_step) * faces) + curve[y, span, :] * g
            )
            gain = time_step * a * (bath_potential - mu)
            if grad_in is not None:
                gain = gain + grad_in[y - 1, span, :]
            grad[y - 1, span, :] = gain

    def own_row(y, _):
        for at, size in chunks(low, high):
            work(y + 1, at, size, True)
        return 0

    def edge_row(i, _):
        for at, size in chunks(low, high):
            work(i * (rows + 1), at, size, False)
        return 0

    lax.fori_loop(0, rows, own_row, 0)
    lax.fori_loop(0, 2, edge_row, 0)


def finish(pot, part, store, rows, low, high, nz):
    lanes = pot.shape[2]

    def row(y, _):
        for at, size in chunks(low, high):
            mask = face_mask((size, lanes), nz)
            span = slice(at, at + size)
            g = pot[y + 1, span, :]
            step_z = (up(g) - g) * mask
            lap = (
                (pot[y + 1, at + 1 : at + size + 1, :] + pot[y + 1, at - 1 : at + size - 1, :])
                + (pot[y, span, :] + pot[y + 2, span, :])
                - 4.0 * g
                + (step_z - down(step_z))
            )
            store(y, at, size, part[y, span, :] - grad_energy * lap)
        return 0

    lax.fori_loop(0, rows, row, 0)


def send_rows(adj_out, to_up, to_dn, rows, cols):
    low, high = pad - 8, pad + cols + 8
    for at in range(depth):
        to_dn[at] = adj_out[at, low:high, :]
        to_up[at] = adj_out[rows - depth + at, low:high, :]


def first_kernel(steps, rows, cols, nz, conc_own, adj_own, rate_own, from_dn, from_up, x_low, x_high,
                 c_low, c_high, adj_out, rate_ext, grad, to_up, to_dn,
                 conc, mob, chem, curve, adj, pot, part):
    places, _ = slots(steps)
    half = cols // 2
    lanes = conc.shape[2]
    lower = lax.broadcasted_iota(jnp.int32, (half, lanes), 1) < nz

    def rows_of(side, base):
        return lambda at: side[pl.ds((base + at) * cols, cols), :]

    def rate_of(side):
        def one(_):
            packed = side[pl.ds(2 * depth * cols, half), :]
            turned = pltpu.roll(packed, lanes // 2, 1)
            return jnp.concatenate(
                [jnp.where(lower, packed, turned), jnp.where(lower, turned, packed)], axis=0
            )

        return one

    sides = (x_low, x_high, c_low, c_high)
    gather_rows(conc, places[1], rows, cols, lambda y: conc_own[0, y], rows_of(from_dn, 0),
                rows_of(from_up, 0), *sides, depth)
    gather_rows(adj, places[0], rows, cols, lambda y: adj_own[y], rows_of(from_dn, depth),
                rows_of(from_up, depth), *sides, depth)
    gather_rows(rate_ext, places[steps + 1], rows, cols, lambda y: rate_own[y], rate_of(from_dn),
                rate_of(from_up), *sides, 1)
    potentials(conc, mob, chem, curve, rows, cols, nz)
    advance(conc, mob, chem, curve, adj, rate_ext, pot, part, grad, None, rows, cols, nz)

    def store(y, at, size, value):
        adj_out[y, at : at + size, :] = value

    finish(pot, part, store, rows, pad - 8, pad + cols + 8, nz)
    send_rows(adj_out, to_up, to_dn, rows, cols)


def prepare_kernel(steps, rows, cols, nz, back, conc_own, from_dn, from_up, x_low, x_high, c_low,
                   c_high, conc, mob, chem, curve):
    places, _ = slots(steps)

    def rows_of(side):
        return lambda at: side[pl.ds(((back - 1) * depth + at) * cols, cols), :]

    gather_rows(conc, places[1 + back], rows, cols, lambda y: conc_own[back, y], rows_of(from_dn),
                rows_of(from_up), x_low, x_high, c_low, c_high, depth)
    potentials(conc, mob, chem, curve, rows, cols, nz)


def extend(adj, own, from_dn, from_up, rows, cols):
    low, high = pad - 8, pad + cols + 8
    for y in range(rows):
        adj[depth + y, low:high, :] = own[y, low:high, :]
    for at in range(depth):
        adj[at, low:high, :] = from_dn[at]
        adj[depth + rows + at, low:high, :] = from_up[at]


def step_kernel(rows, cols, nz, conc, mob, chem, curve, own, from_dn, from_up, rate, grad_in,
                adj_out, grad, to_up, to_dn, adj, pot, part):
    extend(adj, own, from_dn, from_up, rows, cols)
    advance(conc, mob, chem, curve, adj, rate, pot, part, grad, grad_in, rows, cols, nz)

    def store(y, at, size, value):
        adj_out[y, at : at + size, :] = value

    finish(pot, part, store, rows, pad - 8, pad + cols + 8, nz)
    send_rows(adj_out, to_up, to_dn, rows, cols)


def last_kernel(rows, cols, nz, conc, mob, chem, curve, own, from_dn, from_up, rate, grad_in,
                adj_out, grad_out, adj, pot, part, grad, result):
    lanes = conc.shape[2]
    extend(adj, own, from_dn, from_up, rows, cols)
    advance(conc, mob, chem, curve, adj, rate, pot, part, grad, grad_in, rows, cols, nz)

    def store(y, at, size, value):
        result[y, at : at + size, :] = value

    finish(pot, part, store, rows, pad, pad + cols, nz)
    for y in range(rows):
        adj_out[pl.ds(y, lanes, stride=rows), :] = result[y, pad : pad + cols, :].T
        turned = grad[y, pad : pad + cols, :].T
        total = turned[:nz]
        for frame in range(1, lanes // nz):
            total = total + turned[frame * nz : (frame + 1) * nz]
        grad_out[pl.ds(y, nz, stride=rows), :] = total


def call(kernel, outs, scratch, *operands, cost=0):
    return pl.pallas_call(
        kernel,
        out_shape=[jax.ShapeDtypeStruct(shape, f32) for shape in outs],
        in_specs=[pl.BlockSpec(memory_space=pltpu.VMEM)] * len(operands),
        out_specs=[pl.BlockSpec(memory_space=pltpu.VMEM)] * len(outs),
        scratch_shapes=[pltpu.VMEM(shape, f32) for shape in scratch],
        compiler_params=pltpu.CompilerParams(vmem_limit_bytes=vmem_limit),
        cost_estimate=pl.CostEstimate(flops=cost, bytes_accessed=cost // 32, transcendentals=0),
    )(*operands)


def shift(value, axis, by):
    count = lax.axis_size(axis)
    return lax.ppermute(value, axis, [(i, (i + by) % count) for i in range(count)])


def shards(saved_conc, adjoint_end, rate_field):
    steps, frames, nz, rows, cols = saved_conc.shape
    lanes = frames * nz
    _, total = slots(steps)
    width = cols + 2 * pad
    sent = cols + 16
    flat = lanes * rows
    conc_own, adj_own, rate_own, main_up, main_dn, late_up, late_dn, x_right, x_left = call(
        functools.partial(pack_kernel, steps, rows, cols, nz),
        [(steps, rows, cols, lanes), (rows, cols, lanes), (rows, cols, lanes)]
        + [(2 * depth * cols + cols // 2, lanes)] * 2
        + [((steps - 1) * depth * cols, lanes)] * 2
        + [(rows, total, lanes)] * 2,
        [],
        saved_conc.reshape(steps, flat, cols),
        adjoint_end.reshape(flat, cols),
        rate_field.reshape(nz * rows, cols),
    )
    x_low = shift(x_right, "gx", 1)
    x_high = shift(x_left, "gx", -1)
    from_dn = shift(main_up, "gy", 1)
    from_up = shift(main_dn, "gy", -1)
    corner_up = jnp.stack([x_low[rows - depth :], x_high[rows - depth :]])
    corner_dn = jnp.stack([x_low[:depth], x_high[:depth]])
    c_low = shift(corner_up, "gy", 1)
    c_high = shift(corner_dn, "gy", -1)
    late_from_dn = shift(late_up, "gy", 1)
    late_from_up = shift(late_dn, "gy", -1)
    sides = (x_low, x_high, c_low, c_high)

    ext = (rows + 2 * depth, width, lanes)
    rim = (rows + 2, width, lanes)
    own = (rows, width, lanes)
    edge = (depth, sent, lanes)
    adj, rate, grad, to_up, to_dn = call(
        functools.partial(first_kernel, steps, rows, cols, nz),
        [own, rim, own, edge, edge],
        [ext, ext, rim, rim, ext, rim, own],
        conc_own, adj_own, rate_own, from_dn, from_up, *sides,
    )
    for back in range(1, steps):
        low, high = shift(to_up, "gy", 1), shift(to_dn, "gy", -1)
        fields = call(
            functools.partial(prepare_kernel, steps, rows, cols, nz, back),
            [ext, ext, rim, rim],
            [],
            conc_own, late_from_dn, late_from_up, *sides,
        )
        if back < steps - 1:
            adj, grad, to_up, to_dn = call(
                functools.partial(step_kernel, rows, cols, nz),
                [own, own, edge, edge],
                [ext, rim, own],
                *fields, adj, low, high, rate, grad,
            )
        else:
            adj, grad = call(
                functools.partial(last_kernel, rows, cols, nz),
                [(flat, cols), (nz * rows, cols)],
                [ext, rim, own, own, own],
                *fields, adj, low, high, rate, grad,
            )
    return adj.reshape(adjoint_end.shape), grad.reshape(rate_field.shape)


def solution(mesh):
    return jax.shard_map(
        shards,
        mesh=mesh,
        in_specs=(P(None, None, None, "gy", "gx"), P(None, None, "gy", "gx"), P(None, "gy", "gx")),
        out_specs=(P(None, None, "gy", "gx"), P(None, "gy", "gx")),
        check_vma=False,
    )
```

time: 279 us -> 56.2 us (0.20)
  waiting for transfers between devices: 198 us -> 12.5 us
  starting transfers between devices: 47.8 us -> 18.4 us
  other arithmetic: 27.1 us -> 0.01 us
  Pallas kernels: 0 us -> 20.3 us
    ppermute x36 -> x12, waiting for transfers between devices: 198 us -> 12.5 us  [shift(): lax.ppermute(value, axis, [(i, (i + by) % count) for i in range(count)])]
    ppermute x36 -> x12, starting transfers between devices: 47.8 us -> 18.4 us  [shift(): lax.ppermute(value, axis, [(i, (i + by) % count) for i in range(count)])]
    pallas_call x0 -> x6, Pallas kernels: none -> 20.3 us  [call(): pl.pallas_call(kernel, out_shape=[jax.ShapeDtypeStruct(shape, f32) for sh...]
    sub x12 -> x0, other arithmetic: 11.5 us -> none  [the longest x3 7.46 us: potential_rim(): jnp.log(conc / (1.0 - conc)) + mix_energy * (1.0 - 2.0 * conc)]
    mul x13 -> x0, other arithmetic: 9.78 us -> none  [the longest x3 2.95 us: face_rim(): -0.5 * (chem[..., 1:, 1:-1] - chem[..., :-1, 1:-1])]
    slice x10 -> x0, local copies, waits for them, and re-layouts: 3.33 us -> none  [the longest x9 1.87 us: padded_2(): lax.slice_in_dim(block, block.shape[dim] - width, None, axis=dim)]
  transfers between devices with their start and end apart: 36 -> 12, of which waited for: 24 -> 3; matrix products, arithmetic and copies ran while one was open for 7% -> 0% of each run, Pallas kernels for 0% -> 16%
where the time goes in v1:
time: 56.2 us; the launch traced here: 55.9 us
  Pallas kernels  20.3 us (36%)
  starting transfers between devices  18.4 us (33%)
  waiting for transfers between devices  12.5 us (22%)
  local copies, waits for them, and re-layouts  3.91 us (7%)
  between operations  0.72 us (1%)
    pallas_call x6, Pallas kernels, call(): pl.pallas_call(kernel, out_shape=[jax.ShapeDtypeStruct(shape, f32) for sh...  20.3 us
    ppermute x12, starting transfers between devices, shift(): lax.ppermute(value, axis, [(i, (i + by) % count) for i in range(count)])  18.4 us
    ppermute x12, waiting for transfers between devices, shift(): lax.ppermute(value, axis, [(i, (i + by) % count) for i in range(count)])  12.5 us
    unnamed x8, local copies, waits for them, and re-layouts  3.9 us
  transfers between devices with their start and end apart: 12, of which 3 were waited for; matrix products, arithmetic and copies ran while one was open for 0% of the time, Pallas kernels for 16%

profile of v1, /device:TPU:0, one launch (start us, length us, event | category | flops | bytes accessed | tf_op | source)
XLA Modules:
  0.0 55.9 jit_solution(15312036849501729456)
XLA Ops:
  0.6 0.0 copy-start.2
  0.6 1.0 %copy-done.2 = f32[2,64,8,128]{3,2,1,0:T(8,128)S(1)} copy-done((f32[2,64,8,128]{3,2,1,0:T(8,128)S(1)}, f32[2,64,8,128]{3,2,1,0:T(8,128)}, u32[]{:S(2)}) %copy-start.2) | copy-done | bytes 524312
  1.7 0.0 copy-start.3
  1.7 0.9 %copy-done.3 = f32[64,8,128]{2,1,0:T(8,128)S(1)} copy-done((f32[64,8,128]{2,1,0:T(8,128)S(1)}, f32[64,8,128]{2,1,0:T(8,128)}, u32[]{:S(2)}) %copy-start.3) | copy-done | bytes 262168
  2.6 2.2 %shard_map.50 = (f32[3,8,128,128]{3,2,1,0:T(8,128)S(1)}, f32[8,128,128]{2,1,0:T(8,128)S(1)}, f32[8,128,128]{2,1,0:T(8,128)S(1)}, f32[576,128]{1,0:T(8,128)S(1)},...) custom-call(f32[3,1024,128]{2,1,0:T(8,128)} %bitcast.15, ...), custom_call_target="tpu_custom_call" | custom-call | tf_op jit(solution)/shard_map/pallas_call | solution.py:313
  4.8 3.0 %collective-permute-start.2 = (f32[8,24,128]{2,1,0:T(8,128)S(1)}, f32[8,24,128]{2,1,0:T(8,128)S(1)}, u32[]{:S(2)}, u32[]{:S(2)}) collective-permute-start(f32[8,24,128]{2,1,0:T(8,128)S(1)} %get-tuple-element.33), channel_id=1, source_target_pairs={{0,8},{8,16},{16,24},{24,0},{1,9},{9,17},{17,25},{25,1},{2,10},{10... | collective-permute-start | bytes 294920 | tf_op jit(solution)/shard_map/ppermute | solution.py:326
  7.8 1.0 %collective-permute-start.3 = (f32[8,24,128]{2,1,0:T(8,128)S(1)}, f32[8,24,128]{2,1,0:T(8,128)S(1)}, u32[]{:S(2)}, u32[]{:S(2)}) collective-permute-start(f32[8,24,128]{2,1,0:T(8,128)S(1)} %get-tuple-element.34), channel_id=1, source_target_pairs={{0,24},{8,0},{16,8},{24,16},{1,25},{9,1},{17,9},{25,17},{2,26},{10... | collective-permute-start | bytes 294920 | tf_op jit(solution)/shard_map/ppermute | solution.py:326
  8.8 0.0 collective-permute-start
  8.8 3.5 %collective-permute-start.1 = (f32[512,128]{1,0:T(8,128)S(1)}, f32[512,128]{1,0:T(8,128)S(1)}, u32[]{:S(2)}, u32[]{:S(2)}) collective-permute-start(f32[512,128]{1,0:T(8,128)S(1)} %get-tuple-element.32), channel_id=1, source_target_pairs={{0,7},{1,0},{2,1},{3,2},{4,3},{5,4},{6,5},{7,6},{8,15},{9,8},{10,9... | collective-permute-start | bytes 786440 | tf_op jit(solution)/shard_map/ppermute | solution.py:326
  12.3 0.0 collective-permute-start.6
  12.3 0.0 collective-permute-done.2.x_low
  12.3 3.5 %collective-permute-start.7 = (f32[576,128]{1,0:T(8,128)S(1)}, f32[576,128]{1,0:T(8,128)S(1)}, u32[]{:S(2)}, u32[]{:S(2)}) collective-permute-start(f32[576,128]{1,0:T(8,128)S(1)} %get-tuple-element.46), channel_id=1, source_target_pairs={{0,7},{1,0},{2,1},{3,2},{4,3},{5,4},{6,5},{7,6},{8,15},{9,8},{10,9... | collective-permute-start | bytes 884744 | tf_op jit(solution)/shard_map/ppermute | solution.py:326
  15.9 0.0 collective-permute-done.3.x_high
  15.9 0.1 collective-permute-start.4
  16.0 8.5 %collective-permute-done.4.c_low = f32[2,2,24,128]{3,2,1,0:T(8,128)S(1)} collective-permute-done((f32[2,2,24,128]{3,2,1,0:T(8,128)S(1)}, f32[2,2,24,128]{3,2,1,0:T(8,128)S(1)}, u32[]{:S(2)}, u32[]{:S(2)}) %collective-permute-start.4) | collective-permute-done | bytes 49184 | tf_op jit(solution)/shard_map/ppermute | solution.py:326
  24.5 0.0 collective-permute-start.5
  24.5 1.8 %collective-permute-done.5.c_high = f32[2,2,24,128]{3,2,1,0:T(8,128)S(1)} collective-permute-done((f32[2,2,24,128]{3,2,1,0:T(8,128)S(1)}, f32[2,2,24,128]{3,2,1,0:T(8,128)S(1)}, u32[]{:S(2)}, u32[]{:S(2)}) %collective-permute-start.5) | collective-permute-done | bytes 49184 | tf_op jit(solution)/shard_map/ppermute | solution.py:326
  26.3 0.0 collective-permute-done.6.from_dn
  26.3 0.0 collective-permute-done.7.from_up
  26.3 5.2 %shard_map.53 = (f32[8,160,128]{2,1,0:T(8,128)S(1)}, f32[10,160,128]{2,1,0:T(8,128)S(1)}, f32[8,160,128]{2,1,0:T(8,128)S(1)}, f32[2,144,128]{2,1,0:T(8,128)S(1)}, f32[2,144,128]{2,1,0:T(8,128)S(1)}) custom-call(f32[3,8,128,128]{3,2,1,0:T(8,128)S(1)} %get-tuple-element.30.conc_own, f32[8,128,128]{2,1,0:T(8,128)S(1)} %get-tuple-element.43.adj_own, ...), custom_call_target="tpu_custom_call" | custom-call | tf_op jit(solution)/shard_map/pallas_call | solution.py:313
  31.5 0.2 collective-permute-start.8
  31.7 3.4 %collective-permute-start.9 = (f32[2,144,128]{2,1,0:T(8,128)S(1)}, f32[2,144,128]{2,1,0:T(8,128)S(1)}, u32[]{:S(2)}, u32[]{:S(2)}) collective-permute-start(f32[2,144,128]{2,1,0:T(8,128)S(1)} %get-tuple-element.49), channel_id=1, source_target_pairs={{0,7},{1,0},{2,1},{3,2},{4,3},{5,4},{6,5},{7,6},{8,15},{9,8},{10,9... | collective-permute-start | bytes 442376 | tf_op jit(solution)/shard_map/ppermute | solution.py:326
  35.1 0.0 collective-permute-done.from_dn
  35.1 0.0 collective-permute-done.1.from_up
  35.1 1.8 %shard_map.52 = (f32[12,160,128]{2,1,0:T(8,128)S(1)}, f32[12,160,128]{2,1,0:T(8,128)S(1)}, f32[10,160,128]{2,1,0:T(8,128)S(1)}, f32[10,160,128]{2,1,0:T(8,128)S(1)}) custom-call(f32[3,8,128,128]{3,2,1,0:T(8,128)S(1)} %get-tuple-element.30.conc_own, f32[512,128]{1,0:T(8,128)S(1)} %collective-permute-done.from_dn, ...), custom_call_target="tpu_custom_call" | custom-call | tf_op jit(solution)/shard_map/pallas_call | solution.py:313
  36.9 0.0 copy-start
  36.9 0.9 %copy-done = f32[12,160,128]{2,1,0:T(8,128)} copy-done((f32[12,160,128]{2,1,0:T(8,128)}, f32[12,160,128]{2,1,0:T(8,128)S(1)}, u32[]{:S(2)}) %copy-start) | copy-done | bytes 983064
  37.9 0.0 copy-start.1
  37.9 1.0 %copy-done.1 = f32[12,160,128]{2,1,0:T(8,128)} copy-done((f32[12,160,128]{2,1,0:T(8,128)}, f32[12,160,128]{2,1,0:T(8,128)S(1)}, u32[]{:S(2)}) %copy-start.1) | copy-done | bytes 983064
  38.9 0.0 collective-permute-done.8.from_dn
  38.9 0.0 collective-permute-done.9.from_up
  38.9 4.9 %shard_map.54 = (f32[8,160,128]{2,1,0:T(8,128)S(1)}, f32[8,160,128]{2,1,0:T(8,128)S(1)}, f32[2,144,128]{2,1,0:T(8,128)S(1)}, f32[2,144,128]{2,1,0:T(8,128)S(1)}) custom-call(f32[12,160,128]{2,1,0:T(8,128)} %copy-done, f32[12,160,128]{2,1,0:T(8,128)} %copy-done.1, f32[10,160,128]{2,1,0:T(8,128)S(1)} %get-tuple-element.41.chem, ...), custom_call_target="tpu_custom_call" | custom-call | tf_op jit(solution)/shard_map/pallas_call | solution.py:313
  43.7 0.5 collective-permute-start.10
  44.2 3.1 %collective-permute-start.11 = (f32[2,144,128]{2,1,0:T(8,128)S(1)}, f32[2,144,128]{2,1,0:T(8,128)S(1)}, u32[]{:S(2)}, u32[]{:S(2)}) collective-permute-start(f32[2,144,128]{2,1,0:T(8,128)S(1)} %get-tuple-element.54), channel_id=1, source_target_pairs={{0,7},{1,0},{2,1},{3,2},{4,3},{5,4},{6,5},{7,6},{8,15},{9,8},{10,9... | collective-permute-start | bytes 442376 | tf_op jit(solution)/shard_map/ppermute | solution.py:326
  47.3 1.8 %shard_map.51 = (f32[12,160,128]{2,1,0:T(8,128)S(1)}, f32[12,160,128]{2,1,0:T(8,128)S(1)}, f32[10,160,128]{2,1,0:T(8,128)S(1)}, f32[10,160,128]{2,1,0:T(8,128)S(1)}) custom-call(f32[3,8,128,128]{3,2,1,0:T(8,128)S(1)} %get-tuple-element.30.conc_own, f32[512,128]{1,0:T(8,128)S(1)} %collective-permute-done.from_dn, ...), custom_call_target="tpu_custom_call" | custom-call | tf_op jit(solution)/shard_map/pallas_call | solution.py:313
  49.1 2.2 %collective-permute-done.10.from_dn = f32[2,144,128]{2,1,0:T(8,128)S(1)} collective-permute-done((f32[2,144,128]{2,1,0:T(8,128)S(1)}, f32[2,144,128]{2,1,0:T(8,128)S(1)}, u32[]{:S(2)}, u32[]{:S(2)}) %collective-permute-start.10) | collective-permute-done | bytes 147488 | tf_op jit(solution)/shard_map/ppermute | solution.py:326
  51.4 0.0 collective-permute-done.11.from_up
  51.4 4.6 %shard_map.55 = (f32[1024,128]{1,0:T(8,128)}, f32[512,128]{1,0:T(8,128)}) custom-call(f32[12,160,128]{2,1,0:T(8,128)S(1)} %get-tuple-element.35.conc, f32[12,160,128]{2,1,0:T(8,128)S(1)} %get-tuple-element.36.mob, f32[10,160,128]{2,1,0:T(8,128)S(1)} %get-tuple-element.37.chem, f32[10,160,128]{2,1,0:T(8,128)S(1)} %get-tuple-element.38.curve, ...), custom_call_target="tpu_custom_call" | custom-call | tf_op jit(solution)/shard_map/pallas_call | solution.py:313
  (4 shorter events, 0.0 us)
Async XLA Ops:
  0.6 1.0 %copy-start.2 = (f32[2,64,8,128]{3,2,1,0:T(8,128)S(1)}, f32[2,64,8,128]{3,2,1,0:T(8,128)}, u32[]{:S(2)}) copy-start(f32[2,64,8,128]{3,2,1,0:T(8,128)} %param.4) | copy-start | bytes 1572868
  1.7 0.9 %copy-start.3 = (f32[64,8,128]{2,1,0:T(8,128)S(1)}, f32[64,8,128]{2,1,0:T(8,128)}, u32[]{:S(2)}) copy-start(f32[64,8,128]{2,1,0:T(8,128)} %param.5) | copy-start | bytes 786436
  4.8 7.6 %collective-permute-start.2 = (f32[8,24,128]{2,1,0:T(8,128)S(1)}, f32[8,24,128]{2,1,0:T(8,128)S(1)}, u32[]{:S(2)}, u32[]{:S(2)}) collective-permute-start(f32[8,24,128]{2,1,0:T(8,128)S(1)} %get-tuple-element.33), channel_id=1, source_target_pairs={{0,8},{8,16},{16,24},{24,0},{1,9},{9,17},{17,25},{25,1},{2,10},{10... | collective-permute-start | bytes 294920 | tf_op jit(solution)/shard_map/ppermute | solution.py:326
  7.8 8.1 %collective-permute-start.3 = (f32[8,24,128]{2,1,0:T(8,128)S(1)}, f32[8,24,128]{2,1,0:T(8,128)S(1)}, u32[]{:S(2)}, u32[]{:S(2)}) collective-permute-start(f32[8,24,128]{2,1,0:T(8,128)S(1)} %get-tuple-element.34), channel_id=1, source_target_pairs={{0,24},{8,0},{16,8},{24,16},{1,25},{9,1},{17,9},{25,17},{2,26},{10... | collective-permute-start | bytes 294920 | tf_op jit(solution)/shard_map/ppermute | solution.py:326
  8.8 26.3 %collective-permute-start = (f32[512,128]{1,0:T(8,128)S(1)}, f32[512,128]{1,0:T(8,128)S(1)}, u32[]{:S(2)}, u32[]{:S(2)}) collective-permute-start(f32[512,128]{1,0:T(8,128)S(1)} %get-tuple-element.31), channel_id=1, source_target_pairs={{0,1},{1,2},{2,3},{3,4},{4,5},{5,6},{6,7},{7,0},{8,9},{9,10},{10,1... | collective-permute-start | bytes 786440 | tf_op jit(solution)/shard_map/ppermute | solution.py:326
  8.8 26.3 %collective-permute-start.1 = (f32[512,128]{1,0:T(8,128)S(1)}, f32[512,128]{1,0:T(8,128)S(1)}, u32[]{:S(2)}, u32[]{:S(2)}) collective-permute-start(f32[512,128]{1,0:T(8,128)S(1)} %get-tuple-element.32), channel_id=1, source_target_pairs={{0,7},{1,0},{2,1},{3,2},{4,3},{5,4},{6,5},{7,6},{8,15},{9,8},{10,9... | collective-permute-start | bytes 786440 | tf_op jit(solution)/shard_map/ppermute | solution.py:326
  12.3 13.9 %collective-permute-start.6 = (f32[576,128]{1,0:T(8,128)S(1)}, f32[576,128]{1,0:T(8,128)S(1)}, u32[]{:S(2)}, u32[]{:S(2)}) collective-permute-start(f32[576,128]{1,0:T(8,128)S(1)} %get-tuple-element.45), channel_id=1, source_target_pairs={{0,1},{1,2},{2,3},{3,4},{4,5},{5,6},{6,7},{7,0},{8,9},{9,10},{10,1... | collective-permute-start | bytes 884744 | tf_op jit(solution)/shard_map/ppermute | solution.py:326
  12.3 13.9 %collective-permute-start.7 = (f32[576,128]{1,0:T(8,128)S(1)}, f32[576,128]{1,0:T(8,128)S(1)}, u32[]{:S(2)}, u32[]{:S(2)}) collective-permute-start(f32[576,128]{1,0:T(8,128)S(1)} %get-tuple-element.46), channel_id=1, source_target_pairs={{0,7},{1,0},{2,1},{3,2},{4,3},{5,4},{6,5},{7,6},{8,15},{9,8},{10,9... | collective-permute-start | bytes 884744 | tf_op jit(solution)/shard_map/ppermute | solution.py:326
  15.9 8.6 %collective-permute-start.4 = (f32[2,2,24,128]{3,2,1,0:T(8,128)S(1)}, f32[2,2,24,128]{3,2,1,0:T(8,128)S(1)}, u32[]{:S(2)}, u32[]{:S(2)}) collective-permute-start(f32[2,2,24,128]{3,2,1,0:T(8,128)S(1)} %pad_maximum_fusion), channel_id=1, source_target_pairs={{0,1},{1,2},{2,3},{3,4},{4,5},{5,6},{6,7},{7,0},{8,9},{9,10},{10,1... | collective-permute-start | bytes 147464 | tf_op jit(solution)/shard_map/ppermute | solution.py:326
  24.5 1.8 %collective-permute-start.5 = (f32[2,2,24,128]{3,2,1,0:T(8,128)S(1)}, f32[2,2,24,128]{3,2,1,0:T(8,128)S(1)}, u32[]{:S(2)}, u32[]{:S(2)}) collective-permute-start(f32[2,2,24,128]{3,2,1,0:T(8,128)S(1)} %pad_maximum_fusion.1), channel_id=1, source_target_pairs={{0,7},{1,0},{2,1},{3,2},{4,3},{5,4},{6,5},{7,6},{8,15},{9,8},{10,9... | collective-permute-start | bytes 147464 | tf_op jit(solution)/shard_map/ppermute | solution.py:326
  31.5 7.4 %collective-permute-start.8 = (f32[2,144,128]{2,1,0:T(8,128)S(1)}, f32[2,144,128]{2,1,0:T(8,128)S(1)}, u32[]{:S(2)}, u32[]{:S(2)}) collective-permute-start(f32[2,144,128]{2,1,0:T(8,128)S(1)} %get-tuple-element.48), channel_id=1, source_target_pairs={{0,1},{1,2},{2,3},{3,4},{4,5},{5,6},{6,7},{7,0},{8,9},{9,10},{10,1... | collective-permute-start | bytes 442376 | tf_op jit(solution)/shard_map/ppermute | solution.py:326
  31.7 7.2 %collective-permute-start.9 = (f32[2,144,128]{2,1,0:T(8,128)S(1)}, f32[2,144,128]{2,1,0:T(8,128)S(1)}, u32[]{:S(2)}, u32[]{:S(2)}) collective-permute-start(f32[2,144,128]{2,1,0:T(8,128)S(1)} %get-tuple-element.49), channel_id=1, source_target_pairs={{0,7},{1,0},{2,1},{3,2},{4,3},{5,4},{6,5},{7,6},{8,15},{9,8},{10,9... | collective-permute-start | bytes 442376 | tf_op jit(solution)/shard_map/ppermute | solution.py:326
  36.9 1.0 %copy-start = (f32[12,160,128]{2,1,0:T(8,128)}, f32[12,160,128]{2,1,0:T(8,128)S(1)}, u32[]{:S(2)}) copy-start(f32[12,160,128]{2,1,0:T(8,128)S(1)} %get-tuple-element.39.conc) | copy-start | bytes 2949124
  37.9 1.0 %copy-start.1 = (f32[12,160,128]{2,1,0:T(8,128)}, f32[12,160,128]{2,1,0:T(8,128)S(1)}, u32[]{:S(2)}) copy-start(f32[12,160,128]{2,1,0:T(8,128)S(1)} %get-tuple-element.40.mob) | copy-start | bytes 2949124
  43.7 7.6 %collective-permute-start.10 = (f32[2,144,128]{2,1,0:T(8,128)S(1)}, f32[2,144,128]{2,1,0:T(8,128)S(1)}, u32[]{:S(2)}, u32[]{:S(2)}) collective-permute-start(f32[2,144,128]{2,1,0:T(8,128)S(1)} %get-tuple-element.53), channel_id=1, source_target_pairs={{0,1},{1,2},{2,3},{3,4},{4,5},{5,6},{6,7},{7,0},{8,9},{9,10},{10,1... | collective-permute-start | bytes 442376 | tf_op jit(solution)/shard_map/ppermute | solution.py:326
  44.2 7.1 %collective-permute-start.11 = (f32[2,144,128]{2,1,0:T(8,128)S(1)}, f32[2,144,128]{2,1,0:T(8,128)S(1)}, u32[]{:S(2)}, u32[]{:S(2)}) collective-permute-start(f32[2,144,128]{2,1,0:T(8,128)S(1)} %get-tuple-element.54), channel_id=1, source_target_pairs={{0,7},{1,0},{2,1},{3,2},{4,3},{5,4},{6,5},{7,6},{8,15},{9,8},{10,9... | collective-permute-start | bytes 442376 | tf_op jit(solution)/shard_map/ppermute | solution.py:326

commit v2 on v0

v2 whole, which is shorter than its diff:
```python
import functools

import jax
import jax.numpy as jnp
from jax import lax
from jax.experimental import pallas as pl
from jax.experimental.pallas import tpu as pltpu
from jax.sharding import PartitionSpec as P

mix_energy = 2.5
grad_energy = 1.0
time_step = 0.1
diff_step = 0.03
bath_potential = 0.5

pad = 16
chunk = 24
depth = 2
vmem_limit = 20 * 1024 * 1024
far_limit = 20 * 1024 * 1024
f32 = jnp.float32


def slots(steps):
    widths = [2 * steps] + [2 * steps - 2 * back for back in range(steps)] + [2 * steps - 1]
    starts = [sum(widths[:i]) for i in range(len(widths))]
    total = -(-sum(widths) // 8) * 8
    return list(zip(starts, widths)), total


def early(steps):
    return (1 + min(steps, 2)) * depth


def chunks(low, high):
    return [(at, min(chunk, high - at)) for at in range(low, high, chunk)]


def reach(cols):
    return pad - 8, pad + cols + 8


def up(value):
    return pltpu.roll(value, value.shape[1] - 1, 1)


def down(value):
    return pltpu.roll(value, 1, 1)


def face_mask(size, lanes, nz):
    lane = lax.broadcasted_iota(jnp.int32, (size, lanes), 1)
    return jnp.where(lane % nz == nz - 1, 0.0, 1.0).astype(f32)


def row_of(ref, y):
    return lambda dy, cut: ref[y + dy, cut, :]


def laplace(field, at, size, mask):
    span = slice(at, at + size)
    here = field(0, span)
    step_z = (up(here) - here) * mask
    sides = field(0, slice(at + 1, at + size + 1)) + field(0, slice(at - 1, at + size - 1))
    return here, (
        (sides + (field(-1, span) + field(1, span))) - 4.0 * here + (step_z - down(step_z))
    )


def chem_row(conc, chem, curve, at, size, mask):
    c, lap = laplace(conc, at, size, mask)
    inv = 1.0 / (c * (1.0 - c))
    span = slice(at, at + size)
    chem(span, jnp.log(c * c * inv) + mix_energy * (1.0 - 2.0 * c) - grad_energy * lap)
    curve(span, inv - 2.0 * mix_energy)


def face_sums(adj, mob, chem, at, size, mask):
    span = slice(at, at + size)
    a = adj(0, span)
    m = None if mob is None else mob(0, span)
    mu = None if chem is None else chem(0, span)
    flow = pair = None
    for dy, cut in (
        (0, slice(at + 1, at + size + 1)),
        (0, slice(at - 1, at + size - 1)),
        (1, span),
        (-1, span),
    ):
        diff = adj(dy, cut) - a
        if mob is not None:
            term = (mob(dy, cut) + m) * diff
            flow = term if flow is None else flow + term
        if chem is not None:
            term = (chem(dy, cut) - mu) * diff
            pair = term if pair is None else pair + term
    diff = (up(a) - a) * mask
    if mob is not None:
        term = (up(m) + m) * diff
        flow = flow + (term - down(term))
    if chem is not None:
        term = (up(mu) - mu) * diff
        pair = pair + (term + down(term))
    return a, mu, flow, pair


def source(flow, rate, a):
    return (0.5 * diff_step) * flow - time_step * rate * a


def partial(a, c, pair, curve, g):
    return a + (1.0 - 2.0 * c) * ((-0.5 * diff_step) * pair) + curve * g


def gain(a, mu, before):
    value = time_step * a * (bath_potential - mu)
    return value if before is None else before + value


def set_row(ref, y):
    def put(span, value):
        ref[y, span, :] = value

    return put


def interior(rows, cols, nz, conc, mob, chem, curve, adj, rate, pot, part, grad, before, store):
    low, high = reach(cols)
    lanes = adj[0].shape[-1]

    def at_row(field, y):
        return row_of(field[0], field[1] + y)

    def body(y, _):
        for at, size in chunks(low, high):
            mask = face_mask(size, lanes, nz)
            span = slice(at, at + size)
            a, mu, flow, pair = face_sums(
                at_row(adj, y), at_row(mob, y), at_row(chem, y), at, size, mask
            )
            g = source(flow, at_row(rate, y)(0, span), a)
            pot[y - 1, span, :] = g
            part[y - depth, span, :] = partial(
                a, at_row(conc, y)(0, span), pair, at_row(curve, y)(0, span), g
            )
            old = None if before is None else before[y - depth, span, :]
            grad[y - depth, span, :] = gain(a, mu, old)
        return 0

    def edge(i, _):
        y = 1 + i * (rows - 3)
        for at, size in chunks(low, high):
            mask = face_mask(size, lanes, nz)
            a, _mu, flow, _pair = face_sums(at_row(adj, y), at_row(mob, y), None, at, size, mask)
            span = slice(at, at + size)
            pot[y - 1, span, :] = source(flow, at_row(rate, y)(0, span), a)
        return 0

    def close(y, _):
        for at, size in chunks(low, high):
            mask = face_mask(size, lanes, nz)
            span = slice(at, at + size)
            _g, lap = laplace(row_of(pot, y - 1), at, size, mask)
            store(y - depth, span, part[y - depth, span, :] - grad_energy * lap)
        return 0

    lax.fori_loop(depth, rows - depth, body, 0)
    lax.fori_loop(0, 2, edge, 0)
    lax.fori_loop(depth, rows - depth, close, 0)


def boundary(rows, cols, nz, conc, mob, chem, curve, adj, rate, pot, part, grad, before, store,
             fresh):
    low, high = reach(cols)
    lanes = adj[0].shape[-1]
    last = rows - 1

    def at_row(field, y):
        return row_of(field[0], field[1] + y)

    def mirror(s, y):
        return y + s * (last - 2 * y)

    if fresh:

        def mu_side(i, _):
            s, k = i // 2, i % 2
            y = mirror(s, k - 1)
            for at, size in chunks(low, high):
                chem_row(at_row(conc, y), set_row(chem[0], chem[1] + y),
                         set_row(curve[0], curve[1] + y), at, size, face_mask(size, lanes, nz))
            return 0

        lax.fori_loop(0, 4, mu_side, 0)

    def side(s, _):
        y = mirror(s, -1)
        for at, size in chunks(low, high):
            mask = face_mask(size, lanes, nz)
            span = slice(at, at + size)
            a, _mu, flow, _pair = face_sums(at_row(adj, y), at_row(mob, y), None, at, size, mask)
            pot[1 + y, span, :] = source(flow, rate[3 * s, span, :], a)
        y0 = mirror(s, 0)
        for at, size in chunks(low, high):
            mask = face_mask(size, lanes, nz)
            span = slice(at, at + size)
            a, mu, flow, pair = face_sums(
                at_row(adj, y0), at_row(mob, y0), at_row(chem, y0), at, size, mask
            )
            g = source(flow, rate[1 + s, span, :], a)
            pot[1 + y0, span, :] = g
            part[s, 0, span, :] = partial(
                a, at_row(conc, y0)(0, span), pair, at_row(curve, y0)(0, span), g
            )
            old = None if before is None else before[s, 0, span, :]
            grad[s, 0, span, :] = gain(a, mu, old)
        y1 = mirror(s, 1)
        for at, size in chunks(low, high):
            mask = face_mask(size, lanes, nz)
            span = slice(at, at + size)
            a, mu, _flow, pair = face_sums(at_row(adj, y1), None, at_row(chem, y1), at, size, mask)
            part[s, 1, span, :] = partial(
                a, at_row(conc, y1)(0, span), pair, at_row(curve, y1)(0, span), pot[1 + y1, span, :]
            )
            old = None if before is None else before[s, 1, span, :]
            grad[s, 1, span, :] = gain(a, mu, old)
        return 0

    lax.fori_loop(0, 2, side, 0)

    def close(i, _):
        s, k = i // 2, i % 2
        y = mirror(s, k)
        for at, size in chunks(low, high):
            mask = face_mask(size, lanes, nz)
            span = slice(at, at + size)
            _g, lap = laplace(row_of(pot, 1 + y), at, size, mask)
            store(s, k, span, part[s, k, span, :] - grad_energy * lap)
        return 0

    lax.fori_loop(0, 4, close, 0)


def sides_of(rows):
    return [(0, 0, 0), (0, 1, 1), (1, 0, rows - 1), (1, 1, rows - 2)]


def pack_kernel(steps, rows, cols, nz, conc_hbm, adj_hbm, rate_hbm, conc_out, adj_out, rate_out,
                main_up, main_dn, x_right, x_left, conc_in, adj_in, rate_in, sems):
    places, total = slots(steps)
    lanes = adj_out.shape[2]
    half = cols // 2
    lower = lax.broadcasted_iota(jnp.int32, (half, lanes), 1) < nz
    copies = [
        pltpu.make_async_copy(adj_hbm, adj_in, sems.at[0]),
        pltpu.make_async_copy(rate_hbm, rate_in, sems.at[1]),
    ] + [
        pltpu.make_async_copy(conc_hbm.at[steps - 1 - back], conc_in.at[back], sems.at[2 + back])
        for back in range(steps)
    ]
    for copy in copies:
        copy.start()

    def to_x(y, value, place):
        start, width = place
        x_right[y, start : start + width, :] = value[cols - width :, :]
        x_left[y, start : start + width, :] = value[:width, :]

    used = sum(places[-1])
    copies[0].wait()
    for y in range(rows):
        adj = adj_in[pl.ds(y, lanes, stride=rows), :].T
        adj_out[y] = adj
        to_x(y, adj, places[0])
        for side, at in ((main_dn, y), (main_up, y - rows + depth)):
            if 0 <= at < depth:
                side[pl.ds(at * cols, cols), :] = adj
    copies[1].wait()
    for y in range(rows):
        rate = rate_in[pl.ds(y, nz, stride=rows), :]
        rate = jnp.concatenate([rate] * (lanes // nz), axis=0).T
        rate_out[y] = rate
        to_x(y, rate, places[steps + 1])
        if used < total:
            x_right[y, used:, :] = jnp.zeros((total - used, lanes), f32)
            x_left[y, used:, :] = jnp.zeros((total - used, lanes), f32)
        for side, edge in ((main_dn, 0), (main_up, rows - 1)):
            if y == edge:
                side[pl.ds(early(steps) * cols, half), :] = jnp.where(
                    lower, rate[:half], rate[half:]
                )
    for back in range(steps):
        copies[2 + back].wait()
        for y in range(rows):
            conc = conc_in[back, pl.ds(y, lanes, stride=rows), :].T
            conc_out[back, y] = conc
            to_x(y, conc, places[1 + back])
            if back < 2:
                for side, at in ((main_dn, y), (main_up, y - rows + depth)):
                    if 0 <= at < depth:
                        side[pl.ds(((1 + back) * depth + at) * cols, cols), :] = conc


def put_own(out, row, value, y, place, cols, x_low, x_high):
    start, width = place
    right = pad + cols
    out[row, pad:right, :] = value
    out[row, pad - width : pad, :] = x_low[y, start : start + width, :]
    out[row, right : right + width, :] = x_high[y, start : start + width, :]


def put_halo(out, row, value, from_row, place, cols, corner):
    start, width = place
    right = pad + cols
    out[row, pad:right, :] = value
    out[row, pad - width : pad, :] = corner[0, from_row, start : start + width, :]
    out[row, right : right + width, :] = corner[1, from_row, start : start + width, :]


def corner_kernel(rows, x_low, x_high, to_up, to_dn):
    for i, side in enumerate((x_low, x_high)):
        to_up[i] = side[rows - depth :]
        to_dn[i] = side[:depth]


def first_interior(steps, rows, cols, nz, conc_own, adj_own, rate_own, x_low, x_high, edge_up,
                   edge_dn,
                   conc, adj, rate, chem, curve, pot, out, grad, mob, part):
    places, _ = slots(steps)
    low, high = reach(cols)
    lanes = adj.shape[2]
    for y in range(rows):
        at, low_x, high_x = y, x_low, x_high
        if y < depth:
            low_x, high_x = edge_dn.at[0], edge_dn.at[1]
        elif y >= rows - depth:
            at, low_x, high_x = y - rows + depth, edge_up.at[0], edge_up.at[1]
        put_own(conc, y, conc_own[0, y], at, places[1], cols, low_x, high_x)
        put_own(adj, y, adj_own[y], at, places[0], cols, low_x, high_x)
        put_own(rate, y, rate_own[y], at, places[steps + 1], cols, low_x, high_x)
    def mob_row(y, _):
        for at, size in chunks(low - 8, high + 8):
            c = conc[y, at : at + size, :]
            mob[y, at : at + size, :] = c * (1.0 - c)
        return 0

    def mu_row(y, _):
        for at, size in chunks(low, high):
            chem_row(row_of(conc, y), set_row(chem, y - 1), set_row(curve, y - 1), at, size,
                     face_mask(size, lanes, nz))
        return 0

    lax.fori_loop(0, rows, mob_row, 0)
    lax.fori_loop(1, rows - 1, mu_row, 0)

    def store(k, span, value):
        out[k, span, :] = value

    interior(rows, cols, nz, (conc, 0), (mob, 0), (chem, -1), (curve, -1), (adj, 0), (rate, 0),
             pot, part, grad, None, store)


def copy_rows(pairs):
    for out, to, ref, at in pairs:
        out[to] = ref[at]


def send_rows(out, to_up, to_dn, cols):
    low, high = reach(cols)
    for k in range(depth):
        to_dn[k] = out[0, k, low:high, :]
        to_up[depth - 1 - k] = out[1, k, low:high, :]


def first_boundary(steps, rows, cols, nz, conc_in, adj_in, rate_in, chem_in, curve_in, pot_in,
                   from_dn, from_up, c_low, c_high,
                   out, grad, rate, to_up, to_dn, conc, adj, mob, chem, curve, pot, part):
    places, _ = slots(steps)
    low, high = reach(cols)
    half = cols // 2
    lanes = conc.shape[2]
    lower = lax.broadcasted_iota(jnp.int32, (half, lanes), 1) < nz

    def unpack(side):
        packed = side[pl.ds(early(steps) * cols, half), :]
        turned = pltpu.roll(packed, lanes // 2, 1)
        return jnp.concatenate(
            [jnp.where(lower, packed, turned), jnp.where(lower, turned, packed)], axis=0
        )

    near = [0, 1, 2, rows - 3, rows - 2, rows - 1]
    for y in near:
        conc[depth + y] = conc_in[y]
        adj[depth + y] = adj_in[y]
    for y in (1, 2, rows - 3, rows - 2):
        chem[1 + y] = chem_in[y - 1]
        pot[1 + y] = pot_in[y - 1]
    for y in (1, rows - 2):
        curve[1 + y] = curve_in[y - 1]
    for at in range(depth):
        for ref, place, base in ((conc, places[1], depth), (adj, places[0], 0)):
            rows_in = pl.ds((base + at) * cols, cols)
            put_halo(ref, at, from_dn[rows_in, :], at, place, cols, c_low)
            put_halo(ref, depth + rows + at, from_up[rows_in, :], at, place, cols, c_high)
    put_halo(rate, 0, unpack(from_dn), depth - 1, places[steps + 1], cols, c_low)
    rate[1] = rate_in[0]
    rate[2] = rate_in[rows - 1]
    put_halo(rate, 3, unpack(from_up), 0, places[steps + 1], cols, c_high)
    for row in [0, 1, 2, 3, rows, rows + 1, rows + 2, rows + 3]:
        for at, size in chunks(low - 8, high + 8):
            c = conc[row, at : at + size, :]
            mob[row, at : at + size, :] = c * (1.0 - c)

    def store(s, k, span, value):
        out[s, k, span, :] = value

    boundary(rows, cols, nz, (conc, depth), (mob, depth), (chem, 1), (curve, 1), (adj, depth),
             rate, pot, part, grad, None, store, True)
    send_rows(out, to_up, to_dn, cols)


def prepare_kernel(steps, rows, cols, nz, back, conc_own, from_dn, from_up, x_low, x_high, c_low,
                   c_high, conc, mob, chem, curve, *late):
    places, _ = slots(steps)
    low, high = reach(cols)
    lanes = conc.shape[2]
    place = places[1 + back]
    for y in range(rows):
        put_own(conc, depth + y, conc_own[back, y], y, place, cols, x_low, x_high)
    for at in range(depth):
        rows_in = pl.ds((((1 + back) if back < 2 else (back - 2)) * depth + at) * cols, cols)
        put_halo(conc, at, from_dn[rows_in, :], at, place, cols, c_low)
        put_halo(conc, depth + rows + at, from_up[rows_in, :], at, place, cols, c_high)

    if late:
        late_up, late_dn = late
        for after in range(2, steps):
            for at in range(depth):
                span = pl.ds(((after - 2) * depth + at) * cols, cols)
                late_dn[span, :] = conc_own[after, at]
                late_up[span, :] = conc_own[after, rows - depth + at]

    def mob_row(row, _):
        for at, size in chunks(low - 8, high + 8):
            c = conc[row, at : at + size, :]
            mob[row, at : at + size, :] = c * (1.0 - c)
        return 0

    def mu_row(row, _):
        for at, size in chunks(low, high):
            chem_row(row_of(conc, row + 1), set_row(chem, row), set_row(curve, row), at, size,
                     face_mask(size, lanes, nz))
        return 0

    lax.fori_loop(0, rows + 2 * depth, mob_row, 0)
    lax.fori_loop(0, rows + 2, mu_row, 0)


def next_interior(rows, cols, nz, final, conc, mob, chem, curve, rate, inner, outer, before,
                  *rest):
    if final:
        out, grad_out, pot, adj, part, grad, result = rest
    else:
        result, grad, pot, adj, part = rest
    for k in range(rows - 2 * depth):
        adj[depth + k] = inner[k]
    for s, k, y in sides_of(rows):
        adj[y] = outer[s, k]

    def store(k, span, value):
        result[k, span, :] = value

    interior(rows, cols, nz, (conc, depth), (mob, depth), (chem, 1), (curve, 1), (adj, 0),
             (rate, 0), pot, part, grad, before, store)
    if final:
        for k in range(rows - 2 * depth):
            out[k] = result[k, pad : pad + cols, :].T
            grad_out[k] = fold(grad[k, pad : pad + cols, :].T, nz)


def fold(value, nz):
    total = value[:nz]
    for frame in range(1, value.shape[0] // nz):
        total = total + value[frame * nz : (frame + 1) * nz]
    return total


def next_boundary(rows, cols, nz, final, conc, mob, chem, curve, rate, inner, outer, pot_in,
                  before, from_dn, from_up, *rest):
    low, high = reach(cols)
    if final:
        inner_out, inner_grad, out, grad_out, adj, pot, part, grad, result = rest
    else:
        _conc_low, _conc_high, result, grad, to_up, to_dn, adj, pot, part = rest
    adj[2 * depth] = inner[0]
    adj[rows - 1] = inner[rows - 2 * depth - 1]
    for s, k, y in sides_of(rows):
        adj[depth + y] = outer[s, k]
    for at in range(depth):
        adj[at, low:high, :] = from_dn[at]
        adj[depth + rows + at, low:high, :] = from_up[at]
    for y in (1, 2, rows - 3, rows - 2):
        pot[1 + y] = pot_in[y - 1]

    def store(s, k, span, value):
        result[s, k, span, :] = value

    boundary(rows, cols, nz, (conc, depth), (mob, depth), (chem, 1), (curve, 1), (adj, depth),
             rate, pot, part, grad, before, store, False)
    if final:
        lanes = conc.shape[2]
        for k in range(rows - 2 * depth):
            out[pl.ds(depth + k, lanes, stride=rows), :] = inner_out[k]
            grad_out[pl.ds(depth + k, nz, stride=rows), :] = inner_grad[k]
        for s, k, y in sides_of(rows):
            out[pl.ds(y, lanes, stride=rows), :] = result[s, k, pad : pad + cols, :].T
            grad_out[pl.ds(y, nz, stride=rows), :] = fold(grad[s, k, pad : pad + cols, :].T, nz)
    else:
        send_rows(result, to_up, to_dn, cols)


def call(kernel, outs, scratch, *operands, cost=0, far=False):
    space = pltpu.HBM if far else pltpu.VMEM
    limit = far_limit if far else vmem_limit
    return pl.pallas_call(
        kernel,
        out_shape=[jax.ShapeDtypeStruct(shape, f32) for shape in outs],
        in_specs=[pl.BlockSpec(memory_space=space)] * len(operands),
        out_specs=[pl.BlockSpec(memory_space=pltpu.VMEM)] * len(outs),
        scratch_shapes=[pltpu.VMEM(s, f32) if isinstance(s, tuple) else s for s in scratch],
        compiler_params=pltpu.CompilerParams(vmem_limit_bytes=limit),
        cost_estimate=pl.CostEstimate(
            flops=cost * 1_000_000, bytes_accessed=cost * 2_000_000, transcendentals=0
        ),
    )(*operands)


def shift(value, axis, by):
    count = lax.axis_size(axis)
    return lax.ppermute(value, axis, [(i, (i + by) % count) for i in range(count)])


def shards(saved_conc, adjoint_end, rate_field):
    steps, frames, nz, rows, cols = saved_conc.shape
    lanes = frames * nz
    _, total = slots(steps)
    width = cols + 2 * pad
    flat = lanes * rows
    inside = rows - 2 * depth

    def field(count):
        return (count, width, lanes)

    conc_own, adj_own, rate_own, main_up, main_dn, x_right, x_left = call(
        functools.partial(pack_kernel, steps, rows, cols, nz),
        [(steps, rows, cols, lanes), (rows, cols, lanes), (rows, cols, lanes)]
        + [(early(steps) * cols + cols // 2, lanes)] * 2
        + [(rows, total, lanes)] * 2,
        [(steps, flat, cols), (flat, cols), (nz * rows, cols)]
        + [pltpu.SemaphoreType.DMA((2 + steps,))],
        saved_conc.reshape(steps, flat, cols),
        adjoint_end.reshape(flat, cols),
        rate_field.reshape(nz * rows, cols),
        cost=3,
        far=True,
    )
    x_low = shift(x_right, "gx", 1)
    x_high = shift(x_left, "gx", -1)
    from_dn = shift(main_up, "gy", 1)
    from_up = shift(main_dn, "gy", -1)
    corner_up, corner_dn = call(
        functools.partial(corner_kernel, rows), [(2, depth, total, lanes)] * 2, [], x_low, x_high
    )
    c_low = shift(corner_up, "gy", 1)
    c_high = shift(corner_dn, "gy", -1)

    conc, adj, rate_in, chem, curve, pot, inner, inner_grad = call(
        functools.partial(first_interior, steps, rows, cols, nz),
        [field(rows)] * 3 + [field(rows - 2)] * 3 + [field(inside)] * 2,
        [field(rows), field(inside)],
        conc_own, adj_own, rate_own, x_low, x_high, corner_up, corner_dn,
        cost=3,
    )

    both = (2, depth, width, lanes)
    edge = (depth, cols + 16, lanes)
    outer, outer_grad, rate, to_up, to_dn = call(
        functools.partial(first_boundary, steps, rows, cols, nz),
        [both, both, field(4), edge, edge],
        [field(rows + 2 * depth)] * 3 + [field(rows + 2)] * 3 + [both],
        conc, adj, rate_in, chem, curve, pot, from_dn, from_up, c_low, c_high,
        cost=2,
    )
    conc_low, conc_high = from_dn, from_up
    for back in range(1, steps):
        low, high = shift(to_up, "gy", 1), shift(to_dn, "gy", -1)
        final = back == steps - 1
        late = [((steps - 2) * depth * cols, lanes)] * 2 if back == 1 and steps > 2 else []
        fields = call(
            functools.partial(prepare_kernel, steps, rows, cols, nz, back),
            [field(rows + 2 * depth)] * 2 + [field(rows + 2)] * 2 + late,
            [],
            conc_own, conc_low, conc_high, x_low, x_high, c_low, c_high,
            cost=2,
        )
        if late:
            conc_low, conc_high = shift(fields[4], "gy", 1), shift(fields[5], "gy", -1)
            fields = fields[:4]
        tiles = [(inside, lanes, cols), (inside, nz, cols)]
        results = call(
            functools.partial(next_interior, rows, cols, nz, final),
            (tiles if final else [field(inside)] * 2) + [field(rows - 2)],
            [field(rows), field(inside)] + ([field(inside)] * 2 if final else []),
            *fields, rate_in, inner, outer, inner_grad,
            cost=3,
        )
        pot = results[2]
        if final:
            adj, grad = call(
                functools.partial(next_boundary, rows, cols, nz, final),
                [(flat, cols), (nz * rows, cols)],
                [field(rows + 2 * depth), field(rows + 2), both, both, both],
                *fields, rate, inner, outer, pot, outer_grad, low, high, results[0], results[1],
                cost=3,
            )
        else:
            new_outer, outer_grad, to_up, to_dn = call(
                functools.partial(next_boundary, rows, cols, nz, final),
                [both, both, edge, edge],
                [field(rows + 2 * depth), field(rows + 2), both],
                *fields, rate, inner, outer, pot, outer_grad, low, high, conc_low, conc_high,
                cost=2,
            )
            inner, inner_grad, outer = results[0], results[1], new_outer
    return adj.reshape(adjoint_end.shape), grad.reshape(rate_field.shape)


def solution(mesh):
    return jax.shard_map(
        shards,
        mesh=mesh,
        in_specs=(P(None, None, None, "gy", "gx"), P(None, None, "gy", "gx"), P(None, "gy", "gx")),
        out_specs=(P(None, None, "gy", "gx"), P(None, "gy", "gx")),
        check_vma=False,
    )
```

time: 279 us -> 52.3 us (0.19)
  waiting for transfers between devices: 198 us -> 5.33 us
  other arithmetic: 27.1 us -> 0 us
  starting transfers between devices: 47.8 us -> 22.1 us
  Pallas kernels: 0 us -> 20.5 us
    ppermute x36 -> x12, waiting for transfers between devices: 198 us -> 5.33 us  [shift(): lax.ppermute(value, axis, [(i, (i + by) % count) for i in range(count)])]
    ppermute x36 -> x12, starting transfers between devices: 47.8 us -> 22.1 us  [shift(): lax.ppermute(value, axis, [(i, (i + by) % count) for i in range(count)])]
    pallas_call x0 -> x10, Pallas kernels: none -> 20.5 us  [call(): pl.pallas_call(kernel, out_shape=[jax.ShapeDtypeStruct(shape, f32) for sh...]
    sub x12 -> x0, other arithmetic: 11.5 us -> none  [the longest x3 7.46 us: potential_rim(): jnp.log(conc / (1.0 - conc)) + mix_energy * (1.0 - 2.0 * conc)]
    mul x13 -> x0, other arithmetic: 9.78 us -> none  [the longest x3 2.95 us: face_rim(): -0.5 * (chem[..., 1:, 1:-1] - chem[..., :-1, 1:-1])]
    slice x10 -> x0, local copies, waits for them, and re-layouts: 3.33 us -> none  [the longest x9 1.87 us: padded_2(): lax.slice_in_dim(block, block.shape[dim] - width, None, axis=dim)]
  transfers between devices with their start and end apart: 36 -> 12, of which waited for: 24 -> 4; matrix products, arithmetic and copies ran while one was open for 7% -> 0% of each run, Pallas kernels for 0% -> 20%
where the time goes in v2:
time: 52.3 us; the launch traced here: 52.1 us
  starting transfers between devices  22.1 us (42%)
  Pallas kernels  20.5 us (39%)
  waiting for transfers between devices  5.33 us (10%)
  local copies, waits for them, and re-layouts  3.39 us (6%)
  between operations  0.79 us (2%)
    ppermute x12, starting transfers between devices, shift(): lax.ppermute(value, axis, [(i, (i + by) % count) for i in range(count)])  22.1 us
    pallas_call x10, Pallas kernels, call(): pl.pallas_call(kernel, out_shape=[jax.ShapeDtypeStruct(shape, f32) for sh...  20.5 us
    ppermute x12, waiting for transfers between devices, shift(): lax.ppermute(value, axis, [(i, (i + by) % count) for i in range(count)])  5.33 us
    unnamed x6, local copies, waits for them, and re-layouts  3.39 us
  transfers between devices with their start and end apart: 12, of which 4 were waited for; matrix products, arithmetic and copies ran while one was open for 0% of the time, Pallas kernels for 20%

profile of v2, /device:TPU:0, one launch (start us, length us, event | category | flops | bytes accessed | tf_op | source)
XLA Modules:
  0.0 52.1 jit_solution(3693183510531744970)
XLA Ops:
  0.6 0.0 copy-start
  0.6 1.4 %copy-done = f32[3,2,64,8,128]{4,3,2,1,0:T(8,128)S(1)} copy-done((f32[3,2,64,8,128]{4,3,2,1,0:T(8,128)S(1)}, f32[3,2,64,8,128]{4,3,2,1,0:T(8,128)}, u32[]{:S(2)}) %copy-start) | copy-done | bytes 1572888
  2.0 0.0 copy-start.1
  2.0 1.0 %copy-done.1 = f32[2,64,8,128]{3,2,1,0:T(8,128)S(1)} copy-done((f32[2,64,8,128]{3,2,1,0:T(8,128)S(1)}, f32[2,64,8,128]{3,2,1,0:T(8,128)}, u32[]{:S(2)}) %copy-start.1) | copy-done | bytes 524312
  3.1 0.0 copy-start.2
  3.1 0.9 %copy-done.2 = f32[64,8,128]{2,1,0:T(8,128)S(1)} copy-done((f32[64,8,128]{2,1,0:T(8,128)S(1)}, f32[64,8,128]{2,1,0:T(8,128)}, u32[]{:S(2)}) %copy-start.2) | copy-done | bytes 262168
  4.0 1.2 %shard_map.50 = (f32[3,8,128,128]{3,2,1,0:T(8,128)S(1)}, f32[8,128,128]{2,1,0:T(8,128)S(1)}, f32[8,128,128]{2,1,0:T(8,128)S(1)}, f32[832,128]{1,0:T(8,128)S(1)},...) custom-call(f32[3,1024,128]{2,1,0:T(8,128)S(1)} %bitcast.5, ...), custom_call_target="tpu_custom_call" | custom-call | flops 3000000 | bytes 6000000 | tf_op jit(solution)/shard_map/pallas_call | solution.py:525
  5.3 0.5 collective-permute-start
  5.8 4.1 %collective-permute-start.1 = (f32[832,128]{1,0:T(8,128)S(1)}, f32[832,128]{1,0:T(8,128)S(1)}, u32[]{:S(2)}, u32[]{:S(2)}) collective-permute-start(f32[832,128]{1,0:T(8,128)S(1)} %get-tuple-element.48), channel_id=1, source_target_pairs={{0,7},{1,0},{2,1},{3,2},{4,3},{5,4},{6,5},{7,6},{8,15},{9,8},{10,9... | collective-permute-start | bytes 1277960 | tf_op jit(solution)/shard_map/ppermute | solution.py:540
  9.9 1.9 %collective-permute-start.2 = (f32[8,24,128]{2,1,0:T(8,128)S(1)}, f32[8,24,128]{2,1,0:T(8,128)S(1)}, u32[]{:S(2)}, u32[]{:S(2)}) collective-permute-start(f32[8,24,128]{2,1,0:T(8,128)S(1)} %get-tuple-element.49), channel_id=1, source_target_pairs={{0,8},{8,16},{16,24},{24,0},{1,9},{9,17},{17,25},{25,1},{2,10},{10... | collective-permute-start | bytes 294920 | tf_op jit(solution)/shard_map/ppermute | solution.py:540
  11.8 1.0 %collective-permute-start.3 = (f32[8,24,128]{2,1,0:T(8,128)S(1)}, f32[8,24,128]{2,1,0:T(8,128)S(1)}, u32[]{:S(2)}, u32[]{:S(2)}) collective-permute-start(f32[8,24,128]{2,1,0:T(8,128)S(1)} %get-tuple-element.50), channel_id=1, source_target_pairs={{0,24},{8,0},{16,8},{24,16},{1,25},{9,1},{17,9},{25,17},{2,26},{10... | collective-permute-start | bytes 294920 | tf_op jit(solution)/shard_map/ppermute | solution.py:540
  12.8 2.6 %collective-permute-done.2.x_low = f32[8,24,128]{2,1,0:T(8,128)S(1)} collective-permute-done((f32[8,24,128]{2,1,0:T(8,128)S(1)}, f32[8,24,128]{2,1,0:T(8,128)S(1)}, u32[]{:S(2)}, u32[]{:S(2)}) %collective-permute-start.2) | collective-permute-done | bytes 98336 | tf_op jit(solution)/shard_map/ppermute | solution.py:540
  15.4 1.5 %collective-permute-done.3.x_high = f32[8,24,128]{2,1,0:T(8,128)S(1)} collective-permute-done((f32[8,24,128]{2,1,0:T(8,128)S(1)}, f32[8,24,128]{2,1,0:T(8,128)S(1)}, u32[]{:S(2)}, u32[]{:S(2)}) %collective-permute-start.3) | collective-permute-done | bytes 98336 | tf_op jit(solution)/shard_map/ppermute | solution.py:540
  17.0 0.1 collective-permute-start.4
  17.0 3.5 %collective-permute-start.5 = (f32[2,2,24,128]{3,2,1,0:T(8,128)S(1)}, f32[2,2,24,128]{3,2,1,0:T(8,128)S(1)}, u32[]{:S(2)}, u32[]{:S(2)}) collective-permute-start(f32[2,2,24,128]{3,2,1,0:T(8,128)S(1)} %get-tuple-element.52.edge_dn), channel_id=1, source_target_pairs={{0,7},{1,0},{2,1},{3,2},{4,3},{5,4},{6,5},{7,6},{8,15},{9,8},{10,9... | collective-permute-start | bytes 147464 | tf_op jit(solution)/shard_map/ppermute | solution.py:540
  20.6 3.0 %shard_map.54 = (f32[8,160,128]{2,1,0:T(8,128)S(1)}, f32[8,160,128]{2,1,0:T(8,128)S(1)}, f32[8,160,128]{2,1,0:T(8,128)S(1)}, f32[6,160,128]{2,1,0:T(8,128)S(1)},...) custom-call(f32[3,8,128,128]{3,2,1,0:T(8,128)S(1)} %get-tuple-elemen, ...), custom_call_target="tpu_custom_call" | custom-call | flops 3000000 | bytes 6000000 | tf_op jit(solution)/shard_map/pallas_call | solution.py:525
  23.5 0.0 collective-permute-done.4.c_low
  23.5 0.0 collective-permute-done.5.c_high
  23.5 0.0 collective-permute-done.from_dn
  23.6 0.0 collective-permute-done.1.from_up
  23.6 3.1 %shard_map.55 = (f32[2,2,160,128]{3,2,1,0:T(8,128)S(1)}, f32[2,2,160,128]{3,2,1,0:T(8,128)S(1)}, f32[4,160,128]{2,1,0:T(8,128)S(1)}, f32[2,144,128]{2,1,0:T(8,128)S(1)}, f32[2,144,128]{2,1,0:T(8,128)S(1)}) custom-call(f32[8,160,128]{2,1,0:T(8,128)S(1)} %get-tuple-element.61.conc_in, f32[8,160,128]{2,1,0:T(8,128)S(1)} %get-tuple-element.62.adj_in, ...), custom_call_target="tpu_custom_call" | custom-call | flops 2000000 | bytes 4000000 | tf_op jit(solution)/shard_map/pallas_call | solution.py:525
  26.7 0.1 collective-permute-start.8
  26.7 3.5 %collective-permute-start.9 = (f32[2,144,128]{2,1,0:T(8,128)S(1)}, f32[2,144,128]{2,1,0:T(8,128)S(1)}, u32[]{:S(2)}, u32[]{:S(2)}) collective-permute-start(f32[2,144,128]{2,1,0:T(8,128)S(1)} %get-tuple-element.79), channel_id=1, source_target_pairs={{0,7},{1,0},{2,1},{3,2},{4,3},{5,4},{6,5},{7,6},{8,15},{9,8},{10,9... | collective-permute-start | bytes 442376 | tf_op jit(solution)/shard_map/ppermute | solution.py:540
  30.3 1.8 %shard_map.52 = (f32[12,160,128]{2,1,0:T(8,128)S(1)}, f32[12,160,128]{2,1,0:T(8,128)S(1)}, f32[10,160,128]{2,1,0:T(8,128)S(1)}, f32[10,160,128]{2,1,0:T(8,128)S(...) custom-call(f32[3,8,128,128]{3,2,1,0:T(8,128)S(1)} %get-tuple-element.46.conc_own, ...), custom_call_target="tpu_custom_call" | custom-call | flops 2000000 | bytes 4000000 | tf_op jit(solution)/shard_map/pallas_call | solution.py:525
  32.1 0.1 collective-permute-start.6
  32.1 3.5 %collective-permute-start.7 = (f32[256,128]{1,0:T(8,128)S(1)}, f32[256,128]{1,0:T(8,128)S(1)}, u32[]{:S(2)}, u32[]{:S(2)}) collective-permute-start(f32[256,128]{1,0:T(8,128)S(1)} %get-tuple-element.54), channel_id=1, source_target_pairs={{0,7},{1,0},{2,1},{3,2},{4,3},{5,4},{6,5},{7,6},{8,15},{9,8},{10,9... | collective-permute-start | bytes 393224 | tf_op jit(solution)/shard_map/ppermute | solution.py:540
  35.7 1.9 %shard_map.56 = (f32[4,160,128]{2,1,0:T(8,128)S(1)}, f32[4,160,128]{2,1,0:T(8,128)S(1)}, f32[6,160,128]{2,1,0:T(8,128)S(1)}) custom-call(f32[12,160,128]{2,1,0:T(8,128)S(1)} %get-tuple-element.68.conc, f32[12,160,128]{2,1,0:T(8,128)S(1)} %get-tuple-element.69.mob, f32[10,160,128]{2,1,0:T(8,128)S(1)} %get-tuple-element.70.chem, ...), custom_call_target="tpu_custom_call" | custom-call | flops 3000000 | bytes 6000000 | tf_op jit(solution)/shard_map/pallas_call | solution.py:525
  37.5 0.8 %collective-permute-done.6.from_dn.rest_0_ = f32[256,128]{1,0:T(8,128)S(1)} collective-permute-done((f32[256,128]{1,0:T(8,128)S(1)}, f32[256,128]{1,0:T(8,128)S(1)}, u32[]{:S(2)}, u32[]{:S(2)}) %collective-permute-start.6) | collective-permute-done | bytes 131104 | tf_op jit(solution)/shard_map/ppermute | solution.py:540
  38.3 0.4 collective-permute-done.7.from_up.rest_1_
  38.7 0.0 collective-permute-done.8.from_dn
  38.7 0.0 collective-permute-done.9.from_up
  38.7 2.3 %shard_map.57 = (f32[2,2,160,128]{3,2,1,0:T(8,128)S(1)}, f32[2,2,160,128]{3,2,1,0:T(8,128)S(1)}, f32[2,144,128]{2,1,0:T(8,128)S(1)}, f32[2,144,128]{2,1,0:T(8,128)S(1)}) custom-call(f32[12,160,128]{2,1,0:T(8,128)S(1)} %get-tuple-element.68.conc, f32[12,160,128]{2,1,0:T(8,128)S(1)} %get-tuple-element.69.mob, f32[10,160,128]{2,1,0:T(8,128)S(1)} %get-tuple-element.70.chem, ...), custom_call_target="tpu_custom_call" | custom-call | flops 2000000 | bytes 4000000 | tf_op jit(solution)/shard_map/pallas_call | solution.py:525
  41.0 0.1 collective-permute-start.10
  41.1 3.8 %collective-permute-start.11 = (f32[2,144,128]{2,1,0:T(8,128)S(1)}, f32[2,144,128]{2,1,0:T(8,128)S(1)}, u32[]{:S(2)}, u32[]{:S(2)}) collective-permute-start(f32[2,144,128]{2,1,0:T(8,128)S(1)} %get-tuple-element.85), channel_id=1, source_target_pairs={{0,7},{1,0},{2,1},{3,2},{4,3},{5,4},{6,5},{7,6},{8,15},{9,8},{10,9... | collective-permute-start | bytes 442376 | tf_op jit(solution)/shard_map/ppermute | solution.py:540
  44.8 1.8 %shard_map.53 = (f32[12,160,128]{2,1,0:T(8,128)S(1)}, f32[12,160,128]{2,1,0:T(8,128)S(1)}, f32[10,160,128]{2,1,0:T(8,128)S(1)}, f32[10,160,128]{2,1,0:T(8,128)S(1)}) custom-call(f32[3,8,128,128]{3,2,1,0:T(8,128)S(1)} %get-tuple-element.46.conc_own, f32[256,128]{1,0:T(8,128)S(1)} %collective-permute-done.6.from_dn.rest_0_, ...), custom_call_target="tpu_custom_call" | custom-call | flops 2000000 | bytes 4000000 | tf_op jit(solution)/shard_map/pallas_call | solution.py:525
  46.6 2.1 %shard_map.58 = (f32[4,128,128]{2,1,0:T(8,128)S(1)}, f32[4,64,128]{2,1,0:T(8,128)S(1)}, f32[6,160,128]{2,1,0:T(8,128)S(1)}) custom-call(f32[12,160,128]{2,1,0:T(8,128)S(1)} %get-tuple-element.55.conc, f32[12,160,128]{2,1,0:T(8,128)S(1)} %get-tuple-element.56.mob, f32[10,160,128]{2,1,0:T(8,128)S(1)} %get-tuple-element.57.chem, ...), custom_call_target="tpu_custom_call" | custom-call | flops 3000000 | bytes 6000000 | tf_op jit(solution)/shard_map/pallas_call | solution.py:525
  48.7 0.0 collective-permute-done.10.from_dn
  48.7 0.0 collective-permute-done.11.from_up
  48.7 3.4 %shard_map.59 = (f32[1024,128]{1,0:T(8,128)}, f32[512,128]{1,0:T(8,128)}) custom-call(f32[12,160,128]{2,1,0:T(8,128)S(1)} %get-tuple-element.55.conc, f32[12,160,128]{2,1,0:T(8,128)S(1)} %get-tuple-element.56.mob, f32[10,160,128]{2,1,0:T(8,128)S(1)} %get-tuple-element.57.chem, f32[10,160,128]{2,1,0:T(8,128)S(1)} %get-tuple-element.58.curve, ...), custom_call_target="tpu_custom_call" | custom-call | flops 3000000 | bytes 6000000 | tf_op jit(solution)/shard_map/pallas_call | solution.py:525
  (1 shorter events, 0.0 us)
Async XLA Ops:
  0.6 1.4 %copy-start = (f32[3,2,64,8,128]{4,3,2,1,0:T(8,128)S(1)}, f32[3,2,64,8,128]{4,3,2,1,0:T(8,128)}, u32[]{:S(2)}) copy-start(f32[3,2,64,8,128]{4,3,2,1,0:T(8,128)} %param.3) | copy-start | bytes 4718596
  2.0 1.0 %copy-start.1 = (f32[2,64,8,128]{3,2,1,0:T(8,128)S(1)}, f32[2,64,8,128]{3,2,1,0:T(8,128)}, u32[]{:S(2)}) copy-start(f32[2,64,8,128]{3,2,1,0:T(8,128)} %param.4) | copy-start | bytes 1572868
  3.1 0.9 %copy-start.2 = (f32[64,8,128]{2,1,0:T(8,128)S(1)}, f32[64,8,128]{2,1,0:T(8,128)}, u32[]{:S(2)}) copy-start(f32[64,8,128]{2,1,0:T(8,128)} %param.5) | copy-start | bytes 786436
  5.3 18.3 %collective-permute-start = (f32[832,128]{1,0:T(8,128)S(1)}, f32[832,128]{1,0:T(8,128)S(1)}, u32[]{:S(2)}, u32[]{:S(2)}) collective-permute-start(f32[832,128]{1,0:T(8,128)S(1)} %get-tuple-element.47), channel_id=1, source_target_pairs={{0,1},{1,2},{2,3},{3,4},{4,5},{5,6},{6,7},{7,0},{8,9},{9,10},{10,1... | collective-permute-start | bytes 1277960 | tf_op jit(solution)/shard_map/ppermute | solution.py:540
  5.8 17.8 %collective-permute-start.1 = (f32[832,128]{1,0:T(8,128)S(1)}, f32[832,128]{1,0:T(8,128)S(1)}, u32[]{:S(2)}, u32[]{:S(2)}) collective-permute-start(f32[832,128]{1,0:T(8,128)S(1)} %get-tuple-element.48), channel_id=1, source_target_pairs={{0,7},{1,0},{2,1},{3,2},{4,3},{5,4},{6,5},{7,6},{8,15},{9,8},{10,9... | collective-permute-start | bytes 1277960 | tf_op jit(solution)/shard_map/ppermute | solution.py:540
  9.9 5.5 %collective-permute-start.2 = (f32[8,24,128]{2,1,0:T(8,128)S(1)}, f32[8,24,128]{2,1,0:T(8,128)S(1)}, u32[]{:S(2)}, u32[]{:S(2)}) collective-permute-start(f32[8,24,128]{2,1,0:T(8,128)S(1)} %get-tuple-element.49), channel_id=1, source_target_pairs={{0,8},{8,16},{16,24},{24,0},{1,9},{9,17},{17,25},{25,1},{2,10},{10... | collective-permute-start | bytes 294920 | tf_op jit(solution)/shard_map/ppermute | solution.py:540
  11.8 5.1 %collective-permute-start.3 = (f32[8,24,128]{2,1,0:T(8,128)S(1)}, f32[8,24,128]{2,1,0:T(8,128)S(1)}, u32[]{:S(2)}, u32[]{:S(2)}) collective-permute-start(f32[8,24,128]{2,1,0:T(8,128)S(1)} %get-tuple-element.50), channel_id=1, source_target_pairs={{0,24},{8,0},{16,8},{24,16},{1,25},{9,1},{17,9},{25,17},{2,26},{10... | collective-permute-start | bytes 294920 | tf_op jit(solution)/shard_map/ppermute | solution.py:540
  17.0 6.6 %collective-permute-start.4 = (f32[2,2,24,128]{3,2,1,0:T(8,128)S(1)}, f32[2,2,24,128]{3,2,1,0:T(8,128)S(1)}, u32[]{:S(2)}, u32[]{:S(2)}) collective-permute-start(f32[2,2,24,128]{3,2,1,0:T(8,128)S(1)} %get-tuple-element.51.edge_up), channel_id=1, source_target_pairs={{0,1},{1,2},{2,3},{3,4},{4,5},{5,6},{6,7},{7,0},{8,9},{9,10},{10,1... | collective-permute-start | bytes 147464 | tf_op jit(solution)/shard_map/ppermute | solution.py:540
  17.0 6.5 %collective-permute-start.5 = (f32[2,2,24,128]{3,2,1,0:T(8,128)S(1)}, f32[2,2,24,128]{3,2,1,0:T(8,128)S(1)}, u32[]{:S(2)}, u32[]{:S(2)}) collective-permute-start(f32[2,2,24,128]{3,2,1,0:T(8,128)S(1)} %get-tuple-element.52.edge_dn), channel_id=1, source_target_pairs={{0,7},{1,0},{2,1},{3,2},{4,3},{5,4},{6,5},{7,6},{8,15},{9,8},{10,9... | collective-permute-start | bytes 147464 | tf_op jit(solution)/shard_map/ppermute | solution.py:540
  26.7 12.1 %collective-permute-start.8 = (f32[2,144,128]{2,1,0:T(8,128)S(1)}, f32[2,144,128]{2,1,0:T(8,128)S(1)}, u32[]{:S(2)}, u32[]{:S(2)}) collective-permute-start(f32[2,144,128]{2,1,0:T(8,128)S(1)} %get-tuple-element.78), channel_id=1, source_target_pairs={{0,1},{1,2},{2,3},{3,4},{4,5},{5,6},{6,7},{7,0},{8,9},{9,10},{10,1... | collective-permute-start | bytes 442376 | tf_op jit(solution)/shard_map/ppermute | solution.py:540
  26.7 12.0 %collective-permute-start.9 = (f32[2,144,128]{2,1,0:T(8,128)S(1)}, f32[2,144,128]{2,1,0:T(8,128)S(1)}, u32[]{:S(2)}, u32[]{:S(2)}) collective-permute-start(f32[2,144,128]{2,1,0:T(8,128)S(1)} %get-tuple-element.79), channel_id=1, source_target_pairs={{0,7},{1,0},{2,1},{3,2},{4,3},{5,4},{6,5},{7,6},{8,15},{9,8},{10,9... | collective-permute-start | bytes 442376 | tf_op jit(solution)/shard_map/ppermute | solution.py:540
  32.1 6.2 %collective-permute-start.6 = (f32[256,128]{1,0:T(8,128)S(1)}, f32[256,128]{1,0:T(8,128)S(1)}, u32[]{:S(2)}, u32[]{:S(2)}) collective-permute-start(f32[256,128]{1,0:T(8,128)S(1)} %get-tuple-element.53), channel_id=1, source_target_pairs={{0,1},{1,2},{2,3},{3,4},{4,5},{5,6},{6,7},{7,0},{8,9},{9,10},{10,1... | collective-permute-start | bytes 393224 | tf_op jit(solution)/shard_map/ppermute | solution.py:540
  32.1 6.6 %collective-permute-start.7 = (f32[256,128]{1,0:T(8,128)S(1)}, f32[256,128]{1,0:T(8,128)S(1)}, u32[]{:S(2)}, u32[]{:S(2)}) collective-permute-start(f32[256,128]{1,0:T(8,128)S(1)} %get-tuple-element.54), channel_id=1, source_target_pairs={{0,7},{1,0},{2,1},{3,2},{4,3},{5,4},{6,5},{7,6},{8,15},{9,8},{10,9... | collective-permute-start | bytes 393224 | tf_op jit(solution)/shard_map/ppermute | solution.py:540
  41.0 7.7 %collective-permute-start.10 = (f32[2,144,128]{2,1,0:T(8,128)S(1)}, f32[2,144,128]{2,1,0:T(8,128)S(1)}, u32[]{:S(2)}, u32[]{:S(2)}) collective-permute-start(f32[2,144,128]{2,1,0:T(8,128)S(1)} %get-tuple-element.84), channel_id=1, source_target_pairs={{0,1},{1,2},{2,3},{3,4},{4,5},{5,6},{6,7},{7,0},{8,9},{9,10},{10,1... | collective-permute-start | bytes 442376 | tf_op jit(solution)/shard_map/ppermute | solution.py:540
  41.1 7.6 %collective-permute-start.11 = (f32[2,144,128]{2,1,0:T(8,128)S(1)}, f32[2,144,128]{2,1,0:T(8,128)S(1)}, u32[]{:S(2)}, u32[]{:S(2)}) collective-permute-start(f32[2,144,128]{2,1,0:T(8,128)S(1)} %get-tuple-element.85), channel_id=1, source_target_pairs={{0,7},{1,0},{2,1},{3,2},{4,3},{5,4},{6,5},{7,6},{8,15},{9,8},{10,9... | collective-permute-start | bytes 442376 | tf_op jit(solution)/shard_map/ppermute | solution.py:540

commit v3 on v2

--- a/solution.py
+++ b/solution.py
@@ -16,6 +16,7 @@
 pad = 16
 chunk = 24
 depth = 2
+early = 1
 vmem_limit = 20 * 1024 * 1024
 far_limit = 20 * 1024 * 1024
 f32 = jnp.float32
@@ -26,10 +27,6 @@
     starts = [sum(widths[:i]) for i in range(len(widths))]
     total = -(-sum(widths) // 8) * 8
     return list(zip(starts, widths)), total
-
-
-def early(steps):
-    return (1 + min(steps, 2)) * depth
 
 
 def chunks(low, high):
@@ -241,12 +238,28 @@
     lax.fori_loop(0, 4, close, 0)
 
 
+def is_even(axis):
+    return lax.rem(lax.axis_index(axis), 2) == 0
+
+
+def bases(rows):
+    even = is_even("gy")
+    top = rows - depth
+    return jnp.where(even, top, 0), jnp.where(even, 0, top)
+
+
+def landings(rows):
+    even = is_even("gy")
+    top = rows + depth
+    return jnp.where(even, top, 0), jnp.where(even, 0, top)
+
+
 def sides_of(rows):
     return [(0, 0, 0), (0, 1, 1), (1, 0, rows - 1), (1, 1, rows - 2)]
 
 
 def pack_kernel(steps, rows, cols, nz, conc_hbm, adj_hbm, rate_hbm, conc_out, adj_out, rate_out,
-                main_up, main_dn, x_right, x_left, conc_in, adj_in, rate_in, sems):
+                main_a, main_b, x_a, x_b, conc_in, adj_in, rate_in, sems):
     places, total = slots(steps)
     lanes = adj_out.shape[2]
     half = cols // 2
@@ -261,10 +274,13 @@
     for copy in copies:
         copy.start()
 
+    even_x = is_even("gx")
+
     def to_x(y, value, place):
         start, width = place
-        x_right[y, start : start + width, :] = value[cols - width :, :]
-        x_left[y, start : start + width, :] = value[:width, :]
+        last, first = value[cols - width :, :], value[:width, :]
+        x_a[y, start : start + width, :] = jnp.where(even_x, last, first)
+        x_b[y, start : start + width, :] = jnp.where(even_x, first, last)
 
     used = sum(places[-1])
     copies[0].wait()
@@ -272,9 +288,6 @@
         adj = adj_in[pl.ds(y, lanes, stride=rows), :].T
         adj_out[y] = adj
         to_x(y, adj, places[0])
-        for side, at in ((main_dn, y), (main_up, y - rows + depth)):
-            if 0 <= at < depth:
-                side[pl.ds(at * cols, cols), :] = adj
     copies[1].wait()
     for y in range(rows):
         rate = rate_in[pl.ds(y, nz, stride=rows), :]
@@ -282,23 +295,23 @@
         rate_out[y] = rate
         to_x(y, rate, places[steps + 1])
         if used < total:
-            x_right[y, used:, :] = jnp.zeros((total - used, lanes), f32)
-            x_left[y, used:, :] = jnp.zeros((total - used, lanes), f32)
-        for side, edge in ((main_dn, 0), (main_up, rows - 1)):
-            if y == edge:
-                side[pl.ds(early(steps) * cols, half), :] = jnp.where(
-                    lower, rate[:half], rate[half:]
-                )
+            x_a[y, used:, :] = jnp.zeros((total - used, lanes), f32)
+            x_b[y, used:, :] = jnp.zeros((total - used, lanes), f32)
     for back in range(steps):
         copies[2 + back].wait()
         for y in range(rows):
             conc = conc_in[back, pl.ds(y, lanes, stride=rows), :].T
             conc_out[back, y] = conc
             to_x(y, conc, places[1 + back])
-            if back < 2:
-                for side, at in ((main_dn, y), (main_up, y - rows + depth)):
-                    if 0 <= at < depth:
-                        side[pl.ds(((1 + back) * depth + at) * cols, cols), :] = conc
+    for side, base in zip((main_a, main_b), bases(rows)):
+        for at in range(depth):
+            side[pl.ds(at * cols, cols), :] = adj_out[base + at]
+            for back in range(early):
+                side[pl.ds(((1 + back) * depth + at) * cols, cols), :] = conc_out[back, base + at]
+        edge = jnp.where(base == 0, 0, rows - 1)
+        side[pl.ds((1 + early) * depth * cols, half), :] = jnp.where(
+            lower, rate_out[edge, :half, :], rate_out[edge, half:, :]
+        )
 
 
 def put_own(out, row, value, y, place, cols, x_low, x_high):
@@ -317,27 +330,31 @@
     out[row, right : right + width, :] = corner[1, from_row, start : start + width, :]
 
 
-def corner_kernel(rows, x_low, x_high, to_up, to_dn):
-    for i, side in enumerate((x_low, x_high)):
-        to_up[i] = side[rows - depth :]
-        to_dn[i] = side[:depth]
-
-
-def first_interior(steps, rows, cols, nz, conc_own, adj_own, rate_own, x_low, x_high, edge_up,
-                   edge_dn,
+def corner_kernel(steps, rows, cols, got_a, got_b, conc_own, main_a,
+                  x_low, x_high, corner_a, corner_b, *late):
+    even_x = is_even("gx")
+    x_low[...] = jnp.where(even_x, got_b[...], got_a[...])
+    x_high[...] = jnp.where(even_x, got_a[...], got_b[...])
+    for out, base in zip((corner_a, corner_b), bases(rows)):
+        for at in range(depth):
+            out[0, at] = x_low[base + at]
+            out[1, at] = x_high[base + at]
+    for out, base in zip(late, bases(rows)):
+        for back in range(early, steps):
+            for at in range(depth):
+                span = pl.ds(((back - early) * depth + at) * cols, cols)
+                out[span, :] = conc_own[back, base + at]
+
+
+def first_interior(steps, rows, cols, nz, conc_own, adj_own, rate_own, x_low, x_high,
                    conc, adj, rate, chem, curve, pot, out, grad, mob, part):
     places, _ = slots(steps)
     low, high = reach(cols)
     lanes = adj.shape[2]
     for y in range(rows):
-        at, low_x, high_x = y, x_low, x_high
-        if y < depth:
-            low_x, high_x = edge_dn.at[0], edge_dn.at[1]
-        elif y >= rows - depth:
-            at, low_x, high_x = y - rows + depth, edge_up.at[0], edge_up.at[1]
-        put_own(conc, y, conc_own[0, y], at, places[1], cols, low_x, high_x)
-        put_own(adj, y, adj_own[y], at, places[0], cols, low_x, high_x)
-        put_own(rate, y, rate_own[y], at, places[steps + 1], cols, low_x, high_x)
+        put_own(conc, y, conc_own[0, y], y, places[1], cols, x_low, x_high)
+        put_own(adj, y, adj_own[y], y, places[0], cols, x_low, x_high)
+        put_own(rate, y, rate_own[y], y, places[steps + 1], cols, x_low, x_high)
     def mob_row(y, _):
         for at, size in chunks(low - 8, high + 8):
             c = conc[y, at : at + size, :]
@@ -365,16 +382,17 @@
         out[to] = ref[at]
 
 
-def send_rows(out, to_up, to_dn, cols):
+def send_rows(out, to_a, to_b, cols):
     low, high = reach(cols)
+    even = is_even("gy")
     for k in range(depth):
-        to_dn[k] = out[0, k, low:high, :]
-        to_up[depth - 1 - k] = out[1, k, low:high, :]
+        for to, side in ((to_a, jnp.where(even, 1, 0)), (to_b, jnp.where(even, 0, 1))):
+            to[k] = out[side, jnp.where(side == 1, depth - 1 - k, k), low:high, :]
 
 
 def first_boundary(steps, rows, cols, nz, conc_in, adj_in, rate_in, chem_in, curve_in, pot_in,
-                   from_dn, from_up, c_low, c_high,
-                   out, grad, rate, to_up, to_dn, conc, adj, mob, chem, curve, pot, part):
+                   from_a, from_b, corner_a, corner_b,
+                   out, grad, rate, to_a, to_b, conc, adj, mob, chem, curve, pot, part):
     places, _ = slots(steps)
     low, high = reach(cols)
     half = cols // 2
@@ -382,7 +400,7 @@
     lower = lax.broadcasted_iota(jnp.int32, (half, lanes), 1) < nz
 
     def unpack(side):
-        packed = side[pl.ds(early(steps) * cols, half), :]
+        packed = side[pl.ds((1 + early) * depth * cols, half), :]
         turned = pltpu.roll(packed, lanes // 2, 1)
         return jnp.concatenate(
             [jnp.where(lower, packed, turned), jnp.where(lower, turned, packed)], axis=0
@@ -397,15 +415,16 @@
         pot[1 + y] = pot_in[y - 1]
     for y in (1, rows - 2):
         curve[1 + y] = curve_in[y - 1]
-    for at in range(depth):
-        for ref, place, base in ((conc, places[1], depth), (adj, places[0], 0)):
-            rows_in = pl.ds((base + at) * cols, cols)
-            put_halo(ref, at, from_dn[rows_in, :], at, place, cols, c_low)
-            put_halo(ref, depth + rows + at, from_up[rows_in, :], at, place, cols, c_high)
-    put_halo(rate, 0, unpack(from_dn), depth - 1, places[steps + 1], cols, c_low)
     rate[1] = rate_in[0]
     rate[2] = rate_in[rows - 1]
-    put_halo(rate, 3, unpack(from_up), 0, places[steps + 1], cols, c_high)
+    for halo, corner, base in zip((from_a, from_b), (corner_a, corner_b), landings(rows)):
+        for at in range(depth):
+            for ref, place, first in ((adj, places[0], 0), (conc, places[1], depth)):
+                span = pl.ds((first + at) * cols, cols)
+                put_halo(ref, base + at, halo[span, :], at, place, cols, corner)
+        below = base == 0
+        put_halo(rate, jnp.where(below, 0, 3), unpack(halo), jnp.where(below, depth - 1, 0),
+                 places[steps + 1], cols, corner)
     for row in [0, 1, 2, 3, rows, rows + 1, rows + 2, rows + 3]:
         for at, size in chunks(low - 8, high + 8):
             c = conc[row, at : at + size, :]
@@ -416,29 +435,21 @@
 
     boundary(rows, cols, nz, (conc, depth), (mob, depth), (chem, 1), (curve, 1), (adj, depth),
              rate, pot, part, grad, None, store, True)
-    send_rows(out, to_up, to_dn, cols)
-
-
-def prepare_kernel(steps, rows, cols, nz, back, conc_own, from_dn, from_up, x_low, x_high, c_low,
-                   c_high, conc, mob, chem, curve, *late):
+    send_rows(out, to_a, to_b, cols)
+
+
+def prepare_kernel(steps, rows, cols, nz, back, conc_own, from_a, from_b, x_low, x_high,
+                   corner_a, corner_b, conc, mob, chem, curve):
     places, _ = slots(steps)
     low, high = reach(cols)
     lanes = conc.shape[2]
     place = places[1 + back]
     for y in range(rows):
         put_own(conc, depth + y, conc_own[back, y], y, place, cols, x_low, x_high)
-    for at in range(depth):
-        rows_in = pl.ds((((1 + back) if back < 2 else (back - 2)) * depth + at) * cols, cols)
-        put_halo(conc, at, from_dn[rows_in, :], at, place, cols, c_low)
-        put_halo(conc, depth + rows + at, from_up[rows_in, :], at, place, cols, c_high)
-
-    if late:
-        late_up, late_dn = late
-        for after in range(2, steps):
-            for at in range(depth):
-                span = pl.ds(((after - 2) * depth + at) * cols, cols)
-                late_dn[span, :] = conc_own[after, at]
-                late_up[span, :] = conc_own[after, rows - depth + at]
+    for halo, corner, base in zip((from_a, from_b), (corner_a, corner_b), landings(rows)):
+        for at in range(depth):
+            span = pl.ds(((back - early) * depth + at) * cols, cols)
+            put_halo(conc, base + at, halo[span, :], at, place, cols, corner)
 
     def mob_row(row, _):
         for at, size in chunks(low - 8, high + 8):
@@ -486,19 +497,19 @@
 
 
 def next_boundary(rows, cols, nz, final, conc, mob, chem, curve, rate, inner, outer, pot_in,
-                  before, from_dn, from_up, *rest):
+                  before, from_a, from_b, *rest):
     low, high = reach(cols)
     if final:
         inner_out, inner_grad, out, grad_out, adj, pot, part, grad, result = rest
     else:
-        _conc_low, _conc_high, result, grad, to_up, to_dn, adj, pot, part = rest
+        result, grad, to_a, to_b, adj, pot, part = rest
     adj[2 * depth] = inner[0]
     adj[rows - 1] = inner[rows - 2 * depth - 1]
     for s, k, y in sides_of(rows):
         adj[depth + y] = outer[s, k]
-    for at in range(depth):
-        adj[at, low:high, :] = from_dn[at]
-        adj[depth + rows + at, low:high, :] = from_up[at]
+    for halo, base in zip((from_a, from_b), landings(rows)):
+        for at in range(depth):
+            adj[base + at, low:high, :] = halo[at]
     for y in (1, 2, rows - 3, rows - 2):
         pot[1 + y] = pot_in[y - 1]
 
@@ -516,7 +527,7 @@
             out[pl.ds(y, lanes, stride=rows), :] = result[s, k, pad : pad + cols, :].T
             grad_out[pl.ds(y, nz, stride=rows), :] = fold(grad[s, k, pad : pad + cols, :].T, nz)
     else:
-        send_rows(result, to_up, to_dn, cols)
+        send_rows(result, to_a, to_b, cols)
 
 
 def call(kernel, outs, scratch, *operands, cost=0, far=False):
@@ -535,9 +546,11 @@
     )(*operands)
 
 
-def shift(value, axis, by):
+def swap(value_a, value_b, axis):
     count = lax.axis_size(axis)
-    return lax.ppermute(value, axis, [(i, (i + by) % count) for i in range(count)])
+    pairs_a = [(i, i + 1 - 2 * (i % 2)) for i in range(count)]
+    pairs_b = [(i, (i - 1 + 2 * (i % 2)) % count) for i in range(count)]
+    return lax.ppermute(value_a, axis, pairs_a), lax.ppermute(value_b, axis, pairs_b)
 
 
 def shards(saved_conc, adjoint_end, rate_field):
@@ -551,10 +564,10 @@
     def field(count):
         return (count, width, lanes)
 
-    conc_own, adj_own, rate_own, main_up, main_dn, x_right, x_left = call(
+    conc_own, adj_own, rate_own, main_a, main_b, x_a, x_b = call(
         functools.partial(pack_kernel, steps, rows, cols, nz),
         [(steps, rows, cols, lanes), (rows, cols, lanes), (rows, cols, lanes)]
-        + [(early(steps) * cols + cols // 2, lanes)] * 2
+        + [((1 + early) * depth * cols + cols // 2, lanes)] * 2
         + [(rows, total, lanes)] * 2,
         [(steps, flat, cols), (flat, cols), (nz * rows, cols)]
         + [pltpu.SemaphoreType.DMA((2 + steps,))],
@@ -564,48 +577,44 @@
         cost=3,
         far=True,
     )
-    x_low = shift(x_right, "gx", 1)
-    x_high = shift(x_left, "gx", -1)
-    from_dn = shift(main_up, "gy", 1)
-    from_up = shift(main_dn, "gy", -1)
-    corner_up, corner_dn = call(
-        functools.partial(corner_kernel, rows), [(2, depth, total, lanes)] * 2, [], x_low, x_high
+    main_a, main_b = swap(main_a, main_b, "gy")
+    x_a, x_b = swap(x_a, x_b, "gx")
+    x_low, x_high, corner_a, corner_b, late_a, late_b = call(
+        functools.partial(corner_kernel, steps, rows, cols),
+        [(rows, total, lanes)] * 2 + [(2, depth, total, lanes)] * 2
+        + [((steps - early) * depth * cols, lanes)] * 2,
+        [],
+        x_a, x_b, conc_own, main_a,
     )
-    c_low = shift(corner_up, "gy", 1)
-    c_high = shift(corner_dn, "gy", -1)
+    late_a, late_b = swap(late_a, late_b, "gy")
+    corner_a, corner_b = swap(corner_a, corner_b, "gy")
 
     conc, adj, rate_in, chem, curve, pot, inner, inner_grad = call(
         functools.partial(first_interior, steps, rows, cols, nz),
         [field(rows)] * 3 + [field(rows - 2)] * 3 + [field(inside)] * 2,
         [field(rows), field(inside)],
-        conc_own, adj_own, rate_own, x_low, x_high, corner_up, corner_dn,
+        conc_own, adj_own, rate_own, x_low, x_high,
         cost=3,
     )
-
     both = (2, depth, width, lanes)
     edge = (depth, cols + 16, lanes)
-    outer, outer_grad, rate, to_up, to_dn = call(
+    outer, outer_grad, rate, to_a, to_b = call(
         functools.partial(first_boundary, steps, rows, cols, nz),
         [both, both, field(4), edge, edge],
         [field(rows + 2 * depth)] * 3 + [field(rows + 2)] * 3 + [both],
-        conc, adj, rate_in, chem, curve, pot, from_dn, from_up, c_low, c_high,
+        conc, adj, rate_in, chem, curve, pot, main_a, main_b, corner_a, corner_b,
         cost=2,
     )
-    conc_low, conc_high = from_dn, from_up
     for back in range(1, steps):
-        low, high = shift(to_up, "gy", 1), shift(to_dn, "gy", -1)
+        adj_a, adj_b = swap(to_a, to_b, "gy")
         final = back == steps - 1
-        late = [((steps - 2) * depth * cols, lanes)] * 2 if back == 1 and steps > 2 else []
         fields = call(
             functools.partial(prepare_kernel, steps, rows, cols, nz, back),
-            [field(rows + 2 * depth)] * 2 + [field(rows + 2)] * 2 + late,
+            [field(rows + 2 * depth)] * 2 + [field(rows + 2)] * 2,
             [],
-            conc_own, conc_low, conc_high, x_low, x_high, c_low, c_high,
+            conc_own, late_a, late_b, x_low, x_high, corner_a, corner_b,
             cost=2,
         )
-        if late:
-            conc_low, conc_high = shift(fields[4], "gy", 1), shift(fields[5], "gy", -1)
-            fields = fields[:4]
         tiles = [(inside, lanes, cols), (inside, nz, cols)]
         results = call(
             functools.partial(next_interior, rows, cols, nz, final),
@@ -620,15 +629,15 @@
                 functools.partial(next_boundary, rows, cols, nz, final),
                 [(flat, cols), (nz * rows, cols)],
                 [field(rows + 2 * depth), field(rows + 2), both, both, both],
-                *fields, rate, inner, outer, pot, outer_grad, low, high, results[0], results[1],
+                *fields, rate, inner, outer, pot, outer_grad, adj_a, adj_b, results[0], results[1],
                 cost=3,
             )
         else:
-            new_outer, outer_grad, to_up, to_dn = call(
+            new_outer, outer_grad, to_a, to_b = call(
                 functools.partial(next_boundary, rows, cols, nz, final),
                 [both, both, edge, edge],
                 [field(rows + 2 * depth), field(rows + 2), both],
-                *fields, rate, inner, outer, pot, outer_grad, low, high, conc_low, conc_high,
+                *fields, rate, inner, outer, pot, outer_grad, adj_a, adj_b,
                 cost=2,
             )
             inner, inner_grad, outer = results[0], results[1], new_outer

time: 52.3 us -> 50.7 us (0.969)
  starting transfers between devices: 22.1 us -> 14 us
  waiting for transfers between devices: 5.33 us -> 11.7 us
    ppermute x12, starting transfers between devices: 22.1 us -> 14 us  [the longest x6 11.6 us: swap(): lax.ppermute(value_b, axis, pairs_b)]
    ppermute x12, waiting for transfers between devices: 5.33 us -> 11.7 us  [the longest x6 9.78 us: swap(): lax.ppermute(value_b, axis, pairs_b)]
  transfers between devices with their start and end apart: 12 -> 12, of which waited for: 4 -> 5; matrix products, arithmetic and copies ran while one was open for 0% -> 0% of each run, Pallas kernels for 20% -> 27%
where the time goes in v3:
time: 50.7 us; the launch traced here: 50.5 us
  Pallas kernels  20.6 us (41%)
  starting transfers between devices  14 us (28%)
  waiting for transfers between devices  11.7 us (23%)
  local copies, waits for them, and re-layouts  3.39 us (7%)
  between operations  0.77 us (2%)
    pallas_call x10, Pallas kernels, call(): pl.pallas_call(kernel, out_shape=[jax.ShapeDtypeStruct(shape, f32) for sh...  20.6 us
    ppermute x6, starting transfers between devices, swap(): lax.ppermute(value_b, axis, pairs_b)  11.6 us
    ppermute x6, waiting for transfers between devices, swap(): lax.ppermute(value_b, axis, pairs_b)  9.78 us
    unnamed x6, local copies, waits for them, and re-layouts  3.39 us
    ppermute x6, starting transfers between devices, swap(): lax.ppermute(value_a, axis, pairs_a)  2.32 us
    ppermute x6, waiting for transfers between devices, swap(): lax.ppermute(value_a, axis, pairs_a)  1.95 us
  transfers between devices with their start and end apart: 12, of which 5 were waited for; matrix products, arithmetic and copies ran while one was open for 0% of the time, Pallas kernels for 27%

profile of v3, /device:TPU:0, one launch (start us, length us, event | category | flops | bytes accessed | tf_op | source)
XLA Modules:
  0.0 50.5 jit_solution(1216366700313259720)
XLA Ops:
  0.6 0.0 copy-start
  0.6 1.4 %copy-done = f32[3,2,64,8,128]{4,3,2,1,0:T(8,128)S(1)} copy-done((f32[3,2,64,8,128]{4,3,2,1,0:T(8,128)S(1)}, f32[3,2,64,8,128]{4,3,2,1,0:T(8,128)}, u32[]{:S(2)}) %copy-start) | copy-done | bytes 1572888
  2.0 0.0 copy-start.1
  2.0 1.0 %copy-done.1 = f32[2,64,8,128]{3,2,1,0:T(8,128)S(1)} copy-done((f32[2,64,8,128]{3,2,1,0:T(8,128)S(1)}, f32[2,64,8,128]{3,2,1,0:T(8,128)}, u32[]{:S(2)}) %copy-start.1) | copy-done | bytes 524312
  3.1 0.0 copy-start.2
  3.1 0.9 %copy-done.2 = f32[64,8,128]{2,1,0:T(8,128)S(1)} copy-done((f32[64,8,128]{2,1,0:T(8,128)S(1)}, f32[64,8,128]{2,1,0:T(8,128)}, u32[]{:S(2)}) %copy-start.2) | copy-done | bytes 262168
  4.0 1.3 %shard_map.50 = (f32[3,8,128,128]{3,2,1,0:T(8,128)S(1)}, f32[8,128,128]{2,1,0:T(8,128)S(1)}, f32[8,128,128]{2,1,0:T(8,128)S(1)}, f32[576,128]{1,0:T(8,128)S(1)},...) custom-call(f32[3,1024,128]{2,1,0:T(8,128)S(1)} %bitcast.5, ...), custom_call_target="tpu_custom_call" | custom-call | flops 3000000 | bytes 6000000 | tf_op jit(solution)/shard_map/pallas_call | solution.py:536
  5.3 0.5 %collective-permute-start.2 = (f32[576,128]{1,0:T(8,128)S(1)}, f32[576,128]{1,0:T(8,128)S(1)}, u32[]{:S(2)}, u32[]{:S(2)}) collective-permute-start(f32[576,128]{1,0:T(8,128)S(1)} %get-tuple-element.51), channel_id=1, source_target_pairs={{0,1},{1,0},{2,3},{3,2},{4,5},{5,4},{6,7},{7,6},{8,9},{9,8},{10,11... | collective-permute-start | bytes 884744 | tf_op jit(solution)/shard_map/ppermute | solution.py:553
  5.9 4.7 %collective-permute-start.7 = (f32[576,128]{1,0:T(8,128)S(1)}, f32[576,128]{1,0:T(8,128)S(1)}, u32[]{:S(2)}, u32[]{:S(2)}) collective-permute-start(f32[576,128]{1,0:T(8,128)S(1)} %get-tuple-element.70), channel_id=1, source_target_pairs={{0,7},{1,2},{2,1},{3,4},{4,3},{5,6},{6,5},{7,0},{8,15},{9,10},{10,... | collective-permute-start | bytes 884744 | tf_op jit(solution)/shard_map/ppermute | solution.py:553
  10.6 1.5 %collective-permute-start = (f32[8,24,128]{2,1,0:T(8,128)S(1)}, f32[8,24,128]{2,1,0:T(8,128)S(1)}, u32[]{:S(2)}, u32[]{:S(2)}) collective-permute-start(f32[8,24,128]{2,1,0:T(8,128)S(1)} %get-tuple-element.49), channel_id=1, source_target_pairs={{0,8},{8,0},{16,24},{24,16},{1,9},{9,1},{17,25},{25,17},{2,10},{10... | collective-permute-start | bytes 294920 | tf_op jit(solution)/shard_map/ppermute | solution.py:553
  12.1 1.5 %collective-permute-start.1 = (f32[8,24,128]{2,1,0:T(8,128)S(1)}, f32[8,24,128]{2,1,0:T(8,128)S(1)}, u32[]{:S(2)}, u32[]{:S(2)}) collective-permute-start(f32[8,24,128]{2,1,0:T(8,128)S(1)} %get-tuple-element.50), channel_id=1, source_target_pairs={{0,24},{8,16},{16,8},{24,0},{1,25},{9,17},{17,9},{25,1},{2,26},{10... | collective-permute-start | bytes 294920 | tf_op jit(solution)/shard_map/ppermute | solution.py:553
  13.5 1.9 %collective-permute-done.got_a = f32[8,24,128]{2,1,0:T(8,128)S(1)} collective-permute-done((f32[8,24,128]{2,1,0:T(8,128)S(1)}, f32[8,24,128]{2,1,0:T(8,128)S(1)}, u32[]{:S(2)}, u32[]{:S(2)}) %collective-permute-start) | collective-permute-done | bytes 98336 | tf_op jit(solution)/shard_map/ppermute | solution.py:553
  15.5 2.1 %collective-permute-done.1.got_b = f32[8,24,128]{2,1,0:T(8,128)S(1)} collective-permute-done((f32[8,24,128]{2,1,0:T(8,128)S(1)}, f32[8,24,128]{2,1,0:T(8,128)S(1)}, u32[]{:S(2)}, u32[]{:S(2)}) %collective-permute-start.1) | collective-permute-done | bytes 98336 | tf_op jit(solution)/shard_map/ppermute | solution.py:553
  17.6 0.0 collective-permute-done.2.main_a.from_a
  17.6 0.1 shard_map.51
  17.6 0.1 collective-permute-start.3
  17.7 1.3 %collective-permute-start.4 = (f32[512,128]{1,0:T(8,128)S(1)}, f32[512,128]{1,0:T(8,128)S(1)}, u32[]{:S(2)}, u32[]{:S(2)}) collective-permute-start(f32[512,128]{1,0:T(8,128)S(1)} %get-tuple-element.53), channel_id=1, source_target_pairs={{0,7},{1,2},{2,1},{3,4},{4,3},{5,6},{6,5},{7,0},{8,15},{9,10},{10,... | collective-permute-start | bytes 786440 | tf_op jit(solution)/shard_map/ppermute | solution.py:553
  19.0 0.0 collective-permute-start.5
  19.0 2.4 %collective-permute-start.6 = (f32[2,2,24,128]{3,2,1,0:T(8,128)S(1)}, f32[2,2,24,128]{3,2,1,0:T(8,128)S(1)}, u32[]{:S(2)}, u32[]{:S(2)}) collective-permute-start(f32[2,2,24,128]{3,2,1,0:T(8,128)S(1)} %get-tuple-element.57), channel_id=1, source_target_pairs={{0,7},{1,2},{2,1},{3,4},{4,3},{5,6},{6,5},{7,0},{8,15},{9,10},{10,... | collective-permute-start | bytes 147464 | tf_op jit(solution)/shard_map/ppermute | solution.py:553
  21.3 3.0 %shard_map.53 = (f32[8,160,128]{2,1,0:T(8,128)S(1)}, f32[8,160,128]{2,1,0:T(8,128)S(1)}, f32[8,160,128]{2,1,0:T(8,128)S(1)}, f32[6,160,128]{2,1,0:T(8,128)S(1)},...) custom-call(f32[3,8,128,128]{3,2,1,0:T(8,128)S(1)} %get-tuple-elemen, ...), custom_call_target="tpu_custom_call" | custom-call | flops 3000000 | bytes 6000000 | tf_op jit(solution)/shard_map/pallas_call | solution.py:536
  24.3 0.0 collective-permute-done.7.from_b
  24.3 0.0 collective-permute-done.5.corner_a
  24.3 4.1 %collective-permute-done.6.corner_b = f32[2,2,24,128]{3,2,1,0:T(8,128)S(1)} collective-permute-done((f32[2,2,24,128]{3,2,1,0:T(8,128)S(1)}, f32[2,2,24,128]{3,2,1,0:T(8,128)S(1)}, u32[]{:S(2)}, u32[]{:S(2)}) %collective-permute-start.6) | collective-permute-done | bytes 49184 | tf_op jit(solution)/shard_map/ppermute | solution.py:553
  28.4 3.1 %shard_map.54 = (f32[2,2,160,128]{3,2,1,0:T(8,128)S(1)}, f32[2,2,160,128]{3,2,1,0:T(8,128)S(1)}, f32[4,160,128]{2,1,0:T(8,128)S(1)}, f32[2,144,128]{2,1,0:T(8,128)S(1)}, f32[2,144,128]{2,1,0:T(8,128)S(1)}) custom-call(f32[8,160,128]{2,1,0:T(8,128)S(1)} %get-tuple-element.64.conc_in, f32[8,160,128]{2,1,0:T(8,128)S(1)} %get-tuple-element.65.adj_in, ...), custom_call_target="tpu_custom_call" | custom-call | flops 2000000 | bytes 4000000 | tf_op jit(solution)/shard_map/pallas_call | solution.py:536
  31.5 0.1 collective-permute-start.8
  31.6 0.6 %collective-permute-start.9 = (f32[2,144,128]{2,1,0:T(8,128)S(1)}, f32[2,144,128]{2,1,0:T(8,128)S(1)}, u32[]{:S(2)}, u32[]{:S(2)}) collective-permute-start(f32[2,144,128]{2,1,0:T(8,128)S(1)} %get-tuple-element.83), channel_id=1, source_target_pairs={{0,7},{1,2},{2,1},{3,4},{4,3},{5,6},{6,5},{7,0},{8,15},{9,10},{10,... | collective-permute-start | bytes 442376 | tf_op jit(solution)/shard_map/ppermute | solution.py:553
  32.2 0.0 collective-permute-done.3.from_a
  32.2 0.0 collective-permute-done.4.from_b
  32.2 1.8 %shard_map.55 = (f32[12,160,128]{2,1,0:T(8,128)S(1)}, f32[12,160,128]{2,1,0:T(8,128)S(1)}, f32[10,160,128]{2,1,0:T(8,128)S(1)}, f32[10,160,128]{2,1,0:T(8,128)S(1)}) custom-call(f32[3,8,128,128]{3,2,1,0:T(8,128)S(1)} %get-tuple-element.48.conc_own, f32[512,128]{1,0:T(8,128)S(1)} %collective-permute-done.3.from_a, ...), custom_call_target="tpu_custom_call" | custom-call | flops 2000000 | bytes 4000000 | tf_op jit(solution)/shard_map/pallas_call | solution.py:536
  34.0 1.9 %shard_map.56 = (f32[4,160,128]{2,1,0:T(8,128)S(1)}, f32[4,160,128]{2,1,0:T(8,128)S(1)}, f32[6,160,128]{2,1,0:T(8,128)S(1)}) custom-call(f32[12,160,128]{2,1,0:T(8,128)S(1)} %get-tuple-element.72.conc, f32[12,160,128]{2,1,0:T(8,128)S(1)} %get-tuple-element.73.mob, f32[10,160,128]{2,1,0:T(8,128)S(1)} %get-tuple-element.74.chem, ...), custom_call_target="tpu_custom_call" | custom-call | flops 3000000 | bytes 6000000 | tf_op jit(solution)/shard_map/pallas_call | solution.py:536
  35.9 0.0 collective-permute-done.8.from_a
  35.9 2.2 %collective-permute-done.9.from_b = f32[2,144,128]{2,1,0:T(8,128)S(1)} collective-permute-done((f32[2,144,128]{2,1,0:T(8,128)S(1)}, f32[2,144,128]{2,1,0:T(8,128)S(1)}, u32[]{:S(2)}, u32[]{:S(2)}) %collective-permute-start.9) | collective-permute-done | bytes 147488 | tf_op jit(solution)/shard_map/ppermute | solution.py:553
  38.1 2.3 %shard_map.57 = (f32[2,2,160,128]{3,2,1,0:T(8,128)S(1)}, f32[2,2,160,128]{3,2,1,0:T(8,128)S(1)}, f32[2,144,128]{2,1,0:T(8,128)S(1)}, f32[2,144,128]{2,1,0:T(8,128)S(1)}) custom-call(f32[12,160,128]{2,1,0:T(8,128)S(1)} %get-tuple-element.72.conc, f32[12,160,128]{2,1,0:T(8,128)S(1)} %get-tuple-element.73.mob, f32[10,160,128]{2,1,0:T(8,128)S(1)} %get-tuple-element.74.chem, ...), custom_call_target="tpu_custom_call" | custom-call | flops 2000000 | bytes 4000000 | tf_op jit(solution)/shard_map/pallas_call | solution.py:536
  40.4 0.2 collective-permute-start.10
  40.6 1.2 %collective-permute-start.11 = (f32[2,144,128]{2,1,0:T(8,128)S(1)}, f32[2,144,128]{2,1,0:T(8,128)S(1)}, u32[]{:S(2)}, u32[]{:S(2)}) collective-permute-start(f32[2,144,128]{2,1,0:T(8,128)S(1)} %get-tuple-element.89), channel_id=1, source_target_pairs={{0,7},{1,2},{2,1},{3,4},{4,3},{5,6},{6,5},{7,0},{8,15},{9,10},{10,... | collective-permute-start | bytes 442376 | tf_op jit(solution)/shard_map/ppermute | solution.py:553
  41.8 1.8 %shard_map.52 = (f32[12,160,128]{2,1,0:T(8,128)S(1)}, f32[12,160,128]{2,1,0:T(8,128)S(1)}, f32[10,160,128]{2,1,0:T(8,128)S(1)}, f32[10,160,128]{2,1,0:T(8,128)S(1)}) custom-call(f32[3,8,128,128]{3,2,1,0:T(8,128)S(1)} %get-tuple-element.48.conc_own, f32[512,128]{1,0:T(8,128)S(1)} %collective-permute-done.3.from_a, ...), custom_call_target="tpu_custom_call" | custom-call | flops 2000000 | bytes 4000000 | tf_op jit(solution)/shard_map/pallas_call | solution.py:536
  43.6 2.1 %shard_map.58 = (f32[4,128,128]{2,1,0:T(8,128)S(1)}, f32[4,64,128]{2,1,0:T(8,128)S(1)}, f32[6,160,128]{2,1,0:T(8,128)S(1)}) custom-call(f32[12,160,128]{2,1,0:T(8,128)S(1)} %get-tuple-element.58.conc, f32[12,160,128]{2,1,0:T(8,128)S(1)} %get-tuple-element.59.mob, f32[10,160,128]{2,1,0:T(8,128)S(1)} %get-tuple-element.60.chem, ...), custom_call_target="tpu_custom_call" | custom-call | flops 3000000 | bytes 6000000 | tf_op jit(solution)/shard_map/pallas_call | solution.py:536
  45.7 0.0 collective-permute-done.10.from_a
  45.7 1.4 %collective-permute-done.11.from_b = f32[2,144,128]{2,1,0:T(8,128)S(1)} collective-permute-done((f32[2,144,128]{2,1,0:T(8,128)S(1)}, f32[2,144,128]{2,1,0:T(8,128)S(1)}, u32[]{:S(2)}, u32[]{:S(2)}) %collective-permute-start.11) | collective-permute-done | bytes 147488 | tf_op jit(solution)/shard_map/ppermute | solution.py:553
  47.1 3.4 %shard_map.59 = (f32[1024,128]{1,0:T(8,128)}, f32[512,128]{1,0:T(8,128)}) custom-call(f32[12,160,128]{2,1,0:T(8,128)S(1)} %get-tuple-element.58.conc, f32[12,160,128]{2,1,0:T(8,128)S(1)} %get-tuple-element.59.mob, f32[10,160,128]{2,1,0:T(8,128)S(1)} %get-tuple-element.60.chem, f32[10,160,128]{2,1,0:T(8,128)S(1)} %get-tuple-element.61.curve, ...), custom_call_target="tpu_custom_call" | custom-call | flops 3000000 | bytes 6000000 | tf_op jit(solution)/shard_map/pallas_call | solution.py:536
Async XLA Ops:
  0.6 1.4 %copy-start = (f32[3,2,64,8,128]{4,3,2,1,0:T(8,128)S(1)}, f32[3,2,64,8,128]{4,3,2,1,0:T(8,128)}, u32[]{:S(2)}) copy-start(f32[3,2,64,8,128]{4,3,2,1,0:T(8,128)} %param.3) | copy-start | bytes 4718596
  2.0 1.0 %copy-start.1 = (f32[2,64,8,128]{3,2,1,0:T(8,128)S(1)}, f32[2,64,8,128]{3,2,1,0:T(8,128)}, u32[]{:S(2)}) copy-start(f32[2,64,8,128]{3,2,1,0:T(8,128)} %param.4) | copy-start | bytes 1572868
  3.1 0.9 %copy-start.2 = (f32[64,8,128]{2,1,0:T(8,128)S(1)}, f32[64,8,128]{2,1,0:T(8,128)}, u32[]{:S(2)}) copy-start(f32[64,8,128]{2,1,0:T(8,128)} %param.5) | copy-start | bytes 786436
  5.3 12.2 %collective-permute-start.2 = (f32[576,128]{1,0:T(8,128)S(1)}, f32[576,128]{1,0:T(8,128)S(1)}, u32[]{:S(2)}, u32[]{:S(2)}) collective-permute-start(f32[576,128]{1,0:T(8,128)S(1)} %get-tuple-element.51), channel_id=1, source_target_pairs={{0,1},{1,0},{2,3},{3,2},{4,5},{5,4},{6,7},{7,6},{8,9},{9,8},{10,11... | collective-permute-start | bytes 884744 | tf_op jit(solution)/shard_map/ppermute | solution.py:553
  5.9 18.5 %collective-permute-start.7 = (f32[576,128]{1,0:T(8,128)S(1)}, f32[576,128]{1,0:T(8,128)S(1)}, u32[]{:S(2)}, u32[]{:S(2)}) collective-permute-start(f32[576,128]{1,0:T(8,128)S(1)} %get-tuple-element.70), channel_id=1, source_target_pairs={{0,7},{1,2},{2,1},{3,4},{4,3},{5,6},{6,5},{7,0},{8,15},{9,10},{10,... | collective-permute-start | bytes 884744 | tf_op jit(solution)/shard_map/ppermute | solution.py:553
  10.6 4.9 %collective-permute-start = (f32[8,24,128]{2,1,0:T(8,128)S(1)}, f32[8,24,128]{2,1,0:T(8,128)S(1)}, u32[]{:S(2)}, u32[]{:S(2)}) collective-permute-start(f32[8,24,128]{2,1,0:T(8,128)S(1)} %get-tuple-element.49), channel_id=1, source_target_pairs={{0,8},{8,0},{16,24},{24,16},{1,9},{9,1},{17,25},{25,17},{2,10},{10... | collective-permute-start | bytes 294920 | tf_op jit(solution)/shard_map/ppermute | solution.py:553
  12.1 5.5 %collective-permute-start.1 = (f32[8,24,128]{2,1,0:T(8,128)S(1)}, f32[8,24,128]{2,1,0:T(8,128)S(1)}, u32[]{:S(2)}, u32[]{:S(2)}) collective-permute-start(f32[8,24,128]{2,1,0:T(8,128)S(1)} %get-tuple-element.50), channel_id=1, source_target_pairs={{0,24},{8,16},{16,8},{24,0},{1,25},{9,17},{17,9},{25,1},{2,26},{10... | collective-permute-start | bytes 294920 | tf_op jit(solution)/shard_map/ppermute | solution.py:553
  17.6 14.6 %collective-permute-start.3 = (f32[512,128]{1,0:T(8,128)S(1)}, f32[512,128]{1,0:T(8,128)S(1)}, u32[]{:S(2)}, u32[]{:S(2)}) collective-permute-start(f32[512,128]{1,0:T(8,128)S(1)} %get-tuple-element.52), channel_id=1, source_target_pairs={{0,1},{1,0},{2,3},{3,2},{4,5},{5,4},{6,7},{7,6},{8,9},{9,8},{10,11... | collective-permute-start | bytes 786440 | tf_op jit(solution)/shard_map/ppermute | solution.py:553
  17.7 14.5 %collective-permute-start.4 = (f32[512,128]{1,0:T(8,128)S(1)}, f32[512,128]{1,0:T(8,128)S(1)}, u32[]{:S(2)}, u32[]{:S(2)}) collective-permute-start(f32[512,128]{1,0:T(8,128)S(1)} %get-tuple-element.53), channel_id=1, source_target_pairs={{0,7},{1,2},{2,1},{3,4},{4,3},{5,6},{6,5},{7,0},{8,15},{9,10},{10,... | collective-permute-start | bytes 786440 | tf_op jit(solution)/shard_map/ppermute | solution.py:553
  19.0 5.3 %collective-permute-start.5 = (f32[2,2,24,128]{3,2,1,0:T(8,128)S(1)}, f32[2,2,24,128]{3,2,1,0:T(8,128)S(1)}, u32[]{:S(2)}, u32[]{:S(2)}) collective-permute-start(f32[2,2,24,128]{3,2,1,0:T(8,128)S(1)} %get-tuple-element.56), channel_id=1, source_target_pairs={{0,1},{1,0},{2,3},{3,2},{4,5},{5,4},{6,7},{7,6},{8,9},{9,8},{10,11... | collective-permute-start | bytes 147464 | tf_op jit(solution)/shard_map/ppermute | solution.py:553
  19.0 9.4 %collective-permute-start.6 = (f32[2,2,24,128]{3,2,1,0:T(8,128)S(1)}, f32[2,2,24,128]{3,2,1,0:T(8,128)S(1)}, u32[]{:S(2)}, u32[]{:S(2)}) collective-permute-start(f32[2,2,24,128]{3,2,1,0:T(8,128)S(1)} %get-tuple-element.57), channel_id=1, source_target_pairs={{0,7},{1,2},{2,1},{3,4},{4,3},{5,6},{6,5},{7,0},{8,15},{9,10},{10,... | collective-permute-start | bytes 147464 | tf_op jit(solution)/shard_map/ppermute | solution.py:553
  31.5 4.4 %collective-permute-start.8 = (f32[2,144,128]{2,1,0:T(8,128)S(1)}, f32[2,144,128]{2,1,0:T(8,128)S(1)}, u32[]{:S(2)}, u32[]{:S(2)}) collective-permute-start(f32[2,144,128]{2,1,0:T(8,128)S(1)} %get-tuple-element.82), channel_id=1, source_target_pairs={{0,1},{1,0},{2,3},{3,2},{4,5},{5,4},{6,7},{7,6},{8,9},{9,8},{10,11... | collective-permute-start | bytes 442376 | tf_op jit(solution)/shard_map/ppermute | solution.py:553
  31.6 6.5 %collective-permute-start.9 = (f32[2,144,128]{2,1,0:T(8,128)S(1)}, f32[2,144,128]{2,1,0:T(8,128)S(1)}, u32[]{:S(2)}, u32[]{:S(2)}) collective-permute-start(f32[2,144,128]{2,1,0:T(8,128)S(1)} %get-tuple-element.83), channel_id=1, source_target_pairs={{0,7},{1,2},{2,1},{3,4},{4,3},{5,6},{6,5},{7,0},{8,15},{9,10},{10,... | collective-permute-start | bytes 442376 | tf_op jit(solution)/shard_map/ppermute | solution.py:553
  40.4 5.2 %collective-permute-start.10 = (f32[2,144,128]{2,1,0:T(8,128)S(1)}, f32[2,144,128]{2,1,0:T(8,128)S(1)}, u32[]{:S(2)}, u32[]{:S(2)}) collective-permute-start(f32[2,144,128]{2,1,0:T(8,128)S(1)} %get-tuple-element.88), channel_id=1, source_target_pairs={{0,1},{1,0},{2,3},{3,2},{4,5},{5,4},{6,7},{7,6},{8,9},{9,8},{10,11... | collective-permute-start | bytes 442376 | tf_op jit(solution)/shard_map/ppermute | solution.py:553
  40.6 6.5 %collective-permute-start.11 = (f32[2,144,128]{2,1,0:T(8,128)S(1)}, f32[2,144,128]{2,1,0:T(8,128)S(1)}, u32[]{:S(2)}, u32[]{:S(2)}) collective-permute-start(f32[2,144,128]{2,1,0:T(8,128)S(1)} %get-tuple-element.89), channel_id=1, source_target_pairs={{0,7},{1,2},{2,1},{3,4},{4,3},{5,6},{6,5},{7,0},{8,15},{9,10},{10,... | collective-permute-start | bytes 442376 | tf_op jit(solution)/shard_map/ppermute | solution.py:553

commit v4 on v3

--- a/solution.py
+++ b/solution.py
@@ -16,9 +16,7 @@
 pad = 16
 chunk = 24
 depth = 2
-early = 1
 vmem_limit = 20 * 1024 * 1024
-far_limit = 20 * 1024 * 1024
 f32 = jnp.float32
 
 
@@ -258,10 +256,9 @@
     return [(0, 0, 0), (0, 1, 1), (1, 0, rows - 1), (1, 1, rows - 2)]
 
 
-def pack_kernel(steps, rows, cols, nz, conc_hbm, adj_hbm, rate_hbm, conc_out, adj_out, rate_out,
-                main_a, main_b, x_a, x_b, conc_in, adj_in, rate_in, sems):
-    places, total = slots(steps)
-    lanes = adj_out.shape[2]
+def edge_kernel(steps, rows, cols, nz, conc_hbm, adj_hbm, rate_hbm, conc_in, adj_in, rate_in,
+                main_a, main_b, sems):
+    lanes = main_a.shape[1]
     half = cols // 2
     lower = lax.broadcasted_iota(jnp.int32, (half, lanes), 1) < nz
     copies = [
@@ -273,7 +270,35 @@
     ]
     for copy in copies:
         copy.start()
-
+    copies[0].wait()
+    for side, base in zip((main_a, main_b), bases(rows)):
+        for at in range(depth):
+            side[pl.ds(at * cols, cols), :] = adj_in[pl.ds(base + at, lanes, stride=rows), :].T
+    copies[1].wait()
+    for side, base in zip((main_a, main_b), bases(rows)):
+        edge = jnp.where(base == 0, 0, rows - 1)
+        rate = turned_rate(rate_in, edge, rows, nz, lanes)
+        side[pl.ds((1 + steps) * depth * cols, half), :] = jnp.where(
+            lower, rate[:half], rate[half:]
+        )
+    for back in range(steps):
+        copies[2 + back].wait()
+        for side, base in zip((main_a, main_b), bases(rows)):
+            for at in range(depth):
+                side[pl.ds(((1 + back) * depth + at) * cols, cols), :] = conc_in[
+                    back, pl.ds(base + at, lanes, stride=rows), :
+                ].T
+
+
+def turned_rate(rate, y, rows, nz, lanes):
+    value = rate[pl.ds(y, nz, stride=rows), :]
+    return jnp.concatenate([value] * (lanes // nz), axis=0).T
+
+
+def turn_kernel(steps, rows, cols, nz, conc_in, adj_in, rate_in, conc_out, adj_out, rate_out,
+                x_a, x_b):
+    places, total = slots(steps)
+    lanes = adj_out.shape[2]
     even_x = is_even("gx")
 
     def to_x(y, value, place):
@@ -283,35 +308,20 @@
         x_b[y, start : start + width, :] = jnp.where(even_x, first, last)
 
     used = sum(places[-1])
-    copies[0].wait()
     for y in range(rows):
         adj = adj_in[pl.ds(y, lanes, stride=rows), :].T
         adj_out[y] = adj
         to_x(y, adj, places[0])
-    copies[1].wait()
-    for y in range(rows):
-        rate = rate_in[pl.ds(y, nz, stride=rows), :]
-        rate = jnp.concatenate([rate] * (lanes // nz), axis=0).T
+        rate = turned_rate(rate_in, y, rows, nz, lanes)
         rate_out[y] = rate
         to_x(y, rate, places[steps + 1])
         if used < total:
             x_a[y, used:, :] = jnp.zeros((total - used, lanes), f32)
             x_b[y, used:, :] = jnp.zeros((total - used, lanes), f32)
-    for back in range(steps):
-        copies[2 + back].wait()
-        for y in range(rows):
+        for back in range(steps):
             conc = conc_in[back, pl.ds(y, lanes, stride=rows), :].T
             conc_out[back, y] = conc
             to_x(y, conc, places[1 + back])
-    for side, base in zip((main_a, main_b), bases(rows)):
-        for at in range(depth):
-            side[pl.ds(at * cols, cols), :] = adj_out[base + at]
-            for back in range(early):
-                side[pl.ds(((1 + back) * depth + at) * cols, cols), :] = conc_out[back, base + at]
-        edge = jnp.where(base == 0, 0, rows - 1)
-        side[pl.ds((1 + early) * depth * cols, half), :] = jnp.where(
-            lower, rate_out[edge, :half, :], rate_out[edge, half:, :]
-        )
 
 
 def put_own(out, row, value, y, place, cols, x_low, x_high):
@@ -330,8 +340,7 @@
     out[row, right : right + width, :] = corner[1, from_row, start : start + width, :]
 
 
-def corner_kernel(steps, rows, cols, got_a, got_b, conc_own, main_a,
-                  x_low, x_high, corner_a, corner_b, *late):
+def corner_kernel(rows, got_a, got_b, x_low, x_high, corner_a, corner_b):
     even_x = is_even("gx")
     x_low[...] = jnp.where(even_x, got_b[...], got_a[...])
     x_high[...] = jnp.where(even_x, got_a[...], got_b[...])
@@ -339,11 +348,6 @@
         for at in range(depth):
             out[0, at] = x_low[base + at]
             out[1, at] = x_high[base + at]
-    for out, base in zip(late, bases(rows)):
-        for back in range(early, steps):
-            for at in range(depth):
-                span = pl.ds(((back - early) * depth + at) * cols, cols)
-                out[span, :] = conc_own[back, base + at]
 
 
 def first_interior(steps, rows, cols, nz, conc_own, adj_own, rate_own, x_low, x_high,
@@ -400,7 +404,7 @@
     lower = lax.broadcasted_iota(jnp.int32, (half, lanes), 1) < nz
 
     def unpack(side):
-        packed = side[pl.ds((1 + early) * depth * cols, half), :]
+        packed = side[pl.ds((1 + steps) * depth * cols, half), :]
         turned = pltpu.roll(packed, lanes // 2, 1)
         return jnp.concatenate(
             [jnp.where(lower, packed, turned), jnp.where(lower, turned, packed)], axis=0
@@ -448,7 +452,7 @@
         put_own(conc, depth + y, conc_own[back, y], y, place, cols, x_low, x_high)
     for halo, corner, base in zip((from_a, from_b), (corner_a, corner_b), landings(rows)):
         for at in range(depth):
-            span = pl.ds(((back - early) * depth + at) * cols, cols)
+            span = pl.ds(((1 + back) * depth + at) * cols, cols)
             put_halo(conc, base + at, halo[span, :], at, place, cols, corner)
 
     def mob_row(row, _):
@@ -531,15 +535,16 @@
 
 
 def call(kernel, outs, scratch, *operands, cost=0, far=False):
-    space = pltpu.HBM if far else pltpu.VMEM
-    limit = far_limit if far else vmem_limit
+    if far:
+        operands = [pltpu.with_memory_space_constraint(value, pltpu.HBM) for value in operands]
+    space = pl.ANY if far else pltpu.VMEM
     return pl.pallas_call(
         kernel,
         out_shape=[jax.ShapeDtypeStruct(shape, f32) for shape in outs],
         in_specs=[pl.BlockSpec(memory_space=space)] * len(operands),
         out_specs=[pl.BlockSpec(memory_space=pltpu.VMEM)] * len(outs),
         scratch_shapes=[pltpu.VMEM(s, f32) if isinstance(s, tuple) else s for s in scratch],
-        compiler_params=pltpu.CompilerParams(vmem_limit_bytes=limit),
+        compiler_params=pltpu.CompilerParams(vmem_limit_bytes=vmem_limit),
         cost_estimate=pl.CostEstimate(
             flops=cost * 1_000_000, bytes_accessed=cost * 2_000_000, transcendentals=0
         ),
@@ -564,29 +569,31 @@
     def field(count):
         return (count, width, lanes)
 
-    conc_own, adj_own, rate_own, main_a, main_b, x_a, x_b = call(
-        functools.partial(pack_kernel, steps, rows, cols, nz),
-        [(steps, rows, cols, lanes), (rows, cols, lanes), (rows, cols, lanes)]
-        + [((1 + early) * depth * cols + cols // 2, lanes)] * 2
-        + [(rows, total, lanes)] * 2,
-        [(steps, flat, cols), (flat, cols), (nz * rows, cols)]
-        + [pltpu.SemaphoreType.DMA((2 + steps,))],
-        saved_conc.reshape(steps, flat, cols),
-        adjoint_end.reshape(flat, cols),
-        rate_field.reshape(nz * rows, cols),
-        cost=3,
+    raw = [(steps, flat, cols), (flat, cols), (nz * rows, cols)]
+    conc_raw, adj_raw, rate_raw, main_a, main_b = call(
+        functools.partial(edge_kernel, steps, rows, cols, nz),
+        raw + [((1 + steps) * depth * cols + cols // 2, lanes)] * 2,
+        [pltpu.SemaphoreType.DMA((2 + steps,))],
+        saved_conc.reshape(raw[0]), adjoint_end.reshape(raw[1]), rate_field.reshape(raw[2]),
+        cost=2,
         far=True,
     )
     main_a, main_b = swap(main_a, main_b, "gy")
+    conc_own, adj_own, rate_own, x_a, x_b = call(
+        functools.partial(turn_kernel, steps, rows, cols, nz),
+        [(steps, rows, cols, lanes), (rows, cols, lanes), (rows, cols, lanes)]
+        + [(rows, total, lanes)] * 2,
+        [],
+        conc_raw, adj_raw, rate_raw,
+        cost=1,
+    )
     x_a, x_b = swap(x_a, x_b, "gx")
-    x_low, x_high, corner_a, corner_b, late_a, late_b = call(
-        functools.partial(corner_kernel, steps, rows, cols),
-        [(rows, total, lanes)] * 2 + [(2, depth, total, lanes)] * 2
-        + [((steps - early) * depth * cols, lanes)] * 2,
+    x_low, x_high, corner_a, corner_b = call(
+        functools.partial(corner_kernel, rows),
+        [(rows, total, lanes)] * 2 + [(2, depth, total, lanes)] * 2,
         [],
-        x_a, x_b, conc_own, main_a,
+        x_a, x_b,
     )
-    late_a, late_b = swap(late_a, late_b, "gy")
     corner_a, corner_b = swap(corner_a, corner_b, "gy")
 
     conc, adj, rate_in, chem, curve, pot, inner, inner_grad = call(
@@ -612,7 +619,7 @@
             functools.partial(prepare_kernel, steps, rows, cols, nz, back),
             [field(rows + 2 * depth)] * 2 + [field(rows + 2)] * 2,
             [],
-            conc_own, late_a, late_b, x_low, x_high, corner_a, corner_b,
+            conc_own, main_a, main_b, x_low, x_high, corner_a, corner_b,
             cost=2,
         )
         tiles = [(inside, lanes, cols), (inside, nz, cols)]

time: 50.7 us -> 44.5 us (0.88)
  local copies, waits for them, and re-layouts: 3.39 us -> 0 us
  waiting for transfers between devices: 11.7 us -> 8.58 us
  Pallas kernels: 20.6 us -> 21.8 us
  starting transfers between devices: 14 us -> 13.2 us
    unnamed x6 -> x0, local copies, waits for them, and re-layouts: 3.39 us -> none
    ppermute x6 -> x5, waiting for transfers between devices: 9.78 us -> 6.63 us  [swap(): lax.ppermute(value_b, axis, pairs_b)]
    pallas_call x10 -> x11, Pallas kernels: 20.6 us -> 21.8 us  [call(): pl.pallas_call(kernel, out_shape=[jax.ShapeDtypeStruct(shape, f32) for sh...]
    ppermute x6 -> x5, starting transfers between devices: 11.6 us -> 10.9 us  [swap(): lax.ppermute(value_b, axis, pairs_b)]
    ppermute x6 -> x5, starting transfers between devices: 2.32 us -> 2.29 us  [swap(): lax.ppermute(value_a, axis, pairs_a)]
    ppermute x6 -> x5, waiting for transfers between devices: 1.95 us -> 1.95 us  [swap(): lax.ppermute(value_a, axis, pairs_a)]
  transfers between devices with their start and end apart: 12 -> 10, of which waited for: 5 -> 5; matrix products, arithmetic and copies ran while one was open for 0% -> 0% of each run, Pallas kernels for 27% -> 25%
where the time goes in v4:
time: 44.5 us; the launch traced here: 44.3 us
  Pallas kernels  21.8 us (49%)
  starting transfers between devices  13.2 us (30%)
  waiting for transfers between devices  8.58 us (19%)
  between operations  0.76 us (2%)
    pallas_call x11, Pallas kernels, call(): pl.pallas_call(kernel, out_shape=[jax.ShapeDtypeStruct(shape, f32) for sh...  21.8 us
    ppermute x5, starting transfers between devices, swap(): lax.ppermute(value_b, axis, pairs_b)  10.9 us
    ppermute x5, waiting for transfers between devices, swap(): lax.ppermute(value_b, axis, pairs_b)  6.63 us
    ppermute x5, starting transfers between devices, swap(): lax.ppermute(value_a, axis, pairs_a)  2.29 us
    ppermute x5, waiting for transfers between devices, swap(): lax.ppermute(value_a, axis, pairs_a)  1.95 us
  transfers between devices with their start and end apart: 10, of which 5 were waited for; matrix products, arithmetic and copies ran while one was open for 0% of the time, Pallas kernels for 25%

profile of v4, /device:TPU:0, one launch (start us, length us, event | category | flops | bytes accessed | tf_op | source)
XLA Modules:
  0.0 44.3 jit_solution(2967931538198881903)
XLA Ops:
  0.6 1.8 %shard_map.50 = (f32[3,1024,128]{2,1,0:T(8,128)S(1)}, f32[1024,128]{1,0:T(8,128)S(1)}, f32[512,128]{1,0:T(8,128)S(1)}, f32[1088,128]{1,0:T(8,128)S(1)}, f32[1088,128]{1,0:T(8,128)S(1)}) custom-call(f32[3,1024,128]{2,1,0:T(8,128)} %bitcast.5, f32[1024,128]{1,0:T(8,128)} %bitcast.6, f32[512,128]{1,0:T(8,128)} %bitcast.7), custom_call_target="tpu_custom_call" | custom-call | flops 2000000 | bytes 4000000 | tf_op jit(solution)/shard_map/pallas_call | solution.py:541
  2.4 0.5 %collective-permute-start = (f32[1088,128]{1,0:T(8,128)S(1)}, f32[1088,128]{1,0:T(8,128)S(1)}, u32[]{:S(2)}, u32[]{:S(2)}) collective-permute-start(f32[1088,128]{1,0:T(8,128)S(1)} %get-tuple-element.53), channel_id=1, source_target_pairs={{0,1},{1,0},{2,3},{3,2},{4,5},{5,4},{6,7},{7,6},{8,9},{9,8},{10,11... | collective-permute-start | bytes 1671176 | tf_op jit(solution)/shard_map/ppermute | solution.py:558
  2.9 4.7 %collective-permute-start.1 = (f32[1088,128]{1,0:T(8,128)S(1)}, f32[1088,128]{1,0:T(8,128)S(1)}, u32[]{:S(2)}, u32[]{:S(2)}) collective-permute-start(f32[1088,128]{1,0:T(8,128)S(1)} %get-tuple-element.54), channel_id=1, source_target_pairs={{0,7},{1,2},{2,1},{3,4},{4,3},{5,6},{6,5},{7,0},{8,15},{9,10},{10,... | collective-permute-start | bytes 1671176 | tf_op jit(solution)/shard_map/ppermute | solution.py:558
  7.6 0.7 %shard_map.51 = (f32[3,8,128,128]{3,2,1,0:T(8,128)S(1)}, f32[8,128,128]{2,1,0:T(8,128)S(1)}, f32[8,128,128]{2,1,0:T(8,128)S(1)}, f32[8,24,128]{2,1,0:T(8,128)S(1)}, f32[8,24,128]{2,1,0:T(8,128)S(1)}) custom-call(f32[3,1024,128]{2,1,0:T(8,128)S(1)} %get-tuple-element.49.conc_in, f32[1024,128]{1,0:T(8,128)S(1)} %get-tuple-element.50.adj_in, ...), custom_call_target="tpu_custom_call" | custom-call | flops 1000000 | bytes 2000000 | tf_op jit(solution)/shard_map/pallas_call | solution.py:541
  8.4 1.6 %collective-permute-start.2 = (f32[8,24,128]{2,1,0:T(8,128)S(1)}, f32[8,24,128]{2,1,0:T(8,128)S(1)}, u32[]{:S(2)}, u32[]{:S(2)}) collective-permute-start(f32[8,24,128]{2,1,0:T(8,128)S(1)} %get-tuple-element.55), channel_id=1, source_target_pairs={{0,8},{8,0},{16,24},{24,16},{1,9},{9,1},{17,25},{25,17},{2,10},{10... | collective-permute-start | bytes 294920 | tf_op jit(solution)/shard_map/ppermute | solution.py:558
  9.9 1.5 %collective-permute-start.3 = (f32[8,24,128]{2,1,0:T(8,128)S(1)}, f32[8,24,128]{2,1,0:T(8,128)S(1)}, u32[]{:S(2)}, u32[]{:S(2)}) collective-permute-start(f32[8,24,128]{2,1,0:T(8,128)S(1)} %get-tuple-element.56), channel_id=1, source_target_pairs={{0,24},{8,16},{16,8},{24,0},{1,25},{9,17},{17,9},{25,1},{2,26},{10... | collective-permute-start | bytes 294920 | tf_op jit(solution)/shard_map/ppermute | solution.py:558
  11.4 1.9 %collective-permute-done.2.got_a = f32[8,24,128]{2,1,0:T(8,128)S(1)} collective-permute-done((f32[8,24,128]{2,1,0:T(8,128)S(1)}, f32[8,24,128]{2,1,0:T(8,128)S(1)}, u32[]{:S(2)}, u32[]{:S(2)}) %collective-permute-start.2) | collective-permute-done | bytes 98336 | tf_op jit(solution)/shard_map/ppermute | solution.py:558
  13.4 2.1 %collective-permute-done.3.got_b = f32[8,24,128]{2,1,0:T(8,128)S(1)} collective-permute-done((f32[8,24,128]{2,1,0:T(8,128)S(1)}, f32[8,24,128]{2,1,0:T(8,128)S(1)}, u32[]{:S(2)}, u32[]{:S(2)}) %collective-permute-start.3) | collective-permute-done | bytes 98336 | tf_op jit(solution)/shard_map/ppermute | solution.py:558
  15.5 0.1 collective-permute-start.4
  15.6 1.3 %collective-permute-start.5 = (f32[2,2,24,128]{3,2,1,0:T(8,128)S(1)}, f32[2,2,24,128]{3,2,1,0:T(8,128)S(1)}, u32[]{:S(2)}, u32[]{:S(2)}) collective-permute-start(f32[2,2,24,128]{3,2,1,0:T(8,128)S(1)} %get-tuple-element.60), channel_id=1, source_target_pairs={{0,7},{1,2},{2,1},{3,4},{4,3},{5,6},{6,5},{7,0},{8,15},{9,10},{10,... | collective-permute-start | bytes 147464 | tf_op jit(solution)/shard_map/ppermute | solution.py:558
  16.8 3.0 %shard_map.54 = (f32[8,160,128]{2,1,0:T(8,128)S(1)}, f32[8,160,128]{2,1,0:T(8,128)S(1)}, f32[8,160,128]{2,1,0:T(8,128)S(1)}, f32[6,160,128]{2,1,0:T(8,128)S(1)},...) custom-call(f32[3,8,128,128]{3,2,1,0:T(8,128)S(1)} %get-tuple-elemen, ...), custom_call_target="tpu_custom_call" | custom-call | flops 3000000 | bytes 6000000 | tf_op jit(solution)/shard_map/pallas_call | solution.py:541
  19.8 0.0 collective-permute-done.4.corner_a
  19.8 1.7 %collective-permute-done.5.corner_b = f32[2,2,24,128]{3,2,1,0:T(8,128)S(1)} collective-permute-done((f32[2,2,24,128]{3,2,1,0:T(8,128)S(1)}, f32[2,2,24,128]{3,2,1,0:T(8,128)S(1)}, u32[]{:S(2)}, u32[]{:S(2)}) %collective-permute-start.5) | collective-permute-done | bytes 49184 | tf_op jit(solution)/shard_map/ppermute | solution.py:558
  21.6 0.0 collective-permute-done.from_a
  21.6 0.0 collective-permute-done.1.from_b
  21.6 3.1 %shard_map.55 = (f32[2,2,160,128]{3,2,1,0:T(8,128)S(1)}, f32[2,2,160,128]{3,2,1,0:T(8,128)S(1)}, f32[4,160,128]{2,1,0:T(8,128)S(1)}, f32[2,144,128]{2,1,0:T(8,128)S(1)}, f32[2,144,128]{2,1,0:T(8,128)S(1)}) custom-call(f32[8,160,128]{2,1,0:T(8,128)S(1)} %get-tuple-element.67.conc_in, f32[8,160,128]{2,1,0:T(8,128)S(1)} %get-tuple-element.68.adj_in, ...), custom_call_target="tpu_custom_call" | custom-call | flops 2000000 | bytes 4000000 | tf_op jit(solution)/shard_map/pallas_call | solution.py:541
  24.7 0.1 collective-permute-start.6
  24.7 2.1 %collective-permute-start.7 = (f32[2,144,128]{2,1,0:T(8,128)S(1)}, f32[2,144,128]{2,1,0:T(8,128)S(1)}, u32[]{:S(2)}, u32[]{:S(2)}) collective-permute-start(f32[2,144,128]{2,1,0:T(8,128)S(1)} %get-tuple-element.85), channel_id=1, source_target_pairs={{0,7},{1,2},{2,1},{3,4},{4,3},{5,6},{6,5},{7,0},{8,15},{9,10},{10,... | collective-permute-start | bytes 442376 | tf_op jit(solution)/shard_map/ppermute | solution.py:558
  26.9 1.8 %shard_map.56 = (f32[12,160,128]{2,1,0:T(8,128)S(1)}, f32[12,160,128]{2,1,0:T(8,128)S(1)}, f32[10,160,128]{2,1,0:T(8,128)S(1)}, f32[10,160,128]{2,1,0:T(8,128)S(1)}) custom-call(f32[3,8,128,128]{3,2,1,0:T(8,128)S(1)} %get-tuple-element.52.conc_own, f32[1088,128]{1,0:T(8,128)S(1)} %collective-permute-done.from_a, ...), custom_call_target="tpu_custom_call" | custom-call | flops 2000000 | bytes 4000000 | tf_op jit(solution)/shard_map/pallas_call | solution.py:541
  28.7 1.9 %shard_map.57 = (f32[4,160,128]{2,1,0:T(8,128)S(1)}, f32[4,160,128]{2,1,0:T(8,128)S(1)}, f32[6,160,128]{2,1,0:T(8,128)S(1)}) custom-call(f32[12,160,128]{2,1,0:T(8,128)S(1)} %get-tuple-element.74.conc, f32[12,160,128]{2,1,0:T(8,128)S(1)} %get-tuple-element.75.mob, f32[10,160,128]{2,1,0:T(8,128)S(1)} %get-tuple-element.76.chem, ...), custom_call_target="tpu_custom_call" | custom-call | flops 3000000 | bytes 6000000 | tf_op jit(solution)/shard_map/pallas_call | solution.py:541
  30.6 0.0 collective-permute-done.6.from_a
  30.6 1.5 %collective-permute-done.7.from_b = f32[2,144,128]{2,1,0:T(8,128)S(1)} collective-permute-done((f32[2,144,128]{2,1,0:T(8,128)S(1)}, f32[2,144,128]{2,1,0:T(8,128)S(1)}, u32[]{:S(2)}, u32[]{:S(2)}) %collective-permute-start.7) | collective-permute-done | bytes 147488 | tf_op jit(solution)/shard_map/ppermute | solution.py:558
  32.0 2.3 %shard_map.58 = (f32[2,2,160,128]{3,2,1,0:T(8,128)S(1)}, f32[2,2,160,128]{3,2,1,0:T(8,128)S(1)}, f32[2,144,128]{2,1,0:T(8,128)S(1)}, f32[2,144,128]{2,1,0:T(8,128)S(1)}) custom-call(f32[12,160,128]{2,1,0:T(8,128)S(1)} %get-tuple-element.74.conc, f32[12,160,128]{2,1,0:T(8,128)S(1)} %get-tuple-element.75.mob, f32[10,160,128]{2,1,0:T(8,128)S(1)} %get-tuple-element.76.chem, ...), custom_call_target="tpu_custom_call" | custom-call | flops 2000000 | bytes 4000000 | tf_op jit(solution)/shard_map/pallas_call | solution.py:541
  34.3 0.1 collective-permute-start.8
  34.4 1.3 %collective-permute-start.9 = (f32[2,144,128]{2,1,0:T(8,128)S(1)}, f32[2,144,128]{2,1,0:T(8,128)S(1)}, u32[]{:S(2)}, u32[]{:S(2)}) collective-permute-start(f32[2,144,128]{2,1,0:T(8,128)S(1)} %get-tuple-element.91), channel_id=1, source_target_pairs={{0,7},{1,2},{2,1},{3,4},{4,3},{5,6},{6,5},{7,0},{8,15},{9,10},{10,... | collective-permute-start | bytes 442376 | tf_op jit(solution)/shard_map/ppermute | solution.py:558
  35.7 1.8 %shard_map.53 = (f32[12,160,128]{2,1,0:T(8,128)S(1)}, f32[12,160,128]{2,1,0:T(8,128)S(1)}, f32[10,160,128]{2,1,0:T(8,128)S(1)}, f32[10,160,128]{2,1,0:T(8,128)S(1)}) custom-call(f32[3,8,128,128]{3,2,1,0:T(8,128)S(1)} %get-tuple-element.52.conc_own, f32[1088,128]{1,0:T(8,128)S(1)} %collective-permute-done.from_a, ...), custom_call_target="tpu_custom_call" | custom-call | flops 2000000 | bytes 4000000 | tf_op jit(solution)/shard_map/pallas_call | solution.py:541
  37.5 2.1 %shard_map.59 = (f32[4,128,128]{2,1,0:T(8,128)S(1)}, f32[4,64,128]{2,1,0:T(8,128)S(1)}, f32[6,160,128]{2,1,0:T(8,128)S(1)}) custom-call(f32[12,160,128]{2,1,0:T(8,128)S(1)} %get-tuple-element.61.conc, f32[12,160,128]{2,1,0:T(8,128)S(1)} %get-tuple-element.62.mob, f32[10,160,128]{2,1,0:T(8,128)S(1)} %get-tuple-element.63.chem, ...), custom_call_target="tpu_custom_call" | custom-call | flops 3000000 | bytes 6000000 | tf_op jit(solution)/shard_map/pallas_call | solution.py:541
  39.6 0.0 collective-permute-done.8.from_a
  39.6 1.4 %collective-permute-done.9.from_b = f32[2,144,128]{2,1,0:T(8,128)S(1)} collective-permute-done((f32[2,144,128]{2,1,0:T(8,128)S(1)}, f32[2,144,128]{2,1,0:T(8,128)S(1)}, u32[]{:S(2)}, u32[]{:S(2)}) %collective-permute-start.9) | collective-permute-done | bytes 147488 | tf_op jit(solution)/shard_map/ppermute | solution.py:558
  40.9 3.4 %shard_map.60 = (f32[1024,128]{1,0:T(8,128)}, f32[512,128]{1,0:T(8,128)}) custom-call(f32[12,160,128]{2,1,0:T(8,128)S(1)} %get-tuple-element.61.conc, f32[12,160,128]{2,1,0:T(8,128)S(1)} %get-tuple-element.62.mob, f32[10,160,128]{2,1,0:T(8,128)S(1)} %get-tuple-element.63.chem, f32[10,160,128]{2,1,0:T(8,128)S(1)} %get-tuple-element.64.curve, ...), custom_call_target="tpu_custom_call" | custom-call | flops 3000000 | bytes 6000000 | tf_op jit(solution)/shard_map/pallas_call | solution.py:541
  (1 shorter events, 0.0 us)
Async XLA Ops:
  2.4 19.1 %collective-permute-start = (f32[1088,128]{1,0:T(8,128)S(1)}, f32[1088,128]{1,0:T(8,128)S(1)}, u32[]{:S(2)}, u32[]{:S(2)}) collective-permute-start(f32[1088,128]{1,0:T(8,128)S(1)} %get-tuple-element.53), channel_id=1, source_target_pairs={{0,1},{1,0},{2,3},{3,2},{4,5},{5,4},{6,7},{7,6},{8,9},{9,8},{10,11... | collective-permute-start | bytes 1671176 | tf_op jit(solution)/shard_map/ppermute | solution.py:558
  2.9 18.6 %collective-permute-start.1 = (f32[1088,128]{1,0:T(8,128)S(1)}, f32[1088,128]{1,0:T(8,128)S(1)}, u32[]{:S(2)}, u32[]{:S(2)}) collective-permute-start(f32[1088,128]{1,0:T(8,128)S(1)} %get-tuple-element.54), channel_id=1, source_target_pairs={{0,7},{1,2},{2,1},{3,4},{4,3},{5,6},{6,5},{7,0},{8,15},{9,10},{10,... | collective-permute-start | bytes 1671176 | tf_op jit(solution)/shard_map/ppermute | solution.py:558
  8.4 5.0 %collective-permute-start.2 = (f32[8,24,128]{2,1,0:T(8,128)S(1)}, f32[8,24,128]{2,1,0:T(8,128)S(1)}, u32[]{:S(2)}, u32[]{:S(2)}) collective-permute-start(f32[8,24,128]{2,1,0:T(8,128)S(1)} %get-tuple-element.55), channel_id=1, source_target_pairs={{0,8},{8,0},{16,24},{24,16},{1,9},{9,1},{17,25},{25,17},{2,10},{10... | collective-permute-start | bytes 294920 | tf_op jit(solution)/shard_map/ppermute | solution.py:558
  9.9 5.5 %collective-permute-start.3 = (f32[8,24,128]{2,1,0:T(8,128)S(1)}, f32[8,24,128]{2,1,0:T(8,128)S(1)}, u32[]{:S(2)}, u32[]{:S(2)}) collective-permute-start(f32[8,24,128]{2,1,0:T(8,128)S(1)} %get-tuple-element.56), channel_id=1, source_target_pairs={{0,24},{8,16},{16,8},{24,0},{1,25},{9,17},{17,9},{25,1},{2,26},{10... | collective-permute-start | bytes 294920 | tf_op jit(solution)/shard_map/ppermute | solution.py:558
  15.5 4.3 %collective-permute-start.4 = (f32[2,2,24,128]{3,2,1,0:T(8,128)S(1)}, f32[2,2,24,128]{3,2,1,0:T(8,128)S(1)}, u32[]{:S(2)}, u32[]{:S(2)}) collective-permute-start(f32[2,2,24,128]{3,2,1,0:T(8,128)S(1)} %get-tuple-element.59), channel_id=1, source_target_pairs={{0,1},{1,0},{2,3},{3,2},{4,5},{5,4},{6,7},{7,6},{8,9},{9,8},{10,11... | collective-permute-start | bytes 147464 | tf_op jit(solution)/shard_map/ppermute | solution.py:558
  15.6 6.0 %collective-permute-start.5 = (f32[2,2,24,128]{3,2,1,0:T(8,128)S(1)}, f32[2,2,24,128]{3,2,1,0:T(8,128)S(1)}, u32[]{:S(2)}, u32[]{:S(2)}) collective-permute-start(f32[2,2,24,128]{3,2,1,0:T(8,128)S(1)} %get-tuple-element.60), channel_id=1, source_target_pairs={{0,7},{1,2},{2,1},{3,4},{4,3},{5,6},{6,5},{7,0},{8,15},{9,10},{10,... | collective-permute-start | bytes 147464 | tf_op jit(solution)/shard_map/ppermute | solution.py:558
  24.7 5.9 %collective-permute-start.6 = (f32[2,144,128]{2,1,0:T(8,128)S(1)}, f32[2,144,128]{2,1,0:T(8,128)S(1)}, u32[]{:S(2)}, u32[]{:S(2)}) collective-permute-start(f32[2,144,128]{2,1,0:T(8,128)S(1)} %get-tuple-element.84), channel_id=1, source_target_pairs={{0,1},{1,0},{2,3},{3,2},{4,5},{5,4},{6,7},{7,6},{8,9},{9,8},{10,11... | collective-permute-start | bytes 442376 | tf_op jit(solution)/shard_map/ppermute | solution.py:558
  24.7 7.3 %collective-permute-start.7 = (f32[2,144,128]{2,1,0:T(8,128)S(1)}, f32[2,144,128]{2,1,0:T(8,128)S(1)}, u32[]{:S(2)}, u32[]{:S(2)}) collective-permute-start(f32[2,144,128]{2,1,0:T(8,128)S(1)} %get-tuple-element.85), channel_id=1, source_target_pairs={{0,7},{1,2},{2,1},{3,4},{4,3},{5,6},{6,5},{7,0},{8,15},{9,10},{10,... | collective-permute-start | bytes 442376 | tf_op jit(solution)/shard_map/ppermute | solution.py:558
  34.3 5.3 %collective-permute-start.8 = (f32[2,144,128]{2,1,0:T(8,128)S(1)}, f32[2,144,128]{2,1,0:T(8,128)S(1)}, u32[]{:S(2)}, u32[]{:S(2)}) collective-permute-start(f32[2,144,128]{2,1,0:T(8,128)S(1)} %get-tuple-element.90), channel_id=1, source_target_pairs={{0,1},{1,0},{2,3},{3,2},{4,5},{5,4},{6,7},{7,6},{8,9},{9,8},{10,11... | collective-permute-start | bytes 442376 | tf_op jit(solution)/shard_map/ppermute | solution.py:558
  34.4 6.5 %collective-permute-start.9 = (f32[2,144,128]{2,1,0:T(8,128)S(1)}, f32[2,144,128]{2,1,0:T(8,128)S(1)}, u32[]{:S(2)}, u32[]{:S(2)}) collective-permute-start(f32[2,144,128]{2,1,0:T(8,128)S(1)} %get-tuple-element.91), channel_id=1, source_target_pairs={{0,7},{1,2},{2,1},{3,4},{4,3},{5,6},{6,5},{7,0},{8,15},{9,10},{10,... | collective-permute-start | bytes 442376 | tf_op jit(solution)/shard_map/ppermute | solution.py:558

commit v5 on v4

--- a/solution.py
+++ b/solution.py
@@ -14,7 +14,7 @@
 bath_potential = 0.5
 
 pad = 16
-chunk = 24
+chunk = 72
 depth = 2
 vmem_limit = 20 * 1024 * 1024
 f32 = jnp.float32

time: 44.5 us -> 42.8 us (0.962)
  Pallas kernels: 21.8 us -> 20.2 us
    pallas_call x11, Pallas kernels: 21.8 us -> 20.2 us  [call(): pl.pallas_call(kernel, out_shape=[jax.ShapeDtypeStruct(shape, f32) for sh...]
  transfers between devices with their start and end apart: 10 -> 10, of which waited for: 5 -> 5; matrix products, arithmetic and copies ran while one was open for 0% -> 0% of each run, Pallas kernels for 25% -> 26%
where the time goes in v5:
time: 42.8 us; the launch traced here: 42.7 us
  Pallas kernels  20.2 us (47%)
  starting transfers between devices  13.2 us (31%)
  waiting for transfers between devices  8.57 us (20%)
  between operations  0.76 us (2%)
    pallas_call x11, Pallas kernels, call(): pl.pallas_call(kernel, out_shape=[jax.ShapeDtypeStruct(shape, f32) for sh...  20.2 us
    ppermute x5, starting transfers between devices, swap(): lax.ppermute(value_b, axis, pairs_b)  10.9 us
    ppermute x5, waiting for transfers between devices, swap(): lax.ppermute(value_b, axis, pairs_b)  6.62 us
    ppermute x5, starting transfers between devices, swap(): lax.ppermute(value_a, axis, pairs_a)  2.29 us
    ppermute x5, waiting for transfers between devices, swap(): lax.ppermute(value_a, axis, pairs_a)  1.95 us
  transfers between devices with their start and end apart: 10, of which 5 were waited for; matrix products, arithmetic and copies ran while one was open for 0% of the time, Pallas kernels for 26%

profile of v5, /device:TPU:0, one launch (start us, length us, event | category | flops | bytes accessed | tf_op | source)
XLA Modules:
  0.0 42.7 jit_solution(15864320774427427084)
XLA Ops:
  0.6 1.8 %shard_map.50 = (f32[3,1024,128]{2,1,0:T(8,128)S(1)}, f32[1024,128]{1,0:T(8,128)S(1)}, f32[512,128]{1,0:T(8,128)S(1)}, f32[1088,128]{1,0:T(8,128)S(1)}, f32[1088,128]{1,0:T(8,128)S(1)}) custom-call(f32[3,1024,128]{2,1,0:T(8,128)} %bitcast.5, f32[1024,128]{1,0:T(8,128)} %bitcast.6, f32[512,128]{1,0:T(8,128)} %bitcast.7), custom_call_target="tpu_custom_call" | custom-call | flops 2000000 | bytes 4000000 | tf_op jit(solution)/shard_map/pallas_call | solution.py:541
  2.4 0.5 %collective-permute-start = (f32[1088,128]{1,0:T(8,128)S(1)}, f32[1088,128]{1,0:T(8,128)S(1)}, u32[]{:S(2)}, u32[]{:S(2)}) collective-permute-start(f32[1088,128]{1,0:T(8,128)S(1)} %get-tuple-element.53), channel_id=1, source_target_pairs={{0,1},{1,0},{2,3},{3,2},{4,5},{5,4},{6,7},{7,6},{8,9},{9,8},{10,11... | collective-permute-start | bytes 1671176 | tf_op jit(solution)/shard_map/ppermute | solution.py:558
  2.9 4.7 %collective-permute-start.1 = (f32[1088,128]{1,0:T(8,128)S(1)}, f32[1088,128]{1,0:T(8,128)S(1)}, u32[]{:S(2)}, u32[]{:S(2)}) collective-permute-start(f32[1088,128]{1,0:T(8,128)S(1)} %get-tuple-element.54), channel_id=1, source_target_pairs={{0,7},{1,2},{2,1},{3,4},{4,3},{5,6},{6,5},{7,0},{8,15},{9,10},{10,... | collective-permute-start | bytes 1671176 | tf_op jit(solution)/shard_map/ppermute | solution.py:558
  7.6 0.7 %shard_map.51 = (f32[3,8,128,128]{3,2,1,0:T(8,128)S(1)}, f32[8,128,128]{2,1,0:T(8,128)S(1)}, f32[8,128,128]{2,1,0:T(8,128)S(1)}, f32[8,24,128]{2,1,0:T(8,128)S(1)}, f32[8,24,128]{2,1,0:T(8,128)S(1)}) custom-call(f32[3,1024,128]{2,1,0:T(8,128)S(1)} %get-tuple-element.49.conc_in, f32[1024,128]{1,0:T(8,128)S(1)} %get-tuple-element.50.adj_in, ...), custom_call_target="tpu_custom_call" | custom-call | flops 1000000 | bytes 2000000 | tf_op jit(solution)/shard_map/pallas_call | solution.py:541
  8.4 1.6 %collective-permute-start.2 = (f32[8,24,128]{2,1,0:T(8,128)S(1)}, f32[8,24,128]{2,1,0:T(8,128)S(1)}, u32[]{:S(2)}, u32[]{:S(2)}) collective-permute-start(f32[8,24,128]{2,1,0:T(8,128)S(1)} %get-tuple-element.55), channel_id=1, source_target_pairs={{0,8},{8,0},{16,24},{24,16},{1,9},{9,1},{17,25},{25,17},{2,10},{10... | collective-permute-start | bytes 294920 | tf_op jit(solution)/shard_map/ppermute | solution.py:558
  9.9 1.5 %collective-permute-start.3 = (f32[8,24,128]{2,1,0:T(8,128)S(1)}, f32[8,24,128]{2,1,0:T(8,128)S(1)}, u32[]{:S(2)}, u32[]{:S(2)}) collective-permute-start(f32[8,24,128]{2,1,0:T(8,128)S(1)} %get-tuple-element.56), channel_id=1, source_target_pairs={{0,24},{8,16},{16,8},{24,0},{1,25},{9,17},{17,9},{25,1},{2,26},{10... | collective-permute-start | bytes 294920 | tf_op jit(solution)/shard_map/ppermute | solution.py:558
  11.4 1.9 %collective-permute-done.2.got_a = f32[8,24,128]{2,1,0:T(8,128)S(1)} collective-permute-done((f32[8,24,128]{2,1,0:T(8,128)S(1)}, f32[8,24,128]{2,1,0:T(8,128)S(1)}, u32[]{:S(2)}, u32[]{:S(2)}) %collective-permute-start.2) | collective-permute-done | bytes 98336 | tf_op jit(solution)/shard_map/ppermute | solution.py:558
  13.4 2.1 %collective-permute-done.3.got_b = f32[8,24,128]{2,1,0:T(8,128)S(1)} collective-permute-done((f32[8,24,128]{2,1,0:T(8,128)S(1)}, f32[8,24,128]{2,1,0:T(8,128)S(1)}, u32[]{:S(2)}, u32[]{:S(2)}) %collective-permute-start.3) | collective-permute-done | bytes 98336 | tf_op jit(solution)/shard_map/ppermute | solution.py:558
  15.5 0.1 collective-permute-start.4
  15.6 1.3 %collective-permute-start.5 = (f32[2,2,24,128]{3,2,1,0:T(8,128)S(1)}, f32[2,2,24,128]{3,2,1,0:T(8,128)S(1)}, u32[]{:S(2)}, u32[]{:S(2)}) collective-permute-start(f32[2,2,24,128]{3,2,1,0:T(8,128)S(1)} %get-tuple-element.60), channel_id=1, source_target_pairs={{0,7},{1,2},{2,1},{3,4},{4,3},{5,6},{6,5},{7,0},{8,15},{9,10},{10,... | collective-permute-start | bytes 147464 | tf_op jit(solution)/shard_map/ppermute | solution.py:558
  16.8 3.0 %shard_map.54 = (f32[8,160,128]{2,1,0:T(8,128)S(1)}, f32[8,160,128]{2,1,0:T(8,128)S(1)}, f32[8,160,128]{2,1,0:T(8,128)S(1)}, f32[6,160,128]{2,1,0:T(8,128)S(1)},...) custom-call(f32[3,8,128,128]{3,2,1,0:T(8,128)S(1)} %get-tuple-elemen, ...), custom_call_target="tpu_custom_call" | custom-call | flops 3000000 | bytes 6000000 | tf_op jit(solution)/shard_map/pallas_call | solution.py:541
  19.8 0.0 collective-permute-done.4.corner_a
  19.8 1.7 %collective-permute-done.5.corner_b = f32[2,2,24,128]{3,2,1,0:T(8,128)S(1)} collective-permute-done((f32[2,2,24,128]{3,2,1,0:T(8,128)S(1)}, f32[2,2,24,128]{3,2,1,0:T(8,128)S(1)}, u32[]{:S(2)}, u32[]{:S(2)}) %collective-permute-start.5) | collective-permute-done | bytes 49184 | tf_op jit(solution)/shard_map/ppermute | solution.py:558
  21.6 0.0 collective-permute-done.from_a
  21.6 0.0 collective-permute-done.1.from_b
  21.6 2.6 %shard_map.55 = (f32[2,2,160,128]{3,2,1,0:T(8,128)S(1)}, f32[2,2,160,128]{3,2,1,0:T(8,128)S(1)}, f32[4,160,128]{2,1,0:T(8,128)S(1)}, f32[2,144,128]{2,1,0:T(8,128)S(1)}, f32[2,144,128]{2,1,0:T(8,128)S(1)}) custom-call(f32[8,160,128]{2,1,0:T(8,128)S(1)} %get-tuple-element.67.conc_in, f32[8,160,128]{2,1,0:T(8,128)S(1)} %get-tuple-element.68.adj_in, ...), custom_call_target="tpu_custom_call" | custom-call | flops 2000000 | bytes 4000000 | tf_op jit(solution)/shard_map/pallas_call | solution.py:541
  24.1 0.1 collective-permute-start.6
  24.2 2.1 %collective-permute-start.7 = (f32[2,144,128]{2,1,0:T(8,128)S(1)}, f32[2,144,128]{2,1,0:T(8,128)S(1)}, u32[]{:S(2)}, u32[]{:S(2)}) collective-permute-start(f32[2,144,128]{2,1,0:T(8,128)S(1)} %get-tuple-element.85), channel_id=1, source_target_pairs={{0,7},{1,2},{2,1},{3,4},{4,3},{5,6},{6,5},{7,0},{8,15},{9,10},{10,... | collective-permute-start | bytes 442376 | tf_op jit(solution)/shard_map/ppermute | solution.py:558
  26.3 1.8 %shard_map.56 = (f32[12,160,128]{2,1,0:T(8,128)S(1)}, f32[12,160,128]{2,1,0:T(8,128)S(1)}, f32[10,160,128]{2,1,0:T(8,128)S(1)}, f32[10,160,128]{2,1,0:T(8,128)S(1)}) custom-call(f32[3,8,128,128]{3,2,1,0:T(8,128)S(1)} %get-tuple-element.52.conc_own, f32[1088,128]{1,0:T(8,128)S(1)} %collective-permute-done.from_a, ...), custom_call_target="tpu_custom_call" | custom-call | flops 2000000 | bytes 4000000 | tf_op jit(solution)/shard_map/pallas_call | solution.py:541
  28.1 1.9 %shard_map.57 = (f32[4,160,128]{2,1,0:T(8,128)S(1)}, f32[4,160,128]{2,1,0:T(8,128)S(1)}, f32[6,160,128]{2,1,0:T(8,128)S(1)}) custom-call(f32[12,160,128]{2,1,0:T(8,128)S(1)} %get-tuple-element.74.conc, f32[12,160,128]{2,1,0:T(8,128)S(1)} %get-tuple-element.75.mob, f32[10,160,128]{2,1,0:T(8,128)S(1)} %get-tuple-element.76.chem, ...), custom_call_target="tpu_custom_call" | custom-call | flops 3000000 | bytes 6000000 | tf_op jit(solution)/shard_map/pallas_call | solution.py:541
  30.0 0.0 collective-permute-done.6.from_a
  30.0 1.5 %collective-permute-done.7.from_b = f32[2,144,128]{2,1,0:T(8,128)S(1)} collective-permute-done((f32[2,144,128]{2,1,0:T(8,128)S(1)}, f32[2,144,128]{2,1,0:T(8,128)S(1)}, u32[]{:S(2)}, u32[]{:S(2)}) %collective-permute-start.7) | collective-permute-done | bytes 147488 | tf_op jit(solution)/shard_map/ppermute | solution.py:558
  31.5 1.7 %shard_map.58 = (f32[2,2,160,128]{3,2,1,0:T(8,128)S(1)}, f32[2,2,160,128]{3,2,1,0:T(8,128)S(1)}, f32[2,144,128]{2,1,0:T(8,128)S(1)}, f32[2,144,128]{2,1,0:T(8,128)S(1)}) custom-call(f32[12,160,128]{2,1,0:T(8,128)S(1)} %get-tuple-element.74.conc, f32[12,160,128]{2,1,0:T(8,128)S(1)} %get-tuple-element.75.mob, f32[10,160,128]{2,1,0:T(8,128)S(1)} %get-tuple-element.76.chem, ...), custom_call_target="tpu_custom_call" | custom-call | flops 2000000 | bytes 4000000 | tf_op jit(solution)/shard_map/pallas_call | solution.py:541
  33.2 0.1 collective-permute-start.8
  33.3 1.3 %collective-permute-start.9 = (f32[2,144,128]{2,1,0:T(8,128)S(1)}, f32[2,144,128]{2,1,0:T(8,128)S(1)}, u32[]{:S(2)}, u32[]{:S(2)}) collective-permute-start(f32[2,144,128]{2,1,0:T(8,128)S(1)} %get-tuple-element.91), channel_id=1, source_target_pairs={{0,7},{1,2},{2,1},{3,4},{4,3},{5,6},{6,5},{7,0},{8,15},{9,10},{10,... | collective-permute-start | bytes 442376 | tf_op jit(solution)/shard_map/ppermute | solution.py:558
  34.6 1.8 %shard_map.53 = (f32[12,160,128]{2,1,0:T(8,128)S(1)}, f32[12,160,128]{2,1,0:T(8,128)S(1)}, f32[10,160,128]{2,1,0:T(8,128)S(1)}, f32[10,160,128]{2,1,0:T(8,128)S(1)}) custom-call(f32[3,8,128,128]{3,2,1,0:T(8,128)S(1)} %get-tuple-element.52.conc_own, f32[1088,128]{1,0:T(8,128)S(1)} %collective-permute-done.from_a, ...), custom_call_target="tpu_custom_call" | custom-call | flops 2000000 | bytes 4000000 | tf_op jit(solution)/shard_map/pallas_call | solution.py:541
  36.4 2.1 %shard_map.59 = (f32[4,128,128]{2,1,0:T(8,128)S(1)}, f32[4,64,128]{2,1,0:T(8,128)S(1)}, f32[6,160,128]{2,1,0:T(8,128)S(1)}) custom-call(f32[12,160,128]{2,1,0:T(8,128)S(1)} %get-tuple-element.61.conc, f32[12,160,128]{2,1,0:T(8,128)S(1)} %get-tuple-element.62.mob, f32[10,160,128]{2,1,0:T(8,128)S(1)} %get-tuple-element.63.chem, ...), custom_call_target="tpu_custom_call" | custom-call | flops 3000000 | bytes 6000000 | tf_op jit(solution)/shard_map/pallas_call | solution.py:541
  38.5 0.0 collective-permute-done.8.from_a
  38.5 1.4 %collective-permute-done.9.from_b = f32[2,144,128]{2,1,0:T(8,128)S(1)} collective-permute-done((f32[2,144,128]{2,1,0:T(8,128)S(1)}, f32[2,144,128]{2,1,0:T(8,128)S(1)}, u32[]{:S(2)}, u32[]{:S(2)}) %collective-permute-start.9) | collective-permute-done | bytes 147488 | tf_op jit(solution)/shard_map/ppermute | solution.py:558
  39.8 2.8 %shard_map.60 = (f32[1024,128]{1,0:T(8,128)}, f32[512,128]{1,0:T(8,128)}) custom-call(f32[12,160,128]{2,1,0:T(8,128)S(1)} %get-tuple-element.61.conc, f32[12,160,128]{2,1,0:T(8,128)S(1)} %get-tuple-element.62.mob, f32[10,160,128]{2,1,0:T(8,128)S(1)} %get-tuple-element.63.chem, f32[10,160,128]{2,1,0:T(8,128)S(1)} %get-tuple-element.64.curve, ...), custom_call_target="tpu_custom_call" | custom-call | flops 3000000 | bytes 6000000 | tf_op jit(solution)/shard_map/pallas_call | solution.py:541
  (1 shorter events, 0.0 us)
Async XLA Ops:
  2.4 19.1 %collective-permute-start = (f32[1088,128]{1,0:T(8,128)S(1)}, f32[1088,128]{1,0:T(8,128)S(1)}, u32[]{:S(2)}, u32[]{:S(2)}) collective-permute-start(f32[1088,128]{1,0:T(8,128)S(1)} %get-tuple-element.53), channel_id=1, source_target_pairs={{0,1},{1,0},{2,3},{3,2},{4,5},{5,4},{6,7},{7,6},{8,9},{9,8},{10,11... | collective-permute-start | bytes 1671176 | tf_op jit(solution)/shard_map/ppermute | solution.py:558
  2.9 18.6 %collective-permute-start.1 = (f32[1088,128]{1,0:T(8,128)S(1)}, f32[1088,128]{1,0:T(8,128)S(1)}, u32[]{:S(2)}, u32[]{:S(2)}) collective-permute-start(f32[1088,128]{1,0:T(8,128)S(1)} %get-tuple-element.54), channel_id=1, source_target_pairs={{0,7},{1,2},{2,1},{3,4},{4,3},{5,6},{6,5},{7,0},{8,15},{9,10},{10,... | collective-permute-start | bytes 1671176 | tf_op jit(solution)/shard_map/ppermute | solution.py:558
  8.4 5.0 %collective-permute-start.2 = (f32[8,24,128]{2,1,0:T(8,128)S(1)}, f32[8,24,128]{2,1,0:T(8,128)S(1)}, u32[]{:S(2)}, u32[]{:S(2)}) collective-permute-start(f32[8,24,128]{2,1,0:T(8,128)S(1)} %get-tuple-element.55), channel_id=1, source_target_pairs={{0,8},{8,0},{16,24},{24,16},{1,9},{9,1},{17,25},{25,17},{2,10},{10... | collective-permute-start | bytes 294920 | tf_op jit(solution)/shard_map/ppermute | solution.py:558
  9.9 5.5 %collective-permute-start.3 = (f32[8,24,128]{2,1,0:T(8,128)S(1)}, f32[8,24,128]{2,1,0:T(8,128)S(1)}, u32[]{:S(2)}, u32[]{:S(2)}) collective-permute-start(f32[8,24,128]{2,1,0:T(8,128)S(1)} %get-tuple-element.56), channel_id=1, source_target_pairs={{0,24},{8,16},{16,8},{24,0},{1,25},{9,17},{17,9},{25,1},{2,26},{10... | collective-permute-start | bytes 294920 | tf_op jit(solution)/shard_map/ppermute | solution.py:558
  15.5 4.3 %collective-permute-start.4 = (f32[2,2,24,128]{3,2,1,0:T(8,128)S(1)}, f32[2,2,24,128]{3,2,1,0:T(8,128)S(1)}, u32[]{:S(2)}, u32[]{:S(2)}) collective-permute-start(f32[2,2,24,128]{3,2,1,0:T(8,128)S(1)} %get-tuple-element.59), channel_id=1, source_target_pairs={{0,1},{1,0},{2,3},{3,2},{4,5},{5,4},{6,7},{7,6},{8,9},{9,8},{10,11... | collective-permute-start | bytes 147464 | tf_op jit(solution)/shard_map/ppermute | solution.py:558
  15.6 6.0 %collective-permute-start.5 = (f32[2,2,24,128]{3,2,1,0:T(8,128)S(1)}, f32[2,2,24,128]{3,2,1,0:T(8,128)S(1)}, u32[]{:S(2)}, u32[]{:S(2)}) collective-permute-start(f32[2,2,24,128]{3,2,1,0:T(8,128)S(1)} %get-tuple-element.60), channel_id=1, source_target_pairs={{0,7},{1,2},{2,1},{3,4},{4,3},{5,6},{6,5},{7,0},{8,15},{9,10},{10,... | collective-permute-start | bytes 147464 | tf_op jit(solution)/shard_map/ppermute | solution.py:558
  24.1 5.9 %collective-permute-start.6 = (f32[2,144,128]{2,1,0:T(8,128)S(1)}, f32[2,144,128]{2,1,0:T(8,128)S(1)}, u32[]{:S(2)}, u32[]{:S(2)}) collective-permute-start(f32[2,144,128]{2,1,0:T(8,128)S(1)} %get-tuple-element.84), channel_id=1, source_target_pairs={{0,1},{1,0},{2,3},{3,2},{4,5},{5,4},{6,7},{7,6},{8,9},{9,8},{10,11... | collective-permute-start | bytes 442376 | tf_op jit(solution)/shard_map/ppermute | solution.py:558
  24.2 7.3 %collective-permute-start.7 = (f32[2,144,128]{2,1,0:T(8,128)S(1)}, f32[2,144,128]{2,1,0:T(8,128)S(1)}, u32[]{:S(2)}, u32[]{:S(2)}) collective-permute-start(f32[2,144,128]{2,1,0:T(8,128)S(1)} %get-tuple-element.85), channel_id=1, source_target_pairs={{0,7},{1,2},{2,1},{3,4},{4,3},{5,6},{6,5},{7,0},{8,15},{9,10},{10,... | collective-permute-start | bytes 442376 | tf_op jit(solution)/shard_map/ppermute | solution.py:558
  33.2 5.3 %collective-permute-start.8 = (f32[2,144,128]{2,1,0:T(8,128)S(1)}, f32[2,144,128]{2,1,0:T(8,128)S(1)}, u32[]{:S(2)}, u32[]{:S(2)}) collective-permute-start(f32[2,144,128]{2,1,0:T(8,128)S(1)} %get-tuple-element.90), channel_id=1, source_target_pairs={{0,1},{1,0},{2,3},{3,2},{4,5},{5,4},{6,7},{7,6},{8,9},{9,8},{10,11... | collective-permute-start | bytes 442376 | tf_op jit(solution)/shard_map/ppermute | solution.py:558
  33.3 6.5 %collective-permute-start.9 = (f32[2,144,128]{2,1,0:T(8,128)S(1)}, f32[2,144,128]{2,1,0:T(8,128)S(1)}, u32[]{:S(2)}, u32[]{:S(2)}) collective-permute-start(f32[2,144,128]{2,1,0:T(8,128)S(1)} %get-tuple-element.91), channel_id=1, source_target_pairs={{0,7},{1,2},{2,1},{3,4},{4,3},{5,6},{6,5},{7,0},{8,15},{9,10},{10,... | collective-permute-start | bytes 442376 | tf_op jit(solution)/shard_map/ppermute | solution.py:558

commit v6 on v5

--- a/solution.py
+++ b/solution.py
@@ -70,7 +70,7 @@
     curve(span, inv - 2.0 * mix_energy)
 
 
-def face_sums(adj, mob, chem, at, size, mask):
+def face_sums(adj, mob, chem, at, size, mask, across=(1, -1)):
     span = slice(at, at + size)
     a = adj(0, span)
     m = None if mob is None else mob(0, span)
@@ -79,9 +79,7 @@
     for dy, cut in (
         (0, slice(at + 1, at + size + 1)),
         (0, slice(at - 1, at + size - 1)),
-        (1, span),
-        (-1, span),
-    ):
+    ) + tuple((dy, span) for dy in across):
         diff = adj(dy, cut) - a
         if mob is not None:
             term = (mob(dy, cut) + m) * diff
@@ -351,7 +349,7 @@
 
 
 def first_interior(steps, rows, cols, nz, conc_own, adj_own, rate_own, x_low, x_high,
-                   conc, adj, rate, chem, curve, pot, out, grad, mob, part):
+                   conc, adj, rate, chem, curve, pot, out, grad, ahead, mob, part):
     places, _ = slots(steps)
     low, high = reach(cols)
     lanes = adj.shape[2]
@@ -359,6 +357,8 @@
         put_own(conc, y, conc_own[0, y], y, places[1], cols, x_low, x_high)
         put_own(adj, y, adj_own[y], y, places[0], cols, x_low, x_high)
         put_own(rate, y, rate_own[y], y, places[steps + 1], cols, x_low, x_high)
+    put_ahead(ahead, conc_own, 1, x_low, x_high, places, rows, cols)
+
     def mob_row(y, _):
         for at, size in chunks(low - 8, high + 8):
             c = conc[y, at : at + size, :]
@@ -386,17 +386,35 @@
         out[to] = ref[at]
 
 
-def send_rows(out, to_a, to_b, cols):
+def send_rows(out, ahead, rate, to_a, to_b, open_g, cols, nz):
     low, high = reach(cols)
+    rows, lanes = rate.shape[0], rate.shape[2]
+    for s in range(2):
+        for at, size in chunks(low, high):
+            mask = face_mask(size, lanes, nz)
+            a, _mu, flow, _pair = face_sums(
+                lambda dy, cut: out[s, dy, cut, :], lambda dy, cut: ahead[s, dy, cut, :], None,
+                at, size, mask, (1,)
+            )
+            open_g[s, at - low : at - low + size, :] = source(
+                flow, rate[s * (rows - 1), at : at + size, :], a
+            )
     even = is_even("gy")
-    for k in range(depth):
-        for to, side in ((to_a, jnp.where(even, 1, 0)), (to_b, jnp.where(even, 0, 1))):
-            to[k] = out[side, jnp.where(side == 1, depth - 1 - k, k), low:high, :]
+    for to, side in ((to_a, jnp.where(even, 1, 0)), (to_b, jnp.where(even, 0, 1))):
+        to[0] = out[side, 0, low:high, :]
+        to[1] = open_g[side]
+
+
+def put_ahead(ahead, conc_own, back, x_low, x_high, places, rows, cols):
+    for s, k, y in sides_of(rows):
+        put_own(ahead.at[s], k, conc_own[back, y], y, places[1 + back], cols, x_low, x_high)
+        c = ahead[s, k]
+        ahead[s, k] = c * (1.0 - c)
 
 
 def first_boundary(steps, rows, cols, nz, conc_in, adj_in, rate_in, chem_in, curve_in, pot_in,
-                   from_a, from_b, corner_a, corner_b,
-                   out, grad, rate, to_a, to_b, conc, adj, mob, chem, curve, pot, part):
+                   from_a, from_b, corner_a, corner_b, ahead,
+                   out, grad, to_a, to_b, rate, conc, adj, mob, chem, curve, pot, part, open_g):
     places, _ = slots(steps)
     low, high = reach(cols)
     half = cols // 2
@@ -439,11 +457,11 @@
 
     boundary(rows, cols, nz, (conc, depth), (mob, depth), (chem, 1), (curve, 1), (adj, depth),
              rate, pot, part, grad, None, store, True)
-    send_rows(out, to_a, to_b, cols)
+    send_rows(out, ahead, rate_in, to_a, to_b, open_g, cols, nz)
 
 
 def prepare_kernel(steps, rows, cols, nz, back, conc_own, from_a, from_b, x_low, x_high,
-                   corner_a, corner_b, conc, mob, chem, curve):
+                   corner_a, corner_b, conc, mob, chem, curve, *ahead):
     places, _ = slots(steps)
     low, high = reach(cols)
     lanes = conc.shape[2]
@@ -455,6 +473,9 @@
             span = pl.ds(((1 + back) * depth + at) * cols, cols)
             put_halo(conc, base + at, halo[span, :], at, place, cols, corner)
 
+    if ahead:
+        put_ahead(ahead[0], conc_own, back + 1, x_low, x_high, places, rows, cols)
+
     def mob_row(row, _):
         for at, size in chunks(low - 8, high + 8):
             c = conc[row, at : at + size, :]
@@ -471,26 +492,59 @@
     lax.fori_loop(0, rows + 2, mu_row, 0)
 
 
-def next_interior(rows, cols, nz, final, conc, mob, chem, curve, rate, inner, outer, before,
-                  *rest):
+def next_interior(rows, cols, nz, final, conc, mob, chem, curve, rate, inner, outer, *rest):
     if final:
-        out, grad_out, pot, adj, part, grad, result = rest
+        before, out, tiles, grad_out, adj, pot, part, grad = rest
+    elif len(rest) == 8:
+        inner_grad, outer_grad, out, grad, adj, pot, part, before = rest
+        for k in range(rows - 2 * depth):
+            before[depth + k] = inner_grad[k]
+        for s, k, y in sides_of(rows):
+            before[y] = outer_grad[s, k]
     else:
-        result, grad, pot, adj, part = rest
+        before, out, grad, adj, pot, part = rest
+    low, high = reach(cols)
+    lanes = adj.shape[2]
+    skip = (inner.shape[0] - (rows - 2 * depth)) // 2
     for k in range(rows - 2 * depth):
-        adj[depth + k] = inner[k]
+        adj[1 + depth + k] = inner[skip + k]
     for s, k, y in sides_of(rows):
-        adj[y] = outer[s, k]
-
-    def store(k, span, value):
-        result[k, span, :] = value
-
-    interior(rows, cols, nz, (conc, depth), (mob, depth), (chem, 1), (curve, 1), (adj, 0),
-             (rate, 0), pot, part, grad, before, store)
+        adj[1 + y] = outer[s, k]
+    adj[0] = outer[0, 0]
+    adj[1 + rows] = outer[1, 0]
+    pot[0] = jnp.zeros(pot.shape[1:], f32)
+    pot[1 + rows] = jnp.zeros(pot.shape[1:], f32)
+
+    def body(y, _):
+        for at, size in chunks(low, high):
+            mask = face_mask(size, lanes, nz)
+            span = slice(at, at + size)
+            a, mu, flow, pair = face_sums(
+                row_of(adj, y + 1), row_of(mob, y + depth), row_of(chem, y + 1), at, size, mask
+            )
+            g = source(flow, rate[y, span, :], a)
+            pot[y + 1, span, :] = g
+            part[y, span, :] = partial(
+                a, conc[y + depth, span, :], pair, curve[y + 1, span, :], g
+            )
+            grad[y, span, :] = gain(a, mu, before[y, span, :])
+        return 0
+
+    def close(y, _):
+        for at, size in chunks(low, high):
+            mask = face_mask(size, lanes, nz)
+            span = slice(at, at + size)
+            _g, lap = laplace(row_of(pot, y + 1), at, size, mask)
+            out[y, span, :] = part[y, span, :] - grad_energy * lap
+        return 0
+
+    lax.fori_loop(0, rows, body, 0)
+    lax.fori_loop(0, rows, close, 0)
     if final:
-        for k in range(rows - 2 * depth):
-            out[k] = result[k, pad : pad + cols, :].T
-            grad_out[k] = fold(grad[k, pad : pad + cols, :].T, nz)
+        for y in range(rows):
+            grad_out[pl.ds(y, nz, stride=rows), :] = fold(grad[y, pad : pad + cols, :].T, nz)
+        for y in range(depth, rows - depth):
+            tiles[pl.ds(y, lanes, stride=rows), :] = out[y, pad : pad + cols, :].T
 
 
 def fold(value, nz):
@@ -500,38 +554,51 @@
     return total
 
 
-def next_boundary(rows, cols, nz, final, conc, mob, chem, curve, rate, inner, outer, pot_in,
-                  before, from_a, from_b, *rest):
+def next_boundary(rows, cols, nz, final, conc, mob, chem, curve, inside, outer, from_a, from_b,
+                  *rest):
+    if final:
+        tiles, out, halo, delta, result = rest
+    else:
+        ahead, rate, result, to_a, to_b, halo, delta, open_g = rest
     low, high = reach(cols)
+    lanes = conc.shape[2]
+    even = is_even("gy")
+    for got, side in ((from_a, jnp.where(even, 1, 0)), (from_b, jnp.where(even, 0, 1))):
+        for k in range(2):
+            halo[side, k, low:high, :] = got[k]
+    for s in range(2):
+        y, beyond = s * (rows - 1), s * (rows + 1) - 1
+        for at, size in chunks(low, high):
+            span = slice(at, at + size)
+            diff = halo[s, 0, span, :] - outer[s, 0, span, :]
+            both = mob[depth + beyond, span, :] + mob[depth + y, span, :]
+            delta[s, span, :] = (0.5 * diff_step) * both * diff
+        for at, size in chunks(low, high):
+            mask = face_mask(size, lanes, nz)
+            span = slice(at, at + size)
+            more = delta[s, span, :]
+            diff = halo[s, 0, span, :] - outer[s, 0, span, :]
+            pair = (chem[1 + beyond, span, :] - chem[1 + y, span, :]) * diff
+            step_z = (up(more) - more) * mask
+            lap = (
+                (delta[s, at + 1 : at + size + 1, :] + delta[s, at - 1 : at + size - 1, :])
+                + (halo[s, 1, span, :] - more)
+                - 4.0 * more
+                + (step_z - down(step_z))
+            )
+            c = conc[depth + y, span, :]
+            result[s, 0, span, :] = (
+                inside[y, span, :]
+                + ((1.0 - 2.0 * c) * ((-0.5 * diff_step) * pair) + curve[1 + y, span, :] * more)
+                - grad_energy * lap
+            )
+            result[s, 1, span, :] = inside[1 + s * (rows - 3), span, :] - grad_energy * more
     if final:
-        inner_out, inner_grad, out, grad_out, adj, pot, part, grad, result = rest
-    else:
-        result, grad, to_a, to_b, adj, pot, part = rest
-    adj[2 * depth] = inner[0]
-    adj[rows - 1] = inner[rows - 2 * depth - 1]
-    for s, k, y in sides_of(rows):
-        adj[depth + y] = outer[s, k]
-    for halo, base in zip((from_a, from_b), landings(rows)):
-        for at in range(depth):
-            adj[base + at, low:high, :] = halo[at]
-    for y in (1, 2, rows - 3, rows - 2):
-        pot[1 + y] = pot_in[y - 1]
-
-    def store(s, k, span, value):
-        result[s, k, span, :] = value
-
-    boundary(rows, cols, nz, (conc, depth), (mob, depth), (chem, 1), (curve, 1), (adj, depth),
-             rate, pot, part, grad, before, store, False)
-    if final:
-        lanes = conc.shape[2]
-        for k in range(rows - 2 * depth):
-            out[pl.ds(depth + k, lanes, stride=rows), :] = inner_out[k]
-            grad_out[pl.ds(depth + k, nz, stride=rows), :] = inner_grad[k]
+        out[...] = tiles[...]
         for s, k, y in sides_of(rows):
             out[pl.ds(y, lanes, stride=rows), :] = result[s, k, pad : pad + cols, :].T
-            grad_out[pl.ds(y, nz, stride=rows), :] = fold(grad[s, k, pad : pad + cols, :].T, nz)
     else:
-        send_rows(result, to_a, to_b, cols)
+        send_rows(result, ahead, rate, to_a, to_b, open_g, cols, nz)
 
 
 def call(kernel, outs, scratch, *operands, cost=0, far=False):
@@ -569,6 +636,9 @@
     def field(count):
         return (count, width, lanes)
 
+    both = (2, depth, width, lanes)
+    edge = (2, cols + 16, lanes)
+    open_g = (2, cols + 16, lanes)
     raw = [(steps, flat, cols), (flat, cols), (nz * rows, cols)]
     conc_raw, adj_raw, rate_raw, main_a, main_b = call(
         functools.partial(edge_kernel, steps, rows, cols, nz),
@@ -596,58 +666,64 @@
     )
     corner_a, corner_b = swap(corner_a, corner_b, "gy")
 
-    conc, adj, rate_in, chem, curve, pot, inner, inner_grad = call(
+    conc, adj, rate, chem, curve, pot, inner, inner_grad, ahead = call(
         functools.partial(first_interior, steps, rows, cols, nz),
-        [field(rows)] * 3 + [field(rows - 2)] * 3 + [field(inside)] * 2,
+        [field(rows)] * 3 + [field(rows - 2)] * 3 + [field(inside)] * 2 + [both],
         [field(rows), field(inside)],
         conc_own, adj_own, rate_own, x_low, x_high,
         cost=3,
     )
-    both = (2, depth, width, lanes)
-    edge = (depth, cols + 16, lanes)
-    outer, outer_grad, rate, to_a, to_b = call(
+    outer, outer_grad, to_a, to_b = call(
         functools.partial(first_boundary, steps, rows, cols, nz),
-        [both, both, field(4), edge, edge],
-        [field(rows + 2 * depth)] * 3 + [field(rows + 2)] * 3 + [both],
-        conc, adj, rate_in, chem, curve, pot, main_a, main_b, corner_a, corner_b,
+        [both, both, edge, edge],
+        [field(4)] + [field(rows + 2 * depth)] * 3 + [field(rows + 2)] * 3 + [both, open_g],
+        conc, adj, rate, chem, curve, pot, main_a, main_b, corner_a, corner_b, ahead,
         cost=2,
     )
+    before = (inner_grad, outer_grad)
     for back in range(1, steps):
         adj_a, adj_b = swap(to_a, to_b, "gy")
         final = back == steps - 1
         fields = call(
             functools.partial(prepare_kernel, steps, rows, cols, nz, back),
-            [field(rows + 2 * depth)] * 2 + [field(rows + 2)] * 2,
+            [field(rows + 2 * depth)] * 2 + [field(rows + 2)] * 2 + ([] if final else [both]),
             [],
             conc_own, main_a, main_b, x_low, x_high, corner_a, corner_b,
             cost=2,
         )
-        tiles = [(inside, lanes, cols), (inside, nz, cols)]
-        results = call(
-            functools.partial(next_interior, rows, cols, nz, final),
-            (tiles if final else [field(inside)] * 2) + [field(rows - 2)],
-            [field(rows), field(inside)] + ([field(inside)] * 2 if final else []),
-            *fields, rate_in, inner, outer, inner_grad,
-            cost=3,
-        )
-        pot = results[2]
+        fields, ahead = fields[:4], fields[4:]
+        work = [field(rows + 2)] * 2 + [field(rows)]
         if final:
-            adj, grad = call(
+            rows_in, tiles, grad = call(
+                functools.partial(next_interior, rows, cols, nz, final),
+                [field(rows), (flat, cols), (nz * rows, cols)],
+                work + [field(rows)],
+                *fields, rate, inner, outer, *before,
+                cost=3,
+            )
+            (adj,) = call(
                 functools.partial(next_boundary, rows, cols, nz, final),
-                [(flat, cols), (nz * rows, cols)],
-                [field(rows + 2 * depth), field(rows + 2), both, both, both],
-                *fields, rate, inner, outer, pot, outer_grad, adj_a, adj_b, results[0], results[1],
+                [(flat, cols)],
+                [both, field(2), both],
+                *fields, rows_in, outer, adj_a, adj_b, tiles,
+                cost=1,
+            )
+        else:
+            rows_in, grad = call(
+                functools.partial(next_interior, rows, cols, nz, final),
+                [field(rows)] * 2,
+                work + ([field(rows)] if len(before) == 2 else []),
+                *fields, rate, inner, outer, *before,
                 cost=3,
             )
-        else:
-            new_outer, outer_grad, to_a, to_b = call(
+            outer, to_a, to_b = call(
                 functools.partial(next_boundary, rows, cols, nz, final),
-                [both, both, edge, edge],
-                [field(rows + 2 * depth), field(rows + 2), both],
-                *fields, rate, inner, outer, pot, outer_grad, adj_a, adj_b,
-                cost=2,
-            )
-            inner, inner_grad, outer = results[0], results[1], new_outer
+                [both, edge, edge],
+                [both, field(2), open_g],
+                *fields, rows_in, outer, adj_a, adj_b, *ahead, rate,
+                cost=1,
+            )
+            inner, before = rows_in, (grad,)
     return adj.reshape(adjoint_end.shape), grad.reshape(rate_field.shape)
 
 

time: 42.8 us -> 40.5 us (0.946)
  waiting for transfers between devices: 8.57 us -> 5.99 us
    ppermute x5, waiting for transfers between devices: 6.62 us -> 4.04 us  [swap(): lax.ppermute(value_b, axis, pairs_b)]
  transfers between devices with their start and end apart: 10 -> 10, of which waited for: 5 -> 4; matrix products, arithmetic and copies ran while one was open for 0% -> 0% of each run, Pallas kernels for 26% -> 36%
where the time goes in v6:
time: 40.5 us; the launch traced here: 40.3 us
  Pallas kernels  20.5 us (51%)
  starting transfers between devices  13.2 us (33%)
  waiting for transfers between devices  5.99 us (15%)
  between operations  0.73 us (2%)
    pallas_call x11, Pallas kernels, call(): pl.pallas_call(kernel, out_shape=[jax.ShapeDtypeStruct(shape, f32) for sh...  20.5 us
    ppermute x5, starting transfers between devices, swap(): lax.ppermute(value_b, axis, pairs_b)  10.9 us
    ppermute x5, waiting for transfers between devices, swap(): lax.ppermute(value_b, axis, pairs_b)  4.04 us
    ppermute x5, starting transfers between devices, swap(): lax.ppermute(value_a, axis, pairs_a)  2.29 us
    ppermute x5, waiting for transfers between devices, swap(): lax.ppermute(value_a, axis, pairs_a)  1.95 us
  transfers between devices with their start and end apart: 10, of which 4 were waited for; matrix products, arithmetic and copies ran while one was open for 0% of the time, Pallas kernels for 36%

profile of v6, /device:TPU:0, one launch (start us, length us, event | category | flops | bytes accessed | tf_op | source)
XLA Modules:
  0.0 40.3 jit_solution(6170246050134255384)
XLA Ops:
  0.6 1.8 %shard_map.50 = (f32[3,1024,128]{2,1,0:T(8,128)S(1)}, f32[1024,128]{1,0:T(8,128)S(1)}, f32[512,128]{1,0:T(8,128)S(1)}, f32[1088,128]{1,0:T(8,128)S(1)}, f32[1088,128]{1,0:T(8,128)S(1)}) custom-call(f32[3,1024,128]{2,1,0:T(8,128)} %bitcast.5, f32[1024,128]{1,0:T(8,128)} %bitcast.7, f32[512,128]{1,0:T(8,128)} %bitcast.8), custom_call_target="tpu_custom_call" | custom-call | flops 2000000 | bytes 4000000 | tf_op jit(solution)/shard_map/pallas_call | solution.py:608
  2.4 0.5 %collective-permute-start = (f32[1088,128]{1,0:T(8,128)S(1)}, f32[1088,128]{1,0:T(8,128)S(1)}, u32[]{:S(2)}, u32[]{:S(2)}) collective-permute-start(f32[1088,128]{1,0:T(8,128)S(1)} %get-tuple-element.50), channel_id=1, source_target_pairs={{0,1},{1,0},{2,3},{3,2},{4,5},{5,4},{6,7},{7,6},{8,9},{9,8},{10,11... | collective-permute-start | bytes 1671176 | tf_op jit(solution)/shard_map/ppermute | solution.py:625
  2.9 4.7 %collective-permute-start.1 = (f32[1088,128]{1,0:T(8,128)S(1)}, f32[1088,128]{1,0:T(8,128)S(1)}, u32[]{:S(2)}, u32[]{:S(2)}) collective-permute-start(f32[1088,128]{1,0:T(8,128)S(1)} %get-tuple-element.51), channel_id=1, source_target_pairs={{0,7},{1,2},{2,1},{3,4},{4,3},{5,6},{6,5},{7,0},{8,15},{9,10},{10,... | collective-permute-start | bytes 1671176 | tf_op jit(solution)/shard_map/ppermute | solution.py:625
  7.6 0.7 %shard_map.51 = (f32[3,8,128,128]{3,2,1,0:T(8,128)S(1)}, f32[8,128,128]{2,1,0:T(8,128)S(1)}, f32[8,128,128]{2,1,0:T(8,128)S(1)}, f32[8,24,128]{2,1,0:T(8,128)S(1)}, f32[8,24,128]{2,1,0:T(8,128)S(1)}) custom-call(f32[3,1024,128]{2,1,0:T(8,128)S(1)} %get-tuple-element.46.conc_in, f32[1024,128]{1,0:T(8,128)S(1)} %get-tuple-element.47.adj_in, ...), custom_call_target="tpu_custom_call" | custom-call | flops 1000000 | bytes 2000000 | tf_op jit(solution)/shard_map/pallas_call | solution.py:608
  8.4 1.6 %collective-permute-start.2 = (f32[8,24,128]{2,1,0:T(8,128)S(1)}, f32[8,24,128]{2,1,0:T(8,128)S(1)}, u32[]{:S(2)}, u32[]{:S(2)}) collective-permute-start(f32[8,24,128]{2,1,0:T(8,128)S(1)} %get-tuple-element.52), channel_id=1, source_target_pairs={{0,8},{8,0},{16,24},{24,16},{1,9},{9,1},{17,25},{25,17},{2,10},{10... | collective-permute-start | bytes 294920 | tf_op jit(solution)/shard_map/ppermute | solution.py:625
  9.9 1.5 %collective-permute-start.3 = (f32[8,24,128]{2,1,0:T(8,128)S(1)}, f32[8,24,128]{2,1,0:T(8,128)S(1)}, u32[]{:S(2)}, u32[]{:S(2)}) collective-permute-start(f32[8,24,128]{2,1,0:T(8,128)S(1)} %get-tuple-element.53), channel_id=1, source_target_pairs={{0,24},{8,16},{16,8},{24,0},{1,25},{9,17},{17,9},{25,1},{2,26},{10... | collective-permute-start | bytes 294920 | tf_op jit(solution)/shard_map/ppermute | solution.py:625
  11.4 1.9 %collective-permute-done.2.got_a = f32[8,24,128]{2,1,0:T(8,128)S(1)} collective-permute-done((f32[8,24,128]{2,1,0:T(8,128)S(1)}, f32[8,24,128]{2,1,0:T(8,128)S(1)}, u32[]{:S(2)}, u32[]{:S(2)}) %collective-permute-start.2) | collective-permute-done | bytes 98336 | tf_op jit(solution)/shard_map/ppermute | solution.py:625
  13.4 2.1 %collective-permute-done.3.got_b = f32[8,24,128]{2,1,0:T(8,128)S(1)} collective-permute-done((f32[8,24,128]{2,1,0:T(8,128)S(1)}, f32[8,24,128]{2,1,0:T(8,128)S(1)}, u32[]{:S(2)}, u32[]{:S(2)}) %collective-permute-start.3) | collective-permute-done | bytes 98336 | tf_op jit(solution)/shard_map/ppermute | solution.py:625
  15.5 0.1 collective-permute-start.4
  15.6 1.3 %collective-permute-start.5 = (f32[2,2,24,128]{3,2,1,0:T(8,128)S(1)}, f32[2,2,24,128]{3,2,1,0:T(8,128)S(1)}, u32[]{:S(2)}, u32[]{:S(2)}) collective-permute-start(f32[2,2,24,128]{3,2,1,0:T(8,128)S(1)} %get-tuple-element.57), channel_id=1, source_target_pairs={{0,7},{1,2},{2,1},{3,4},{4,3},{5,6},{6,5},{7,0},{8,15},{9,10},{10,... | collective-permute-start | bytes 147464 | tf_op jit(solution)/shard_map/ppermute | solution.py:625
  16.8 3.0 %shard_map.54 = (f32[8,160,128]{2,1,0:T(8,128)S(1)}, f32[8,160,128]{2,1,0:T(8,128)S(1)}, f32[8,160,128]{2,1,0:T(8,128)S(1)}, f32[6,160,128]{2,1,0:T(8,128)S(1)},...) custom-call(f32[3,8,128,128]{3,2,1,0:T(8,128)S(1)} %get-tuple-elemen, ...), custom_call_target="tpu_custom_call" | custom-call | flops 3000000 | bytes 6000000 | tf_op jit(solution)/shard_map/pallas_call | solution.py:608
  19.9 0.0 collective-permute-done.4.corner_a
  19.9 1.7 %collective-permute-done.5.corner_b = f32[2,2,24,128]{3,2,1,0:T(8,128)S(1)} collective-permute-done((f32[2,2,24,128]{3,2,1,0:T(8,128)S(1)}, f32[2,2,24,128]{3,2,1,0:T(8,128)S(1)}, u32[]{:S(2)}, u32[]{:S(2)}) %collective-permute-start.5) | collective-permute-done | bytes 49184 | tf_op jit(solution)/shard_map/ppermute | solution.py:625
  21.6 0.0 collective-permute-done.from_a
  21.6 0.0 collective-permute-done.1.from_b
  21.6 2.8 %shard_map.56 = (f32[2,2,160,128]{3,2,1,0:T(8,128)S(1)}, f32[2,2,160,128]{3,2,1,0:T(8,128)S(1)}, f32[2,144,128]{2,1,0:T(8,128)S(1)}, f32[2,144,128]{2,1,0:T(8,128)S(1)}) custom-call(f32[8,160,128]{2,1,0:T(8,128)S(1)} %get-tuple-element.70.conc_in, f32[8,160,128]{2,1,0:T(8,128)S(1)} %get-tuple-element.71.adj_in, ...), custom_call_target="tpu_custom_call" | custom-call | flops 2000000 | bytes 4000000 | tf_op jit(solution)/shard_map/pallas_call | solution.py:608
  24.4 0.1 collective-permute-start.6
  24.4 2.1 %collective-permute-start.7 = (f32[2,144,128]{2,1,0:T(8,128)S(1)}, f32[2,144,128]{2,1,0:T(8,128)S(1)}, u32[]{:S(2)}, u32[]{:S(2)}) collective-permute-start(f32[2,144,128]{2,1,0:T(8,128)S(1)} %get-tuple-element.81), channel_id=1, source_target_pairs={{0,7},{1,2},{2,1},{3,4},{4,3},{5,6},{6,5},{7,0},{8,15},{9,10},{10,... | collective-permute-start | bytes 442376 | tf_op jit(solution)/shard_map/ppermute | solution.py:625
  26.6 1.8 %shard_map.55 = (f32[12,160,128]{2,1,0:T(8,128)S(1)}, f32[12,160,128]{2,1,0:T(8,128)S(1)}, f32[10,160,128]{2,1,0:T(8,128)S(1)}, f32[10,160,128]{2,1,0:T(8,128)S(1)}, f32[2,2,160,128]{3,2,1,0:T(8,128)S(1)}) custom-call(f32[3,8,128,128]{3,2,1,0:T(8,128)S(1)} %get-tuple-element.49.conc_own, f32[1088,128]{1,0:T(8,128)S(1)} %collective-permute-done.from_a, ...), custom_call_target="tpu_custom_call" | custom-call | flops 2000000 | bytes 4000000 | tf_op jit(solution)/shard_map/pallas_call | solution.py:608
  28.4 3.1 %shard_map.57 = (f32[8,160,128]{2,1,0:T(8,128)S(1)}, f32[8,160,128]{2,1,0:T(8,128)S(1)}) custom-call(f32[12,160,128]{2,1,0:T(8,128)S(1)} %get-tuple-element.65.conc, f32[12,160,128]{2,1,0:T(8,128)S(1)} %get-tuple-element.66.mob, f32[10,160,128]{2,1,0:T(8,128)S(1)} %get-tuple-element.67.chem, f32[10,160,128]{2,1,0:T(8,128)S(1)} %get-tuple-element.68.curve, ...), custom_call_target="tpu_custom_call" | custom-call | flops 3000000 | bytes 6000000 | tf_op jit(solution)/shard_map/pallas_call | solution.py:608
  31.4 0.0 collective-permute-done.6.from_a
  31.5 0.3 collective-permute-done.7.from_b
  31.7 0.4 %shard_map.58 = (f32[2,2,160,128]{3,2,1,0:T(8,128)S(1)}, f32[2,144,128]{2,1,0:T(8,128)S(1)}, f32[2,144,128]{2,1,0:T(8,128)S(1)}) custom-call(f32[12,160,128]{2,1,0:T(8,128)S(1)} %get-tuple-element.65.conc, f32[12,160,128]{2,1,0:T(8,128)S(1)} %get-tuple-element.66.mob, f32[10,160,128]{2,1,0:T(8,128)S(1)} %get-tuple-element.67.chem, ...), custom_call_target="tpu_custom_call" | custom-call | flops 1000000 | bytes 2000000 | tf_op jit(solution)/shard_map/pallas_call | solution.py:608
  32.1 0.1 collective-permute-start.8
  32.2 1.3 %collective-permute-start.9 = (f32[2,144,128]{2,1,0:T(8,128)S(1)}, f32[2,144,128]{2,1,0:T(8,128)S(1)}, u32[]{:S(2)}, u32[]{:S(2)}) collective-permute-start(f32[2,144,128]{2,1,0:T(8,128)S(1)} %get-tuple-element.87), channel_id=1, source_target_pairs={{0,7},{1,2},{2,1},{3,4},{4,3},{5,6},{6,5},{7,0},{8,15},{9,10},{10,... | collective-permute-start | bytes 442376 | tf_op jit(solution)/shard_map/ppermute | solution.py:625
  33.5 1.8 %shard_map.53 = (f32[12,160,128]{2,1,0:T(8,128)S(1)}, f32[12,160,128]{2,1,0:T(8,128)S(1)}, f32[10,160,128]{2,1,0:T(8,128)S(1)}, f32[10,160,128]{2,1,0:T(8,128)S(1)}) custom-call(f32[3,8,128,128]{3,2,1,0:T(8,128)S(1)} %get-tuple-element.49.conc_own, f32[1088,128]{1,0:T(8,128)S(1)} %collective-permute-done.from_a, ...), custom_call_target="tpu_custom_call" | custom-call | flops 2000000 | bytes 4000000 | tf_op jit(solution)/shard_map/pallas_call | solution.py:608
  35.3 3.9 %shard_map.59 = (f32[8,160,128]{2,1,0:T(8,128)S(1)}, f32[1024,128]{1,0:T(8,128)S(1)}, f32[512,128]{1,0:T(8,128)}) custom-call(f32[12,160,128]{2,1,0:T(8,128)S(1)} %get-tuple-element.58.conc, f32[12,160,128]{2,1,0:T(8,128)S(1)} %get-tuple-element.59.mob, f32[10,160,128]{2,1,0:T(8,128)S(1)} %get-tuple-element.60.chem, ...), custom_call_target="tpu_custom_call" | custom-call | flops 3000000 | bytes 6000000 | tf_op jit(solution)/shard_map/pallas_call | solution.py:608
  39.2 0.0 collective-permute-done.8.from_a
  39.2 0.0 collective-permute-done.9.from_b
  39.2 1.1 %shard_map.60 = f32[1024,128]{1,0:T(8,128)} custom-call(f32[12,160,128]{2,1,0:T(8,128)S(1)} %get-tuple-element.58.conc, f32[12,160,128]{2,1,0:T(8,128)S(1)} %get-tuple-element.59.mob, f32[10,160,128]{2,1,0:T(8,128)S(1)} %get-tuple-element.60.chem, f32[10,160,128]{2,1,0:T(8,128)S(1)} %get-tuple-element.61.curve, f32[8,160,128]{2,1,0:T(8,128)S(1)} %get-tuple-element.85.inside, ...), custom_call_target="tpu_custom_call" | custom-call | flops 1000000 | bytes 2000000 | tf_op jit(solution)/shard_map/pallas_call | solution.py:608
  (1 shorter events, 0.0 us)
Async XLA Ops:
  2.4 19.1 %collective-permute-start = (f32[1088,128]{1,0:T(8,128)S(1)}, f32[1088,128]{1,0:T(8,128)S(1)}, u32[]{:S(2)}, u32[]{:S(2)}) collective-permute-start(f32[1088,128]{1,0:T(8,128)S(1)} %get-tuple-element.50), channel_id=1, source_target_pairs={{0,1},{1,0},{2,3},{3,2},{4,5},{5,4},{6,7},{7,6},{8,9},{9,8},{10,11... | collective-permute-start | bytes 1671176 | tf_op jit(solution)/shard_map/ppermute | solution.py:625
  2.9 18.6 %collective-permute-start.1 = (f32[1088,128]{1,0:T(8,128)S(1)}, f32[1088,128]{1,0:T(8,128)S(1)}, u32[]{:S(2)}, u32[]{:S(2)}) collective-permute-start(f32[1088,128]{1,0:T(8,128)S(1)} %get-tuple-element.51), channel_id=1, source_target_pairs={{0,7},{1,2},{2,1},{3,4},{4,3},{5,6},{6,5},{7,0},{8,15},{9,10},{10,... | collective-permute-start | bytes 1671176 | tf_op jit(solution)/shard_map/ppermute | solution.py:625
  8.4 5.0 %collective-permute-start.2 = (f32[8,24,128]{2,1,0:T(8,128)S(1)}, f32[8,24,128]{2,1,0:T(8,128)S(1)}, u32[]{:S(2)}, u32[]{:S(2)}) collective-permute-start(f32[8,24,128]{2,1,0:T(8,128)S(1)} %get-tuple-element.52), channel_id=1, source_target_pairs={{0,8},{8,0},{16,24},{24,16},{1,9},{9,1},{17,25},{25,17},{2,10},{10... | collective-permute-start | bytes 294920 | tf_op jit(solution)/shard_map/ppermute | solution.py:625
  9.9 5.5 %collective-permute-start.3 = (f32[8,24,128]{2,1,0:T(8,128)S(1)}, f32[8,24,128]{2,1,0:T(8,128)S(1)}, u32[]{:S(2)}, u32[]{:S(2)}) collective-permute-start(f32[8,24,128]{2,1,0:T(8,128)S(1)} %get-tuple-element.53), channel_id=1, source_target_pairs={{0,24},{8,16},{16,8},{24,0},{1,25},{9,17},{17,9},{25,1},{2,26},{10... | collective-permute-start | bytes 294920 | tf_op jit(solution)/shard_map/ppermute | solution.py:625
  15.5 4.4 %collective-permute-start.4 = (f32[2,2,24,128]{3,2,1,0:T(8,128)S(1)}, f32[2,2,24,128]{3,2,1,0:T(8,128)S(1)}, u32[]{:S(2)}, u32[]{:S(2)}) collective-permute-start(f32[2,2,24,128]{3,2,1,0:T(8,128)S(1)} %get-tuple-element.56), channel_id=1, source_target_pairs={{0,1},{1,0},{2,3},{3,2},{4,5},{5,4},{6,7},{7,6},{8,9},{9,8},{10,11... | collective-permute-start | bytes 147464 | tf_op jit(solution)/shard_map/ppermute | solution.py:625
  15.6 6.0 %collective-permute-start.5 = (f32[2,2,24,128]{3,2,1,0:T(8,128)S(1)}, f32[2,2,24,128]{3,2,1,0:T(8,128)S(1)}, u32[]{:S(2)}, u32[]{:S(2)}) collective-permute-start(f32[2,2,24,128]{3,2,1,0:T(8,128)S(1)} %get-tuple-element.57), channel_id=1, source_target_pairs={{0,7},{1,2},{2,1},{3,4},{4,3},{5,6},{6,5},{7,0},{8,15},{9,10},{10,... | collective-permute-start | bytes 147464 | tf_op jit(solution)/shard_map/ppermute | solution.py:625
  24.4 7.1 %collective-permute-start.6 = (f32[2,144,128]{2,1,0:T(8,128)S(1)}, f32[2,144,128]{2,1,0:T(8,128)S(1)}, u32[]{:S(2)}, u32[]{:S(2)}) collective-permute-start(f32[2,144,128]{2,1,0:T(8,128)S(1)} %get-tuple-element.80), channel_id=1, source_target_pairs={{0,1},{1,0},{2,3},{3,2},{4,5},{5,4},{6,7},{7,6},{8,9},{9,8},{10,11... | collective-permute-start | bytes 442376 | tf_op jit(solution)/shard_map/ppermute | solution.py:625
  24.4 7.3 %collective-permute-start.7 = (f32[2,144,128]{2,1,0:T(8,128)S(1)}, f32[2,144,128]{2,1,0:T(8,128)S(1)}, u32[]{:S(2)}, u32[]{:S(2)}) collective-permute-start(f32[2,144,128]{2,1,0:T(8,128)S(1)} %get-tuple-element.81), channel_id=1, source_target_pairs={{0,7},{1,2},{2,1},{3,4},{4,3},{5,6},{6,5},{7,0},{8,15},{9,10},{10,... | collective-permute-start | bytes 442376 | tf_op jit(solution)/shard_map/ppermute | solution.py:625
  32.1 7.1 %collective-permute-start.8 = (f32[2,144,128]{2,1,0:T(8,128)S(1)}, f32[2,144,128]{2,1,0:T(8,128)S(1)}, u32[]{:S(2)}, u32[]{:S(2)}) collective-permute-start(f32[2,144,128]{2,1,0:T(8,128)S(1)} %get-tuple-element.86), channel_id=1, source_target_pairs={{0,1},{1,0},{2,3},{3,2},{4,5},{5,4},{6,7},{7,6},{8,9},{9,8},{10,11... | collective-permute-start | bytes 442376 | tf_op jit(solution)/shard_map/ppermute | solution.py:625
  32.2 7.0 %collective-permute-start.9 = (f32[2,144,128]{2,1,0:T(8,128)S(1)}, f32[2,144,128]{2,1,0:T(8,128)S(1)}, u32[]{:S(2)}, u32[]{:S(2)}) collective-permute-start(f32[2,144,128]{2,1,0:T(8,128)S(1)} %get-tuple-element.87), channel_id=1, source_target_pairs={{0,7},{1,2},{2,1},{3,4},{4,3},{5,6},{6,5},{7,0},{8,15},{9,10},{10,... | collective-permute-start | bytes 442376 | tf_op jit(solution)/shard_map/ppermute | solution.py:625

commit v7 on v6

--- a/solution.py
+++ b/solution.py
@@ -35,6 +35,10 @@
     return pad - 8, pad + cols + 8
 
 
+def sent(cols):
+    return pad - 4, pad + cols + 4
+
+
 def up(value):
     return pltpu.roll(value, value.shape[1] - 1, 1)
 
@@ -43,8 +47,8 @@
     return pltpu.roll(value, 1, 1)
 
 
-def face_mask(size, lanes, nz):
-    lane = lax.broadcasted_iota(jnp.int32, (size, lanes), 1)
+def face_mask(lanes, nz):
+    lane = lax.broadcasted_iota(jnp.int32, (1, lanes), 1)
     return jnp.where(lane % nz == nz - 1, 0.0, 1.0).astype(f32)
 
 
@@ -62,12 +66,21 @@
     )
 
 
-def chem_row(conc, chem, curve, at, size, mask):
+def mobility(c):
+    return (0.5 * diff_step) * c * (1.0 - c)
+
+
+def chem_row(conc, chem, curve, swing, at, size, mask):
     c, lap = laplace(conc, at, size, mask)
     inv = 1.0 / (c * (1.0 - c))
     span = slice(at, at + size)
-    chem(span, jnp.log(c * c * inv) + mix_energy * (1.0 - 2.0 * c) - grad_energy * lap)
+    chem(
+        span,
+        time_step * (jnp.log(c * c * inv) - grad_energy * lap)
+        + (time_step * (mix_energy - bath_potential) - (2.0 * time_step * mix_energy) * c),
+    )
     curve(span, inv - 2.0 * mix_energy)
+    swing(span, c * (diff_step / time_step) - 0.5 * diff_step / time_step)
 
 
 def face_sums(adj, mob, chem, at, size, mask, across=(1, -1)):
@@ -97,17 +110,13 @@
     return a, mu, flow, pair
 
 
-def source(flow, rate, a):
-    return (0.5 * diff_step) * flow - time_step * rate * a
-
-
-def partial(a, c, pair, curve, g):
-    return a + (1.0 - 2.0 * c) * ((-0.5 * diff_step) * pair) + curve * g
-
-
-def gain(a, mu, before):
-    value = time_step * a * (bath_potential - mu)
-    return value if before is None else before + value
+def partial(a, swing, pair, curve, g):
+    return a + swing * pair + curve * g
+
+
+def gain(a, chem, before):
+    value = a * chem
+    return -value if before is None else before - value
 
 
 def set_row(ref, y):
@@ -117,41 +126,38 @@
     return put
 
 
-def interior(rows, cols, nz, conc, mob, chem, curve, adj, rate, pot, part, grad, before, store):
+def interior(rows, cols, nz, swing, mob, chem, curve, adj, rate, pot, part, grad, store):
     low, high = reach(cols)
     lanes = adj[0].shape[-1]
+    mask = face_mask(lanes, nz)
 
     def at_row(field, y):
         return row_of(field[0], field[1] + y)
 
     def body(y, _):
         for at, size in chunks(low, high):
-            mask = face_mask(size, lanes, nz)
             span = slice(at, at + size)
             a, mu, flow, pair = face_sums(
                 at_row(adj, y), at_row(mob, y), at_row(chem, y), at, size, mask
             )
-            g = source(flow, at_row(rate, y)(0, span), a)
+            g = flow - at_row(rate, y)(0, span) * a
             pot[y - 1, span, :] = g
             part[y - depth, span, :] = partial(
-                a, at_row(conc, y)(0, span), pair, at_row(curve, y)(0, span), g
-            )
-            old = None if before is None else before[y - depth, span, :]
-            grad[y - depth, span, :] = gain(a, mu, old)
+                a, at_row(swing, y)(0, span), pair, at_row(curve, y)(0, span), g
+            )
+            grad[y - depth, span, :] = gain(a, mu, None)
         return 0
 
     def edge(i, _):
         y = 1 + i * (rows - 3)
         for at, size in chunks(low, high):
-            mask = face_mask(size, lanes, nz)
             a, _mu, flow, _pair = face_sums(at_row(adj, y), at_row(mob, y), None, at, size, mask)
             span = slice(at, at + size)
-            pot[y - 1, span, :] = source(flow, at_row(rate, y)(0, span), a)
+            pot[y - 1, span, :] = flow - at_row(rate, y)(0, span) * a
         return 0
 
     def close(y, _):
         for at, size in chunks(low, high):
-            mask = face_mask(size, lanes, nz)
             span = slice(at, at + size)
             _g, lap = laplace(row_of(pot, y - 1), at, size, mask)
             store(y - depth, span, part[y - depth, span, :] - grad_energy * lap)
@@ -162,10 +168,10 @@
     lax.fori_loop(depth, rows - depth, close, 0)
 
 
-def boundary(rows, cols, nz, conc, mob, chem, curve, adj, rate, pot, part, grad, before, store,
-             fresh):
+def boundary(rows, cols, nz, conc, mob, chem, curve, swing, adj, rate, pot, part, grad, store):
     low, high = reach(cols)
     lanes = adj[0].shape[-1]
+    mask = face_mask(lanes, nz)
     last = rows - 1
 
     def at_row(field, y):
@@ -174,49 +180,43 @@
     def mirror(s, y):
         return y + s * (last - 2 * y)
 
-    if fresh:
-
-        def mu_side(i, _):
-            s, k = i // 2, i % 2
-            y = mirror(s, k - 1)
-            for at, size in chunks(low, high):
-                chem_row(at_row(conc, y), set_row(chem[0], chem[1] + y),
-                         set_row(curve[0], curve[1] + y), at, size, face_mask(size, lanes, nz))
-            return 0
-
-        lax.fori_loop(0, 4, mu_side, 0)
+    def mu_side(i, _):
+        s, k = i // 2, i % 2
+        y = mirror(s, k - 1)
+        for at, size in chunks(low, high):
+            chem_row(at_row(conc, y), set_row(chem[0], chem[1] + y),
+                     set_row(curve[0], curve[1] + y), set_row(swing[0], swing[1] + y), at, size,
+                     mask)
+        return 0
+
+    lax.fori_loop(0, 4, mu_side, 0)
 
     def side(s, _):
         y = mirror(s, -1)
         for at, size in chunks(low, high):
-            mask = face_mask(size, lanes, nz)
             span = slice(at, at + size)
             a, _mu, flow, _pair = face_sums(at_row(adj, y), at_row(mob, y), None, at, size, mask)
-            pot[1 + y, span, :] = source(flow, rate[3 * s, span, :], a)
+            pot[1 + y, span, :] = flow - rate[3 * s, span, :] * a
         y0 = mirror(s, 0)
         for at, size in chunks(low, high):
-            mask = face_mask(size, lanes, nz)
             span = slice(at, at + size)
             a, mu, flow, pair = face_sums(
                 at_row(adj, y0), at_row(mob, y0), at_row(chem, y0), at, size, mask
             )
-            g = source(flow, rate[1 + s, span, :], a)
+            g = flow - rate[1 + s, span, :] * a
             pot[1 + y0, span, :] = g
             part[s, 0, span, :] = partial(
-                a, at_row(conc, y0)(0, span), pair, at_row(curve, y0)(0, span), g
-            )
-            old = None if before is None else before[s, 0, span, :]
-            grad[s, 0, span, :] = gain(a, mu, old)
+                a, at_row(swing, y0)(0, span), pair, at_row(curve, y0)(0, span), g
+            )
+            grad[s, 0, span, :] = gain(a, mu, None)
         y1 = mirror(s, 1)
         for at, size in chunks(low, high):
-            mask = face_mask(size, lanes, nz)
             span = slice(at, at + size)
             a, mu, _flow, pair = face_sums(at_row(adj, y1), None, at_row(chem, y1), at, size, mask)
             part[s, 1, span, :] = partial(
-                a, at_row(conc, y1)(0, span), pair, at_row(curve, y1)(0, span), pot[1 + y1, span, :]
-            )
-            old = None if before is None else before[s, 1, span, :]
-            grad[s, 1, span, :] = gain(a, mu, old)
+                a, at_row(swing, y1)(0, span), pair, at_row(curve, y1)(0, span), pot[1 + y1, span, :]
+            )
+            grad[s, 1, span, :] = gain(a, mu, None)
         return 0
 
     lax.fori_loop(0, 2, side, 0)
@@ -225,7 +225,6 @@
         s, k = i // 2, i % 2
         y = mirror(s, k)
         for at, size in chunks(low, high):
-            mask = face_mask(size, lanes, nz)
             span = slice(at, at + size)
             _g, lap = laplace(row_of(pot, 1 + y), at, size, mask)
             store(s, k, span, part[s, k, span, :] - grad_energy * lap)
@@ -234,20 +233,20 @@
     lax.fori_loop(0, 4, close, 0)
 
 
-def is_even(axis):
-    return lax.rem(lax.axis_index(axis), 2) == 0
+def is_odd(axis):
+    return lax.rem(lax.axis_index(axis), 2) == 1
 
 
 def bases(rows):
-    even = is_even("gy")
+    odd = is_odd("gy")
     top = rows - depth
-    return jnp.where(even, top, 0), jnp.where(even, 0, top)
+    return jnp.where(odd, top, 0), jnp.where(odd, 0, top)
 
 
 def landings(rows):
-    even = is_even("gy")
+    odd = is_odd("gy")
     top = rows + depth
-    return jnp.where(even, top, 0), jnp.where(even, 0, top)
+    return jnp.where(odd, top, 0), jnp.where(odd, 0, top)
 
 
 def sides_of(rows):
@@ -289,7 +288,7 @@
 
 
 def turned_rate(rate, y, rows, nz, lanes):
-    value = rate[pl.ds(y, nz, stride=rows), :]
+    value = time_step * rate[pl.ds(y, nz, stride=rows), :]
     return jnp.concatenate([value] * (lanes // nz), axis=0).T
 
 
@@ -297,13 +296,13 @@
                 x_a, x_b):
     places, total = slots(steps)
     lanes = adj_out.shape[2]
-    even_x = is_even("gx")
+    odd_x = is_odd("gx")
 
     def to_x(y, value, place):
         start, width = place
         last, first = value[cols - width :, :], value[:width, :]
-        x_a[y, start : start + width, :] = jnp.where(even_x, last, first)
-        x_b[y, start : start + width, :] = jnp.where(even_x, first, last)
+        x_a[y, start : start + width, :] = jnp.where(odd_x, last, first)
+        x_b[y, start : start + width, :] = jnp.where(odd_x, first, last)
 
     used = sum(places[-1])
     for y in range(rows):
@@ -339,9 +338,9 @@
 
 
 def corner_kernel(rows, got_a, got_b, x_low, x_high, corner_a, corner_b):
-    even_x = is_even("gx")
-    x_low[...] = jnp.where(even_x, got_b[...], got_a[...])
-    x_high[...] = jnp.where(even_x, got_a[...], got_b[...])
+    odd_x = is_odd("gx")
+    x_low[...] = jnp.where(odd_x, got_b[...], got_a[...])
+    x_high[...] = jnp.where(odd_x, got_a[...], got_b[...])
     for out, base in zip((corner_a, corner_b), bases(rows)):
         for at in range(depth):
             out[0, at] = x_low[base + at]
@@ -349,10 +348,11 @@
 
 
 def first_interior(steps, rows, cols, nz, conc_own, adj_own, rate_own, x_low, x_high,
-                   conc, adj, rate, chem, curve, pot, out, grad, ahead, mob, part):
+                   conc, adj, rate, chem, curve, swing, pot, out, grad, ahead, mob, part):
     places, _ = slots(steps)
     low, high = reach(cols)
     lanes = adj.shape[2]
+    mask = face_mask(lanes, nz)
     for y in range(rows):
         put_own(conc, y, conc_own[0, y], y, places[1], cols, x_low, x_high)
         put_own(adj, y, adj_own[y], y, places[0], cols, x_low, x_high)
@@ -362,13 +362,13 @@
     def mob_row(y, _):
         for at, size in chunks(low - 8, high + 8):
             c = conc[y, at : at + size, :]
-            mob[y, at : at + size, :] = c * (1.0 - c)
+            mob[y, at : at + size, :] = mobility(c)
         return 0
 
     def mu_row(y, _):
         for at, size in chunks(low, high):
-            chem_row(row_of(conc, y), set_row(chem, y - 1), set_row(curve, y - 1), at, size,
-                     face_mask(size, lanes, nz))
+            chem_row(row_of(conc, y), set_row(chem, y - 1), set_row(curve, y - 1),
+                     set_row(swing, y - 1), at, size, mask)
         return 0
 
     lax.fori_loop(0, rows, mob_row, 0)
@@ -377,8 +377,8 @@
     def store(k, span, value):
         out[k, span, :] = value
 
-    interior(rows, cols, nz, (conc, 0), (mob, 0), (chem, -1), (curve, -1), (adj, 0), (rate, 0),
-             pot, part, grad, None, store)
+    interior(rows, cols, nz, (swing, -1), (mob, 0), (chem, -1), (curve, -1), (adj, 0), (rate, 0),
+             pot, part, grad, store)
 
 
 def copy_rows(pairs):
@@ -388,33 +388,35 @@
 
 def send_rows(out, ahead, rate, to_a, to_b, open_g, cols, nz):
     low, high = reach(cols)
+    first, last = sent(cols)
     rows, lanes = rate.shape[0], rate.shape[2]
+    mask = face_mask(lanes, nz)
     for s in range(2):
         for at, size in chunks(low, high):
-            mask = face_mask(size, lanes, nz)
             a, _mu, flow, _pair = face_sums(
                 lambda dy, cut: out[s, dy, cut, :], lambda dy, cut: ahead[s, dy, cut, :], None,
                 at, size, mask, (1,)
             )
-            open_g[s, at - low : at - low + size, :] = source(
-                flow, rate[s * (rows - 1), at : at + size, :], a
-            )
-    even = is_even("gy")
-    for to, side in ((to_a, jnp.where(even, 1, 0)), (to_b, jnp.where(even, 0, 1))):
-        to[0] = out[side, 0, low:high, :]
-        to[1] = open_g[side]
+            open_g[s, at - low : at - low + size, :] = (
+                flow - rate[s * (rows - 1), at : at + size, :] * a
+            )
+    odd = is_odd("gy")
+    for to, side in ((to_a, jnp.where(odd, 1, 0)), (to_b, jnp.where(odd, 0, 1))):
+        to[0] = out[side, 0, first:last, :]
+        to[1] = open_g[side, first - low : last - low, :]
 
 
 def put_ahead(ahead, conc_own, back, x_low, x_high, places, rows, cols):
     for s, k, y in sides_of(rows):
         put_own(ahead.at[s], k, conc_own[back, y], y, places[1 + back], cols, x_low, x_high)
-        c = ahead[s, k]
-        ahead[s, k] = c * (1.0 - c)
-
-
-def first_boundary(steps, rows, cols, nz, conc_in, adj_in, rate_in, chem_in, curve_in, pot_in,
+        ahead[s, k] = mobility(ahead[s, k])
+
+
+def first_boundary(steps, rows, cols, nz, conc_in, adj_in, rate_in, chem_in, curve_in, swing_in,
+                   pot_in,
                    from_a, from_b, corner_a, corner_b, ahead,
-                   out, grad, to_a, to_b, rate, conc, adj, mob, chem, curve, pot, part, open_g):
+                   out, grad, to_a, to_b, rate, conc, adj, mob, chem, curve, swing, pot,
+                   part, open_g):
     places, _ = slots(steps)
     low, high = reach(cols)
     half = cols // 2
@@ -437,6 +439,7 @@
         pot[1 + y] = pot_in[y - 1]
     for y in (1, rows - 2):
         curve[1 + y] = curve_in[y - 1]
+        swing[1 + y] = swing_in[y - 1]
     rate[1] = rate_in[0]
     rate[2] = rate_in[rows - 1]
     for halo, corner, base in zip((from_a, from_b), (corner_a, corner_b), landings(rows)):
@@ -450,21 +453,23 @@
     for row in [0, 1, 2, 3, rows, rows + 1, rows + 2, rows + 3]:
         for at, size in chunks(low - 8, high + 8):
             c = conc[row, at : at + size, :]
-            mob[row, at : at + size, :] = c * (1.0 - c)
+            mob[row, at : at + size, :] = mobility(c)
 
     def store(s, k, span, value):
         out[s, k, span, :] = value
 
-    boundary(rows, cols, nz, (conc, depth), (mob, depth), (chem, 1), (curve, 1), (adj, depth),
-             rate, pot, part, grad, None, store, True)
+    boundary(rows, cols, nz, (conc, depth), (mob, depth), (chem, 1), (curve, 1), (swing, 1),
+             (adj, depth), rate, pot, part, grad, store)
     send_rows(out, ahead, rate_in, to_a, to_b, open_g, cols, nz)
 
 
 def prepare_kernel(steps, rows, cols, nz, back, conc_own, from_a, from_b, x_low, x_high,
-                   corner_a, corner_b, conc, mob, chem, curve, *ahead):
+                   corner_a, corner_b, mob, chem, curve, swing, *rest):
+    *ahead, conc = rest
     places, _ = slots(steps)
     low, high = reach(cols)
     lanes = conc.shape[2]
+    mask = face_mask(lanes, nz)
     place = places[1 + back]
     for y in range(rows):
         put_own(conc, depth + y, conc_own[back, y], y, place, cols, x_low, x_high)
@@ -479,20 +484,20 @@
     def mob_row(row, _):
         for at, size in chunks(low - 8, high + 8):
             c = conc[row, at : at + size, :]
-            mob[row, at : at + size, :] = c * (1.0 - c)
+            mob[row, at : at + size, :] = mobility(c)
         return 0
 
     def mu_row(row, _):
         for at, size in chunks(low, high):
-            chem_row(row_of(conc, row + 1), set_row(chem, row), set_row(curve, row), at, size,
-                     face_mask(size, lanes, nz))
+            chem_row(row_of(conc, row + 1), set_row(chem, row), set_row(curve, row),
+                     set_row(swing, row), at, size, mask)
         return 0
 
     lax.fori_loop(0, rows + 2 * depth, mob_row, 0)
     lax.fori_loop(0, rows + 2, mu_row, 0)
 
 
-def next_interior(rows, cols, nz, final, conc, mob, chem, curve, rate, inner, outer, *rest):
+def next_interior(rows, cols, nz, final, mob, chem, curve, swing, rate, inner, outer, *rest):
     if final:
         before, out, tiles, grad_out, adj, pot, part, grad = rest
     elif len(rest) == 8:
@@ -505,6 +510,7 @@
         before, out, grad, adj, pot, part = rest
     low, high = reach(cols)
     lanes = adj.shape[2]
+    mask = face_mask(lanes, nz)
     skip = (inner.shape[0] - (rows - 2 * depth)) // 2
     for k in range(rows - 2 * depth):
         adj[1 + depth + k] = inner[skip + k]
@@ -517,22 +523,20 @@
 
     def body(y, _):
         for at, size in chunks(low, high):
-            mask = face_mask(size, lanes, nz)
             span = slice(at, at + size)
             a, mu, flow, pair = face_sums(
                 row_of(adj, y + 1), row_of(mob, y + depth), row_of(chem, y + 1), at, size, mask
             )
-            g = source(flow, rate[y, span, :], a)
+            g = flow - rate[y, span, :] * a
             pot[y + 1, span, :] = g
             part[y, span, :] = partial(
-                a, conc[y + depth, span, :], pair, curve[y + 1, span, :], g
+                a, swing[y + 1, span, :], pair, curve[y + 1, span, :], g
             )
             grad[y, span, :] = gain(a, mu, before[y, span, :])
         return 0
 
     def close(y, _):
         for at, size in chunks(low, high):
-            mask = face_mask(size, lanes, nz)
             span = slice(at, at + size)
             _g, lap = laplace(row_of(pot, y + 1), at, size, mask)
             out[y, span, :] = part[y, span, :] - grad_energy * lap
@@ -554,27 +558,28 @@
     return total
 
 
-def next_boundary(rows, cols, nz, final, conc, mob, chem, curve, inside, outer, from_a, from_b,
+def next_boundary(rows, cols, nz, final, mob, chem, curve, swing, inside, outer, from_a, from_b,
                   *rest):
     if final:
         tiles, out, halo, delta, result = rest
     else:
         ahead, rate, result, to_a, to_b, halo, delta, open_g = rest
     low, high = reach(cols)
-    lanes = conc.shape[2]
-    even = is_even("gy")
-    for got, side in ((from_a, jnp.where(even, 1, 0)), (from_b, jnp.where(even, 0, 1))):
+    first, last = sent(cols)
+    lanes = mob.shape[2]
+    mask = face_mask(lanes, nz)
+    odd = is_odd("gy")
+    for got, side in ((from_a, jnp.where(odd, 1, 0)), (from_b, jnp.where(odd, 0, 1))):
         for k in range(2):
-            halo[side, k, low:high, :] = got[k]
+            halo[side, k, first:last, :] = got[k]
     for s in range(2):
         y, beyond = s * (rows - 1), s * (rows + 1) - 1
         for at, size in chunks(low, high):
             span = slice(at, at + size)
             diff = halo[s, 0, span, :] - outer[s, 0, span, :]
             both = mob[depth + beyond, span, :] + mob[depth + y, span, :]
-            delta[s, span, :] = (0.5 * diff_step) * both * diff
-        for at, size in chunks(low, high):
-            mask = face_mask(size, lanes, nz)
+            delta[s, span, :] = both * diff
+        for at, size in chunks(low, high):
             span = slice(at, at + size)
             more = delta[s, span, :]
             diff = halo[s, 0, span, :] - outer[s, 0, span, :]
@@ -586,10 +591,9 @@
                 - 4.0 * more
                 + (step_z - down(step_z))
             )
-            c = conc[depth + y, span, :]
             result[s, 0, span, :] = (
                 inside[y, span, :]
-                + ((1.0 - 2.0 * c) * ((-0.5 * diff_step) * pair) + curve[1 + y, span, :] * more)
+                + (swing[1 + y, span, :] * pair + curve[1 + y, span, :] * more)
                 - grad_energy * lap
             )
             result[s, 1, span, :] = inside[1 + s * (rows - 3), span, :] - grad_energy * more
@@ -620,8 +624,8 @@
 
 def swap(value_a, value_b, axis):
     count = lax.axis_size(axis)
-    pairs_a = [(i, i + 1 - 2 * (i % 2)) for i in range(count)]
-    pairs_b = [(i, (i - 1 + 2 * (i % 2)) % count) for i in range(count)]
+    pairs_a = [(i, (i - 1 + 2 * (i % 2)) % count) for i in range(count)]
+    pairs_b = [(i, i + 1 - 2 * (i % 2)) for i in range(count)]
     return lax.ppermute(value_a, axis, pairs_a), lax.ppermute(value_b, axis, pairs_b)
 
 
@@ -637,7 +641,7 @@
         return (count, width, lanes)
 
     both = (2, depth, width, lanes)
-    edge = (2, cols + 16, lanes)
+    edge = (2, cols + 8, lanes)
     open_g = (2, cols + 16, lanes)
     raw = [(steps, flat, cols), (flat, cols), (nz * rows, cols)]
     conc_raw, adj_raw, rate_raw, main_a, main_b = call(
@@ -666,9 +670,9 @@
     )
     corner_a, corner_b = swap(corner_a, corner_b, "gy")
 
-    conc, adj, rate, chem, curve, pot, inner, inner_grad, ahead = call(
+    conc, adj, rate, chem, curve, swing, pot, inner, inner_grad, ahead = call(
         functools.partial(first_interior, steps, rows, cols, nz),
-        [field(rows)] * 3 + [field(rows - 2)] * 3 + [field(inside)] * 2 + [both],
+        [field(rows)] * 3 + [field(rows - 2)] * 4 + [field(inside)] * 2 + [both],
         [field(rows), field(inside)],
         conc_own, adj_own, rate_own, x_low, x_high,
         cost=3,
@@ -676,8 +680,8 @@
     outer, outer_grad, to_a, to_b = call(
         functools.partial(first_boundary, steps, rows, cols, nz),
         [both, both, edge, edge],
-        [field(4)] + [field(rows + 2 * depth)] * 3 + [field(rows + 2)] * 3 + [both, open_g],
-        conc, adj, rate, chem, curve, pot, main_a, main_b, corner_a, corner_b, ahead,
+        [field(4)] + [field(rows + 2 * depth)] * 3 + [field(rows + 2)] * 4 + [both, open_g],
+        conc, adj, rate, chem, curve, swing, pot, main_a, main_b, corner_a, corner_b, ahead,
         cost=2,
     )
     before = (inner_grad, outer_grad)
@@ -686,8 +690,8 @@
         final = back == steps - 1
         fields = call(
             functools.partial(prepare_kernel, steps, rows, cols, nz, back),
-            [field(rows + 2 * depth)] * 2 + [field(rows + 2)] * 2 + ([] if final else [both]),
-            [],
+            [field(rows + 2 * depth)] + [field(rows + 2)] * 3 + ([] if final else [both]),
+            [field(rows + 2 * depth)],
             conc_own, main_a, main_b, x_low, x_high, corner_a, corner_b,
             cost=2,
         )

time: 40.5 us -> 40.5 us (level)
  starting transfers between devices: 13.2 us -> 11.2 us
  waiting for transfers between devices: 5.99 us -> 7.72 us
    ppermute x5, starting transfers between devices: 10.9 us -> 0.61 us  [swap(): lax.ppermute(value_b, axis, pairs_b)]
    ppermute x5, starting transfers between devices: 2.29 us -> 10.6 us  [swap(): lax.ppermute(value_a, axis, pairs_a)]
    ppermute x5, waiting for transfers between devices: 1.95 us -> 5.93 us  [swap(): lax.ppermute(value_a, axis, pairs_a)]
    ppermute x5, waiting for transfers between devices: 4.04 us -> 1.79 us  [swap(): lax.ppermute(value_b, axis, pairs_b)]
where the time goes in v7:
time: 40.5 us; the launch traced here: 40.3 us
  Pallas kernels  20.7 us (51%)
  starting transfers between devices  11.2 us (28%)
  waiting for transfers between devices  7.72 us (19%)
  between operations  0.71 us (2%)
    pallas_call x11, Pallas kernels, call(): pl.pallas_call(kernel, out_shape=[jax.ShapeDtypeStruct(shape, f32) for sh...  20.7 us
    ppermute x5, starting transfers between devices, swap(): lax.ppermute(value_a, axis, pairs_a)  10.6 us
    ppermute x5, waiting for transfers between devices, swap(): lax.ppermute(value_a, axis, pairs_a)  5.93 us
    ppermute x5, waiting for transfers between devices, swap(): lax.ppermute(value_b, axis, pairs_b)  1.79 us
  transfers between devices with their start and end apart: 10, of which 4 were waited for; matrix products, arithmetic and copies ran while one was open for 0% of the time, Pallas kernels for 36%

profile of v7, /device:TPU:0, one launch (start us, length us, event | category | flops | bytes accessed | tf_op | source)
XLA Modules:
  0.0 40.3 jit_solution(18306779781497917429)
XLA Ops:
  0.6 1.8 %shard_map.50 = (f32[3,1024,128]{2,1,0:T(8,128)S(1)}, f32[1024,128]{1,0:T(8,128)S(1)}, f32[512,128]{1,0:T(8,128)S(1)}, f32[1088,128]{1,0:T(8,128)S(1)}, f32[1088,128]{1,0:T(8,128)S(1)}) custom-call(f32[3,1024,128]{2,1,0:T(8,128)} %bitcast.5, f32[1024,128]{1,0:T(8,128)} %bitcast.6, f32[512,128]{1,0:T(8,128)} %bitcast.8), custom_call_target="tpu_custom_call" | custom-call | flops 2000000 | bytes 4000000 | tf_op jit(solution)/shard_map/pallas_call | solution.py:612
  2.4 4.6 %collective-permute-start = (f32[1088,128]{1,0:T(8,128)S(1)}, f32[1088,128]{1,0:T(8,128)S(1)}, u32[]{:S(2)}, u32[]{:S(2)}) collective-permute-start(f32[1088,128]{1,0:T(8,128)S(1)} %get-tuple-element.51), channel_id=1, source_target_pairs={{0,7},{1,2},{2,1},{3,4},{4,3},{5,6},{6,5},{7,0},{8,15},{9,10},{10,... | collective-permute-start | bytes 1671176 | tf_op jit(solution)/shard_map/ppermute | solution.py:629
  7.0 0.0 collective-permute-start.1
  7.0 0.7 %shard_map.51 = (f32[3,8,128,128]{3,2,1,0:T(8,128)S(1)}, f32[8,128,128]{2,1,0:T(8,128)S(1)}, f32[8,128,128]{2,1,0:T(8,128)S(1)}, f32[8,24,128]{2,1,0:T(8,128)S(1)}, f32[8,24,128]{2,1,0:T(8,128)S(1)}) custom-call(f32[3,1024,128]{2,1,0:T(8,128)S(1)} %get-tuple-element.47.conc_in, f32[1024,128]{1,0:T(8,128)S(1)} %get-tuple-element.48.adj_in, ...), custom_call_target="tpu_custom_call" | custom-call | flops 1000000 | bytes 2000000 | tf_op jit(solution)/shard_map/pallas_call | solution.py:612
  7.7 2.5 %collective-permute-start.2 = (f32[8,24,128]{2,1,0:T(8,128)S(1)}, f32[8,24,128]{2,1,0:T(8,128)S(1)}, u32[]{:S(2)}, u32[]{:S(2)}) collective-permute-start(f32[8,24,128]{2,1,0:T(8,128)S(1)} %get-tuple-element.53), channel_id=1, source_target_pairs={{0,24},{8,16},{16,8},{24,0},{1,25},{9,17},{17,9},{25,1},{2,26},{10... | collective-permute-start | bytes 294920 | tf_op jit(solution)/shard_map/ppermute | solution.py:629
  10.2 0.5 %collective-permute-start.3 = (f32[8,24,128]{2,1,0:T(8,128)S(1)}, f32[8,24,128]{2,1,0:T(8,128)S(1)}, u32[]{:S(2)}, u32[]{:S(2)}) collective-permute-start(f32[8,24,128]{2,1,0:T(8,128)S(1)} %get-tuple-element.54), channel_id=1, source_target_pairs={{0,8},{8,0},{16,24},{24,16},{1,9},{9,1},{17,25},{25,17},{2,10},{10... | collective-permute-start | bytes 294920 | tf_op jit(solution)/shard_map/ppermute | solution.py:629
  10.8 3.5 %collective-permute-done.2.got_a = f32[8,24,128]{2,1,0:T(8,128)S(1)} collective-permute-done((f32[8,24,128]{2,1,0:T(8,128)S(1)}, f32[8,24,128]{2,1,0:T(8,128)S(1)}, u32[]{:S(2)}, u32[]{:S(2)}) %collective-permute-start.2) | collective-permute-done | bytes 98336 | tf_op jit(solution)/shard_map/ppermute | solution.py:629
  14.3 1.8 %collective-permute-done.3.got_b = f32[8,24,128]{2,1,0:T(8,128)S(1)} collective-permute-done((f32[8,24,128]{2,1,0:T(8,128)S(1)}, f32[8,24,128]{2,1,0:T(8,128)S(1)}, u32[]{:S(2)}, u32[]{:S(2)}) %collective-permute-start.3) | collective-permute-done | bytes 98336 | tf_op jit(solution)/shard_map/ppermute | solution.py:629
  16.1 0.1 collective-permute-start.4
  16.2 0.1 collective-permute-start.5
  16.3 3.1 %shard_map.54 = (f32[8,160,128]{2,1,0:T(8,128)S(1)}, f32[8,160,128]{2,1,0:T(8,128)S(1)}, f32[8,160,128]{2,1,0:T(8,128)S(1)}, f32[6,160,128]{2,1,0:T(8,128)S(1)},...) custom-call(f32[3,8,128,128]{3,2,1,0:T(8,128)S(1)} %get-tuple-elemen, ...), custom_call_target="tpu_custom_call" | custom-call | flops 3000000 | bytes 6000000 | tf_op jit(solution)/shard_map/pallas_call | solution.py:612
  19.3 2.2 %collective-permute-done.4.corner_a = f32[2,2,24,128]{3,2,1,0:T(8,128)S(1)} collective-permute-done((f32[2,2,24,128]{3,2,1,0:T(8,128)S(1)}, f32[2,2,24,128]{3,2,1,0:T(8,128)S(1)}, u32[]{:S(2)}, u32[]{:S(2)}) %collective-permute-start.4) | collective-permute-done | bytes 49184 | tf_op jit(solution)/shard_map/ppermute | solution.py:629
  21.5 0.0 collective-permute-done.5.corner_b
  21.5 0.0 collective-permute-done.from_a
  21.5 0.0 collective-permute-done.1.from_b
  21.5 2.8 %shard_map.56 = (f32[2,2,160,128]{3,2,1,0:T(8,128)S(1)}, f32[2,2,160,128]{3,2,1,0:T(8,128)S(1)}, f32[2,136,128]{2,1,0:T(8,128)S(1)}, f32[2,136,128]{2,1,0:T(8,128)S(1)}) custom-call(f32[8,160,128]{2,1,0:T(8,128)S(1)} %get-tuple-element.71.conc_in, f32[8,160,128]{2,1,0:T(8,128)S(1)} %get-tuple-element.72.adj_in, ...), custom_call_target="tpu_custom_call" | custom-call | flops 2000000 | bytes 4000000 | tf_op jit(solution)/shard_map/pallas_call | solution.py:612
  24.3 1.4 %collective-permute-start.6 = (f32[2,136,128]{2,1,0:T(8,128)S(1)}, f32[2,136,128]{2,1,0:T(8,128)S(1)}, u32[]{:S(2)}, u32[]{:S(2)}) collective-permute-start(f32[2,136,128]{2,1,0:T(8,128)S(1)} %get-tuple-element.82), channel_id=1, source_target_pairs={{0,7},{1,2},{2,1},{3,4},{4,3},{5,6},{6,5},{7,0},{8,15},{9,10},{10,... | collective-permute-start | bytes 417800 | tf_op jit(solution)/shard_map/ppermute | solution.py:629
  25.7 0.0 collective-permute-start.7
  25.7 1.9 %shard_map.55 = (f32[12,160,128]{2,1,0:T(8,128)S(1)}, f32[10,160,128]{2,1,0:T(8,128)S(1)}, f32[10,160,128]{2,1,0:T(8,128)S(1)}, f32[10,160,128]{2,1,0:T(8,128)S(1)}, f32[2,2,160,128]{3,2,1,0:T(8,128)S(1)}) custom-call(f32[3,8,128,128]{3,2,1,0:T(8,128)S(1)} %get-tuple-element.50.conc_own, f32[1088,128]{1,0:T(8,128)S(1)} %collective-permute-done.from_a, ...), custom_call_target="tpu_custom_call" | custom-call | flops 2000000 | bytes 4000000 | tf_op jit(solution)/shard_map/pallas_call | solution.py:612
  27.6 3.1 %shard_map.57 = (f32[8,160,128]{2,1,0:T(8,128)S(1)}, f32[8,160,128]{2,1,0:T(8,128)S(1)}) custom-call(f32[12,160,128]{2,1,0:T(8,128)S(1)} %get-tuple-element.66.mob, f32[10,160,128]{2,1,0:T(8,128)S(1)} %get-tuple-element.67.chem, f32[10,160,128]{2,1,0:T(8,128)S(1)} %get-tuple-element.68.curve, f32[10,160,128]{2,1,0:T(8,128)S(1)} %get-tuple-element.69.swing, ...), custom_call_target="tpu_custom_call" | custom-call | flops 3000000 | bytes 6000000 | tf_op jit(solution)/shard_map/pallas_call | solution.py:612
  30.7 0.3 collective-permute-done.6.from_a
  31.0 0.0 collective-permute-done.7.from_b
  31.0 0.4 shard_map.58
  31.4 2.0 %collective-permute-start.8 = (f32[2,136,128]{2,1,0:T(8,128)S(1)}, f32[2,136,128]{2,1,0:T(8,128)S(1)}, u32[]{:S(2)}, u32[]{:S(2)}) collective-permute-start(f32[2,136,128]{2,1,0:T(8,128)S(1)} %get-tuple-element.88), channel_id=1, source_target_pairs={{0,7},{1,2},{2,1},{3,4},{4,3},{5,6},{6,5},{7,0},{8,15},{9,10},{10,... | collective-permute-start | bytes 417800 | tf_op jit(solution)/shard_map/ppermute | solution.py:629
  33.4 0.0 collective-permute-start.9
  33.4 1.8 %shard_map.53 = (f32[12,160,128]{2,1,0:T(8,128)S(1)}, f32[10,160,128]{2,1,0:T(8,128)S(1)}, f32[10,160,128]{2,1,0:T(8,128)S(1)}, f32[10,160,128]{2,1,0:T(8,128)S(1)}) custom-call(f32[3,8,128,128]{3,2,1,0:T(8,128)S(1)} %get-tuple-element.50.conc_own, f32[1088,128]{1,0:T(8,128)S(1)} %collective-permute-done.from_a, ...), custom_call_target="tpu_custom_call" | custom-call | flops 2000000 | bytes 4000000 | tf_op jit(solution)/shard_map/pallas_call | solution.py:612
  35.2 3.9 %shard_map.59 = (f32[8,160,128]{2,1,0:T(8,128)S(1)}, f32[1024,128]{1,0:T(8,128)S(1)}, f32[512,128]{1,0:T(8,128)}) custom-call(f32[12,160,128]{2,1,0:T(8,128)S(1)} %get-tuple-element.59.mob, f32[10,160,128]{2,1,0:T(8,128)S(1)} %get-tuple-element.60.chem, f32[10,160,128]{2,1,0:T(8,128)S(1)} %get-tuple-element.61.curve, ...), custom_call_target="tpu_custom_call" | custom-call | flops 3000000 | bytes 6000000 | tf_op jit(solution)/shard_map/pallas_call | solution.py:612
  39.2 0.0 collective-permute-done.8.from_a
  39.2 0.0 collective-permute-done.9.from_b
  39.2 1.1 %shard_map.60 = f32[1024,128]{1,0:T(8,128)} custom-call(f32[12,160,128]{2,1,0:T(8,128)S(1)} %get-tuple-element.59.mob, f32[10,160,128]{2,1,0:T(8,128)S(1)} %get-tuple-element.60.chem, f32[10,160,128]{2,1,0:T(8,128)S(1)} %get-tuple-element.61.curve, f32[10,160,128]{2,1,0:T(8,128)S(1)} %get-tuple-element.62.swing, ...), custom_call_target="tpu_custom_call" | custom-call | flops 1000000 | bytes 2000000 | tf_op jit(solution)/shard_map/pallas_call | solution.py:612
  (1 shorter events, 0.0 us)
Async XLA Ops:
  2.4 19.1 %collective-permute-start = (f32[1088,128]{1,0:T(8,128)S(1)}, f32[1088,128]{1,0:T(8,128)S(1)}, u32[]{:S(2)}, u32[]{:S(2)}) collective-permute-start(f32[1088,128]{1,0:T(8,128)S(1)} %get-tuple-element.51), channel_id=1, source_target_pairs={{0,7},{1,2},{2,1},{3,4},{4,3},{5,6},{6,5},{7,0},{8,15},{9,10},{10,... | collective-permute-start | bytes 1671176 | tf_op jit(solution)/shard_map/ppermute | solution.py:629
  7.0 14.5 %collective-permute-start.1 = (f32[1088,128]{1,0:T(8,128)S(1)}, f32[1088,128]{1,0:T(8,128)S(1)}, u32[]{:S(2)}, u32[]{:S(2)}) collective-permute-start(f32[1088,128]{1,0:T(8,128)S(1)} %get-tuple-element.52), channel_id=1, source_target_pairs={{0,1},{1,0},{2,3},{3,2},{4,5},{5,4},{6,7},{7,6},{8,9},{9,8},{10,11... | collective-permute-start | bytes 1671176 | tf_op jit(solution)/shard_map/ppermute | solution.py:629
  7.7 6.6 %collective-permute-start.2 = (f32[8,24,128]{2,1,0:T(8,128)S(1)}, f32[8,24,128]{2,1,0:T(8,128)S(1)}, u32[]{:S(2)}, u32[]{:S(2)}) collective-permute-start(f32[8,24,128]{2,1,0:T(8,128)S(1)} %get-tuple-element.53), channel_id=1, source_target_pairs={{0,24},{8,16},{16,8},{24,0},{1,25},{9,17},{17,9},{25,1},{2,26},{10... | collective-permute-start | bytes 294920 | tf_op jit(solution)/shard_map/ppermute | solution.py:629
  10.2 5.8 %collective-permute-start.3 = (f32[8,24,128]{2,1,0:T(8,128)S(1)}, f32[8,24,128]{2,1,0:T(8,128)S(1)}, u32[]{:S(2)}, u32[]{:S(2)}) collective-permute-start(f32[8,24,128]{2,1,0:T(8,128)S(1)} %get-tuple-element.54), channel_id=1, source_target_pairs={{0,8},{8,0},{16,24},{24,16},{1,9},{9,1},{17,25},{25,17},{2,10},{10... | collective-permute-start | bytes 294920 | tf_op jit(solution)/shard_map/ppermute | solution.py:629
  16.1 5.4 %collective-permute-start.4 = (f32[2,2,24,128]{3,2,1,0:T(8,128)S(1)}, f32[2,2,24,128]{3,2,1,0:T(8,128)S(1)}, u32[]{:S(2)}, u32[]{:S(2)}) collective-permute-start(f32[2,2,24,128]{3,2,1,0:T(8,128)S(1)} %get-tuple-element.57), channel_id=1, source_target_pairs={{0,7},{1,2},{2,1},{3,4},{4,3},{5,6},{6,5},{7,0},{8,15},{9,10},{10,... | collective-permute-start | bytes 147464 | tf_op jit(solution)/shard_map/ppermute | solution.py:629
  16.2 5.3 %collective-permute-start.5 = (f32[2,2,24,128]{3,2,1,0:T(8,128)S(1)}, f32[2,2,24,128]{3,2,1,0:T(8,128)S(1)}, u32[]{:S(2)}, u32[]{:S(2)}) collective-permute-start(f32[2,2,24,128]{3,2,1,0:T(8,128)S(1)} %get-tuple-element.58), channel_id=1, source_target_pairs={{0,1},{1,0},{2,3},{3,2},{4,5},{5,4},{6,7},{7,6},{8,9},{9,8},{10,11... | collective-permute-start | bytes 147464 | tf_op jit(solution)/shard_map/ppermute | solution.py:629
  24.3 6.6 %collective-permute-start.6 = (f32[2,136,128]{2,1,0:T(8,128)S(1)}, f32[2,136,128]{2,1,0:T(8,128)S(1)}, u32[]{:S(2)}, u32[]{:S(2)}) collective-permute-start(f32[2,136,128]{2,1,0:T(8,128)S(1)} %get-tuple-element.82), channel_id=1, source_target_pairs={{0,7},{1,2},{2,1},{3,4},{4,3},{5,6},{6,5},{7,0},{8,15},{9,10},{10,... | collective-permute-start | bytes 417800 | tf_op jit(solution)/shard_map/ppermute | solution.py:629
  25.7 5.2 %collective-permute-start.7 = (f32[2,136,128]{2,1,0:T(8,128)S(1)}, f32[2,136,128]{2,1,0:T(8,128)S(1)}, u32[]{:S(2)}, u32[]{:S(2)}) collective-permute-start(f32[2,136,128]{2,1,0:T(8,128)S(1)} %get-tuple-element.83), channel_id=1, source_target_pairs={{0,1},{1,0},{2,3},{3,2},{4,5},{5,4},{6,7},{7,6},{8,9},{9,8},{10,11... | collective-permute-start | bytes 417800 | tf_op jit(solution)/shard_map/ppermute | solution.py:629
  31.4 7.8 %collective-permute-start.8 = (f32[2,136,128]{2,1,0:T(8,128)S(1)}, f32[2,136,128]{2,1,0:T(8,128)S(1)}, u32[]{:S(2)}, u32[]{:S(2)}) collective-permute-start(f32[2,136,128]{2,1,0:T(8,128)S(1)} %get-tuple-element.88), channel_id=1, source_target_pairs={{0,7},{1,2},{2,1},{3,4},{4,3},{5,6},{6,5},{7,0},{8,15},{9,10},{10,... | collective-permute-start | bytes 417800 | tf_op jit(solution)/shard_map/ppermute | solution.py:629
  33.4 5.8 %collective-permute-start.9 = (f32[2,136,128]{2,1,0:T(8,128)S(1)}, f32[2,136,128]{2,1,0:T(8,128)S(1)}, u32[]{:S(2)}, u32[]{:S(2)}) collective-permute-start(f32[2,136,128]{2,1,0:T(8,128)S(1)} %get-tuple-element.89), channel_id=1, source_target_pairs={{0,1},{1,0},{2,3},{3,2},{4,5},{5,4},{6,7},{7,6},{8,9},{9,8},{10,11... | collective-permute-start | bytes 417800 | tf_op jit(solution)/shard_map/ppermute | solution.py:629

commit v8 on v7

--- a/solution.py
+++ b/solution.py
@@ -15,7 +15,9 @@
 
 pad = 16
 chunk = 72
+piece = 24
 depth = 2
+early = 2
 vmem_limit = 20 * 1024 * 1024
 f32 = jnp.float32
 
@@ -27,8 +29,8 @@
     return list(zip(starts, widths)), total
 
 
-def chunks(low, high):
-    return [(at, min(chunk, high - at)) for at in range(low, high, chunk)]
+def chunks(low, high, most=chunk):
+    return [(at, min(most, high - at)) for at in range(low, high, most)]
 
 
 def reach(cols):
@@ -126,46 +128,92 @@
     return put
 
 
+class Rows:
+    def __init__(self, row, at, size):
+        self.row, self.at, self.size = row, at, size
+        self.wide = {}
+
+    def around(self, y):
+        if y not in self.wide:
+            self.wide[y] = self.row(y, slice(self.at - 8, self.at + self.size + 8))
+        return self.wide[y]
+
+    def here(self, y):
+        return self.around(y)[8 : 8 + self.size]
+
+    def sides(self, y):
+        wide = self.around(y)
+        count = self.size + 16
+        return (
+            pltpu.roll(wide, count - 1, 0)[8 : 8 + self.size],
+            pltpu.roll(wide, 1, 0)[8 : 8 + self.size],
+        )
+
+
+def sweep(g_rows, term_rows, own_rows, adj, mob, chem, mask, cols, emit):
+    for at, size in chunks(*reach(cols), piece):
+        adj_rows, mob_rows, chem_rows = (Rows(f, at, size) for f in (adj, mob, chem))
+        for y in g_rows:
+            with_terms = y in term_rows
+            a, m = adj_rows.here(y), mob_rows.here(y)
+            mu = chem_rows.here(y) if with_terms else None
+            across = [other for other in (y + 1, y - 1) if other in own_rows]
+            diffs = [other - a for other in adj_rows.sides(y)]
+            diffs += [adj_rows.here(other) - a for other in across]
+            mobs = list(mob_rows.sides(y)) + [mob_rows.here(other) for other in across]
+            flow = sum_of([(other + m) * diff for other, diff in zip(mobs, diffs)])
+            diff = (up(a) - a) * mask
+            term = (up(m) + m) * diff
+            flow = flow + (term - down(term))
+            pair = None
+            if with_terms:
+                chems = list(chem_rows.sides(y)) + [chem_rows.here(other) for other in across]
+                pair = sum_of([(other - mu) * diff for other, diff in zip(chems, diffs)])
+                term = (up(mu) - mu) * diff
+                pair = pair + (term + down(term))
+            emit(y, slice(at, at + size), a, mu, flow, pair)
+
+
+def sum_of(values):
+    total = values[0]
+    for value in values[1:]:
+        total = total + value
+    return total
+
+
+def close_rows(out_rows, pot_rows, pot, mask, cols, emit):
+    for at, size in chunks(*reach(cols), piece):
+        held = Rows(pot, at, size)
+        for y in out_rows:
+            g = held.here(y)
+            step_z = (up(g) - g) * mask
+            values = list(held.sides(y)) + [held.here(k) for k in (y - 1, y + 1) if k in pot_rows]
+            emit(y, slice(at, at + size), sum_of(values) - 4.0 * g + (step_z - down(step_z)))
+
+
 def interior(rows, cols, nz, swing, mob, chem, curve, adj, rate, pot, part, grad, store):
-    low, high = reach(cols)
     lanes = adj[0].shape[-1]
     mask = face_mask(lanes, nz)
-
-    def at_row(field, y):
-        return row_of(field[0], field[1] + y)
-
-    def body(y, _):
-        for at, size in chunks(low, high):
-            span = slice(at, at + size)
-            a, mu, flow, pair = face_sums(
-                at_row(adj, y), at_row(mob, y), at_row(chem, y), at, size, mask
-            )
-            g = flow - at_row(rate, y)(0, span) * a
-            pot[y - 1, span, :] = g
+    inside = range(depth, rows - depth)
+
+    def reader(field):
+        return lambda y, span: field[0][field[1] + y, span, :]
+
+    def emit(y, span, a, mu, flow, pair):
+        g = flow - reader(rate)(y, span) * a
+        pot[y - 1, span, :] = g
+        if pair is not None:
             part[y - depth, span, :] = partial(
-                a, at_row(swing, y)(0, span), pair, at_row(curve, y)(0, span), g
+                a, reader(swing)(y, span), pair, reader(curve)(y, span), g
             )
             grad[y - depth, span, :] = gain(a, mu, None)
-        return 0
-
-    def edge(i, _):
-        y = 1 + i * (rows - 3)
-        for at, size in chunks(low, high):
-            a, _mu, flow, _pair = face_sums(at_row(adj, y), at_row(mob, y), None, at, size, mask)
-            span = slice(at, at + size)
-            pot[y - 1, span, :] = flow - at_row(rate, y)(0, span) * a
-        return 0
-
-    def close(y, _):
-        for at, size in chunks(low, high):
-            span = slice(at, at + size)
-            _g, lap = laplace(row_of(pot, y - 1), at, size, mask)
-            store(y - depth, span, part[y - depth, span, :] - grad_energy * lap)
-        return 0
-
-    lax.fori_loop(depth, rows - depth, body, 0)
-    lax.fori_loop(0, 2, edge, 0)
-    lax.fori_loop(depth, rows - depth, close, 0)
+
+    def close(y, span, lap):
+        store(y - depth, span, part[y - depth, span, :] - grad_energy * lap)
+
+    sweep(range(1, rows - 1), inside, range(rows), reader(adj), reader(mob), reader(chem), mask,
+          cols, emit)
+    close_rows(inside, range(1, rows - 1), lambda y, span: pot[y - 1, span, :], mask, cols, close)
 
 
 def boundary(rows, cols, nz, conc, mob, chem, curve, swing, adj, rate, pot, part, grad, store):
@@ -275,11 +323,13 @@
     for side, base in zip((main_a, main_b), bases(rows)):
         edge = jnp.where(base == 0, 0, rows - 1)
         rate = turned_rate(rate_in, edge, rows, nz, lanes)
-        side[pl.ds((1 + steps) * depth * cols, half), :] = jnp.where(
+        side[pl.ds((1 + early) * depth * cols, half), :] = jnp.where(
             lower, rate[:half], rate[half:]
         )
     for back in range(steps):
         copies[2 + back].wait()
+        if back >= early:
+            continue
         for side, base in zip((main_a, main_b), bases(rows)):
             for at in range(depth):
                 side[pl.ds(((1 + back) * depth + at) * cols, cols), :] = conc_in[
@@ -424,7 +474,7 @@
     lower = lax.broadcasted_iota(jnp.int32, (half, lanes), 1) < nz
 
     def unpack(side):
-        packed = side[pl.ds((1 + steps) * depth * cols, half), :]
+        packed = side[pl.ds((1 + early) * depth * cols, half), :]
         turned = pltpu.roll(packed, lanes // 2, 1)
         return jnp.concatenate(
             [jnp.where(lower, packed, turned), jnp.where(lower, turned, packed)], axis=0
@@ -465,7 +515,7 @@
 
 def prepare_kernel(steps, rows, cols, nz, back, conc_own, from_a, from_b, x_low, x_high,
                    corner_a, corner_b, mob, chem, curve, swing, *rest):
-    *ahead, conc = rest
+    *more, conc = rest
     places, _ = slots(steps)
     low, high = reach(cols)
     lanes = conc.shape[2]
@@ -475,11 +525,20 @@
         put_own(conc, depth + y, conc_own[back, y], y, place, cols, x_low, x_high)
     for halo, corner, base in zip((from_a, from_b), (corner_a, corner_b), landings(rows)):
         for at in range(depth):
-            span = pl.ds(((1 + back) * depth + at) * cols, cols)
+            first = (1 + back) * depth if back < early else (back - early) * depth
+            span = pl.ds((first + at) * cols, cols)
             put_halo(conc, base + at, halo[span, :], at, place, cols, corner)
 
-    if ahead:
-        put_ahead(ahead[0], conc_own, back + 1, x_low, x_high, places, rows, cols)
+    if more:
+        ahead, late_a, late_b = more
+        put_ahead(ahead, conc_own, back + 1, x_low, x_high, places, rows, cols)
+        for side, base in zip((late_a, late_b), bases(rows)):
+            for after in range(early, steps):
+                for at in range(depth):
+                    span = pl.ds(((after - early) * depth + at) * cols, cols)
+                    side[span, :] = conc_own[after, base + at]
+            used = (steps - early) * depth * cols
+            side[used:, :] = jnp.zeros((side.shape[0] - used, lanes), f32)
 
     def mob_row(row, _):
         for at, size in chunks(low - 8, high + 8):
@@ -499,56 +558,46 @@
 
 def next_interior(rows, cols, nz, final, mob, chem, curve, swing, rate, inner, outer, *rest):
     if final:
-        before, out, tiles, grad_out, adj, pot, part, grad = rest
-    elif len(rest) == 8:
-        inner_grad, outer_grad, out, grad, adj, pot, part, before = rest
-        for k in range(rows - 2 * depth):
-            before[depth + k] = inner_grad[k]
-        for s, k, y in sides_of(rows):
-            before[y] = outer_grad[s, k]
+        *before, out, tiles, grad_out, pot, part, grad = rest
     else:
-        before, out, grad, adj, pot, part = rest
-    low, high = reach(cols)
-    lanes = adj.shape[2]
-    mask = face_mask(lanes, nz)
+        *before, out, grad, pot, part = rest
+    mask = face_mask(mob.shape[2], nz)
     skip = (inner.shape[0] - (rows - 2 * depth)) // 2
-    for k in range(rows - 2 * depth):
-        adj[1 + depth + k] = inner[skip + k]
-    for s, k, y in sides_of(rows):
-        adj[1 + y] = outer[s, k]
-    adj[0] = outer[0, 0]
-    adj[1 + rows] = outer[1, 0]
-    pot[0] = jnp.zeros(pot.shape[1:], f32)
-    pot[1 + rows] = jnp.zeros(pot.shape[1:], f32)
-
-    def body(y, _):
-        for at, size in chunks(low, high):
-            span = slice(at, at + size)
-            a, mu, flow, pair = face_sums(
-                row_of(adj, y + 1), row_of(mob, y + depth), row_of(chem, y + 1), at, size, mask
-            )
-            g = flow - rate[y, span, :] * a
-            pot[y + 1, span, :] = g
-            part[y, span, :] = partial(
-                a, swing[y + 1, span, :], pair, curve[y + 1, span, :], g
-            )
-            grad[y, span, :] = gain(a, mu, before[y, span, :])
-        return 0
-
-    def close(y, _):
-        for at, size in chunks(low, high):
-            span = slice(at, at + size)
-            _g, lap = laplace(row_of(pot, y + 1), at, size, mask)
-            out[y, span, :] = part[y, span, :] - grad_energy * lap
-        return 0
-
-    lax.fori_loop(0, rows, body, 0)
-    lax.fori_loop(0, rows, close, 0)
+    edges = {y: (s, k) for s, k, y in sides_of(rows)}
+
+    def pick(middle, middle_skip, ends, y, span):
+        if y in edges:
+            return ends[(*edges[y], span)]
+        return middle[y - depth + middle_skip, span]
+
+    def earlier(y, span):
+        if len(before) == 1:
+            return before[0][y, span, :]
+        return pick(before[0], 0, before[1], y, span)
+
+    def emit(y, span, a, mu, flow, pair):
+        g = flow - rate[y, span, :] * a
+        pot[y, span, :] = g
+        part[y, span, :] = partial(a, swing[y + 1, span, :], pair, curve[y + 1, span, :], g)
+        grad[y, span, :] = gain(a, mu, earlier(y, span))
+
+    def close(y, span, lap):
+        out[y, span, :] = part[y, span, :] - grad_energy * lap
+
+    every = range(rows)
+    sweep(every, every, every, lambda y, span: pick(inner, skip, outer, y, span),
+          lambda y, span: mob[depth + y, span, :], lambda y, span: chem[1 + y, span, :], mask,
+          cols, emit)
+    close_rows(every, every, lambda y, span: pot[y, span, :], mask, cols, close)
     if final:
         for y in range(rows):
             grad_out[pl.ds(y, nz, stride=rows), :] = fold(grad[y, pad : pad + cols, :].T, nz)
         for y in range(depth, rows - depth):
-            tiles[pl.ds(y, lanes, stride=rows), :] = out[y, pad : pad + cols, :].T
+            tiles[pl.ds(y, lanes_of(out), stride=rows), :] = out[y, pad : pad + cols, :].T
+
+
+def lanes_of(ref):
+    return ref.shape[-1]
 
 
 def fold(value, nz):
@@ -646,7 +695,7 @@
     raw = [(steps, flat, cols), (flat, cols), (nz * rows, cols)]
     conc_raw, adj_raw, rate_raw, main_a, main_b = call(
         functools.partial(edge_kernel, steps, rows, cols, nz),
-        raw + [((1 + steps) * depth * cols + cols // 2, lanes)] * 2,
+        raw + [((1 + early) * depth * cols + cols // 2, lanes)] * 2,
         [pltpu.SemaphoreType.DMA((2 + steps,))],
         saved_conc.reshape(raw[0]), adjoint_end.reshape(raw[1]), rate_field.reshape(raw[2]),
         cost=2,
@@ -685,18 +734,23 @@
         cost=2,
     )
     before = (inner_grad, outer_grad)
+    got = main_a, main_b
+    late = (max((steps - early) * depth * cols, 2 * (cols + 8) + 8), lanes)
     for back in range(1, steps):
         adj_a, adj_b = swap(to_a, to_b, "gy")
         final = back == steps - 1
         fields = call(
             functools.partial(prepare_kernel, steps, rows, cols, nz, back),
-            [field(rows + 2 * depth)] + [field(rows + 2)] * 3 + ([] if final else [both]),
+            [field(rows + 2 * depth)] + [field(rows + 2)] * 3
+            + ([] if final else [both, late, late]),
             [field(rows + 2 * depth)],
-            conc_own, main_a, main_b, x_low, x_high, corner_a, corner_b,
+            conc_own, *got, x_low, x_high, corner_a, corner_b,
             cost=2,
         )
-        fields, ahead = fields[:4], fields[4:]
-        work = [field(rows + 2)] * 2 + [field(rows)]
+        fields, ahead, more = fields[:4], fields[4:5], fields[5:]
+        if not final:
+            got = swap(*more, "gy")
+        work = [field(rows)] * 2
         if final:
             rows_in, tiles, grad = call(
                 functools.partial(next_interior, rows, cols, nz, final),
@@ -716,7 +770,7 @@
             rows_in, grad = call(
                 functools.partial(next_interior, rows, cols, nz, final),
                 [field(rows)] * 2,
-                work + ([field(rows)] if len(before) == 2 else []),
+                work,
                 *fields, rate, inner, outer, *before,
                 cost=3,
             )

time: 40.5 us -> 58.4 us (1.44)
  Pallas kernels: 20.7 us -> 37.2 us
  starting transfers between devices: 11.2 us -> 14.9 us
  waiting for transfers between devices: 7.72 us -> 5.31 us
    pallas_call x11, Pallas kernels: 20.7 us -> 37.2 us  [call(): pl.pallas_call(kernel, out_shape=[jax.ShapeDtypeStruct(shape, f32) for sh...]
    ppermute x5 -> x6, starting transfers between devices: 10.6 us -> 14.3 us  [swap(): lax.ppermute(value_a, axis, pairs_a)]
    ppermute x5 -> x6, waiting for transfers between devices: 5.93 us -> 3.52 us  [swap(): lax.ppermute(value_a, axis, pairs_a)]
    ppermute x5 -> x6, waiting for transfers between devices: 1.79 us -> 1.79 us  [swap(): lax.ppermute(value_b, axis, pairs_b)]
  transfers between devices with their start and end apart: 10 -> 12, of which waited for: 4 -> 2; matrix products, arithmetic and copies ran while one was open for 0% -> 0% of each run, Pallas kernels for 36% -> 54%
where the time goes in v8:
time: 58.4 us; the launch traced here: 58.2 us
  Pallas kernels  37.2 us (64%)
  starting transfers between devices  14.9 us (26%)
  waiting for transfers between devices  5.31 us (9%)
  between operations  0.76 us (1%)
    pallas_call x11, Pallas kernels, call(): pl.pallas_call(kernel, out_shape=[jax.ShapeDtypeStruct(shape, f32) for sh...  37.2 us
    ppermute x6, starting transfers between devices, swap(): lax.ppermute(value_a, axis, pairs_a)  14.3 us
    ppermute x6, waiting for transfers between devices, swap(): lax.ppermute(value_a, axis, pairs_a)  3.52 us
    ppermute x6, waiting for transfers between devices, swap(): lax.ppermute(value_b, axis, pairs_b)  1.79 us
  transfers between devices with their start and end apart: 12, of which 2 were waited for; matrix products, arithmetic and copies ran while one was open for 0% of the time, Pallas kernels for 54%

profile of v8, /device:TPU:0, one launch (start us, length us, event | category | flops | bytes accessed | tf_op | source)
XLA Modules:
  0.0 58.2 jit_solution(17807299802622273204)
XLA Ops:
  0.6 1.6 %shard_map.50 = (f32[3,1024,128]{2,1,0:T(8,128)S(1)}, f32[1024,128]{1,0:T(8,128)S(1)}, f32[512,128]{1,0:T(8,128)S(1)}, f32[832,128]{1,0:T(8,128)S(1)}, f32[832,128]{1,0:T(8,128)S(1)}) custom-call(f32[3,1024,128]{2,1,0:T(8,128)} %bitcast.5, f32[1024,128]{1,0:T(8,128)} %bitcast.6, f32[512,128]{1,0:T(8,128)} %bitcast.8), custom_call_target="tpu_custom_call" | custom-call | flops 2000000 | bytes 4000000 | tf_op jit(solution)/shard_map/pallas_call | solution.py:661
  2.3 4.6 %collective-permute-start = (f32[832,128]{1,0:T(8,128)S(1)}, f32[832,128]{1,0:T(8,128)S(1)}, u32[]{:S(2)}, u32[]{:S(2)}) collective-permute-start(f32[832,128]{1,0:T(8,128)S(1)} %get-tuple-element.53), channel_id=1, source_target_pairs={{0,7},{1,2},{2,1},{3,4},{4,3},{5,6},{6,5},{7,0},{8,15},{9,10},{10,... | collective-permute-start | bytes 1277960 | tf_op jit(solution)/shard_map/ppermute | solution.py:678
  6.8 0.0 collective-permute-start.1
  6.8 0.7 %shard_map.51 = (f32[3,8,128,128]{3,2,1,0:T(8,128)S(1)}, f32[8,128,128]{2,1,0:T(8,128)S(1)}, f32[8,128,128]{2,1,0:T(8,128)S(1)}, f32[8,24,128]{2,1,0:T(8,128)S(1)}, f32[8,24,128]{2,1,0:T(8,128)S(1)}) custom-call(f32[3,1024,128]{2,1,0:T(8,128)S(1)} %get-tuple-element.49.conc_in, f32[1024,128]{1,0:T(8,128)S(1)} %get-tuple-element.50.adj_in, ...), custom_call_target="tpu_custom_call" | custom-call | flops 1000000 | bytes 2000000 | tf_op jit(solution)/shard_map/pallas_call | solution.py:661
  7.6 2.5 %collective-permute-start.2 = (f32[8,24,128]{2,1,0:T(8,128)S(1)}, f32[8,24,128]{2,1,0:T(8,128)S(1)}, u32[]{:S(2)}, u32[]{:S(2)}) collective-permute-start(f32[8,24,128]{2,1,0:T(8,128)S(1)} %get-tuple-element.55), channel_id=1, source_target_pairs={{0,24},{8,16},{16,8},{24,0},{1,25},{9,17},{17,9},{25,1},{2,26},{10... | collective-permute-start | bytes 294920 | tf_op jit(solution)/shard_map/ppermute | solution.py:678
  10.1 0.5 collective-permute-start.3
  10.6 3.5 %collective-permute-done.2.got_a = f32[8,24,128]{2,1,0:T(8,128)S(1)} collective-permute-done((f32[8,24,128]{2,1,0:T(8,128)S(1)}, f32[8,24,128]{2,1,0:T(8,128)S(1)}, u32[]{:S(2)}, u32[]{:S(2)}) %collective-permute-start.2) | collective-permute-done | bytes 98336 | tf_op jit(solution)/shard_map/ppermute | solution.py:678
  14.1 1.8 %collective-permute-done.3.got_b = f32[8,24,128]{2,1,0:T(8,128)S(1)} collective-permute-done((f32[8,24,128]{2,1,0:T(8,128)S(1)}, f32[8,24,128]{2,1,0:T(8,128)S(1)}, u32[]{:S(2)}, u32[]{:S(2)}) %collective-permute-start.3) | collective-permute-done | bytes 98336 | tf_op jit(solution)/shard_map/ppermute | solution.py:678
  16.0 0.1 collective-permute-start.4
  16.0 0.1 collective-permute-start.5
  16.1 6.2 %shard_map.55 = (f32[8,160,128]{2,1,0:T(8,128)S(1)}, f32[8,160,128]{2,1,0:T(8,128)S(1)}, f32[8,160,128]{2,1,0:T(8,128)S(1)}, f32[6,160,128]{2,1,0:T(8,128)S(1)},...) custom-call(f32[3,8,128,128]{3,2,1,0:T(8,128)S(1)} %get-tuple-elemen, ...), custom_call_target="tpu_custom_call" | custom-call | flops 3000000 | bytes 6000000 | tf_op jit(solution)/shard_map/pallas_call | solution.py:661
  22.3 0.0 collective-permute-done.4.corner_a
  22.3 0.0 collective-permute-done.5.corner_b
  22.3 0.0 collective-permute-done.from_a
  22.4 0.0 collective-permute-done.1.from_b
  22.4 2.8 %shard_map.56 = (f32[2,2,160,128]{3,2,1,0:T(8,128)S(1)}, f32[2,2,160,128]{3,2,1,0:T(8,128)S(1)}, f32[2,136,128]{2,1,0:T(8,128)S(1)}, f32[2,136,128]{2,1,0:T(8,128)S(1)}) custom-call(f32[8,160,128]{2,1,0:T(8,128)S(1)} %get-tuple-element.75.conc_in, f32[8,160,128]{2,1,0:T(8,128)S(1)} %get-tuple-element.76.adj_in, ...), custom_call_target="tpu_custom_call" | custom-call | flops 2000000 | bytes 4000000 | tf_op jit(solution)/shard_map/pallas_call | solution.py:661
  25.2 3.5 %collective-permute-start.8 = (f32[2,136,128]{2,1,0:T(8,128)S(1)}, f32[2,136,128]{2,1,0:T(8,128)S(1)}, u32[]{:S(2)}, u32[]{:S(2)}) collective-permute-start(f32[2,136,128]{2,1,0:T(8,128)S(1)} %get-tuple-element.86), channel_id=1, source_target_pairs={{0,7},{1,2},{2,1},{3,4},{4,3},{5,6},{6,5},{7,0},{8,15},{9,10},{10,... | collective-permute-start | bytes 417800 | tf_op jit(solution)/shard_map/ppermute | solution.py:678
  28.7 0.0 collective-permute-start.9
  28.7 1.9 %shard_map.53 = (f32[12,160,128]{2,1,0:T(8,128)S(1)}, f32[10,160,128]{2,1,0:T(8,128)S(1)}, f32[10,160,128]{2,1,0:T(8,128)S(1)}, f32[10,160,128]{2,1,0:T(8,128)S(...) custom-call(f32[3,8,128,128]{3,2,1,0:T(8,128)S(1)} %get-tuple-element.52.conc_own, ...), custom_call_target="tpu_custom_call" | custom-call | flops 2000000 | bytes 4000000 | tf_op jit(solution)/shard_map/pallas_call | solution.py:661
  30.6 0.6 %collective-permute-start.6 = (f32[280,128]{1,0:T(8,128)S(1)}, f32[280,128]{1,0:T(8,128)S(1)}, u32[]{:S(2)}, u32[]{:S(2)}) collective-permute-start(f32[280,128]{1,0:T(8,128)S(1)} %get-tuple-element.61), channel_id=1, source_target_pairs={{0,7},{1,2},{2,1},{3,4},{4,3},{5,6},{6,5},{7,0},{8,15},{9,10},{10,... | collective-permute-start | bytes 430088 | tf_op jit(solution)/shard_map/ppermute | solution.py:678
  31.3 0.0 collective-permute-start.7
  31.3 9.4 %shard_map.57 = (f32[8,160,128]{2,1,0:T(8,128)S(1)}, f32[8,160,128]{2,1,0:T(8,128)S(1)}) custom-call(f32[12,160,128]{2,1,0:T(8,128)S(1)} %get-tuple-element.70.mob, f32[10,160,128]{2,1,0:T(8,128)S(1)} %get-tuple-element.71.chem, f32[10,160,128]{2,1,0:T(8,128)S(1)} %get-tuple-element.72.curve, f32[10,160,128]{2,1,0:T(8,128)S(1)} %get-tuple-element.73.swing, ...), custom_call_target="tpu_custom_call" | custom-call | flops 3000000 | bytes 6000000 | tf_op jit(solution)/shard_map/pallas_call | solution.py:661
  40.7 0.0 collective-permute-done.8.from_a
  40.7 0.0 collective-permute-done.9.from_b
  40.7 0.5 shard_map.58
  41.2 3.0 %collective-permute-start.10 = (f32[2,136,128]{2,1,0:T(8,128)S(1)}, f32[2,136,128]{2,1,0:T(8,128)S(1)}, u32[]{:S(2)}, u32[]{:S(2)}) collective-permute-start(f32[2,136,128]{2,1,0:T(8,128)S(1)} %get-tuple-element.92), channel_id=1, source_target_pairs={{0,7},{1,2},{2,1},{3,4},{4,3},{5,6},{6,5},{7,0},{8,15},{9,10},{10,... | collective-permute-start | bytes 417800 | tf_op jit(solution)/shard_map/ppermute | solution.py:678
  44.2 0.0 collective-permute-start.11
  44.2 0.0 collective-permute-done.6.from_a
  44.2 0.0 collective-permute-done.7.from_b
  44.2 1.9 %shard_map.54 = (f32[12,160,128]{2,1,0:T(8,128)S(1)}, f32[10,160,128]{2,1,0:T(8,128)S(1)}, f32[10,160,128]{2,1,0:T(8,128)S(1)}, f32[10,160,128]{2,1,0:T(8,128)S(1)}) custom-call(f32[3,8,128,128]{3,2,1,0:T(8,128)S(1)} %get-tuple-element.52.conc_own, f32[280,128]{1,0:T(8,128)S(1)} %collective-permute-done.6.from_a, ...), custom_call_target="tpu_custom_call" | custom-call | flops 2000000 | bytes 4000000 | tf_op jit(solution)/shard_map/pallas_call | solution.py:661
  46.1 11.0 %shard_map.59 = (f32[8,160,128]{2,1,0:T(8,128)S(1)}, f32[1024,128]{1,0:T(8,128)S(1)}, f32[512,128]{1,0:T(8,128)}) custom-call(f32[12,160,128]{2,1,0:T(8,128)S(1)} %get-tuple-element.63.mob, f32[10,160,128]{2,1,0:T(8,128)S(1)} %get-tuple-element.64.chem, f32[10,160,128]{2,1,0:T(8,128)S(1)} %get-tuple-element.65.curve, ...), custom_call_target="tpu_custom_call" | custom-call | flops 3000000 | bytes 6000000 | tf_op jit(solution)/shard_map/pallas_call | solution.py:661
  57.1 0.0 collective-permute-done.10.from_a
  57.1 0.0 collective-permute-done.11.from_b
  57.1 1.1 %shard_map.60 = f32[1024,128]{1,0:T(8,128)} custom-call(f32[12,160,128]{2,1,0:T(8,128)S(1)} %get-tuple-element.63.mob, f32[10,160,128]{2,1,0:T(8,128)S(1)} %get-tuple-element.64.chem, f32[10,160,128]{2,1,0:T(8,128)S(1)} %get-tuple-element.65.curve, f32[10,160,128]{2,1,0:T(8,128)S(1)} %get-tuple-element.66.swing, ...), custom_call_target="tpu_custom_call" | custom-call | flops 1000000 | bytes 2000000 | tf_op jit(solution)/shard_map/pallas_call | solution.py:661
  (1 shorter events, 0.0 us)
Async XLA Ops:
  2.3 20.1 %collective-permute-start = (f32[832,128]{1,0:T(8,128)S(1)}, f32[832,128]{1,0:T(8,128)S(1)}, u32[]{:S(2)}, u32[]{:S(2)}) collective-permute-start(f32[832,128]{1,0:T(8,128)S(1)} %get-tuple-element.53), channel_id=1, source_target_pairs={{0,7},{1,2},{2,1},{3,4},{4,3},{5,6},{6,5},{7,0},{8,15},{9,10},{10,... | collective-permute-start | bytes 1277960 | tf_op jit(solution)/shard_map/ppermute | solution.py:678
  6.8 15.5 %collective-permute-start.1 = (f32[832,128]{1,0:T(8,128)S(1)}, f32[832,128]{1,0:T(8,128)S(1)}, u32[]{:S(2)}, u32[]{:S(2)}) collective-permute-start(f32[832,128]{1,0:T(8,128)S(1)} %get-tuple-element.54), channel_id=1, source_target_pairs={{0,1},{1,0},{2,3},{3,2},{4,5},{5,4},{6,7},{7,6},{8,9},{9,8},{10,11... | collective-permute-start | bytes 1277960 | tf_op jit(solution)/shard_map/ppermute | solution.py:678
  7.6 6.6 %collective-permute-start.2 = (f32[8,24,128]{2,1,0:T(8,128)S(1)}, f32[8,24,128]{2,1,0:T(8,128)S(1)}, u32[]{:S(2)}, u32[]{:S(2)}) collective-permute-start(f32[8,24,128]{2,1,0:T(8,128)S(1)} %get-tuple-element.55), channel_id=1, source_target_pairs={{0,24},{8,16},{16,8},{24,0},{1,25},{9,17},{17,9},{25,1},{2,26},{10... | collective-permute-start | bytes 294920 | tf_op jit(solution)/shard_map/ppermute | solution.py:678
  10.1 5.8 %collective-permute-start.3 = (f32[8,24,128]{2,1,0:T(8,128)S(1)}, f32[8,24,128]{2,1,0:T(8,128)S(1)}, u32[]{:S(2)}, u32[]{:S(2)}) collective-permute-start(f32[8,24,128]{2,1,0:T(8,128)S(1)} %get-tuple-element.56), channel_id=1, source_target_pairs={{0,8},{8,0},{16,24},{24,16},{1,9},{9,1},{17,25},{25,17},{2,10},{10... | collective-permute-start | bytes 294920 | tf_op jit(solution)/shard_map/ppermute | solution.py:678
  16.0 6.4 %collective-permute-start.4 = (f32[2,2,24,128]{3,2,1,0:T(8,128)S(1)}, f32[2,2,24,128]{3,2,1,0:T(8,128)S(1)}, u32[]{:S(2)}, u32[]{:S(2)}) collective-permute-start(f32[2,2,24,128]{3,2,1,0:T(8,128)S(1)} %get-tuple-element.59), channel_id=1, source_target_pairs={{0,7},{1,2},{2,1},{3,4},{4,3},{5,6},{6,5},{7,0},{8,15},{9,10},{10,... | collective-permute-start | bytes 147464 | tf_op jit(solution)/shard_map/ppermute | solution.py:678
  16.0 6.3 %collective-permute-start.5 = (f32[2,2,24,128]{3,2,1,0:T(8,128)S(1)}, f32[2,2,24,128]{3,2,1,0:T(8,128)S(1)}, u32[]{:S(2)}, u32[]{:S(2)}) collective-permute-start(f32[2,2,24,128]{3,2,1,0:T(8,128)S(1)} %get-tuple-element.60), channel_id=1, source_target_pairs={{0,1},{1,0},{2,3},{3,2},{4,5},{5,4},{6,7},{7,6},{8,9},{9,8},{10,11... | collective-permute-start | bytes 147464 | tf_op jit(solution)/shard_map/ppermute | solution.py:678
  25.2 15.5 %collective-permute-start.8 = (f32[2,136,128]{2,1,0:T(8,128)S(1)}, f32[2,136,128]{2,1,0:T(8,128)S(1)}, u32[]{:S(2)}, u32[]{:S(2)}) collective-permute-start(f32[2,136,128]{2,1,0:T(8,128)S(1)} %get-tuple-element.86), channel_id=1, source_target_pairs={{0,7},{1,2},{2,1},{3,4},{4,3},{5,6},{6,5},{7,0},{8,15},{9,10},{10,... | collective-permute-start | bytes 417800 | tf_op jit(solution)/shard_map/ppermute | solution.py:678
  28.7 12.0 %collective-permute-start.9 = (f32[2,136,128]{2,1,0:T(8,128)S(1)}, f32[2,136,128]{2,1,0:T(8,128)S(1)}, u32[]{:S(2)}, u32[]{:S(2)}) collective-permute-start(f32[2,136,128]{2,1,0:T(8,128)S(1)} %get-tuple-element.87), channel_id=1, source_target_pairs={{0,1},{1,0},{2,3},{3,2},{4,5},{5,4},{6,7},{7,6},{8,9},{9,8},{10,11... | collective-permute-start | bytes 417800 | tf_op jit(solution)/shard_map/ppermute | solution.py:678
  30.6 13.6 %collective-permute-start.6 = (f32[280,128]{1,0:T(8,128)S(1)}, f32[280,128]{1,0:T(8,128)S(1)}, u32[]{:S(2)}, u32[]{:S(2)}) collective-permute-start(f32[280,128]{1,0:T(8,128)S(1)} %get-tuple-element.61), channel_id=1, source_target_pairs={{0,7},{1,2},{2,1},{3,4},{4,3},{5,6},{6,5},{7,0},{8,15},{9,10},{10,... | collective-permute-start | bytes 430088 | tf_op jit(solution)/shard_map/ppermute | solution.py:678
  31.3 12.9 %collective-permute-start.7 = (f32[280,128]{1,0:T(8,128)S(1)}, f32[280,128]{1,0:T(8,128)S(1)}, u32[]{:S(2)}, u32[]{:S(2)}) collective-permute-start(f32[280,128]{1,0:T(8,128)S(1)} %get-tuple-element.62), channel_id=1, source_target_pairs={{0,1},{1,0},{2,3},{3,2},{4,5},{5,4},{6,7},{7,6},{8,9},{9,8},{10,11... | collective-permute-start | bytes 430088 | tf_op jit(solution)/shard_map/ppermute | solution.py:678
  41.2 15.9 %collective-permute-start.10 = (f32[2,136,128]{2,1,0:T(8,128)S(1)}, f32[2,136,128]{2,1,0:T(8,128)S(1)}, u32[]{:S(2)}, u32[]{:S(2)}) collective-permute-start(f32[2,136,128]{2,1,0:T(8,128)S(1)} %get-tuple-element.92), channel_id=1, source_target_pairs={{0,7},{1,2},{2,1},{3,4},{4,3},{5,6},{6,5},{7,0},{8,15},{9,10},{10,... | collective-permute-start | bytes 417800 | tf_op jit(solution)/shard_map/ppermute | solution.py:678
  44.2 12.9 %collective-permute-start.11 = (f32[2,136,128]{2,1,0:T(8,128)S(1)}, f32[2,136,128]{2,1,0:T(8,128)S(1)}, u32[]{:S(2)}, u32[]{:S(2)}) collective-permute-start(f32[2,136,128]{2,1,0:T(8,128)S(1)} %get-tuple-element.93), channel_id=1, source_target_pairs={{0,1},{1,0},{2,3},{3,2},{4,5},{5,4},{6,7},{7,6},{8,9},{9,8},{10,11... | collective-permute-start | bytes 417800 | tf_op jit(solution)/shard_map/ppermute | solution.py:678

commit v9 on v7

--- a/solution.py
+++ b/solution.py
@@ -16,6 +16,7 @@
 pad = 16
 chunk = 72
 depth = 2
+early = 2
 vmem_limit = 20 * 1024 * 1024
 f32 = jnp.float32
 
@@ -275,11 +276,13 @@
     for side, base in zip((main_a, main_b), bases(rows)):
         edge = jnp.where(base == 0, 0, rows - 1)
         rate = turned_rate(rate_in, edge, rows, nz, lanes)
-        side[pl.ds((1 + steps) * depth * cols, half), :] = jnp.where(
+        side[pl.ds((1 + early) * depth * cols, half), :] = jnp.where(
             lower, rate[:half], rate[half:]
         )
     for back in range(steps):
         copies[2 + back].wait()
+        if back >= early:
+            continue
         for side, base in zip((main_a, main_b), bases(rows)):
             for at in range(depth):
                 side[pl.ds(((1 + back) * depth + at) * cols, cols), :] = conc_in[
@@ -424,7 +427,7 @@
     lower = lax.broadcasted_iota(jnp.int32, (half, lanes), 1) < nz
 
     def unpack(side):
-        packed = side[pl.ds((1 + steps) * depth * cols, half), :]
+        packed = side[pl.ds((1 + early) * depth * cols, half), :]
         turned = pltpu.roll(packed, lanes // 2, 1)
         return jnp.concatenate(
             [jnp.where(lower, packed, turned), jnp.where(lower, turned, packed)], axis=0
@@ -465,7 +468,7 @@
 
 def prepare_kernel(steps, rows, cols, nz, back, conc_own, from_a, from_b, x_low, x_high,
                    corner_a, corner_b, mob, chem, curve, swing, *rest):
-    *ahead, conc = rest
+    *more, conc = rest
     places, _ = slots(steps)
     low, high = reach(cols)
     lanes = conc.shape[2]
@@ -475,11 +478,20 @@
         put_own(conc, depth + y, conc_own[back, y], y, place, cols, x_low, x_high)
     for halo, corner, base in zip((from_a, from_b), (corner_a, corner_b), landings(rows)):
         for at in range(depth):
-            span = pl.ds(((1 + back) * depth + at) * cols, cols)
+            first = (1 + back) * depth if back < early else (back - early) * depth
+            span = pl.ds((first + at) * cols, cols)
             put_halo(conc, base + at, halo[span, :], at, place, cols, corner)
 
-    if ahead:
-        put_ahead(ahead[0], conc_own, back + 1, x_low, x_high, places, rows, cols)
+    if more:
+        ahead, late_a, late_b = more
+        put_ahead(ahead, conc_own, back + 1, x_low, x_high, places, rows, cols)
+        for side, base in zip((late_a, late_b), bases(rows)):
+            for after in range(early, steps):
+                for at in range(depth):
+                    span = pl.ds(((after - early) * depth + at) * cols, cols)
+                    side[span, :] = conc_own[after, base + at]
+            used = (steps - early) * depth * cols
+            side[used:, :] = jnp.zeros((side.shape[0] - used, lanes), f32)
 
     def mob_row(row, _):
         for at, size in chunks(low - 8, high + 8):
@@ -646,7 +658,7 @@
     raw = [(steps, flat, cols), (flat, cols), (nz * rows, cols)]
     conc_raw, adj_raw, rate_raw, main_a, main_b = call(
         functools.partial(edge_kernel, steps, rows, cols, nz),
-        raw + [((1 + steps) * depth * cols + cols // 2, lanes)] * 2,
+        raw + [((1 + early) * depth * cols + cols // 2, lanes)] * 2,
         [pltpu.SemaphoreType.DMA((2 + steps,))],
         saved_conc.reshape(raw[0]), adjoint_end.reshape(raw[1]), rate_field.reshape(raw[2]),
         cost=2,
@@ -685,17 +697,22 @@
         cost=2,
     )
     before = (inner_grad, outer_grad)
+    got = main_a, main_b
+    late = (max((steps - early) * depth * cols, 2 * (cols + 8) + 8), lanes)
     for back in range(1, steps):
         adj_a, adj_b = swap(to_a, to_b, "gy")
         final = back == steps - 1
         fields = call(
             functools.partial(prepare_kernel, steps, rows, cols, nz, back),
-            [field(rows + 2 * depth)] + [field(rows + 2)] * 3 + ([] if final else [both]),
+            [field(rows + 2 * depth)] + [field(rows + 2)] * 3
+            + ([] if final else [both, late, late]),
             [field(rows + 2 * depth)],
-            conc_own, main_a, main_b, x_low, x_high, corner_a, corner_b,
+            conc_own, *got, x_low, x_high, corner_a, corner_b,
             cost=2,
         )
-        fields, ahead = fields[:4], fields[4:]
+        fields, ahead, more = fields[:4], fields[4:5], fields[5:]
+        if not final:
+            got = swap(*more, "gy")
         work = [field(rows + 2)] * 2 + [field(rows)]
         if final:
             rows_in, tiles, grad = call(

time: 40.5 us -> 42 us (1.037)
  starting transfers between devices: 11.2 us -> 12.8 us
    ppermute x5 -> x6, starting transfers between devices: 10.6 us -> 12.2 us  [swap(): lax.ppermute(value_a, axis, pairs_a)]
    ppermute x5 -> x6, waiting for transfers between devices: 5.93 us -> 5.67 us  [swap(): lax.ppermute(value_a, axis, pairs_a)]
    ppermute x5 -> x6, waiting for transfers between devices: 1.79 us -> 1.79 us  [swap(): lax.ppermute(value_b, axis, pairs_b)]
  transfers between devices with their start and end apart: 10 -> 12, of which waited for: 4 -> 3; matrix products, arithmetic and copies ran while one was open for 0% -> 0% of each run, Pallas kernels for 36% -> 36%
where the time goes in v9:
time: 42 us; the launch traced here: 41.8 us
  Pallas kernels  20.8 us (50%)
  starting transfers between devices  12.8 us (30%)
  waiting for transfers between devices  7.46 us (18%)
  between operations  0.73 us (2%)
    pallas_call x11, Pallas kernels, call(): pl.pallas_call(kernel, out_shape=[jax.ShapeDtypeStruct(shape, f32) for sh...  20.8 us
    ppermute x6, starting transfers between devices, swap(): lax.ppermute(value_a, axis, pairs_a)  12.2 us
    ppermute x6, waiting for transfers between devices, swap(): lax.ppermute(value_a, axis, pairs_a)  5.67 us
    ppermute x6, waiting for transfers between devices, swap(): lax.ppermute(value_b, axis, pairs_b)  1.79 us
  transfers between devices with their start and end apart: 12, of which 3 were waited for; matrix products, arithmetic and copies ran while one was open for 0% of the time, Pallas kernels for 36%

profile of v9, /device:TPU:0, one launch (start us, length us, event | category | flops | bytes accessed | tf_op | source)
XLA Modules:
  0.0 41.8 jit_solution(12698644395275435105)
XLA Ops:
  0.6 1.6 %shard_map.50 = (f32[3,1024,128]{2,1,0:T(8,128)S(1)}, f32[1024,128]{1,0:T(8,128)S(1)}, f32[512,128]{1,0:T(8,128)S(1)}, f32[832,128]{1,0:T(8,128)S(1)}, f32[832,128]{1,0:T(8,128)S(1)}) custom-call(f32[3,1024,128]{2,1,0:T(8,128)} %bitcast.5, f32[1024,128]{1,0:T(8,128)} %bitcast.6, f32[512,128]{1,0:T(8,128)} %bitcast.8), custom_call_target="tpu_custom_call" | custom-call | flops 2000000 | bytes 4000000 | tf_op jit(solution)/shard_map/pallas_call | solution.py:624
  2.3 4.6 %collective-permute-start = (f32[832,128]{1,0:T(8,128)S(1)}, f32[832,128]{1,0:T(8,128)S(1)}, u32[]{:S(2)}, u32[]{:S(2)}) collective-permute-start(f32[832,128]{1,0:T(8,128)S(1)} %get-tuple-element.53), channel_id=1, source_target_pairs={{0,7},{1,2},{2,1},{3,4},{4,3},{5,6},{6,5},{7,0},{8,15},{9,10},{10,... | collective-permute-start | bytes 1277960 | tf_op jit(solution)/shard_map/ppermute | solution.py:641
  6.8 0.0 collective-permute-start.1
  6.8 0.7 %shard_map.51 = (f32[3,8,128,128]{3,2,1,0:T(8,128)S(1)}, f32[8,128,128]{2,1,0:T(8,128)S(1)}, f32[8,128,128]{2,1,0:T(8,128)S(1)}, f32[8,24,128]{2,1,0:T(8,128)S(1)}, f32[8,24,128]{2,1,0:T(8,128)S(1)}) custom-call(f32[3,1024,128]{2,1,0:T(8,128)S(1)} %get-tuple-element.49.conc_in, f32[1024,128]{1,0:T(8,128)S(1)} %get-tuple-element.50.adj_in, ...), custom_call_target="tpu_custom_call" | custom-call | flops 1000000 | bytes 2000000 | tf_op jit(solution)/shard_map/pallas_call | solution.py:624
  7.6 2.5 %collective-permute-start.2 = (f32[8,24,128]{2,1,0:T(8,128)S(1)}, f32[8,24,128]{2,1,0:T(8,128)S(1)}, u32[]{:S(2)}, u32[]{:S(2)}) collective-permute-start(f32[8,24,128]{2,1,0:T(8,128)S(1)} %get-tuple-element.55), channel_id=1, source_target_pairs={{0,24},{8,16},{16,8},{24,0},{1,25},{9,17},{17,9},{25,1},{2,26},{10... | collective-permute-start | bytes 294920 | tf_op jit(solution)/shard_map/ppermute | solution.py:641
  10.1 0.5 %collective-permute-start.3 = (f32[8,24,128]{2,1,0:T(8,128)S(1)}, f32[8,24,128]{2,1,0:T(8,128)S(1)}, u32[]{:S(2)}, u32[]{:S(2)}) collective-permute-start(f32[8,24,128]{2,1,0:T(8,128)S(1)} %get-tuple-element.56), channel_id=1, source_target_pairs={{0,8},{8,0},{16,24},{24,16},{1,9},{9,1},{17,25},{25,17},{2,10},{10... | collective-permute-start | bytes 294920 | tf_op jit(solution)/shard_map/ppermute | solution.py:641
  10.6 3.5 %collective-permute-done.2.got_a = f32[8,24,128]{2,1,0:T(8,128)S(1)} collective-permute-done((f32[8,24,128]{2,1,0:T(8,128)S(1)}, f32[8,24,128]{2,1,0:T(8,128)S(1)}, u32[]{:S(2)}, u32[]{:S(2)}) %collective-permute-start.2) | collective-permute-done | bytes 98336 | tf_op jit(solution)/shard_map/ppermute | solution.py:641
  14.1 1.8 %collective-permute-done.3.got_b = f32[8,24,128]{2,1,0:T(8,128)S(1)} collective-permute-done((f32[8,24,128]{2,1,0:T(8,128)S(1)}, f32[8,24,128]{2,1,0:T(8,128)S(1)}, u32[]{:S(2)}, u32[]{:S(2)}) %collective-permute-start.3) | collective-permute-done | bytes 98336 | tf_op jit(solution)/shard_map/ppermute | solution.py:641
  16.0 0.1 collective-permute-start.4
  16.0 0.1 collective-permute-start.5
  16.1 3.1 %shard_map.55 = (f32[8,160,128]{2,1,0:T(8,128)S(1)}, f32[8,160,128]{2,1,0:T(8,128)S(1)}, f32[8,160,128]{2,1,0:T(8,128)S(1)}, f32[6,160,128]{2,1,0:T(8,128)S(1)},...) custom-call(f32[3,8,128,128]{3,2,1,0:T(8,128)S(1)} %get-tuple-elemen, ...), custom_call_target="tpu_custom_call" | custom-call | flops 3000000 | bytes 6000000 | tf_op jit(solution)/shard_map/pallas_call | solution.py:624
  19.2 2.2 %collective-permute-done.4.corner_a = f32[2,2,24,128]{3,2,1,0:T(8,128)S(1)} collective-permute-done((f32[2,2,24,128]{3,2,1,0:T(8,128)S(1)}, f32[2,2,24,128]{3,2,1,0:T(8,128)S(1)}, u32[]{:S(2)}, u32[]{:S(2)}) %collective-permute-start.4) | collective-permute-done | bytes 49184 | tf_op jit(solution)/shard_map/ppermute | solution.py:641
  21.3 0.0 collective-permute-done.5.corner_b
  21.3 0.0 collective-permute-done.from_a
  21.3 0.0 collective-permute-done.1.from_b
  21.4 2.8 %shard_map.56 = (f32[2,2,160,128]{3,2,1,0:T(8,128)S(1)}, f32[2,2,160,128]{3,2,1,0:T(8,128)S(1)}, f32[2,136,128]{2,1,0:T(8,128)S(1)}, f32[2,136,128]{2,1,0:T(8,128)S(1)}) custom-call(f32[8,160,128]{2,1,0:T(8,128)S(1)} %get-tuple-element.75.conc_in, f32[8,160,128]{2,1,0:T(8,128)S(1)} %get-tuple-element.76.adj_in, ...), custom_call_target="tpu_custom_call" | custom-call | flops 2000000 | bytes 4000000 | tf_op jit(solution)/shard_map/pallas_call | solution.py:624
  24.2 1.4 %collective-permute-start.8 = (f32[2,136,128]{2,1,0:T(8,128)S(1)}, f32[2,136,128]{2,1,0:T(8,128)S(1)}, u32[]{:S(2)}, u32[]{:S(2)}) collective-permute-start(f32[2,136,128]{2,1,0:T(8,128)S(1)} %get-tuple-element.86), channel_id=1, source_target_pairs={{0,7},{1,2},{2,1},{3,4},{4,3},{5,6},{6,5},{7,0},{8,15},{9,10},{10,... | collective-permute-start | bytes 417800 | tf_op jit(solution)/shard_map/ppermute | solution.py:641
  25.6 0.0 collective-permute-start.9
  25.6 1.9 %shard_map.53 = (f32[12,160,128]{2,1,0:T(8,128)S(1)}, f32[10,160,128]{2,1,0:T(8,128)S(1)}, f32[10,160,128]{2,1,0:T(8,128)S(1)}, f32[10,160,128]{2,1,0:T(8,128)S(...) custom-call(f32[3,8,128,128]{3,2,1,0:T(8,128)S(1)} %get-tuple-element.52.conc_own, ...), custom_call_target="tpu_custom_call" | custom-call | flops 2000000 | bytes 4000000 | tf_op jit(solution)/shard_map/pallas_call | solution.py:624
  27.5 2.3 %collective-permute-start.6 = (f32[280,128]{1,0:T(8,128)S(1)}, f32[280,128]{1,0:T(8,128)S(1)}, u32[]{:S(2)}, u32[]{:S(2)}) collective-permute-start(f32[280,128]{1,0:T(8,128)S(1)} %get-tuple-element.61), channel_id=1, source_target_pairs={{0,7},{1,2},{2,1},{3,4},{4,3},{5,6},{6,5},{7,0},{8,15},{9,10},{10,... | collective-permute-start | bytes 430088 | tf_op jit(solution)/shard_map/ppermute | solution.py:641
  29.8 0.0 collective-permute-start.7
  29.8 3.2 %shard_map.57 = (f32[8,160,128]{2,1,0:T(8,128)S(1)}, f32[8,160,128]{2,1,0:T(8,128)S(1)}) custom-call(f32[12,160,128]{2,1,0:T(8,128)S(1)} %get-tuple-element.70.mob, f32[10,160,128]{2,1,0:T(8,128)S(1)} %get-tuple-element.71.chem, f32[10,160,128]{2,1,0:T(8,128)S(1)} %get-tuple-element.72.curve, f32[10,160,128]{2,1,0:T(8,128)S(1)} %get-tuple-element.73.swing, ...), custom_call_target="tpu_custom_call" | custom-call | flops 3000000 | bytes 6000000 | tf_op jit(solution)/shard_map/pallas_call | solution.py:624
  33.0 0.0 collective-permute-done.8.from_a
  33.0 0.0 collective-permute-done.9.from_b
  33.0 0.5 %shard_map.58 = (f32[2,2,160,128]{3,2,1,0:T(8,128)S(1)}, f32[2,136,128]{2,1,0:T(8,128)S(1)}, f32[2,136,128]{2,1,0:T(8,128)S(1)}) custom-call(f32[12,160,128]{2,1,0:T(8,128)S(1)} %get-tuple-element.70.mob, f32[10,160,128]{2,1,0:T(8,128)S(1)} %get-tuple-element.71.chem, f32[10,160,128]{2,1,0:T(8,128)S(1)} %get-tuple-element.72.curve, ...), custom_call_target="tpu_custom_call" | custom-call | flops 1000000 | bytes 2000000 | tf_op jit(solution)/shard_map/pallas_call | solution.py:624
  33.5 1.4 %collective-permute-start.10 = (f32[2,136,128]{2,1,0:T(8,128)S(1)}, f32[2,136,128]{2,1,0:T(8,128)S(1)}, u32[]{:S(2)}, u32[]{:S(2)}) collective-permute-start(f32[2,136,128]{2,1,0:T(8,128)S(1)} %get-tuple-element.92), channel_id=1, source_target_pairs={{0,7},{1,2},{2,1},{3,4},{4,3},{5,6},{6,5},{7,0},{8,15},{9,10},{10,... | collective-permute-start | bytes 417800 | tf_op jit(solution)/shard_map/ppermute | solution.py:641
  34.9 0.0 collective-permute-start.11
  34.9 0.0 collective-permute-done.6.from_a
  34.9 0.0 collective-permute-done.7.from_b
  34.9 1.9 %shard_map.54 = (f32[12,160,128]{2,1,0:T(8,128)S(1)}, f32[10,160,128]{2,1,0:T(8,128)S(1)}, f32[10,160,128]{2,1,0:T(8,128)S(1)}, f32[10,160,128]{2,1,0:T(8,128)S(1)}) custom-call(f32[3,8,128,128]{3,2,1,0:T(8,128)S(1)} %get-tuple-element.52.conc_own, f32[280,128]{1,0:T(8,128)S(1)} %collective-permute-done.6.from_a, ...), custom_call_target="tpu_custom_call" | custom-call | flops 2000000 | bytes 4000000 | tf_op jit(solution)/shard_map/pallas_call | solution.py:624
  36.8 3.9 %shard_map.59 = (f32[8,160,128]{2,1,0:T(8,128)S(1)}, f32[1024,128]{1,0:T(8,128)S(1)}, f32[512,128]{1,0:T(8,128)}) custom-call(f32[12,160,128]{2,1,0:T(8,128)S(1)} %get-tuple-element.63.mob, f32[10,160,128]{2,1,0:T(8,128)S(1)} %get-tuple-element.64.chem, f32[10,160,128]{2,1,0:T(8,128)S(1)} %get-tuple-element.65.curve, ...), custom_call_target="tpu_custom_call" | custom-call | flops 3000000 | bytes 6000000 | tf_op jit(solution)/shard_map/pallas_call | solution.py:624
  40.7 0.0 collective-permute-done.10.from_a
  40.7 0.0 collective-permute-done.11.from_b
  40.7 1.1 %shard_map.60 = f32[1024,128]{1,0:T(8,128)} custom-call(f32[12,160,128]{2,1,0:T(8,128)S(1)} %get-tuple-element.63.mob, f32[10,160,128]{2,1,0:T(8,128)S(1)} %get-tuple-element.64.chem, f32[10,160,128]{2,1,0:T(8,128)S(1)} %get-tuple-element.65.curve, f32[10,160,128]{2,1,0:T(8,128)S(1)} %get-tuple-element.66.swing, ...), custom_call_target="tpu_custom_call" | custom-call | flops 1000000 | bytes 2000000 | tf_op jit(solution)/shard_map/pallas_call | solution.py:624
  (1 shorter events, 0.0 us)
Async XLA Ops:
  2.3 19.1 %collective-permute-start = (f32[832,128]{1,0:T(8,128)S(1)}, f32[832,128]{1,0:T(8,128)S(1)}, u32[]{:S(2)}, u32[]{:S(2)}) collective-permute-start(f32[832,128]{1,0:T(8,128)S(1)} %get-tuple-element.53), channel_id=1, source_target_pairs={{0,7},{1,2},{2,1},{3,4},{4,3},{5,6},{6,5},{7,0},{8,15},{9,10},{10,... | collective-permute-start | bytes 1277960 | tf_op jit(solution)/shard_map/ppermute | solution.py:641
  6.8 14.5 %collective-permute-start.1 = (f32[832,128]{1,0:T(8,128)S(1)}, f32[832,128]{1,0:T(8,128)S(1)}, u32[]{:S(2)}, u32[]{:S(2)}) collective-permute-start(f32[832,128]{1,0:T(8,128)S(1)} %get-tuple-element.54), channel_id=1, source_target_pairs={{0,1},{1,0},{2,3},{3,2},{4,5},{5,4},{6,7},{7,6},{8,9},{9,8},{10,11... | collective-permute-start | bytes 1277960 | tf_op jit(solution)/shard_map/ppermute | solution.py:641
  7.6 6.6 %collective-permute-start.2 = (f32[8,24,128]{2,1,0:T(8,128)S(1)}, f32[8,24,128]{2,1,0:T(8,128)S(1)}, u32[]{:S(2)}, u32[]{:S(2)}) collective-permute-start(f32[8,24,128]{2,1,0:T(8,128)S(1)} %get-tuple-element.55), channel_id=1, source_target_pairs={{0,24},{8,16},{16,8},{24,0},{1,25},{9,17},{17,9},{25,1},{2,26},{10... | collective-permute-start | bytes 294920 | tf_op jit(solution)/shard_map/ppermute | solution.py:641
  10.1 5.8 %collective-permute-start.3 = (f32[8,24,128]{2,1,0:T(8,128)S(1)}, f32[8,24,128]{2,1,0:T(8,128)S(1)}, u32[]{:S(2)}, u32[]{:S(2)}) collective-permute-start(f32[8,24,128]{2,1,0:T(8,128)S(1)} %get-tuple-element.56), channel_id=1, source_target_pairs={{0,8},{8,0},{16,24},{24,16},{1,9},{9,1},{17,25},{25,17},{2,10},{10... | collective-permute-start | bytes 294920 | tf_op jit(solution)/shard_map/ppermute | solution.py:641
  16.0 5.4 %collective-permute-start.4 = (f32[2,2,24,128]{3,2,1,0:T(8,128)S(1)}, f32[2,2,24,128]{3,2,1,0:T(8,128)S(1)}, u32[]{:S(2)}, u32[]{:S(2)}) collective-permute-start(f32[2,2,24,128]{3,2,1,0:T(8,128)S(1)} %get-tuple-element.59), channel_id=1, source_target_pairs={{0,7},{1,2},{2,1},{3,4},{4,3},{5,6},{6,5},{7,0},{8,15},{9,10},{10,... | collective-permute-start | bytes 147464 | tf_op jit(solution)/shard_map/ppermute | solution.py:641
  16.0 5.3 %collective-permute-start.5 = (f32[2,2,24,128]{3,2,1,0:T(8,128)S(1)}, f32[2,2,24,128]{3,2,1,0:T(8,128)S(1)}, u32[]{:S(2)}, u32[]{:S(2)}) collective-permute-start(f32[2,2,24,128]{3,2,1,0:T(8,128)S(1)} %get-tuple-element.60), channel_id=1, source_target_pairs={{0,1},{1,0},{2,3},{3,2},{4,5},{5,4},{6,7},{7,6},{8,9},{9,8},{10,11... | collective-permute-start | bytes 147464 | tf_op jit(solution)/shard_map/ppermute | solution.py:641
  24.2 8.8 %collective-permute-start.8 = (f32[2,136,128]{2,1,0:T(8,128)S(1)}, f32[2,136,128]{2,1,0:T(8,128)S(1)}, u32[]{:S(2)}, u32[]{:S(2)}) collective-permute-start(f32[2,136,128]{2,1,0:T(8,128)S(1)} %get-tuple-element.86), channel_id=1, source_target_pairs={{0,7},{1,2},{2,1},{3,4},{4,3},{5,6},{6,5},{7,0},{8,15},{9,10},{10,... | collective-permute-start | bytes 417800 | tf_op jit(solution)/shard_map/ppermute | solution.py:641
  25.6 7.5 %collective-permute-start.9 = (f32[2,136,128]{2,1,0:T(8,128)S(1)}, f32[2,136,128]{2,1,0:T(8,128)S(1)}, u32[]{:S(2)}, u32[]{:S(2)}) collective-permute-start(f32[2,136,128]{2,1,0:T(8,128)S(1)} %get-tuple-element.87), channel_id=1, source_target_pairs={{0,1},{1,0},{2,3},{3,2},{4,5},{5,4},{6,7},{7,6},{8,9},{9,8},{10,11... | collective-permute-start | bytes 417800 | tf_op jit(solution)/shard_map/ppermute | solution.py:641
  27.5 7.4 %collective-permute-start.6 = (f32[280,128]{1,0:T(8,128)S(1)}, f32[280,128]{1,0:T(8,128)S(1)}, u32[]{:S(2)}, u32[]{:S(2)}) collective-permute-start(f32[280,128]{1,0:T(8,128)S(1)} %get-tuple-element.61), channel_id=1, source_target_pairs={{0,7},{1,2},{2,1},{3,4},{4,3},{5,6},{6,5},{7,0},{8,15},{9,10},{10,... | collective-permute-start | bytes 430088 | tf_op jit(solution)/shard_map/ppermute | solution.py:641
  29.8 5.1 %collective-permute-start.7 = (f32[280,128]{1,0:T(8,128)S(1)}, f32[280,128]{1,0:T(8,128)S(1)}, u32[]{:S(2)}, u32[]{:S(2)}) collective-permute-start(f32[280,128]{1,0:T(8,128)S(1)} %get-tuple-element.62), channel_id=1, source_target_pairs={{0,1},{1,0},{2,3},{3,2},{4,5},{5,4},{6,7},{7,6},{8,9},{9,8},{10,11... | collective-permute-start | bytes 430088 | tf_op jit(solution)/shard_map/ppermute | solution.py:641
  33.5 7.2 %collective-permute-start.10 = (f32[2,136,128]{2,1,0:T(8,128)S(1)}, f32[2,136,128]{2,1,0:T(8,128)S(1)}, u32[]{:S(2)}, u32[]{:S(2)}) collective-permute-start(f32[2,136,128]{2,1,0:T(8,128)S(1)} %get-tuple-element.92), channel_id=1, source_target_pairs={{0,7},{1,2},{2,1},{3,4},{4,3},{5,6},{6,5},{7,0},{8,15},{9,10},{10,... | collective-permute-start | bytes 417800 | tf_op jit(solution)/shard_map/ppermute | solution.py:641
  34.9 5.8 %collective-permute-start.11 = (f32[2,136,128]{2,1,0:T(8,128)S(1)}, f32[2,136,128]{2,1,0:T(8,128)S(1)}, u32[]{:S(2)}, u32[]{:S(2)}) collective-permute-start(f32[2,136,128]{2,1,0:T(8,128)S(1)} %get-tuple-element.93), channel_id=1, source_target_pairs={{0,1},{1,0},{2,3},{3,2},{4,5},{5,4},{6,7},{7,6},{8,9},{9,8},{10,11... | collective-permute-start | bytes 417800 | tf_op jit(solution)/shard_map/ppermute | solution.py:641

commit v10 on v7

--- a/solution.py
+++ b/solution.py
@@ -16,6 +16,7 @@
 pad = 16
 chunk = 72
 depth = 2
+first_pair = {"gx": 0, "gy": 1}
 vmem_limit = 20 * 1024 * 1024
 f32 = jnp.float32
 
@@ -233,20 +234,20 @@
     lax.fori_loop(0, 4, close, 0)
 
 
-def is_odd(axis):
-    return lax.rem(lax.axis_index(axis), 2) == 1
+def a_is_next(axis):
+    return lax.rem(lax.axis_index(axis), 2) == first_pair[axis]
 
 
 def bases(rows):
-    odd = is_odd("gy")
+    to_next = a_is_next("gy")
     top = rows - depth
-    return jnp.where(odd, top, 0), jnp.where(odd, 0, top)
+    return jnp.where(to_next, top, 0), jnp.where(to_next, 0, top)
 
 
 def landings(rows):
-    odd = is_odd("gy")
+    to_next = a_is_next("gy")
     top = rows + depth
-    return jnp.where(odd, top, 0), jnp.where(odd, 0, top)
+    return jnp.where(to_next, top, 0), jnp.where(to_next, 0, top)
 
 
 def sides_of(rows):
@@ -296,13 +297,13 @@
                 x_a, x_b):
     places, total = slots(steps)
     lanes = adj_out.shape[2]
-    odd_x = is_odd("gx")
+    next_x = a_is_next("gx")
 
     def to_x(y, value, place):
         start, width = place
         last, first = value[cols - width :, :], value[:width, :]
-        x_a[y, start : start + width, :] = jnp.where(odd_x, last, first)
-        x_b[y, start : start + width, :] = jnp.where(odd_x, first, last)
+        x_a[y, start : start + width, :] = jnp.where(next_x, last, first)
+        x_b[y, start : start + width, :] = jnp.where(next_x, first, last)
 
     used = sum(places[-1])
     for y in range(rows):
@@ -338,9 +339,9 @@
 
 
 def corner_kernel(rows, got_a, got_b, x_low, x_high, corner_a, corner_b):
-    odd_x = is_odd("gx")
-    x_low[...] = jnp.where(odd_x, got_b[...], got_a[...])
-    x_high[...] = jnp.where(odd_x, got_a[...], got_b[...])
+    next_x = a_is_next("gx")
+    x_low[...] = jnp.where(next_x, got_b[...], got_a[...])
+    x_high[...] = jnp.where(next_x, got_a[...], got_b[...])
     for out, base in zip((corner_a, corner_b), bases(rows)):
         for at in range(depth):
             out[0, at] = x_low[base + at]
@@ -400,8 +401,8 @@
             open_g[s, at - low : at - low + size, :] = (
                 flow - rate[s * (rows - 1), at : at + size, :] * a
             )
-    odd = is_odd("gy")
-    for to, side in ((to_a, jnp.where(odd, 1, 0)), (to_b, jnp.where(odd, 0, 1))):
+    to_next = a_is_next("gy")
+    for to, side in ((to_a, jnp.where(to_next, 1, 0)), (to_b, jnp.where(to_next, 0, 1))):
         to[0] = out[side, 0, first:last, :]
         to[1] = open_g[side, first - low : last - low, :]
 
@@ -568,8 +569,8 @@
     first, last = sent(cols)
     lanes = mob.shape[2]
     mask = face_mask(lanes, nz)
-    odd = is_odd("gy")
-    for got, side in ((from_a, jnp.where(odd, 1, 0)), (from_b, jnp.where(odd, 0, 1))):
+    to_next = a_is_next("gy")
+    for got, side in ((from_a, jnp.where(to_next, 1, 0)), (from_b, jnp.where(to_next, 0, 1))):
         for k in range(2):
             halo[side, k, first:last, :] = got[k]
     for s in range(2):
@@ -623,9 +624,9 @@
 
 
 def swap(value_a, value_b, axis):
-    count = lax.axis_size(axis)
-    pairs_a = [(i, (i - 1 + 2 * (i % 2)) % count) for i in range(count)]
-    pairs_b = [(i, i + 1 - 2 * (i % 2)) for i in range(count)]
+    count, start = lax.axis_size(axis), first_pair[axis]
+    pairs_a = [(i, (i + 1 - 2 * ((i + start) % 2)) % count) for i in range(count)]
+    pairs_b = [(i, (i - 1 + 2 * ((i + start) % 2)) % count) for i in range(count)]
     return lax.ppermute(value_a, axis, pairs_a), lax.ppermute(value_b, axis, pairs_b)
 
 

time: 40.5 us -> 40.5 us (level)
    ppermute x5, waiting for transfers between devices: 1.79 us -> 3.07 us  [swap(): lax.ppermute(value_b, axis, pairs_b)]
    ppermute x5, waiting for transfers between devices: 5.93 us -> 4.64 us  [swap(): lax.ppermute(value_a, axis, pairs_a)]
    ppermute x5, starting transfers between devices: 10.6 us -> 9.62 us  [swap(): lax.ppermute(value_a, axis, pairs_a)]
    ppermute x5, starting transfers between devices: 0.61 us -> 1.57 us  [swap(): lax.ppermute(value_b, axis, pairs_b)]
where the time goes in v10:
time: 40.5 us; the launch traced here: 40.3 us
  Pallas kernels  20.7 us (51%)
  starting transfers between devices  11.2 us (28%)
  waiting for transfers between devices  7.72 us (19%)
  between operations  0.71 us (2%)
    pallas_call x11, Pallas kernels, call(): pl.pallas_call(kernel, out_shape=[jax.ShapeDtypeStruct(shape, f32) for sh...  20.7 us
    ppermute x5, starting transfers between devices, swap(): lax.ppermute(value_a, axis, pairs_a)  9.62 us
    ppermute x5, waiting for transfers between devices, swap(): lax.ppermute(value_a, axis, pairs_a)  4.64 us
    ppermute x5, waiting for transfers between devices, swap(): lax.ppermute(value_b, axis, pairs_b)  3.07 us
    ppermute x5, starting transfers between devices, swap(): lax.ppermute(value_b, axis, pairs_b)  1.57 us
  transfers between devices with their start and end apart: 10, of which 4 were waited for; matrix products, arithmetic and copies ran while one was open for 0% of the time, Pallas kernels for 36%

profile of v10, /device:TPU:0, one launch (start us, length us, event | category | flops | bytes accessed | tf_op | source)
XLA Modules:
  0.0 40.3 jit_solution(11574066016612823447)
XLA Ops:
  0.6 1.8 %shard_map.50 = (f32[3,1024,128]{2,1,0:T(8,128)S(1)}, f32[1024,128]{1,0:T(8,128)S(1)}, f32[512,128]{1,0:T(8,128)S(1)}, f32[1088,128]{1,0:T(8,128)S(1)}, f32[1088,128]{1,0:T(8,128)S(1)}) custom-call(f32[3,1024,128]{2,1,0:T(8,128)} %bitcast.5, f32[1024,128]{1,0:T(8,128)} %bitcast.6, f32[512,128]{1,0:T(8,128)} %bitcast.8), custom_call_target="tpu_custom_call" | custom-call | flops 2000000 | bytes 4000000 | tf_op jit(solution)/shard_map/pallas_call | solution.py:613
  2.4 4.6 %collective-permute-start = (f32[1088,128]{1,0:T(8,128)S(1)}, f32[1088,128]{1,0:T(8,128)S(1)}, u32[]{:S(2)}, u32[]{:S(2)}) collective-permute-start(f32[1088,128]{1,0:T(8,128)S(1)} %get-tuple-element.51), channel_id=1, source_target_pairs={{0,7},{1,2},{2,1},{3,4},{4,3},{5,6},{6,5},{7,0},{8,15},{9,10},{10,... | collective-permute-start | bytes 1671176 | tf_op jit(solution)/shard_map/ppermute | solution.py:630
  7.0 0.0 collective-permute-start.1
  7.0 0.7 %shard_map.51 = (f32[3,8,128,128]{3,2,1,0:T(8,128)S(1)}, f32[8,128,128]{2,1,0:T(8,128)S(1)}, f32[8,128,128]{2,1,0:T(8,128)S(1)}, f32[8,24,128]{2,1,0:T(8,128)S(1)}, f32[8,24,128]{2,1,0:T(8,128)S(1)}) custom-call(f32[3,1024,128]{2,1,0:T(8,128)S(1)} %get-tuple-element.47.conc_in, f32[1024,128]{1,0:T(8,128)S(1)} %get-tuple-element.48.adj_in, ...), custom_call_target="tpu_custom_call" | custom-call | flops 1000000 | bytes 2000000 | tf_op jit(solution)/shard_map/pallas_call | solution.py:613
  7.7 1.6 %collective-permute-start.2 = (f32[8,24,128]{2,1,0:T(8,128)S(1)}, f32[8,24,128]{2,1,0:T(8,128)S(1)}, u32[]{:S(2)}, u32[]{:S(2)}) collective-permute-start(f32[8,24,128]{2,1,0:T(8,128)S(1)} %get-tuple-element.53), channel_id=1, source_target_pairs={{0,8},{8,0},{16,24},{24,16},{1,9},{9,1},{17,25},{25,17},{2,10},{10... | collective-permute-start | bytes 294920 | tf_op jit(solution)/shard_map/ppermute | solution.py:630
  9.3 1.5 %collective-permute-start.3 = (f32[8,24,128]{2,1,0:T(8,128)S(1)}, f32[8,24,128]{2,1,0:T(8,128)S(1)}, u32[]{:S(2)}, u32[]{:S(2)}) collective-permute-start(f32[8,24,128]{2,1,0:T(8,128)S(1)} %get-tuple-element.54), channel_id=1, source_target_pairs={{0,24},{8,16},{16,8},{24,0},{1,25},{9,17},{17,9},{25,1},{2,26},{10... | collective-permute-start | bytes 294920 | tf_op jit(solution)/shard_map/ppermute | solution.py:630
  10.8 2.2 %collective-permute-done.2.got_a = f32[8,24,128]{2,1,0:T(8,128)S(1)} collective-permute-done((f32[8,24,128]{2,1,0:T(8,128)S(1)}, f32[8,24,128]{2,1,0:T(8,128)S(1)}, u32[]{:S(2)}, u32[]{:S(2)}) %collective-permute-start.2) | collective-permute-done | bytes 98336 | tf_op jit(solution)/shard_map/ppermute | solution.py:630
  13.0 3.1 %collective-permute-done.3.got_b = f32[8,24,128]{2,1,0:T(8,128)S(1)} collective-permute-done((f32[8,24,128]{2,1,0:T(8,128)S(1)}, f32[8,24,128]{2,1,0:T(8,128)S(1)}, u32[]{:S(2)}, u32[]{:S(2)}) %collective-permute-start.3) | collective-permute-done | bytes 98336 | tf_op jit(solution)/shard_map/ppermute | solution.py:630
  16.1 0.1 collective-permute-start.4
  16.2 0.1 collective-permute-start.5
  16.3 3.1 %shard_map.54 = (f32[8,160,128]{2,1,0:T(8,128)S(1)}, f32[8,160,128]{2,1,0:T(8,128)S(1)}, f32[8,160,128]{2,1,0:T(8,128)S(1)}, f32[6,160,128]{2,1,0:T(8,128)S(1)},...) custom-call(f32[3,8,128,128]{3,2,1,0:T(8,128)S(1)} %get-tuple-elemen, ...), custom_call_target="tpu_custom_call" | custom-call | flops 3000000 | bytes 6000000 | tf_op jit(solution)/shard_map/pallas_call | solution.py:613
  19.3 2.2 %collective-permute-done.4.corner_a = f32[2,2,24,128]{3,2,1,0:T(8,128)S(1)} collective-permute-done((f32[2,2,24,128]{3,2,1,0:T(8,128)S(1)}, f32[2,2,24,128]{3,2,1,0:T(8,128)S(1)}, u32[]{:S(2)}, u32[]{:S(2)}) %collective-permute-start.4) | collective-permute-done | bytes 49184 | tf_op jit(solution)/shard_map/ppermute | solution.py:630
  21.5 0.0 collective-permute-done.5.corner_b
  21.5 0.0 collective-permute-done.from_a
  21.5 0.0 collective-permute-done.1.from_b
  21.5 2.8 %shard_map.56 = (f32[2,2,160,128]{3,2,1,0:T(8,128)S(1)}, f32[2,2,160,128]{3,2,1,0:T(8,128)S(1)}, f32[2,136,128]{2,1,0:T(8,128)S(1)}, f32[2,136,128]{2,1,0:T(8,128)S(1)}) custom-call(f32[8,160,128]{2,1,0:T(8,128)S(1)} %get-tuple-element.71.conc_in, f32[8,160,128]{2,1,0:T(8,128)S(1)} %get-tuple-element.72.adj_in, ...), custom_call_target="tpu_custom_call" | custom-call | flops 2000000 | bytes 4000000 | tf_op jit(solution)/shard_map/pallas_call | solution.py:613
  24.3 1.4 %collective-permute-start.6 = (f32[2,136,128]{2,1,0:T(8,128)S(1)}, f32[2,136,128]{2,1,0:T(8,128)S(1)}, u32[]{:S(2)}, u32[]{:S(2)}) collective-permute-start(f32[2,136,128]{2,1,0:T(8,128)S(1)} %get-tuple-element.82), channel_id=1, source_target_pairs={{0,7},{1,2},{2,1},{3,4},{4,3},{5,6},{6,5},{7,0},{8,15},{9,10},{10,... | collective-permute-start | bytes 417800 | tf_op jit(solution)/shard_map/ppermute | solution.py:630
  25.7 0.0 collective-permute-start.7
  25.7 1.9 %shard_map.55 = (f32[12,160,128]{2,1,0:T(8,128)S(1)}, f32[10,160,128]{2,1,0:T(8,128)S(1)}, f32[10,160,128]{2,1,0:T(8,128)S(1)}, f32[10,160,128]{2,1,0:T(8,128)S(1)}, f32[2,2,160,128]{3,2,1,0:T(8,128)S(1)}) custom-call(f32[3,8,128,128]{3,2,1,0:T(8,128)S(1)} %get-tuple-element.50.conc_own, f32[1088,128]{1,0:T(8,128)S(1)} %collective-permute-done.from_a, ...), custom_call_target="tpu_custom_call" | custom-call | flops 2000000 | bytes 4000000 | tf_op jit(solution)/shard_map/pallas_call | solution.py:613
  27.6 3.1 %shard_map.57 = (f32[8,160,128]{2,1,0:T(8,128)S(1)}, f32[8,160,128]{2,1,0:T(8,128)S(1)}) custom-call(f32[12,160,128]{2,1,0:T(8,128)S(1)} %get-tuple-element.66.mob, f32[10,160,128]{2,1,0:T(8,128)S(1)} %get-tuple-element.67.chem, f32[10,160,128]{2,1,0:T(8,128)S(1)} %get-tuple-element.68.curve, f32[10,160,128]{2,1,0:T(8,128)S(1)} %get-tuple-element.69.swing, ...), custom_call_target="tpu_custom_call" | custom-call | flops 3000000 | bytes 6000000 | tf_op jit(solution)/shard_map/pallas_call | solution.py:613
  30.7 0.3 collective-permute-done.6.from_a
  31.0 0.0 collective-permute-done.7.from_b
  31.0 0.4 shard_map.58
  31.4 2.0 %collective-permute-start.8 = (f32[2,136,128]{2,1,0:T(8,128)S(1)}, f32[2,136,128]{2,1,0:T(8,128)S(1)}, u32[]{:S(2)}, u32[]{:S(2)}) collective-permute-start(f32[2,136,128]{2,1,0:T(8,128)S(1)} %get-tuple-element.88), channel_id=1, source_target_pairs={{0,7},{1,2},{2,1},{3,4},{4,3},{5,6},{6,5},{7,0},{8,15},{9,10},{10,... | collective-permute-start | bytes 417800 | tf_op jit(solution)/shard_map/ppermute | solution.py:630
  33.4 0.0 collective-permute-start.9
  33.4 1.8 %shard_map.53 = (f32[12,160,128]{2,1,0:T(8,128)S(1)}, f32[10,160,128]{2,1,0:T(8,128)S(1)}, f32[10,160,128]{2,1,0:T(8,128)S(1)}, f32[10,160,128]{2,1,0:T(8,128)S(1)}) custom-call(f32[3,8,128,128]{3,2,1,0:T(8,128)S(1)} %get-tuple-element.50.conc_own, f32[1088,128]{1,0:T(8,128)S(1)} %collective-permute-done.from_a, ...), custom_call_target="tpu_custom_call" | custom-call | flops 2000000 | bytes 4000000 | tf_op jit(solution)/shard_map/pallas_call | solution.py:613
  35.2 3.9 %shard_map.59 = (f32[8,160,128]{2,1,0:T(8,128)S(1)}, f32[1024,128]{1,0:T(8,128)S(1)}, f32[512,128]{1,0:T(8,128)}) custom-call(f32[12,160,128]{2,1,0:T(8,128)S(1)} %get-tuple-element.59.mob, f32[10,160,128]{2,1,0:T(8,128)S(1)} %get-tuple-element.60.chem, f32[10,160,128]{2,1,0:T(8,128)S(1)} %get-tuple-element.61.curve, ...), custom_call_target="tpu_custom_call" | custom-call | flops 3000000 | bytes 6000000 | tf_op jit(solution)/shard_map/pallas_call | solution.py:613
  39.2 0.0 collective-permute-done.8.from_a
  39.2 0.0 collective-permute-done.9.from_b
  39.2 1.1 %shard_map.60 = f32[1024,128]{1,0:T(8,128)} custom-call(f32[12,160,128]{2,1,0:T(8,128)S(1)} %get-tuple-element.59.mob, f32[10,160,128]{2,1,0:T(8,128)S(1)} %get-tuple-element.60.chem, f32[10,160,128]{2,1,0:T(8,128)S(1)} %get-tuple-element.61.curve, f32[10,160,128]{2,1,0:T(8,128)S(1)} %get-tuple-element.62.swing, ...), custom_call_target="tpu_custom_call" | custom-call | flops 1000000 | bytes 2000000 | tf_op jit(solution)/shard_map/pallas_call | solution.py:613
  (1 shorter events, 0.0 us)
Async XLA Ops:
  2.4 19.1 %collective-permute-start = (f32[1088,128]{1,0:T(8,128)S(1)}, f32[1088,128]{1,0:T(8,128)S(1)}, u32[]{:S(2)}, u32[]{:S(2)}) collective-permute-start(f32[1088,128]{1,0:T(8,128)S(1)} %get-tuple-element.51), channel_id=1, source_target_pairs={{0,7},{1,2},{2,1},{3,4},{4,3},{5,6},{6,5},{7,0},{8,15},{9,10},{10,... | collective-permute-start | bytes 1671176 | tf_op jit(solution)/shard_map/ppermute | solution.py:630
  7.0 14.5 %collective-permute-start.1 = (f32[1088,128]{1,0:T(8,128)S(1)}, f32[1088,128]{1,0:T(8,128)S(1)}, u32[]{:S(2)}, u32[]{:S(2)}) collective-permute-start(f32[1088,128]{1,0:T(8,128)S(1)} %get-tuple-element.52), channel_id=1, source_target_pairs={{0,1},{1,0},{2,3},{3,2},{4,5},{5,4},{6,7},{7,6},{8,9},{9,8},{10,11... | collective-permute-start | bytes 1671176 | tf_op jit(solution)/shard_map/ppermute | solution.py:630
  7.7 5.3 %collective-permute-start.2 = (f32[8,24,128]{2,1,0:T(8,128)S(1)}, f32[8,24,128]{2,1,0:T(8,128)S(1)}, u32[]{:S(2)}, u32[]{:S(2)}) collective-permute-start(f32[8,24,128]{2,1,0:T(8,128)S(1)} %get-tuple-element.53), channel_id=1, source_target_pairs={{0,8},{8,0},{16,24},{24,16},{1,9},{9,1},{17,25},{25,17},{2,10},{10... | collective-permute-start | bytes 294920 | tf_op jit(solution)/shard_map/ppermute | solution.py:630
  9.3 6.8 %collective-permute-start.3 = (f32[8,24,128]{2,1,0:T(8,128)S(1)}, f32[8,24,128]{2,1,0:T(8,128)S(1)}, u32[]{:S(2)}, u32[]{:S(2)}) collective-permute-start(f32[8,24,128]{2,1,0:T(8,128)S(1)} %get-tuple-element.54), channel_id=1, source_target_pairs={{0,24},{8,16},{16,8},{24,0},{1,25},{9,17},{17,9},{25,1},{2,26},{10... | collective-permute-start | bytes 294920 | tf_op jit(solution)/shard_map/ppermute | solution.py:630
  16.1 5.4 %collective-permute-start.4 = (f32[2,2,24,128]{3,2,1,0:T(8,128)S(1)}, f32[2,2,24,128]{3,2,1,0:T(8,128)S(1)}, u32[]{:S(2)}, u32[]{:S(2)}) collective-permute-start(f32[2,2,24,128]{3,2,1,0:T(8,128)S(1)} %get-tuple-element.57), channel_id=1, source_target_pairs={{0,7},{1,2},{2,1},{3,4},{4,3},{5,6},{6,5},{7,0},{8,15},{9,10},{10,... | collective-permute-start | bytes 147464 | tf_op jit(solution)/shard_map/ppermute | solution.py:630
  16.2 5.3 %collective-permute-start.5 = (f32[2,2,24,128]{3,2,1,0:T(8,128)S(1)}, f32[2,2,24,128]{3,2,1,0:T(8,128)S(1)}, u32[]{:S(2)}, u32[]{:S(2)}) collective-permute-start(f32[2,2,24,128]{3,2,1,0:T(8,128)S(1)} %get-tuple-element.58), channel_id=1, source_target_pairs={{0,1},{1,0},{2,3},{3,2},{4,5},{5,4},{6,7},{7,6},{8,9},{9,8},{10,11... | collective-permute-start | bytes 147464 | tf_op jit(solution)/shard_map/ppermute | solution.py:630
  24.3 6.6 %collective-permute-start.6 = (f32[2,136,128]{2,1,0:T(8,128)S(1)}, f32[2,136,128]{2,1,0:T(8,128)S(1)}, u32[]{:S(2)}, u32[]{:S(2)}) collective-permute-start(f32[2,136,128]{2,1,0:T(8,128)S(1)} %get-tuple-element.82), channel_id=1, source_target_pairs={{0,7},{1,2},{2,1},{3,4},{4,3},{5,6},{6,5},{7,0},{8,15},{9,10},{10,... | collective-permute-start | bytes 417800 | tf_op jit(solution)/shard_map/ppermute | solution.py:630
  25.7 5.2 %collective-permute-start.7 = (f32[2,136,128]{2,1,0:T(8,128)S(1)}, f32[2,136,128]{2,1,0:T(8,128)S(1)}, u32[]{:S(2)}, u32[]{:S(2)}) collective-permute-start(f32[2,136,128]{2,1,0:T(8,128)S(1)} %get-tuple-element.83), channel_id=1, source_target_pairs={{0,1},{1,0},{2,3},{3,2},{4,5},{5,4},{6,7},{7,6},{8,9},{9,8},{10,11... | collective-permute-start | bytes 417800 | tf_op jit(solution)/shard_map/ppermute | solution.py:630
  31.4 7.8 %collective-permute-start.8 = (f32[2,136,128]{2,1,0:T(8,128)S(1)}, f32[2,136,128]{2,1,0:T(8,128)S(1)}, u32[]{:S(2)}, u32[]{:S(2)}) collective-permute-start(f32[2,136,128]{2,1,0:T(8,128)S(1)} %get-tuple-element.88), channel_id=1, source_target_pairs={{0,7},{1,2},{2,1},{3,4},{4,3},{5,6},{6,5},{7,0},{8,15},{9,10},{10,... | collective-permute-start | bytes 417800 | tf_op jit(solution)/shard_map/ppermute | solution.py:630
  33.4 5.8 %collective-permute-start.9 = (f32[2,136,128]{2,1,0:T(8,128)S(1)}, f32[2,136,128]{2,1,0:T(8,128)S(1)}, u32[]{:S(2)}, u32[]{:S(2)}) collective-permute-start(f32[2,136,128]{2,1,0:T(8,128)S(1)} %get-tuple-element.89), channel_id=1, source_target_pairs={{0,1},{1,0},{2,3},{3,2},{4,5},{5,4},{6,7},{7,6},{8,9},{9,8},{10,11... | collective-permute-start | bytes 417800 | tf_op jit(solution)/shard_map/ppermute | solution.py:630

commit v11 on v10

--- a/solution.py
+++ b/solution.py
@@ -16,7 +16,7 @@
 pad = 16
 chunk = 72
 depth = 2
-first_pair = {"gx": 0, "gy": 1}
+x_first, main_first, round_first = 0, 0, 1
 vmem_limit = 20 * 1024 * 1024
 f32 = jnp.float32
 
@@ -234,18 +234,18 @@
     lax.fori_loop(0, 4, close, 0)
 
 
-def a_is_next(axis):
-    return lax.rem(lax.axis_index(axis), 2) == first_pair[axis]
-
-
-def bases(rows):
-    to_next = a_is_next("gy")
+def a_is_next(axis, first):
+    return lax.rem(lax.axis_index(axis), 2) == first
+
+
+def bases(rows, first):
+    to_next = a_is_next("gy", first)
     top = rows - depth
     return jnp.where(to_next, top, 0), jnp.where(to_next, 0, top)
 
 
-def landings(rows):
-    to_next = a_is_next("gy")
+def landings(rows, first):
+    to_next = a_is_next("gy", first)
     top = rows + depth
     return jnp.where(to_next, top, 0), jnp.where(to_next, 0, top)
 
@@ -269,11 +269,11 @@
     for copy in copies:
         copy.start()
     copies[0].wait()
-    for side, base in zip((main_a, main_b), bases(rows)):
+    for side, base in zip((main_a, main_b), bases(rows, main_first)):
         for at in range(depth):
             side[pl.ds(at * cols, cols), :] = adj_in[pl.ds(base + at, lanes, stride=rows), :].T
     copies[1].wait()
-    for side, base in zip((main_a, main_b), bases(rows)):
+    for side, base in zip((main_a, main_b), bases(rows, main_first)):
         edge = jnp.where(base == 0, 0, rows - 1)
         rate = turned_rate(rate_in, edge, rows, nz, lanes)
         side[pl.ds((1 + steps) * depth * cols, half), :] = jnp.where(
@@ -281,7 +281,7 @@
         )
     for back in range(steps):
         copies[2 + back].wait()
-        for side, base in zip((main_a, main_b), bases(rows)):
+        for side, base in zip((main_a, main_b), bases(rows, main_first)):
             for at in range(depth):
                 side[pl.ds(((1 + back) * depth + at) * cols, cols), :] = conc_in[
                     back, pl.ds(base + at, lanes, stride=rows), :
@@ -297,7 +297,7 @@
                 x_a, x_b):
     places, total = slots(steps)
     lanes = adj_out.shape[2]
-    next_x = a_is_next("gx")
+    next_x = a_is_next("gx", x_first)
 
     def to_x(y, value, place):
         start, width = place
@@ -339,10 +339,10 @@
 
 
 def corner_kernel(rows, got_a, got_b, x_low, x_high, corner_a, corner_b):
-    next_x = a_is_next("gx")
+    next_x = a_is_next("gx", x_first)
     x_low[...] = jnp.where(next_x, got_b[...], got_a[...])
     x_high[...] = jnp.where(next_x, got_a[...], got_b[...])
-    for out, base in zip((corner_a, corner_b), bases(rows)):
+    for out, base in zip((corner_a, corner_b), bases(rows, round_first)):
         for at in range(depth):
             out[0, at] = x_low[base + at]
             out[1, at] = x_high[base + at]
@@ -401,7 +401,7 @@
             open_g[s, at - low : at - low + size, :] = (
                 flow - rate[s * (rows - 1), at : at + size, :] * a
             )
-    to_next = a_is_next("gy")
+    to_next = a_is_next("gy", round_first)
     for to, side in ((to_a, jnp.where(to_next, 1, 0)), (to_b, jnp.where(to_next, 0, 1))):
         to[0] = out[side, 0, first:last, :]
         to[1] = open_g[side, first - low : last - low, :]
@@ -415,7 +415,7 @@
 
 def first_boundary(steps, rows, cols, nz, conc_in, adj_in, rate_in, chem_in, curve_in, swing_in,
                    pot_in,
-                   from_a, from_b, corner_a, corner_b, ahead,
+                   from_a, from_b, corner_b, corner_a, ahead,
                    out, grad, to_a, to_b, rate, conc, adj, mob, chem, curve, swing, pot,
                    part, open_g):
     places, _ = slots(steps)
@@ -443,7 +443,7 @@
         swing[1 + y] = swing_in[y - 1]
     rate[1] = rate_in[0]
     rate[2] = rate_in[rows - 1]
-    for halo, corner, base in zip((from_a, from_b), (corner_a, corner_b), landings(rows)):
+    for halo, corner, base in zip((from_a, from_b), (corner_a, corner_b), landings(rows, main_first)):
         for at in range(depth):
             for ref, place, first in ((adj, places[0], 0), (conc, places[1], depth)):
                 span = pl.ds((first + at) * cols, cols)
@@ -465,7 +465,7 @@
 
 
 def prepare_kernel(steps, rows, cols, nz, back, conc_own, from_a, from_b, x_low, x_high,
-                   corner_a, corner_b, mob, chem, curve, swing, *rest):
+                   corner_b, corner_a, mob, chem, curve, swing, *rest):
     *ahead, conc = rest
     places, _ = slots(steps)
     low, high = reach(cols)
@@ -474,7 +474,7 @@
     place = places[1 + back]
     for y in range(rows):
         put_own(conc, depth + y, conc_own[back, y], y, place, cols, x_low, x_high)
-    for halo, corner, base in zip((from_a, from_b), (corner_a, corner_b), landings(rows)):
+    for halo, corner, base in zip((from_a, from_b), (corner_a, corner_b), landings(rows, main_first)):
         for at in range(depth):
             span = pl.ds(((1 + back) * depth + at) * cols, cols)
             put_halo(conc, base + at, halo[span, :], at, place, cols, corner)
@@ -569,7 +569,7 @@
     first, last = sent(cols)
     lanes = mob.shape[2]
     mask = face_mask(lanes, nz)
-    to_next = a_is_next("gy")
+    to_next = a_is_next("gy", round_first)
     for got, side in ((from_a, jnp.where(to_next, 1, 0)), (from_b, jnp.where(to_next, 0, 1))):
         for k in range(2):
             halo[side, k, first:last, :] = got[k]
@@ -623,10 +623,10 @@
     )(*operands)
 
 
-def swap(value_a, value_b, axis):
-    count, start = lax.axis_size(axis), first_pair[axis]
-    pairs_a = [(i, (i + 1 - 2 * ((i + start) % 2)) % count) for i in range(count)]
-    pairs_b = [(i, (i - 1 + 2 * ((i + start) % 2)) % count) for i in range(count)]
+def swap(value_a, value_b, axis, first):
+    count = lax.axis_size(axis)
+    pairs_a = [(i, (i + 1 - 2 * ((i + first) % 2)) % count) for i in range(count)]
+    pairs_b = [(i, (i - 1 + 2 * ((i + first) % 2)) % count) for i in range(count)]
     return lax.ppermute(value_a, axis, pairs_a), lax.ppermute(value_b, axis, pairs_b)
 
 
@@ -653,7 +653,7 @@
         cost=2,
         far=True,
     )
-    main_a, main_b = swap(main_a, main_b, "gy")
+    main_a, main_b = swap(main_a, main_b, "gy", main_first)
     conc_own, adj_own, rate_own, x_a, x_b = call(
         functools.partial(turn_kernel, steps, rows, cols, nz),
         [(steps, rows, cols, lanes), (rows, cols, lanes), (rows, cols, lanes)]
@@ -662,14 +662,15 @@
         conc_raw, adj_raw, rate_raw,
         cost=1,
     )
-    x_a, x_b = swap(x_a, x_b, "gx")
+    x_a, x_b = swap(x_a, x_b, "gx", x_first)
     x_low, x_high, corner_a, corner_b = call(
         functools.partial(corner_kernel, rows),
         [(rows, total, lanes)] * 2 + [(2, depth, total, lanes)] * 2,
         [],
         x_a, x_b,
     )
-    corner_a, corner_b = swap(corner_a, corner_b, "gy")
+    corners = swap(corner_a, corner_b, "gy", round_first)
+    corner_a, corner_b = corners if main_first == round_first else corners[::-1]
 
     conc, adj, rate, chem, curve, swing, pot, inner, inner_grad, ahead = call(
         functools.partial(first_interior, steps, rows, cols, nz),
@@ -682,18 +683,18 @@
         functools.partial(first_boundary, steps, rows, cols, nz),
         [both, both, edge, edge],
         [field(4)] + [field(rows + 2 * depth)] * 3 + [field(rows + 2)] * 4 + [both, open_g],
-        conc, adj, rate, chem, curve, swing, pot, main_a, main_b, corner_a, corner_b, ahead,
+        conc, adj, rate, chem, curve, swing, pot, main_a, main_b, corner_b, corner_a, ahead,
         cost=2,
     )
     before = (inner_grad, outer_grad)
     for back in range(1, steps):
-        adj_a, adj_b = swap(to_a, to_b, "gy")
+        adj_a, adj_b = swap(to_a, to_b, "gy", round_first)
         final = back == steps - 1
         fields = call(
             functools.partial(prepare_kernel, steps, rows, cols, nz, back),
             [field(rows + 2 * depth)] + [field(rows + 2)] * 3 + ([] if final else [both]),
             [field(rows + 2 * depth)],
-            conc_own, main_a, main_b, x_low, x_high, corner_a, corner_b,
+            conc_own, main_a, main_b, x_low, x_high, corner_b, corner_a,
             cost=2,
         )
         fields, ahead = fields[:4], fields[4:]

time: 40.5 us -> 40.5 us (level)
  waiting for transfers between devices: 7.72 us -> 7.08 us
  starting transfers between devices: 11.2 us -> 11.8 us
    ppermute x5, starting transfers between devices: 1.57 us -> 6.28 us  [swap(): lax.ppermute(value_b, axis, pairs_b)]
    ppermute x5, starting transfers between devices: 9.62 us -> 5.55 us  [swap(): lax.ppermute(value_a, axis, pairs_a)]
    ppermute x5, waiting for transfers between devices: 3.07 us -> 2.1 us  [swap(): lax.ppermute(value_b, axis, pairs_b)]
where the time goes in v11:
time: 40.5 us; the launch traced here: 40.3 us
  Pallas kernels  20.7 us (51%)
  starting transfers between devices  11.8 us (29%)
  waiting for transfers between devices  7.08 us (17%)
  between operations  0.71 us (2%)
    pallas_call x11, Pallas kernels, call(): pl.pallas_call(kernel, out_shape=[jax.ShapeDtypeStruct(shape, f32) for sh...  20.7 us
    ppermute x5, starting transfers between devices, swap(): lax.ppermute(value_b, axis, pairs_b)  6.28 us
    ppermute x5, starting transfers between devices, swap(): lax.ppermute(value_a, axis, pairs_a)  5.55 us
    ppermute x5, waiting for transfers between devices, swap(): lax.ppermute(value_a, axis, pairs_a)  4.98 us
    ppermute x5, waiting for transfers between devices, swap(): lax.ppermute(value_b, axis, pairs_b)  2.1 us
  transfers between devices with their start and end apart: 10, of which 4 were waited for; matrix products, arithmetic and copies ran while one was open for 0% of the time, Pallas kernels for 36%

profile of v11, /device:TPU:0, one launch (start us, length us, event | category | flops | bytes accessed | tf_op | source)
XLA Modules:
  0.0 40.3 jit_solution(10304550103789191815)
XLA Ops:
  0.6 1.8 %shard_map.50 = (f32[3,1024,128]{2,1,0:T(8,128)S(1)}, f32[1024,128]{1,0:T(8,128)S(1)}, f32[512,128]{1,0:T(8,128)S(1)}, f32[1088,128]{1,0:T(8,128)S(1)}, f32[1088,128]{1,0:T(8,128)S(1)}) custom-call(f32[3,1024,128]{2,1,0:T(8,128)} %bitcast.5, f32[1024,128]{1,0:T(8,128)} %bitcast.6, f32[512,128]{1,0:T(8,128)} %bitcast.8), custom_call_target="tpu_custom_call" | custom-call | flops 2000000 | bytes 4000000 | tf_op jit(solution)/shard_map/pallas_call | solution.py:613
  2.4 0.5 %collective-permute-start = (f32[1088,128]{1,0:T(8,128)S(1)}, f32[1088,128]{1,0:T(8,128)S(1)}, u32[]{:S(2)}, u32[]{:S(2)}) collective-permute-start(f32[1088,128]{1,0:T(8,128)S(1)} %get-tuple-element.51), channel_id=1, source_target_pairs={{0,1},{1,0},{2,3},{3,2},{4,5},{5,4},{6,7},{7,6},{8,9},{9,8},{10,11... | collective-permute-start | bytes 1671176 | tf_op jit(solution)/shard_map/ppermute | solution.py:630
  2.9 4.7 %collective-permute-start.1 = (f32[1088,128]{1,0:T(8,128)S(1)}, f32[1088,128]{1,0:T(8,128)S(1)}, u32[]{:S(2)}, u32[]{:S(2)}) collective-permute-start(f32[1088,128]{1,0:T(8,128)S(1)} %get-tuple-element.52), channel_id=1, source_target_pairs={{0,7},{1,2},{2,1},{3,4},{4,3},{5,6},{6,5},{7,0},{8,15},{9,10},{10,... | collective-permute-start | bytes 1671176 | tf_op jit(solution)/shard_map/ppermute | solution.py:630
  7.6 0.7 %shard_map.51 = (f32[3,8,128,128]{3,2,1,0:T(8,128)S(1)}, f32[8,128,128]{2,1,0:T(8,128)S(1)}, f32[8,128,128]{2,1,0:T(8,128)S(1)}, f32[8,24,128]{2,1,0:T(8,128)S(1)}, f32[8,24,128]{2,1,0:T(8,128)S(1)}) custom-call(f32[3,1024,128]{2,1,0:T(8,128)S(1)} %get-tuple-element.47.conc_in, f32[1024,128]{1,0:T(8,128)S(1)} %get-tuple-element.48.adj_in, ...), custom_call_target="tpu_custom_call" | custom-call | flops 1000000 | bytes 2000000 | tf_op jit(solution)/shard_map/pallas_call | solution.py:613
  8.4 1.6 %collective-permute-start.2 = (f32[8,24,128]{2,1,0:T(8,128)S(1)}, f32[8,24,128]{2,1,0:T(8,128)S(1)}, u32[]{:S(2)}, u32[]{:S(2)}) collective-permute-start(f32[8,24,128]{2,1,0:T(8,128)S(1)} %get-tuple-element.53), channel_id=1, source_target_pairs={{0,8},{8,0},{16,24},{24,16},{1,9},{9,1},{17,25},{25,17},{2,10},{10... | collective-permute-start | bytes 294920 | tf_op jit(solution)/shard_map/ppermute | solution.py:630
  9.9 1.5 %collective-permute-start.3 = (f32[8,24,128]{2,1,0:T(8,128)S(1)}, f32[8,24,128]{2,1,0:T(8,128)S(1)}, u32[]{:S(2)}, u32[]{:S(2)}) collective-permute-start(f32[8,24,128]{2,1,0:T(8,128)S(1)} %get-tuple-element.54), channel_id=1, source_target_pairs={{0,24},{8,16},{16,8},{24,0},{1,25},{9,17},{17,9},{25,1},{2,26},{10... | collective-permute-start | bytes 294920 | tf_op jit(solution)/shard_map/ppermute | solution.py:630
  11.4 1.9 %collective-permute-done.2.got_a = f32[8,24,128]{2,1,0:T(8,128)S(1)} collective-permute-done((f32[8,24,128]{2,1,0:T(8,128)S(1)}, f32[8,24,128]{2,1,0:T(8,128)S(1)}, u32[]{:S(2)}, u32[]{:S(2)}) %collective-permute-start.2) | collective-permute-done | bytes 98336 | tf_op jit(solution)/shard_map/ppermute | solution.py:630
  13.4 2.1 %collective-permute-done.3.got_b = f32[8,24,128]{2,1,0:T(8,128)S(1)} collective-permute-done((f32[8,24,128]{2,1,0:T(8,128)S(1)}, f32[8,24,128]{2,1,0:T(8,128)S(1)}, u32[]{:S(2)}, u32[]{:S(2)}) %collective-permute-start.3) | collective-permute-done | bytes 98336 | tf_op jit(solution)/shard_map/ppermute | solution.py:630
  15.5 0.1 collective-permute-start.4
  15.6 0.1 collective-permute-start.5
  15.7 3.1 %shard_map.54 = (f32[8,160,128]{2,1,0:T(8,128)S(1)}, f32[8,160,128]{2,1,0:T(8,128)S(1)}, f32[8,160,128]{2,1,0:T(8,128)S(1)}, f32[6,160,128]{2,1,0:T(8,128)S(1)},...) custom-call(f32[3,8,128,128]{3,2,1,0:T(8,128)S(1)} %get-tuple-elemen, ...), custom_call_target="tpu_custom_call" | custom-call | flops 3000000 | bytes 6000000 | tf_op jit(solution)/shard_map/pallas_call | solution.py:613
  18.7 2.7 %collective-permute-done.4.corner_b = f32[2,2,24,128]{3,2,1,0:T(8,128)S(1)} collective-permute-done((f32[2,2,24,128]{3,2,1,0:T(8,128)S(1)}, f32[2,2,24,128]{3,2,1,0:T(8,128)S(1)}, u32[]{:S(2)}, u32[]{:S(2)}) %collective-permute-start.4) | collective-permute-done | bytes 49184 | tf_op jit(solution)/shard_map/ppermute | solution.py:630
  21.5 0.0 collective-permute-done.5.corner_a
  21.5 0.0 collective-permute-done.from_a
  21.5 0.0 collective-permute-done.1.from_b
  21.5 2.8 %shard_map.56 = (f32[2,2,160,128]{3,2,1,0:T(8,128)S(1)}, f32[2,2,160,128]{3,2,1,0:T(8,128)S(1)}, f32[2,136,128]{2,1,0:T(8,128)S(1)}, f32[2,136,128]{2,1,0:T(8,128)S(1)}) custom-call(f32[8,160,128]{2,1,0:T(8,128)S(1)} %get-tuple-element.71.conc_in, f32[8,160,128]{2,1,0:T(8,128)S(1)} %get-tuple-element.72.adj_in, ...), custom_call_target="tpu_custom_call" | custom-call | flops 2000000 | bytes 4000000 | tf_op jit(solution)/shard_map/pallas_call | solution.py:613
  24.3 1.5 %collective-permute-start.6 = (f32[2,136,128]{2,1,0:T(8,128)S(1)}, f32[2,136,128]{2,1,0:T(8,128)S(1)}, u32[]{:S(2)}, u32[]{:S(2)}) collective-permute-start(f32[2,136,128]{2,1,0:T(8,128)S(1)} %get-tuple-element.82), channel_id=1, source_target_pairs={{0,7},{1,2},{2,1},{3,4},{4,3},{5,6},{6,5},{7,0},{8,15},{9,10},{10,... | collective-permute-start | bytes 417800 | tf_op jit(solution)/shard_map/ppermute | solution.py:630
  25.8 0.0 collective-permute-start.7
  25.8 1.9 %shard_map.55 = (f32[12,160,128]{2,1,0:T(8,128)S(1)}, f32[10,160,128]{2,1,0:T(8,128)S(1)}, f32[10,160,128]{2,1,0:T(8,128)S(1)}, f32[10,160,128]{2,1,0:T(8,128)S(1)}, f32[2,2,160,128]{3,2,1,0:T(8,128)S(1)}) custom-call(f32[3,8,128,128]{3,2,1,0:T(8,128)S(1)} %get-tuple-element.50.conc_own, f32[1088,128]{1,0:T(8,128)S(1)} %collective-permute-done.from_a, ...), custom_call_target="tpu_custom_call" | custom-call | flops 2000000 | bytes 4000000 | tf_op jit(solution)/shard_map/pallas_call | solution.py:613
  27.7 3.1 %shard_map.57 = (f32[8,160,128]{2,1,0:T(8,128)S(1)}, f32[8,160,128]{2,1,0:T(8,128)S(1)}) custom-call(f32[12,160,128]{2,1,0:T(8,128)S(1)} %get-tuple-element.66.mob, f32[10,160,128]{2,1,0:T(8,128)S(1)} %get-tuple-element.67.chem, f32[10,160,128]{2,1,0:T(8,128)S(1)} %get-tuple-element.68.curve, f32[10,160,128]{2,1,0:T(8,128)S(1)} %get-tuple-element.69.swing, ...), custom_call_target="tpu_custom_call" | custom-call | flops 3000000 | bytes 6000000 | tf_op jit(solution)/shard_map/pallas_call | solution.py:613
  30.8 0.3 collective-permute-done.6.from_a
  31.1 0.0 collective-permute-done.7.from_b
  31.1 0.4 shard_map.58
  31.5 1.9 %collective-permute-start.8 = (f32[2,136,128]{2,1,0:T(8,128)S(1)}, f32[2,136,128]{2,1,0:T(8,128)S(1)}, u32[]{:S(2)}, u32[]{:S(2)}) collective-permute-start(f32[2,136,128]{2,1,0:T(8,128)S(1)} %get-tuple-element.88), channel_id=1, source_target_pairs={{0,7},{1,2},{2,1},{3,4},{4,3},{5,6},{6,5},{7,0},{8,15},{9,10},{10,... | collective-permute-start | bytes 417800 | tf_op jit(solution)/shard_map/ppermute | solution.py:630
  33.4 0.0 collective-permute-start.9
  33.4 1.8 %shard_map.53 = (f32[12,160,128]{2,1,0:T(8,128)S(1)}, f32[10,160,128]{2,1,0:T(8,128)S(1)}, f32[10,160,128]{2,1,0:T(8,128)S(1)}, f32[10,160,128]{2,1,0:T(8,128)S(1)}) custom-call(f32[3,8,128,128]{3,2,1,0:T(8,128)S(1)} %get-tuple-element.50.conc_own, f32[1088,128]{1,0:T(8,128)S(1)} %collective-permute-done.from_a, ...), custom_call_target="tpu_custom_call" | custom-call | flops 2000000 | bytes 4000000 | tf_op jit(solution)/shard_map/pallas_call | solution.py:613
  35.2 3.9 %shard_map.59 = (f32[8,160,128]{2,1,0:T(8,128)S(1)}, f32[1024,128]{1,0:T(8,128)S(1)}, f32[512,128]{1,0:T(8,128)}) custom-call(f32[12,160,128]{2,1,0:T(8,128)S(1)} %get-tuple-element.59.mob, f32[10,160,128]{2,1,0:T(8,128)S(1)} %get-tuple-element.60.chem, f32[10,160,128]{2,1,0:T(8,128)S(1)} %get-tuple-element.61.curve, ...), custom_call_target="tpu_custom_call" | custom-call | flops 3000000 | bytes 6000000 | tf_op jit(solution)/shard_map/pallas_call | solution.py:613
  39.2 0.0 collective-permute-done.8.from_a
  39.2 0.0 collective-permute-done.9.from_b
  39.2 1.1 %shard_map.60 = f32[1024,128]{1,0:T(8,128)} custom-call(f32[12,160,128]{2,1,0:T(8,128)S(1)} %get-tuple-element.59.mob, f32[10,160,128]{2,1,0:T(8,128)S(1)} %get-tuple-element.60.chem, f32[10,160,128]{2,1,0:T(8,128)S(1)} %get-tuple-element.61.curve, f32[10,160,128]{2,1,0:T(8,128)S(1)} %get-tuple-element.62.swing, ...), custom_call_target="tpu_custom_call" | custom-call | flops 1000000 | bytes 2000000 | tf_op jit(solution)/shard_map/pallas_call | solution.py:613
  (1 shorter events, 0.0 us)
Async XLA Ops:
  2.4 19.1 %collective-permute-start = (f32[1088,128]{1,0:T(8,128)S(1)}, f32[1088,128]{1,0:T(8,128)S(1)}, u32[]{:S(2)}, u32[]{:S(2)}) collective-permute-start(f32[1088,128]{1,0:T(8,128)S(1)} %get-tuple-element.51), channel_id=1, source_target_pairs={{0,1},{1,0},{2,3},{3,2},{4,5},{5,4},{6,7},{7,6},{8,9},{9,8},{10,11... | collective-permute-start | bytes 1671176 | tf_op jit(solution)/shard_map/ppermute | solution.py:630
  2.9 18.6 %collective-permute-start.1 = (f32[1088,128]{1,0:T(8,128)S(1)}, f32[1088,128]{1,0:T(8,128)S(1)}, u32[]{:S(2)}, u32[]{:S(2)}) collective-permute-start(f32[1088,128]{1,0:T(8,128)S(1)} %get-tuple-element.52), channel_id=1, source_target_pairs={{0,7},{1,2},{2,1},{3,4},{4,3},{5,6},{6,5},{7,0},{8,15},{9,10},{10,... | collective-permute-start | bytes 1671176 | tf_op jit(solution)/shard_map/ppermute | solution.py:630
  8.4 5.0 %collective-permute-start.2 = (f32[8,24,128]{2,1,0:T(8,128)S(1)}, f32[8,24,128]{2,1,0:T(8,128)S(1)}, u32[]{:S(2)}, u32[]{:S(2)}) collective-permute-start(f32[8,24,128]{2,1,0:T(8,128)S(1)} %get-tuple-element.53), channel_id=1, source_target_pairs={{0,8},{8,0},{16,24},{24,16},{1,9},{9,1},{17,25},{25,17},{2,10},{10... | collective-permute-start | bytes 294920 | tf_op jit(solution)/shard_map/ppermute | solution.py:630
  9.9 5.5 %collective-permute-start.3 = (f32[8,24,128]{2,1,0:T(8,128)S(1)}, f32[8,24,128]{2,1,0:T(8,128)S(1)}, u32[]{:S(2)}, u32[]{:S(2)}) collective-permute-start(f32[8,24,128]{2,1,0:T(8,128)S(1)} %get-tuple-element.54), channel_id=1, source_target_pairs={{0,24},{8,16},{16,8},{24,0},{1,25},{9,17},{17,9},{25,1},{2,26},{10... | collective-permute-start | bytes 294920 | tf_op jit(solution)/shard_map/ppermute | solution.py:630
  15.5 6.0 %collective-permute-start.4 = (f32[2,2,24,128]{3,2,1,0:T(8,128)S(1)}, f32[2,2,24,128]{3,2,1,0:T(8,128)S(1)}, u32[]{:S(2)}, u32[]{:S(2)}) collective-permute-start(f32[2,2,24,128]{3,2,1,0:T(8,128)S(1)} %get-tuple-element.57), channel_id=1, source_target_pairs={{0,7},{1,2},{2,1},{3,4},{4,3},{5,6},{6,5},{7,0},{8,15},{9,10},{10,... | collective-permute-start | bytes 147464 | tf_op jit(solution)/shard_map/ppermute | solution.py:630
  15.6 5.9 %collective-permute-start.5 = (f32[2,2,24,128]{3,2,1,0:T(8,128)S(1)}, f32[2,2,24,128]{3,2,1,0:T(8,128)S(1)}, u32[]{:S(2)}, u32[]{:S(2)}) collective-permute-start(f32[2,2,24,128]{3,2,1,0:T(8,128)S(1)} %get-tuple-element.58), channel_id=1, source_target_pairs={{0,1},{1,0},{2,3},{3,2},{4,5},{5,4},{6,7},{7,6},{8,9},{9,8},{10,11... | collective-permute-start | bytes 147464 | tf_op jit(solution)/shard_map/ppermute | solution.py:630
  24.3 6.7 %collective-permute-start.6 = (f32[2,136,128]{2,1,0:T(8,128)S(1)}, f32[2,136,128]{2,1,0:T(8,128)S(1)}, u32[]{:S(2)}, u32[]{:S(2)}) collective-permute-start(f32[2,136,128]{2,1,0:T(8,128)S(1)} %get-tuple-element.82), channel_id=1, source_target_pairs={{0,7},{1,2},{2,1},{3,4},{4,3},{5,6},{6,5},{7,0},{8,15},{9,10},{10,... | collective-permute-start | bytes 417800 | tf_op jit(solution)/shard_map/ppermute | solution.py:630
  25.8 5.3 %collective-permute-start.7 = (f32[2,136,128]{2,1,0:T(8,128)S(1)}, f32[2,136,128]{2,1,0:T(8,128)S(1)}, u32[]{:S(2)}, u32[]{:S(2)}) collective-permute-start(f32[2,136,128]{2,1,0:T(8,128)S(1)} %get-tuple-element.83), channel_id=1, source_target_pairs={{0,1},{1,0},{2,3},{3,2},{4,5},{5,4},{6,7},{7,6},{8,9},{9,8},{10,11... | collective-permute-start | bytes 417800 | tf_op jit(solution)/shard_map/ppermute | solution.py:630
  31.5 7.7 %collective-permute-start.8 = (f32[2,136,128]{2,1,0:T(8,128)S(1)}, f32[2,136,128]{2,1,0:T(8,128)S(1)}, u32[]{:S(2)}, u32[]{:S(2)}) collective-permute-start(f32[2,136,128]{2,1,0:T(8,128)S(1)} %get-tuple-element.88), channel_id=1, source_target_pairs={{0,7},{1,2},{2,1},{3,4},{4,3},{5,6},{6,5},{7,0},{8,15},{9,10},{10,... | collective-permute-start | bytes 417800 | tf_op jit(solution)/shard_map/ppermute | solution.py:630
  33.4 5.8 %collective-permute-start.9 = (f32[2,136,128]{2,1,0:T(8,128)S(1)}, f32[2,136,128]{2,1,0:T(8,128)S(1)}, u32[]{:S(2)}, u32[]{:S(2)}) collective-permute-start(f32[2,136,128]{2,1,0:T(8,128)S(1)} %get-tuple-element.89), channel_id=1, source_target_pairs={{0,1},{1,0},{2,3},{3,2},{4,5},{5,4},{6,7},{7,6},{8,9},{9,8},{10,11... | collective-permute-start | bytes 417800 | tf_op jit(solution)/shard_map/ppermute | solution.py:630

commit v12 on v11

--- a/solution.py
+++ b/solution.py
@@ -127,111 +127,36 @@
     return put
 
 
-def interior(rows, cols, nz, swing, mob, chem, curve, adj, rate, pot, part, grad, store):
+def all_rows(rows, cols, nz, adj, mob, mob_skip, chem, curve, swing, rate, before, pot, part, out,
+             grad):
     low, high = reach(cols)
-    lanes = adj[0].shape[-1]
-    mask = face_mask(lanes, nz)
-
-    def at_row(field, y):
-        return row_of(field[0], field[1] + y)
+    mask = face_mask(adj.shape[2], nz)
 
     def body(y, _):
         for at, size in chunks(low, high):
             span = slice(at, at + size)
             a, mu, flow, pair = face_sums(
-                at_row(adj, y), at_row(mob, y), at_row(chem, y), at, size, mask
-            )
-            g = flow - at_row(rate, y)(0, span) * a
-            pot[y - 1, span, :] = g
-            part[y - depth, span, :] = partial(
-                a, at_row(swing, y)(0, span), pair, at_row(curve, y)(0, span), g
-            )
-            grad[y - depth, span, :] = gain(a, mu, None)
+                row_of(adj, y + 1), row_of(mob, y + mob_skip), row_of(chem, y + 1), at, size, mask
+            )
+            g = flow - rate[y, span, :] * a
+            pot[y + 1, span, :] = g
+            part[y, span, :] = partial(
+                a, swing[y + 1, span, :], pair, curve[y + 1, span, :], g
+            )
+            grad[y, span, :] = gain(a, mu, None if before is None else before[y, span, :])
         return 0
 
-    def edge(i, _):
-        y = 1 + i * (rows - 3)
-        for at, size in chunks(low, high):
-            a, _mu, flow, _pair = face_sums(at_row(adj, y), at_row(mob, y), None, at, size, mask)
+    def close(y, _):
+        for at, size in chunks(low, high):
             span = slice(at, at + size)
-            pot[y - 1, span, :] = flow - at_row(rate, y)(0, span) * a
+            _g, lap = laplace(row_of(pot, y + 1), at, size, mask)
+            out[y, span, :] = part[y, span, :] - grad_energy * lap
         return 0
 
-    def close(y, _):
-        for at, size in chunks(low, high):
-            span = slice(at, at + size)
-            _g, lap = laplace(row_of(pot, y - 1), at, size, mask)
-            store(y - depth, span, part[y - depth, span, :] - grad_energy * lap)
-        return 0
-
-    lax.fori_loop(depth, rows - depth, body, 0)
-    lax.fori_loop(0, 2, edge, 0)
-    lax.fori_loop(depth, rows - depth, close, 0)
-
-
-def boundary(rows, cols, nz, conc, mob, chem, curve, swing, adj, rate, pot, part, grad, store):
-    low, high = reach(cols)
-    lanes = adj[0].shape[-1]
-    mask = face_mask(lanes, nz)
-    last = rows - 1
-
-    def at_row(field, y):
-        return row_of(field[0], field[1] + y)
-
-    def mirror(s, y):
-        return y + s * (last - 2 * y)
-
-    def mu_side(i, _):
-        s, k = i // 2, i % 2
-        y = mirror(s, k - 1)
-        for at, size in chunks(low, high):
-            chem_row(at_row(conc, y), set_row(chem[0], chem[1] + y),
-                     set_row(curve[0], curve[1] + y), set_row(swing[0], swing[1] + y), at, size,
-                     mask)
-        return 0
-
-    lax.fori_loop(0, 4, mu_side, 0)
-
-    def side(s, _):
-        y = mirror(s, -1)
-        for at, size in chunks(low, high):
-            span = slice(at, at + size)
-            a, _mu, flow, _pair = face_sums(at_row(adj, y), at_row(mob, y), None, at, size, mask)
-            pot[1 + y, span, :] = flow - rate[3 * s, span, :] * a
-        y0 = mirror(s, 0)
-        for at, size in chunks(low, high):
-            span = slice(at, at + size)
-            a, mu, flow, pair = face_sums(
-                at_row(adj, y0), at_row(mob, y0), at_row(chem, y0), at, size, mask
-            )
-            g = flow - rate[1 + s, span, :] * a
-            pot[1 + y0, span, :] = g
-            part[s, 0, span, :] = partial(
-                a, at_row(swing, y0)(0, span), pair, at_row(curve, y0)(0, span), g
-            )
-            grad[s, 0, span, :] = gain(a, mu, None)
-        y1 = mirror(s, 1)
-        for at, size in chunks(low, high):
-            span = slice(at, at + size)
-            a, mu, _flow, pair = face_sums(at_row(adj, y1), None, at_row(chem, y1), at, size, mask)
-            part[s, 1, span, :] = partial(
-                a, at_row(swing, y1)(0, span), pair, at_row(curve, y1)(0, span), pot[1 + y1, span, :]
-            )
-            grad[s, 1, span, :] = gain(a, mu, None)
-        return 0
-
-    lax.fori_loop(0, 2, side, 0)
-
-    def close(i, _):
-        s, k = i // 2, i % 2
-        y = mirror(s, k)
-        for at, size in chunks(low, high):
-            span = slice(at, at + size)
-            _g, lap = laplace(row_of(pot, 1 + y), at, size, mask)
-            store(s, k, span, part[s, k, span, :] - grad_energy * lap)
-        return 0
-
-    lax.fori_loop(0, 4, close, 0)
+    for row in (0, rows + 1):
+        pot[row] = jnp.zeros(pot.shape[1:], f32)
+    lax.fori_loop(0, rows, body, 0)
+    lax.fori_loop(0, rows, close, 0)
 
 
 def a_is_next(axis, first):
@@ -330,12 +255,12 @@
     out[row, right : right + width, :] = x_high[y, start : start + width, :]
 
 
-def put_halo(out, row, value, from_row, place, cols, corner):
+def put_halo(out, index, value, from_row, place, cols, corner):
     start, width = place
     right = pad + cols
-    out[row, pad:right, :] = value
-    out[row, pad - width : pad, :] = corner[0, from_row, start : start + width, :]
-    out[row, right : right + width, :] = corner[1, from_row, start : start + width, :]
+    out[(*index, slice(pad, right))] = value
+    out[(*index, slice(pad - width, pad))] = corner[0, from_row, start : start + width, :]
+    out[(*index, slice(right, right + width))] = corner[1, from_row, start : start + width, :]
 
 
 def corner_kernel(rows, got_a, got_b, x_low, x_high, corner_a, corner_b):
@@ -349,42 +274,35 @@
 
 
 def first_interior(steps, rows, cols, nz, conc_own, adj_own, rate_own, x_low, x_high,
-                   conc, adj, rate, chem, curve, swing, pot, out, grad, ahead, mob, part):
+                   conc, adj, rate, chem, curve, swing, out, grad, ahead, mob, pot, part):
     places, _ = slots(steps)
     low, high = reach(cols)
     lanes = adj.shape[2]
     mask = face_mask(lanes, nz)
     for y in range(rows):
-        put_own(conc, y, conc_own[0, y], y, places[1], cols, x_low, x_high)
-        put_own(adj, y, adj_own[y], y, places[0], cols, x_low, x_high)
+        put_own(conc, 1 + y, conc_own[0, y], y, places[1], cols, x_low, x_high)
+        put_own(adj, 1 + y, adj_own[y], y, places[0], cols, x_low, x_high)
         put_own(rate, y, rate_own[y], y, places[steps + 1], cols, x_low, x_high)
+    for row, beside in ((0, 1), (rows + 1, rows)):
+        adj[row] = adj[beside]
+        for ref in (conc, chem, mob):
+            ref[row] = jnp.zeros(ref.shape[1:], f32)
     put_ahead(ahead, conc_own, 1, x_low, x_high, places, rows, cols)
 
-    def mob_row(y, _):
+    def mob_row(row, _):
         for at, size in chunks(low - 8, high + 8):
-            c = conc[y, at : at + size, :]
-            mob[y, at : at + size, :] = mobility(c)
+            mob[row, at : at + size, :] = mobility(conc[row, at : at + size, :])
         return 0
 
-    def mu_row(y, _):
-        for at, size in chunks(low, high):
-            chem_row(row_of(conc, y), set_row(chem, y - 1), set_row(curve, y - 1),
-                     set_row(swing, y - 1), at, size, mask)
+    def mu_row(row, _):
+        for at, size in chunks(low, high):
+            chem_row(row_of(conc, row), set_row(chem, row), set_row(curve, row),
+                     set_row(swing, row), at, size, mask)
         return 0
 
-    lax.fori_loop(0, rows, mob_row, 0)
-    lax.fori_loop(1, rows - 1, mu_row, 0)
-
-    def store(k, span, value):
-        out[k, span, :] = value
-
-    interior(rows, cols, nz, (swing, -1), (mob, 0), (chem, -1), (curve, -1), (adj, 0), (rate, 0),
-             pot, part, grad, store)
-
-
-def copy_rows(pairs):
-    for out, to, ref, at in pairs:
-        out[to] = ref[at]
+    lax.fori_loop(1, rows + 1, mob_row, 0)
+    lax.fori_loop(1, rows + 1, mu_row, 0)
+    all_rows(rows, cols, nz, adj, mob, 1, chem, curve, swing, rate, None, pot, part, out, grad)
 
 
 def send_rows(out, ahead, rate, to_a, to_b, open_g, cols, nz):
@@ -413,16 +331,17 @@
         ahead[s, k] = mobility(ahead[s, k])
 
 
-def first_boundary(steps, rows, cols, nz, conc_in, adj_in, rate_in, chem_in, curve_in, swing_in,
-                   pot_in,
+def first_boundary(steps, rows, cols, nz, conc, adj, rate, chem, curve, swing, inside, grad,
                    from_a, from_b, corner_b, corner_a, ahead,
-                   out, grad, to_a, to_b, rate, conc, adj, mob, chem, curve, swing, pot,
-                   part, open_g):
+                   out, edge_grad, to_a, to_b, far_conc, far_adj, far_rate, far_mob, far_chem,
+                   far_pot, delta, open_g):
     places, _ = slots(steps)
     low, high = reach(cols)
     half = cols // 2
     lanes = conc.shape[2]
+    mask = face_mask(lanes, nz)
     lower = lax.broadcasted_iota(jnp.int32, (half, lanes), 1) < nz
+    to_next = a_is_next("gy", main_first)
 
     def unpack(side):
         packed = side[pl.ds((1 + steps) * depth * cols, half), :]
@@ -431,37 +350,70 @@
             [jnp.where(lower, packed, turned), jnp.where(lower, turned, packed)], axis=0
         )
 
-    near = [0, 1, 2, rows - 3, rows - 2, rows - 1]
-    for y in near:
-        conc[depth + y] = conc_in[y]
-        adj[depth + y] = adj_in[y]
-    for y in (1, 2, rows - 3, rows - 2):
-        chem[1 + y] = chem_in[y - 1]
-        pot[1 + y] = pot_in[y - 1]
-    for y in (1, rows - 2):
-        curve[1 + y] = curve_in[y - 1]
-        swing[1 + y] = swing_in[y - 1]
-    rate[1] = rate_in[0]
-    rate[2] = rate_in[rows - 1]
-    for halo, corner, base in zip((from_a, from_b), (corner_a, corner_b), landings(rows, main_first)):
+    for halo, corner, side in (
+        (from_a, corner_a, jnp.where(to_next, 1, 0)),
+        (from_b, corner_b, jnp.where(to_next, 0, 1)),
+    ):
         for at in range(depth):
-            for ref, place, first in ((adj, places[0], 0), (conc, places[1], depth)):
+            step = jnp.where(side == 1, at, depth - 1 - at)
+            for ref, place, first in ((far_adj, places[0], 0), (far_conc, places[1], depth)):
                 span = pl.ds((first + at) * cols, cols)
-                put_halo(ref, base + at, halo[span, :], at, place, cols, corner)
-        below = base == 0
-        put_halo(rate, jnp.where(below, 0, 3), unpack(halo), jnp.where(below, depth - 1, 0),
+                put_halo(ref, (side, step), halo[span, :], at, place, cols, corner)
+        put_halo(far_rate, (side,), unpack(halo), jnp.where(side == 1, 0, depth - 1),
                  places[steps + 1], cols, corner)
-    for row in [0, 1, 2, 3, rows, rows + 1, rows + 2, rows + 3]:
+
+    share = time_step * grad_energy
+    for s in range(2):
+        y, y1 = s * (rows - 1), 1 + s * (rows - 3)
         for at, size in chunks(low - 8, high + 8):
-            c = conc[row, at : at + size, :]
-            mob[row, at : at + size, :] = mobility(c)
-
-    def store(s, k, span, value):
-        out[s, k, span, :] = value
-
-    boundary(rows, cols, nz, (conc, depth), (mob, depth), (chem, 1), (curve, 1), (swing, 1),
-             (adj, depth), rate, pot, part, grad, store)
-    send_rows(out, ahead, rate_in, to_a, to_b, open_g, cols, nz)
+            span = slice(at, at + size)
+            far_mob[s, span, :] = mobility(far_conc[s, 0, span, :])
+
+        def conc_at(dy, cut):
+            return conc[1 + y, cut, :] if dy == 1 else far_conc[s, -dy, cut, :]
+
+        def adj_at(dy, cut):
+            return adj[1 + y, cut, :] if dy == 1 else far_adj[s, -dy, cut, :]
+
+        def mob_at(dy, cut):
+            return far_mob[s, cut, :] if dy == 0 else mobility(conc_at(dy, cut))
+
+        for at, size in chunks(low, high):
+            span = slice(at, at + size)
+            chem_row(conc_at, set_row(far_chem, s), lambda *_: None, lambda *_: None, at, size,
+                     mask)
+            a, _mu, flow, _pair = face_sums(adj_at, mob_at, None, at, size, mask)
+            far_pot[s, span, :] = flow - far_rate[s, span, :] * a
+            diff = a - adj[1 + y, span, :]
+            delta[s, span, :] = (far_mob[s, span, :] + mobility(conc[1 + y, span, :])) * diff
+        for at, size in chunks(low, high):
+            span = slice(at, at + size)
+            a, c, _flow, spread = face_sums(
+                lambda dy, cut: adj[1 + y, cut, :], None, lambda dy, cut: far_conc[s, 0, cut, :],
+                at, size, mask, ()
+            )
+            less = share * c
+            inward = less * (adj[1 + y1, span, :] - a)
+            pair = (far_chem[s, span, :] - (chem[1 + y, span, :] - less)) * (
+                far_adj[s, 0, span, :] - a
+            ) + (inward - share * spread)
+            more = delta[s, span, :]
+            step_z = (up(more) - more) * mask
+            lap = (
+                (delta[s, at + 1 : at + size + 1, :] + delta[s, at - 1 : at + size - 1, :])
+                + (far_pot[s, span, :] - 4.0 * more)
+                + (step_z - down(step_z))
+            )
+            out[s, 0, span, :] = (
+                inside[y, span, :]
+                + (swing[1 + y, span, :] * pair + curve[1 + y, span, :] * more)
+                - grad_energy * lap
+            )
+            out[s, 1, span, :] = (
+                inside[y1, span, :] + swing[1 + y1, span, :] * inward - grad_energy * more
+            )
+            edge_grad[s, span, :] = grad[y, span, :] + less * a
+    send_rows(out, ahead, rate, to_a, to_b, open_g, cols, nz)
 
 
 def prepare_kernel(steps, rows, cols, nz, back, conc_own, from_a, from_b, x_low, x_high,
@@ -477,7 +429,7 @@
     for halo, corner, base in zip((from_a, from_b), (corner_a, corner_b), landings(rows, main_first)):
         for at in range(depth):
             span = pl.ds(((1 + back) * depth + at) * cols, cols)
-            put_halo(conc, base + at, halo[span, :], at, place, cols, corner)
+            put_halo(conc, (base + at,), halo[span, :], at, place, cols, corner)
 
     if ahead:
         put_ahead(ahead[0], conc_own, back + 1, x_low, x_high, places, rows, cols)
@@ -498,53 +450,25 @@
     lax.fori_loop(0, rows + 2, mu_row, 0)
 
 
-def next_interior(rows, cols, nz, final, mob, chem, curve, swing, rate, inner, outer, *rest):
+def next_interior(rows, cols, nz, final, mob, chem, curve, swing, rate, inner, outer, before, *rest):
     if final:
-        before, out, tiles, grad_out, adj, pot, part, grad = rest
-    elif len(rest) == 8:
-        inner_grad, outer_grad, out, grad, adj, pot, part, before = rest
-        for k in range(rows - 2 * depth):
-            before[depth + k] = inner_grad[k]
-        for s, k, y in sides_of(rows):
-            before[y] = outer_grad[s, k]
+        out, tiles, grad_out, adj, pot, part, grad = rest
     else:
-        before, out, grad, adj, pot, part = rest
-    low, high = reach(cols)
+        edge_before, out, grad, adj, pot, part, sums = rest
+        for y in range(rows):
+            sums[y] = before[y]
+        for s, y in ((0, 0), (1, rows - 1)):
+            sums[y] = edge_before[s]
+        before = sums
     lanes = adj.shape[2]
-    mask = face_mask(lanes, nz)
-    skip = (inner.shape[0] - (rows - 2 * depth)) // 2
-    for k in range(rows - 2 * depth):
-        adj[1 + depth + k] = inner[skip + k]
+    for y in range(depth, rows - depth):
+        adj[1 + y] = inner[y]
     for s, k, y in sides_of(rows):
         adj[1 + y] = outer[s, k]
     adj[0] = outer[0, 0]
     adj[1 + rows] = outer[1, 0]
-    pot[0] = jnp.zeros(pot.shape[1:], f32)
-    pot[1 + rows] = jnp.zeros(pot.shape[1:], f32)
-
-    def body(y, _):
-        for at, size in chunks(low, high):
-            span = slice(at, at + size)
-            a, mu, flow, pair = face_sums(
-                row_of(adj, y + 1), row_of(mob, y + depth), row_of(chem, y + 1), at, size, mask
-            )
-            g = flow - rate[y, span, :] * a
-            pot[y + 1, span, :] = g
-            part[y, span, :] = partial(
-                a, swing[y + 1, span, :], pair, curve[y + 1, span, :], g
-            )
-            grad[y, span, :] = gain(a, mu, before[y, span, :])
-        return 0
-
-    def close(y, _):
-        for at, size in chunks(low, high):
-            span = slice(at, at + size)
-            _g, lap = laplace(row_of(pot, y + 1), at, size, mask)
-            out[y, span, :] = part[y, span, :] - grad_energy * lap
-        return 0
-
-    lax.fori_loop(0, rows, body, 0)
-    lax.fori_loop(0, rows, close, 0)
+    all_rows(rows, cols, nz, adj, mob, depth, chem, curve, swing, rate, before, pot, part, out,
+             grad)
     if final:
         for y in range(rows):
             grad_out[pl.ds(y, nz, stride=rows), :] = fold(grad[y, pad : pad + cols, :].T, nz)
@@ -636,7 +560,6 @@
     _, total = slots(steps)
     width = cols + 2 * pad
     flat = lanes * rows
-    inside = rows - 2 * depth
 
     def field(count):
         return (count, width, lanes)
@@ -672,21 +595,21 @@
     corners = swap(corner_a, corner_b, "gy", round_first)
     corner_a, corner_b = corners if main_first == round_first else corners[::-1]
 
-    conc, adj, rate, chem, curve, swing, pot, inner, inner_grad, ahead = call(
+    conc, adj, rate, chem, curve, swing, inner, grad, ahead = call(
         functools.partial(first_interior, steps, rows, cols, nz),
-        [field(rows)] * 3 + [field(rows - 2)] * 4 + [field(inside)] * 2 + [both],
-        [field(rows), field(inside)],
+        [field(rows + 2)] * 2 + [field(rows)] + [field(rows + 2)] * 3 + [field(rows)] * 2 + [both],
+        [field(rows + 2)] * 2 + [field(rows)],
         conc_own, adj_own, rate_own, x_low, x_high,
         cost=3,
     )
-    outer, outer_grad, to_a, to_b = call(
+    outer, edge_grad, to_a, to_b = call(
         functools.partial(first_boundary, steps, rows, cols, nz),
-        [both, both, edge, edge],
-        [field(4)] + [field(rows + 2 * depth)] * 3 + [field(rows + 2)] * 4 + [both, open_g],
-        conc, adj, rate, chem, curve, swing, pot, main_a, main_b, corner_b, corner_a, ahead,
+        [both, field(2), edge, edge],
+        [both, both] + [field(2)] * 5 + [open_g],
+        conc, adj, rate, chem, curve, swing, inner, grad, main_a, main_b, corner_b, corner_a, ahead,
         cost=2,
     )
-    before = (inner_grad, outer_grad)
+    sums = (grad, edge_grad)
     for back in range(1, steps):
         adj_a, adj_b = swap(to_a, to_b, "gy", round_first)
         final = back == steps - 1
@@ -698,38 +621,38 @@
             cost=2,
         )
         fields, ahead = fields[:4], fields[4:]
-        work = [field(rows + 2)] * 2 + [field(rows)]
+        work = [field(rows + 2)] * 2 + [field(rows)] * 2
         if final:
-            rows_in, tiles, grad = call(
+            inner, tiles, grad = call(
                 functools.partial(next_interior, rows, cols, nz, final),
                 [field(rows), (flat, cols), (nz * rows, cols)],
-                work + [field(rows)],
-                *fields, rate, inner, outer, *before,
+                work,
+                *fields, rate, inner, outer, *sums,
                 cost=3,
             )
             (adj,) = call(
                 functools.partial(next_boundary, rows, cols, nz, final),
                 [(flat, cols)],
                 [both, field(2), both],
-                *fields, rows_in, outer, adj_a, adj_b, tiles,
+                *fields, inner, outer, adj_a, adj_b, tiles,
                 cost=1,
             )
         else:
-            rows_in, grad = call(
+            inner, grad = call(
                 functools.partial(next_interior, rows, cols, nz, final),
                 [field(rows)] * 2,
-                work + ([field(rows)] if len(before) == 2 else []),
-                *fields, rate, inner, outer, *before,
+                work,
+                *fields, rate, inner, outer, *sums,
                 cost=3,
             )
             outer, to_a, to_b = call(
                 functools.partial(next_boundary, rows, cols, nz, final),
                 [both, edge, edge],
                 [both, field(2), open_g],
-                *fields, rows_in, outer, adj_a, adj_b, *ahead, rate,
+                *fields, inner, outer, adj_a, adj_b, *ahead, rate,
                 cost=1,
             )
-            inner, before = rows_in, (grad,)
+            sums = (grad,)
     return adj.reshape(adjoint_end.shape), grad.reshape(rate_field.shape)
 
 

time: 40.5 us -> 39.2 us (0.968)
  waiting for transfers between devices: 7.08 us -> 5.31 us
    ppermute x5, waiting for transfers between devices: 4.98 us -> 3.22 us  [swap(): lax.ppermute(value_a, axis, pairs_a)]
  transfers between devices with their start and end apart: 10 -> 10, of which waited for: 4 -> 3; matrix products, arithmetic and copies ran while one was open for 0% -> 0% of each run, Pallas kernels for 36% -> 41%
where the time goes in v12:
time: 39.2 us; the launch traced here: 39 us
  Pallas kernels  20.8 us (53%)
  starting transfers between devices  12.1 us (31%)
  waiting for transfers between devices  5.31 us (14%)
  between operations  0.73 us (2%)
    pallas_call x11, Pallas kernels, call(): pl.pallas_call(kernel, out_shape=[jax.ShapeDtypeStruct(shape, f32) for sh...  20.8 us
    ppermute x5, starting transfers between devices, swap(): lax.ppermute(value_b, axis, pairs_b)  6.28 us
    ppermute x5, starting transfers between devices, swap(): lax.ppermute(value_a, axis, pairs_a)  5.82 us
    ppermute x5, waiting for transfers between devices, swap(): lax.ppermute(value_a, axis, pairs_a)  3.22 us
    ppermute x5, waiting for transfers between devices, swap(): lax.ppermute(value_b, axis, pairs_b)  2.1 us
  transfers between devices with their start and end apart: 10, of which 3 were waited for; matrix products, arithmetic and copies ran while one was open for 0% of the time, Pallas kernels for 41%

profile of v12, /device:TPU:0, one launch (start us, length us, event | category | flops | bytes accessed | tf_op | source)
XLA Modules:
  0.0 39.0 jit_solution(11363742679658099762)
XLA Ops:
  0.6 1.8 %shard_map.50 = (f32[3,1024,128]{2,1,0:T(8,128)S(1)}, f32[1024,128]{1,0:T(8,128)S(1)}, f32[512,128]{1,0:T(8,128)S(1)}, f32[1088,128]{1,0:T(8,128)S(1)}, f32[1088,128]{1,0:T(8,128)S(1)}) custom-call(f32[3,1024,128]{2,1,0:T(8,128)} %bitcast.5, f32[1024,128]{1,0:T(8,128)} %bitcast.6, f32[512,128]{1,0:T(8,128)} %bitcast.8), custom_call_target="tpu_custom_call" | custom-call | flops 2000000 | bytes 4000000 | tf_op jit(solution)/shard_map/pallas_call | solution.py:537
  2.4 0.5 %collective-permute-start = (f32[1088,128]{1,0:T(8,128)S(1)}, f32[1088,128]{1,0:T(8,128)S(1)}, u32[]{:S(2)}, u32[]{:S(2)}) collective-permute-start(f32[1088,128]{1,0:T(8,128)S(1)} %get-tuple-element.50), channel_id=1, source_target_pairs={{0,1},{1,0},{2,3},{3,2},{4,5},{5,4},{6,7},{7,6},{8,9},{9,8},{10,11... | collective-permute-start | bytes 1671176 | tf_op jit(solution)/shard_map/ppermute | solution.py:554
  2.9 4.7 %collective-permute-start.1 = (f32[1088,128]{1,0:T(8,128)S(1)}, f32[1088,128]{1,0:T(8,128)S(1)}, u32[]{:S(2)}, u32[]{:S(2)}) collective-permute-start(f32[1088,128]{1,0:T(8,128)S(1)} %get-tuple-element.51), channel_id=1, source_target_pairs={{0,7},{1,2},{2,1},{3,4},{4,3},{5,6},{6,5},{7,0},{8,15},{9,10},{10,... | collective-permute-start | bytes 1671176 | tf_op jit(solution)/shard_map/ppermute | solution.py:554
  7.6 0.7 %shard_map.51 = (f32[3,8,128,128]{3,2,1,0:T(8,128)S(1)}, f32[8,128,128]{2,1,0:T(8,128)S(1)}, f32[8,128,128]{2,1,0:T(8,128)S(1)}, f32[8,24,128]{2,1,0:T(8,128)S(1)}, f32[8,24,128]{2,1,0:T(8,128)S(1)}) custom-call(f32[3,1024,128]{2,1,0:T(8,128)S(1)} %get-tuple-element.46.conc_in, f32[1024,128]{1,0:T(8,128)S(1)} %get-tuple-element.47.adj_in, ...), custom_call_target="tpu_custom_call" | custom-call | flops 1000000 | bytes 2000000 | tf_op jit(solution)/shard_map/pallas_call | solution.py:537
  8.4 1.6 %collective-permute-start.2 = (f32[8,24,128]{2,1,0:T(8,128)S(1)}, f32[8,24,128]{2,1,0:T(8,128)S(1)}, u32[]{:S(2)}, u32[]{:S(2)}) collective-permute-start(f32[8,24,128]{2,1,0:T(8,128)S(1)} %get-tuple-element.52), channel_id=1, source_target_pairs={{0,8},{8,0},{16,24},{24,16},{1,9},{9,1},{17,25},{25,17},{2,10},{10... | collective-permute-start | bytes 294920 | tf_op jit(solution)/shard_map/ppermute | solution.py:554
  9.9 1.5 %collective-permute-start.3 = (f32[8,24,128]{2,1,0:T(8,128)S(1)}, f32[8,24,128]{2,1,0:T(8,128)S(1)}, u32[]{:S(2)}, u32[]{:S(2)}) collective-permute-start(f32[8,24,128]{2,1,0:T(8,128)S(1)} %get-tuple-element.53), channel_id=1, source_target_pairs={{0,24},{8,16},{16,8},{24,0},{1,25},{9,17},{17,9},{25,1},{2,26},{10... | collective-permute-start | bytes 294920 | tf_op jit(solution)/shard_map/ppermute | solution.py:554
  11.4 1.9 %collective-permute-done.2.got_a = f32[8,24,128]{2,1,0:T(8,128)S(1)} collective-permute-done((f32[8,24,128]{2,1,0:T(8,128)S(1)}, f32[8,24,128]{2,1,0:T(8,128)S(1)}, u32[]{:S(2)}, u32[]{:S(2)}) %collective-permute-start.2) | collective-permute-done | bytes 98336 | tf_op jit(solution)/shard_map/ppermute | solution.py:554
  13.4 2.1 %collective-permute-done.3.got_b = f32[8,24,128]{2,1,0:T(8,128)S(1)} collective-permute-done((f32[8,24,128]{2,1,0:T(8,128)S(1)}, f32[8,24,128]{2,1,0:T(8,128)S(1)}, u32[]{:S(2)}, u32[]{:S(2)}) %collective-permute-start.3) | collective-permute-done | bytes 98336 | tf_op jit(solution)/shard_map/ppermute | solution.py:554
  15.5 0.1 collective-permute-start.4
  15.6 0.1 collective-permute-start.5
  15.7 4.5 %shard_map.54 = (f32[10,160,128]{2,1,0:T(8,128)S(1)}, f32[10,160,128]{2,1,0:T(8,128)S(1)}, f32[8,160,128]{2,1,0:T(8,128)S(1)}, f32[10,160,128]{2,1,0:T(8,128)S(1...) custom-call(f32[3,8,128,128]{3,2,1,0:T(8,128)S(1)} %get-tuple-elemen, ...), custom_call_target="tpu_custom_call" | custom-call | flops 3000000 | bytes 6000000 | tf_op jit(solution)/shard_map/pallas_call | solution.py:537
  20.2 1.3 %collective-permute-done.4.corner_b = f32[2,2,24,128]{3,2,1,0:T(8,128)S(1)} collective-permute-done((f32[2,2,24,128]{3,2,1,0:T(8,128)S(1)}, f32[2,2,24,128]{3,2,1,0:T(8,128)S(1)}, u32[]{:S(2)}, u32[]{:S(2)}) %collective-permute-start.4) | collective-permute-done | bytes 49184 | tf_op jit(solution)/shard_map/ppermute | solution.py:554
  21.5 0.0 collective-permute-done.5.corner_a
  21.5 0.0 collective-permute-done.from_a
  21.5 0.0 collective-permute-done.1.from_b
  21.5 1.5 %shard_map.56 = (f32[2,2,160,128]{3,2,1,0:T(8,128)S(1)}, f32[2,160,128]{2,1,0:T(8,128)S(1)}, f32[2,136,128]{2,1,0:T(8,128)S(1)}, f32[2,136,128]{2,1,0:T(8,128)S(1)}) custom-call(f32[10,160,128]{2,1,0:T(8,128)S(1)} %get-tuple-element.70.conc, f32[10,160,128]{2,1,0:T(8,128)S(1)} %get-tuple-element.71.adj, f32[8,160,128]{2,1,0:T(8,128)S(1)} %get-tuple-element.64.rate.rest_1_, ...), custom_call_target="tpu_custom_call" | custom-call | flops 2000000 | bytes 4000000 | tf_op jit(solution)/shard_map/pallas_call | solution.py:537
  23.0 2.3 %collective-permute-start.6 = (f32[2,136,128]{2,1,0:T(8,128)S(1)}, f32[2,136,128]{2,1,0:T(8,128)S(1)}, u32[]{:S(2)}, u32[]{:S(2)}) collective-permute-start(f32[2,136,128]{2,1,0:T(8,128)S(1)} %get-tuple-element.80), channel_id=1, source_target_pairs={{0,7},{1,2},{2,1},{3,4},{4,3},{5,6},{6,5},{7,0},{8,15},{9,10},{10,... | collective-permute-start | bytes 417800 | tf_op jit(solution)/shard_map/ppermute | solution.py:554
  25.3 0.0 collective-permute-start.7
  25.3 1.9 %shard_map.55 = (f32[12,160,128]{2,1,0:T(8,128)S(1)}, f32[10,160,128]{2,1,0:T(8,128)S(1)}, f32[10,160,128]{2,1,0:T(8,128)S(1)}, f32[10,160,128]{2,1,0:T(8,128)S(1)}, f32[2,2,160,128]{3,2,1,0:T(8,128)S(1)}) custom-call(f32[3,8,128,128]{3,2,1,0:T(8,128)S(1)} %get-tuple-element.49.conc_own, f32[1088,128]{1,0:T(8,128)S(1)} %collective-permute-done.from_a, ...), custom_call_target="tpu_custom_call" | custom-call | flops 2000000 | bytes 4000000 | tf_op jit(solution)/shard_map/pallas_call | solution.py:537
  27.2 3.1 %shard_map.57 = (f32[8,160,128]{2,1,0:T(8,128)S(1)}, f32[8,160,128]{2,1,0:T(8,128)S(1)}) custom-call(f32[12,160,128]{2,1,0:T(8,128)S(1)} %get-tuple-element.65.mob, f32[10,160,128]{2,1,0:T(8,128)S(1)} %get-tuple-element.66.chem, f32[10,160,128]{2,1,0:T(8,128)S(1)} %get-tuple-element.67.curve, f32[10,160,128]{2,1,0:T(8,128)S(1)} %get-tuple-element.68.swing, ...), custom_call_target="tpu_custom_call" | custom-call | flops 3000000 | bytes 6000000 | tf_op jit(solution)/shard_map/pallas_call | solution.py:537
  30.2 0.0 collective-permute-done.6.from_a
  30.3 0.0 collective-permute-done.7.from_b
  30.3 0.4 %shard_map.58 = (f32[2,2,160,128]{3,2,1,0:T(8,128)S(1)}, f32[2,136,128]{2,1,0:T(8,128)S(1)}, f32[2,136,128]{2,1,0:T(8,128)S(1)}) custom-call(f32[12,160,128]{2,1,0:T(8,128)S(1)} %get-tuple-element.65.mob, f32[10,160,128]{2,1,0:T(8,128)S(1)} %get-tuple-element.66.chem, f32[10,160,128]{2,1,0:T(8,128)S(1)} %get-tuple-element.67.curve, ...), custom_call_target="tpu_custom_call" | custom-call | flops 1000000 | bytes 2000000 | tf_op jit(solution)/shard_map/pallas_call | solution.py:537
  30.7 1.4 %collective-permute-start.8 = (f32[2,136,128]{2,1,0:T(8,128)S(1)}, f32[2,136,128]{2,1,0:T(8,128)S(1)}, u32[]{:S(2)}, u32[]{:S(2)}) collective-permute-start(f32[2,136,128]{2,1,0:T(8,128)S(1)} %get-tuple-element.86), channel_id=1, source_target_pairs={{0,7},{1,2},{2,1},{3,4},{4,3},{5,6},{6,5},{7,0},{8,15},{9,10},{10,... | collective-permute-start | bytes 417800 | tf_op jit(solution)/shard_map/ppermute | solution.py:554
  32.1 0.0 collective-permute-start.9
  32.1 1.8 %shard_map.53 = (f32[12,160,128]{2,1,0:T(8,128)S(1)}, f32[10,160,128]{2,1,0:T(8,128)S(1)}, f32[10,160,128]{2,1,0:T(8,128)S(1)}, f32[10,160,128]{2,1,0:T(8,128)S(1)}) custom-call(f32[3,8,128,128]{3,2,1,0:T(8,128)S(1)} %get-tuple-element.49.conc_own, f32[1088,128]{1,0:T(8,128)S(1)} %collective-permute-done.from_a, ...), custom_call_target="tpu_custom_call" | custom-call | flops 2000000 | bytes 4000000 | tf_op jit(solution)/shard_map/pallas_call | solution.py:537
  33.9 3.9 %shard_map.59 = (f32[8,160,128]{2,1,0:T(8,128)S(1)}, f32[1024,128]{1,0:T(8,128)S(1)}, f32[512,128]{1,0:T(8,128)}) custom-call(f32[12,160,128]{2,1,0:T(8,128)S(1)} %get-tuple-element.58.mob, f32[10,160,128]{2,1,0:T(8,128)S(1)} %get-tuple-element.59.chem, f32[10,160,128]{2,1,0:T(8,128)S(1)} %get-tuple-element.60.curve, ...), custom_call_target="tpu_custom_call" | custom-call | flops 3000000 | bytes 6000000 | tf_op jit(solution)/shard_map/pallas_call | solution.py:537
  37.8 0.0 collective-permute-done.8.from_a
  37.8 0.0 collective-permute-done.9.from_b
  37.8 1.1 %shard_map.60 = f32[1024,128]{1,0:T(8,128)} custom-call(f32[12,160,128]{2,1,0:T(8,128)S(1)} %get-tuple-element.58.mob, f32[10,160,128]{2,1,0:T(8,128)S(1)} %get-tuple-element.59.chem, f32[10,160,128]{2,1,0:T(8,128)S(1)} %get-tuple-element.60.curve, f32[10,160,128]{2,1,0:T(8,128)S(1)} %get-tuple-element.61.swing, ...), custom_call_target="tpu_custom_call" | custom-call | flops 1000000 | bytes 2000000 | tf_op jit(solution)/shard_map/pallas_call | solution.py:537
  (1 shorter events, 0.0 us)
Async XLA Ops:
  2.4 19.1 %collective-permute-start = (f32[1088,128]{1,0:T(8,128)S(1)}, f32[1088,128]{1,0:T(8,128)S(1)}, u32[]{:S(2)}, u32[]{:S(2)}) collective-permute-start(f32[1088,128]{1,0:T(8,128)S(1)} %get-tuple-element.50), channel_id=1, source_target_pairs={{0,1},{1,0},{2,3},{3,2},{4,5},{5,4},{6,7},{7,6},{8,9},{9,8},{10,11... | collective-permute-start | bytes 1671176 | tf_op jit(solution)/shard_map/ppermute | solution.py:554
  2.9 18.6 %collective-permute-start.1 = (f32[1088,128]{1,0:T(8,128)S(1)}, f32[1088,128]{1,0:T(8,128)S(1)}, u32[]{:S(2)}, u32[]{:S(2)}) collective-permute-start(f32[1088,128]{1,0:T(8,128)S(1)} %get-tuple-element.51), channel_id=1, source_target_pairs={{0,7},{1,2},{2,1},{3,4},{4,3},{5,6},{6,5},{7,0},{8,15},{9,10},{10,... | collective-permute-start | bytes 1671176 | tf_op jit(solution)/shard_map/ppermute | solution.py:554
  8.4 5.0 %collective-permute-start.2 = (f32[8,24,128]{2,1,0:T(8,128)S(1)}, f32[8,24,128]{2,1,0:T(8,128)S(1)}, u32[]{:S(2)}, u32[]{:S(2)}) collective-permute-start(f32[8,24,128]{2,1,0:T(8,128)S(1)} %get-tuple-element.52), channel_id=1, source_target_pairs={{0,8},{8,0},{16,24},{24,16},{1,9},{9,1},{17,25},{25,17},{2,10},{10... | collective-permute-start | bytes 294920 | tf_op jit(solution)/shard_map/ppermute | solution.py:554
  9.9 5.5 %collective-permute-start.3 = (f32[8,24,128]{2,1,0:T(8,128)S(1)}, f32[8,24,128]{2,1,0:T(8,128)S(1)}, u32[]{:S(2)}, u32[]{:S(2)}) collective-permute-start(f32[8,24,128]{2,1,0:T(8,128)S(1)} %get-tuple-element.53), channel_id=1, source_target_pairs={{0,24},{8,16},{16,8},{24,0},{1,25},{9,17},{17,9},{25,1},{2,26},{10... | collective-permute-start | bytes 294920 | tf_op jit(solution)/shard_map/ppermute | solution.py:554
  15.5 6.0 %collective-permute-start.4 = (f32[2,2,24,128]{3,2,1,0:T(8,128)S(1)}, f32[2,2,24,128]{3,2,1,0:T(8,128)S(1)}, u32[]{:S(2)}, u32[]{:S(2)}) collective-permute-start(f32[2,2,24,128]{3,2,1,0:T(8,128)S(1)} %get-tuple-element.56), channel_id=1, source_target_pairs={{0,7},{1,2},{2,1},{3,4},{4,3},{5,6},{6,5},{7,0},{8,15},{9,10},{10,... | collective-permute-start | bytes 147464 | tf_op jit(solution)/shard_map/ppermute | solution.py:554
  15.6 5.9 %collective-permute-start.5 = (f32[2,2,24,128]{3,2,1,0:T(8,128)S(1)}, f32[2,2,24,128]{3,2,1,0:T(8,128)S(1)}, u32[]{:S(2)}, u32[]{:S(2)}) collective-permute-start(f32[2,2,24,128]{3,2,1,0:T(8,128)S(1)} %get-tuple-element.57), channel_id=1, source_target_pairs={{0,1},{1,0},{2,3},{3,2},{4,5},{5,4},{6,7},{7,6},{8,9},{9,8},{10,11... | collective-permute-start | bytes 147464 | tf_op jit(solution)/shard_map/ppermute | solution.py:554
  23.0 7.2 %collective-permute-start.6 = (f32[2,136,128]{2,1,0:T(8,128)S(1)}, f32[2,136,128]{2,1,0:T(8,128)S(1)}, u32[]{:S(2)}, u32[]{:S(2)}) collective-permute-start(f32[2,136,128]{2,1,0:T(8,128)S(1)} %get-tuple-element.80), channel_id=1, source_target_pairs={{0,7},{1,2},{2,1},{3,4},{4,3},{5,6},{6,5},{7,0},{8,15},{9,10},{10,... | collective-permute-start | bytes 417800 | tf_op jit(solution)/shard_map/ppermute | solution.py:554
  25.3 5.0 %collective-permute-start.7 = (f32[2,136,128]{2,1,0:T(8,128)S(1)}, f32[2,136,128]{2,1,0:T(8,128)S(1)}, u32[]{:S(2)}, u32[]{:S(2)}) collective-permute-start(f32[2,136,128]{2,1,0:T(8,128)S(1)} %get-tuple-element.81), channel_id=1, source_target_pairs={{0,1},{1,0},{2,3},{3,2},{4,5},{5,4},{6,7},{7,6},{8,9},{9,8},{10,11... | collective-permute-start | bytes 417800 | tf_op jit(solution)/shard_map/ppermute | solution.py:554
  30.7 7.2 %collective-permute-start.8 = (f32[2,136,128]{2,1,0:T(8,128)S(1)}, f32[2,136,128]{2,1,0:T(8,128)S(1)}, u32[]{:S(2)}, u32[]{:S(2)}) collective-permute-start(f32[2,136,128]{2,1,0:T(8,128)S(1)} %get-tuple-element.86), channel_id=1, source_target_pairs={{0,7},{1,2},{2,1},{3,4},{4,3},{5,6},{6,5},{7,0},{8,15},{9,10},{10,... | collective-permute-start | bytes 417800 | tf_op jit(solution)/shard_map/ppermute | solution.py:554
  32.1 5.8 %collective-permute-start.9 = (f32[2,136,128]{2,1,0:T(8,128)S(1)}, f32[2,136,128]{2,1,0:T(8,128)S(1)}, u32[]{:S(2)}, u32[]{:S(2)}) collective-permute-start(f32[2,136,128]{2,1,0:T(8,128)S(1)} %get-tuple-element.87), channel_id=1, source_target_pairs={{0,1},{1,0},{2,3},{3,2},{4,5},{5,4},{6,7},{7,6},{8,9},{9,8},{10,11... | collective-permute-start | bytes 417800 | tf_op jit(solution)/shard_map/ppermute | solution.py:554

commit v13 on v12

--- a/solution.py
+++ b/solution.py
@@ -263,7 +263,7 @@
     out[(*index, slice(right, right + width))] = corner[1, from_row, start : start + width, :]
 
 
-def corner_kernel(rows, got_a, got_b, x_low, x_high, corner_a, corner_b):
+def corner_kernel(rows, got_a, got_b, _core, x_low, x_high, corner_a, corner_b):
     next_x = a_is_next("gx", x_first)
     x_low[...] = jnp.where(next_x, got_b[...], got_a[...])
     x_high[...] = jnp.where(next_x, got_a[...], got_b[...])
@@ -416,16 +416,42 @@
     send_rows(out, ahead, rate, to_a, to_b, open_g, cols, nz)
 
 
+def core_kernel(steps, rows, cols, nz, conc_own, mob, chem, curve, swing, conc):
+    lanes = conc.shape[2]
+    mask = face_mask(lanes, nz)
+    own = pad, pad + cols
+    for row in (0, rows + 1):
+        conc[row] = jnp.zeros(conc.shape[1:], f32)
+    for i in range(steps - 1):
+        for y in range(rows):
+            conc[1 + y, pad : pad + cols, :] = conc_own[1 + i, y]
+
+        def row(y, _):
+            for at, size in chunks(*own):
+                mob[i, y, at : at + size, :] = mobility(conc[1 + y, at : at + size, :])
+                chem_row(row_of(conc, 1 + y), set_row(chem.at[i], y), set_row(curve.at[i], y),
+                         set_row(swing.at[i], y), at, size, mask)
+            return 0
+
+        lax.fori_loop(0, rows, row, 0)
+
+
 def prepare_kernel(steps, rows, cols, nz, back, conc_own, from_a, from_b, x_low, x_high,
-                   corner_b, corner_a, mob, chem, curve, swing, *rest):
+                   corner_b, corner_a, mob_core, chem_core, curve_core, swing_core,
+                   mob, chem, curve, swing, *rest):
     *ahead, conc = rest
     places, _ = slots(steps)
     low, high = reach(cols)
     lanes = conc.shape[2]
     mask = face_mask(lanes, nz)
     place = places[1 + back]
+    own = slice(pad, pad + cols)
     for y in range(rows):
         put_own(conc, depth + y, conc_own[back, y], y, place, cols, x_low, x_high)
+        mob[depth + y, own, :] = mob_core[back - 1, y, own, :]
+        chem[1 + y, own, :] = chem_core[back - 1, y, own, :]
+        curve[1 + y, own, :] = curve_core[back - 1, y, own, :]
+        swing[1 + y, own, :] = swing_core[back - 1, y, own, :]
     for halo, corner, base in zip((from_a, from_b), (corner_a, corner_b), landings(rows, main_first)):
         for at in range(depth):
             span = pl.ds(((1 + back) * depth + at) * cols, cols)
@@ -434,20 +460,32 @@
     if ahead:
         put_ahead(ahead[0], conc_own, back + 1, x_low, x_high, places, rows, cols)
 
-    def mob_row(row, _):
+    def rim_row(y, _):
+        for at in (low - 8, pad + cols):
+            span = slice(at, at + 16)
+            mob[depth + y, span, :] = mobility(conc[depth + y, span, :])
+        for at in (low, pad + cols - 8):
+            chem_row(row_of(conc, depth + y), set_row(chem, 1 + y), set_row(curve, 1 + y),
+                     set_row(swing, 1 + y), at, 16, mask)
+        return 0
+
+    lax.fori_loop(0, rows, rim_row, 0)
+    for y, beyond in ((0, -1), (rows - 1, rows)):
+        inner = slice(pad + 8, pad + cols - 8)
+        chem[1 + y, inner, :] = chem[1 + y, inner, :] - (time_step * grad_energy) * (
+            conc[depth + beyond, inner, :]
+        )
+
+    def far_row(s, _):
+        y = s * (rows + 1) - 1
         for at, size in chunks(low - 8, high + 8):
-            c = conc[row, at : at + size, :]
-            mob[row, at : at + size, :] = mobility(c)
+            mob[depth + y, at : at + size, :] = mobility(conc[depth + y, at : at + size, :])
+        for at, size in chunks(low, high):
+            chem_row(row_of(conc, depth + y), set_row(chem, 1 + y), lambda *_: None,
+                     lambda *_: None, at, size, mask)
         return 0
 
-    def mu_row(row, _):
-        for at, size in chunks(low, high):
-            chem_row(row_of(conc, row + 1), set_row(chem, row), set_row(curve, row),
-                     set_row(swing, row), at, size, mask)
-        return 0
-
-    lax.fori_loop(0, rows + 2 * depth, mob_row, 0)
-    lax.fori_loop(0, rows + 2, mu_row, 0)
+    lax.fori_loop(0, 2, far_row, 0)
 
 
 def next_interior(rows, cols, nz, final, mob, chem, curve, swing, rate, inner, outer, before, *rest):
@@ -586,11 +624,19 @@
         cost=1,
     )
     x_a, x_b = swap(x_a, x_b, "gx", x_first)
+    whole = (steps - 1, rows, width, lanes)
+    core = call(
+        functools.partial(core_kernel, steps, rows, cols, nz),
+        [whole] * 4,
+        [field(rows + 2)],
+        conc_own,
+        cost=2,
+    )
     x_low, x_high, corner_a, corner_b = call(
         functools.partial(corner_kernel, rows),
         [(rows, total, lanes)] * 2 + [(2, depth, total, lanes)] * 2,
         [],
-        x_a, x_b,
+        x_a, x_b, core[1],
     )
     corners = swap(corner_a, corner_b, "gy", round_first)
     corner_a, corner_b = corners if main_first == round_first else corners[::-1]
@@ -617,7 +663,7 @@
             functools.partial(prepare_kernel, steps, rows, cols, nz, back),
             [field(rows + 2 * depth)] + [field(rows + 2)] * 3 + ([] if final else [both]),
             [field(rows + 2 * depth)],
-            conc_own, main_a, main_b, x_low, x_high, corner_b, corner_a,
+            conc_own, main_a, main_b, x_low, x_high, corner_b, corner_a, *core,
             cost=2,
         )
         fields, ahead = fields[:4], fields[4:]

time: 39.2 us -> 39 us (level)
  waiting for transfers between devices: 5.31 us -> 2.75 us
  Pallas kernels: 20.8 us -> 23.2 us
    pallas_call x11 -> x12, Pallas kernels: 20.8 us -> 23.2 us  [call(): pl.pallas_call(kernel, out_shape=[jax.ShapeDtypeStruct(shape, f32) for sh...]
    ppermute x5, waiting for transfers between devices: 3.22 us -> 1.37 us  [swap(): lax.ppermute(value_a, axis, pairs_a)]
    ppermute x5, waiting for transfers between devices: 2.1 us -> 1.38 us  [swap(): lax.ppermute(value_b, axis, pairs_b)]
  transfers between devices with their start and end apart: 10 -> 10, of which waited for: 3 -> 3; matrix products, arithmetic and copies ran while one was open for 0% -> 0% of each run, Pallas kernels for 41% -> 47%
where the time goes in v13:
time: 39 us; the launch traced here: 38.8 us
  Pallas kernels  23.2 us (59%)
  starting transfers between devices  12.1 us (31%)
  waiting for transfers between devices  2.75 us (7%)
  between operations  0.73 us (2%)
    pallas_call x12, Pallas kernels, call(): pl.pallas_call(kernel, out_shape=[jax.ShapeDtypeStruct(shape, f32) for sh...  23.2 us
    ppermute x5, starting transfers between devices, swap(): lax.ppermute(value_b, axis, pairs_b)  6.28 us
    ppermute x5, starting transfers between devices, swap(): lax.ppermute(value_a, axis, pairs_a)  5.85 us
    ppermute x5, waiting for transfers between devices, swap(): lax.ppermute(value_b, axis, pairs_b)  1.38 us
    ppermute x5, waiting for transfers between devices, swap(): lax.ppermute(value_a, axis, pairs_a)  1.37 us
  transfers between devices with their start and end apart: 10, of which 3 were waited for; matrix products, arithmetic and copies ran while one was open for 0% of the time, Pallas kernels for 47%

profile of v13, /device:TPU:0, one launch (start us, length us, event | category | flops | bytes accessed | tf_op | source)
XLA Modules:
  0.0 38.8 jit_solution(10085711169903804319)
XLA Ops:
  0.6 1.8 %shard_map.50 = (f32[3,1024,128]{2,1,0:T(8,128)S(1)}, f32[1024,128]{1,0:T(8,128)S(1)}, f32[512,128]{1,0:T(8,128)S(1)}, f32[1088,128]{1,0:T(8,128)S(1)}, f32[1088,128]{1,0:T(8,128)S(1)}) custom-call(f32[3,1024,128]{2,1,0:T(8,128)} %bitcast.5, f32[1024,128]{1,0:T(8,128)} %bitcast.6, f32[512,128]{1,0:T(8,128)} %bitcast.8), custom_call_target="tpu_custom_call" | custom-call | flops 2000000 | bytes 4000000 | tf_op jit(solution)/shard_map/pallas_call | solution.py:575
  2.4 0.5 %collective-permute-start = (f32[1088,128]{1,0:T(8,128)S(1)}, f32[1088,128]{1,0:T(8,128)S(1)}, u32[]{:S(2)}, u32[]{:S(2)}) collective-permute-start(f32[1088,128]{1,0:T(8,128)S(1)} %get-tuple-element.54), channel_id=1, source_target_pairs={{0,1},{1,0},{2,3},{3,2},{4,5},{5,4},{6,7},{7,6},{8,9},{9,8},{10,11... | collective-permute-start | bytes 1671176 | tf_op jit(solution)/shard_map/ppermute | solution.py:592
  2.9 4.7 %collective-permute-start.1 = (f32[1088,128]{1,0:T(8,128)S(1)}, f32[1088,128]{1,0:T(8,128)S(1)}, u32[]{:S(2)}, u32[]{:S(2)}) collective-permute-start(f32[1088,128]{1,0:T(8,128)S(1)} %get-tuple-element.55), channel_id=1, source_target_pairs={{0,7},{1,2},{2,1},{3,4},{4,3},{5,6},{6,5},{7,0},{8,15},{9,10},{10,... | collective-permute-start | bytes 1671176 | tf_op jit(solution)/shard_map/ppermute | solution.py:592
  7.6 0.7 %shard_map.51 = (f32[3,8,128,128]{3,2,1,0:T(8,128)S(1)}, f32[8,128,128]{2,1,0:T(8,128)S(1)}, f32[8,128,128]{2,1,0:T(8,128)S(1)}, f32[8,24,128]{2,1,0:T(8,128)S(1)}, f32[8,24,128]{2,1,0:T(8,128)S(1)}) custom-call(f32[3,1024,128]{2,1,0:T(8,128)S(1)} %get-tuple-element.50.conc_in, f32[1024,128]{1,0:T(8,128)S(1)} %get-tuple-element.51.adj_in, ...), custom_call_target="tpu_custom_call" | custom-call | flops 1000000 | bytes 2000000 | tf_op jit(solution)/shard_map/pallas_call | solution.py:575
  8.4 1.6 %collective-permute-start.2 = (f32[8,24,128]{2,1,0:T(8,128)S(1)}, f32[8,24,128]{2,1,0:T(8,128)S(1)}, u32[]{:S(2)}, u32[]{:S(2)}) collective-permute-start(f32[8,24,128]{2,1,0:T(8,128)S(1)} %get-tuple-element.56), channel_id=1, source_target_pairs={{0,8},{8,0},{16,24},{24,16},{1,9},{9,1},{17,25},{25,17},{2,10},{10... | collective-permute-start | bytes 294920 | tf_op jit(solution)/shard_map/ppermute | solution.py:592
  9.9 1.5 %collective-permute-start.3 = (f32[8,24,128]{2,1,0:T(8,128)S(1)}, f32[8,24,128]{2,1,0:T(8,128)S(1)}, u32[]{:S(2)}, u32[]{:S(2)}) collective-permute-start(f32[8,24,128]{2,1,0:T(8,128)S(1)} %get-tuple-element.57), channel_id=1, source_target_pairs={{0,24},{8,16},{16,8},{24,0},{1,25},{9,17},{17,9},{25,1},{2,26},{10... | collective-permute-start | bytes 294920 | tf_op jit(solution)/shard_map/ppermute | solution.py:592
  11.4 2.6 %shard_map.52 = (f32[2,8,160,128]{3,2,1,0:T(8,128)S(1)}, f32[2,8,160,128]{3,2,1,0:T(8,128)S(1)}, f32[2,8,160,128]{3,2,1,0:T(8,128)S(1)}, f32[2,8,160,128]{3,2,1,0:T(8,128)S(1)}) custom-call(f32[3,8,128,128]{3,2,1,0:T(8,128)S(1)} %get-tuple-element.53.conc_own), custom_call_target="tpu_custom_call" | custom-call | flops 2000000 | bytes 4000000 | tf_op jit(solution)/shard_map/pallas_call | solution.py:575
  14.1 0.0 collective-permute-done.2.got_a
  14.1 1.4 %collective-permute-done.3.got_b = f32[8,24,128]{2,1,0:T(8,128)S(1)} collective-permute-done((f32[8,24,128]{2,1,0:T(8,128)S(1)}, f32[8,24,128]{2,1,0:T(8,128)S(1)}, u32[]{:S(2)}, u32[]{:S(2)}) %collective-permute-start.3) | collective-permute-done | bytes 98336 | tf_op jit(solution)/shard_map/ppermute | solution.py:592
  15.5 0.1 collective-permute-start.4
  15.6 0.1 collective-permute-start.5
  15.7 4.5 %shard_map.55 = (f32[10,160,128]{2,1,0:T(8,128)S(1)}, f32[10,160,128]{2,1,0:T(8,128)S(1)}, f32[8,160,128]{2,1,0:T(8,128)S(1)}, f32[10,160,128]{2,1,0:T(8,128)S(1...) custom-call(f32[3,8,128,128]{3,2,1,0:T(8,128)S(1)} %get-tuple-elemen, ...), custom_call_target="tpu_custom_call" | custom-call | flops 3000000 | bytes 6000000 | tf_op jit(solution)/shard_map/pallas_call | solution.py:575
  20.2 1.3 %collective-permute-done.4.corner_b = f32[2,2,24,128]{3,2,1,0:T(8,128)S(1)} collective-permute-done((f32[2,2,24,128]{3,2,1,0:T(8,128)S(1)}, f32[2,2,24,128]{3,2,1,0:T(8,128)S(1)}, u32[]{:S(2)}, u32[]{:S(2)}) %collective-permute-start.4) | collective-permute-done | bytes 49184 | tf_op jit(solution)/shard_map/ppermute | solution.py:592
  21.5 0.0 collective-permute-done.5.corner_a
  21.5 0.0 collective-permute-done.from_a
  21.5 0.0 collective-permute-done.1.from_b
  21.5 1.5 %shard_map.57 = (f32[2,2,160,128]{3,2,1,0:T(8,128)S(1)}, f32[2,160,128]{2,1,0:T(8,128)S(1)}, f32[2,136,128]{2,1,0:T(8,128)S(1)}, f32[2,136,128]{2,1,0:T(8,128)S(1)}) custom-call(f32[10,160,128]{2,1,0:T(8,128)S(1)} %get-tuple-element.78.conc, f32[10,160,128]{2,1,0:T(8,128)S(1)} %get-tuple-element.79.adj, f32[8,160,128]{2,1,0:T(8,128)S(1)} %get-tuple-element.72.rate.rest_1_, ...), custom_call_target="tpu_custom_call" | custom-call | flops 2000000 | bytes 4000000 | tf_op jit(solution)/shard_map/pallas_call | solution.py:575
  23.0 2.3 %collective-permute-start.6 = (f32[2,136,128]{2,1,0:T(8,128)S(1)}, f32[2,136,128]{2,1,0:T(8,128)S(1)}, u32[]{:S(2)}, u32[]{:S(2)}) collective-permute-start(f32[2,136,128]{2,1,0:T(8,128)S(1)} %get-tuple-element.88), channel_id=1, source_target_pairs={{0,7},{1,2},{2,1},{3,4},{4,3},{5,6},{6,5},{7,0},{8,15},{9,10},{10,... | collective-permute-start | bytes 417800 | tf_op jit(solution)/shard_map/ppermute | solution.py:592
  25.3 0.0 collective-permute-start.7
  25.3 1.8 %shard_map.56 = (f32[12,160,128]{2,1,0:T(8,128)S(1)}, f32[10,160,128]{2,1,0:T(8,128)S(1)}, f32[10,160,128]{2,1,0:T(8,128)S(1)}, f32[10,160,128]{2,1,0:T(8,128)S(1)}, f32[2,2,160,128]{3,2,1,0:T(8,128)S(1)}) custom-call(f32[3,8,128,128]{3,2,1,0:T(8,128)S(1)} %get-tuple-element.53.conc_own, f32[1088,128]{1,0:T(8,128)S(1)} %collective-permute-done.from_a, ...), custom_call_target="tpu_custom_call" | custom-call | flops 2000000 | bytes 4000000 | tf_op jit(solution)/shard_map/pallas_call | solution.py:575
  27.1 3.1 %shard_map.58 = (f32[8,160,128]{2,1,0:T(8,128)S(1)}, f32[8,160,128]{2,1,0:T(8,128)S(1)}) custom-call(f32[12,160,128]{2,1,0:T(8,128)S(1)} %get-tuple-element.73.mob, f32[10,160,128]{2,1,0:T(8,128)S(1)} %get-tuple-element.74.chem, f32[10,160,128]{2,1,0:T(8,128)S(1)} %get-tuple-element.75.curve, f32[10,160,128]{2,1,0:T(8,128)S(1)} %get-tuple-element.76.swing, ...), custom_call_target="tpu_custom_call" | custom-call | flops 3000000 | bytes 6000000 | tf_op jit(solution)/shard_map/pallas_call | solution.py:575
  30.1 0.1 collective-permute-done.6.from_a
  30.2 0.0 collective-permute-done.7.from_b
  30.2 0.4 %shard_map.59 = (f32[2,2,160,128]{3,2,1,0:T(8,128)S(1)}, f32[2,136,128]{2,1,0:T(8,128)S(1)}, f32[2,136,128]{2,1,0:T(8,128)S(1)}) custom-call(f32[12,160,128]{2,1,0:T(8,128)S(1)} %get-tuple-element.73.mob, f32[10,160,128]{2,1,0:T(8,128)S(1)} %get-tuple-element.74.chem, f32[10,160,128]{2,1,0:T(8,128)S(1)} %get-tuple-element.75.curve, ...), custom_call_target="tpu_custom_call" | custom-call | flops 1000000 | bytes 2000000 | tf_op jit(solution)/shard_map/pallas_call | solution.py:575
  30.6 1.4 %collective-permute-start.8 = (f32[2,136,128]{2,1,0:T(8,128)S(1)}, f32[2,136,128]{2,1,0:T(8,128)S(1)}, u32[]{:S(2)}, u32[]{:S(2)}) collective-permute-start(f32[2,136,128]{2,1,0:T(8,128)S(1)} %get-tuple-element.94), channel_id=1, source_target_pairs={{0,7},{1,2},{2,1},{3,4},{4,3},{5,6},{6,5},{7,0},{8,15},{9,10},{10,... | collective-permute-start | bytes 417800 | tf_op jit(solution)/shard_map/ppermute | solution.py:592
  32.0 0.0 collective-permute-start.9
  32.0 1.7 %shard_map.54 = (f32[12,160,128]{2,1,0:T(8,128)S(1)}, f32[10,160,128]{2,1,0:T(8,128)S(1)}, f32[10,160,128]{2,1,0:T(8,128)S(1)}, f32[10,160,128]{2,1,0:T(8,128)S(1)}) custom-call(f32[3,8,128,128]{3,2,1,0:T(8,128)S(1)} %get-tuple-element.53.conc_own, f32[1088,128]{1,0:T(8,128)S(1)} %collective-permute-done.from_a, ...), custom_call_target="tpu_custom_call" | custom-call | flops 2000000 | bytes 4000000 | tf_op jit(solution)/shard_map/pallas_call | solution.py:575
  33.8 3.9 %shard_map.60 = (f32[8,160,128]{2,1,0:T(8,128)S(1)}, f32[1024,128]{1,0:T(8,128)S(1)}, f32[512,128]{1,0:T(8,128)}) custom-call(f32[12,160,128]{2,1,0:T(8,128)S(1)} %get-tuple-element.66.mob, f32[10,160,128]{2,1,0:T(8,128)S(1)} %get-tuple-element.67.chem, f32[10,160,128]{2,1,0:T(8,128)S(1)} %get-tuple-element.68.curve, ...), custom_call_target="tpu_custom_call" | custom-call | flops 3000000 | bytes 6000000 | tf_op jit(solution)/shard_map/pallas_call | solution.py:575
  37.7 0.0 collective-permute-done.8.from_a
  37.7 0.0 collective-permute-done.9.from_b
  37.7 1.1 %shard_map.61 = f32[1024,128]{1,0:T(8,128)} custom-call(f32[12,160,128]{2,1,0:T(8,128)S(1)} %get-tuple-element.66.mob, f32[10,160,128]{2,1,0:T(8,128)S(1)} %get-tuple-element.67.chem, f32[10,160,128]{2,1,0:T(8,128)S(1)} %get-tuple-element.68.curve, f32[10,160,128]{2,1,0:T(8,128)S(1)} %get-tuple-element.69.swing, ...), custom_call_target="tpu_custom_call" | custom-call | flops 1000000 | bytes 2000000 | tf_op jit(solution)/shard_map/pallas_call | solution.py:575
  (1 shorter events, 0.0 us)
Async XLA Ops:
  2.4 19.1 %collective-permute-start = (f32[1088,128]{1,0:T(8,128)S(1)}, f32[1088,128]{1,0:T(8,128)S(1)}, u32[]{:S(2)}, u32[]{:S(2)}) collective-permute-start(f32[1088,128]{1,0:T(8,128)S(1)} %get-tuple-element.54), channel_id=1, source_target_pairs={{0,1},{1,0},{2,3},{3,2},{4,5},{5,4},{6,7},{7,6},{8,9},{9,8},{10,11... | collective-permute-start | bytes 1671176 | tf_op jit(solution)/shard_map/ppermute | solution.py:592
  2.9 18.6 %collective-permute-start.1 = (f32[1088,128]{1,0:T(8,128)S(1)}, f32[1088,128]{1,0:T(8,128)S(1)}, u32[]{:S(2)}, u32[]{:S(2)}) collective-permute-start(f32[1088,128]{1,0:T(8,128)S(1)} %get-tuple-element.55), channel_id=1, source_target_pairs={{0,7},{1,2},{2,1},{3,4},{4,3},{5,6},{6,5},{7,0},{8,15},{9,10},{10,... | collective-permute-start | bytes 1671176 | tf_op jit(solution)/shard_map/ppermute | solution.py:592
  8.4 5.7 %collective-permute-start.2 = (f32[8,24,128]{2,1,0:T(8,128)S(1)}, f32[8,24,128]{2,1,0:T(8,128)S(1)}, u32[]{:S(2)}, u32[]{:S(2)}) collective-permute-start(f32[8,24,128]{2,1,0:T(8,128)S(1)} %get-tuple-element.56), channel_id=1, source_target_pairs={{0,8},{8,0},{16,24},{24,16},{1,9},{9,1},{17,25},{25,17},{2,10},{10... | collective-permute-start | bytes 294920 | tf_op jit(solution)/shard_map/ppermute | solution.py:592
  9.9 5.5 %collective-permute-start.3 = (f32[8,24,128]{2,1,0:T(8,128)S(1)}, f32[8,24,128]{2,1,0:T(8,128)S(1)}, u32[]{:S(2)}, u32[]{:S(2)}) collective-permute-start(f32[8,24,128]{2,1,0:T(8,128)S(1)} %get-tuple-element.57), channel_id=1, source_target_pairs={{0,24},{8,16},{16,8},{24,0},{1,25},{9,17},{17,9},{25,1},{2,26},{10... | collective-permute-start | bytes 294920 | tf_op jit(solution)/shard_map/ppermute | solution.py:592
  15.5 6.0 %collective-permute-start.4 = (f32[2,2,24,128]{3,2,1,0:T(8,128)S(1)}, f32[2,2,24,128]{3,2,1,0:T(8,128)S(1)}, u32[]{:S(2)}, u32[]{:S(2)}) collective-permute-start(f32[2,2,24,128]{3,2,1,0:T(8,128)S(1)} %get-tuple-element.61), channel_id=1, source_target_pairs={{0,7},{1,2},{2,1},{3,4},{4,3},{5,6},{6,5},{7,0},{8,15},{9,10},{10,... | collective-permute-start | bytes 147464 | tf_op jit(solution)/shard_map/ppermute | solution.py:592
  15.6 5.9 %collective-permute-start.5 = (f32[2,2,24,128]{3,2,1,0:T(8,128)S(1)}, f32[2,2,24,128]{3,2,1,0:T(8,128)S(1)}, u32[]{:S(2)}, u32[]{:S(2)}) collective-permute-start(f32[2,2,24,128]{3,2,1,0:T(8,128)S(1)} %get-tuple-element.62), channel_id=1, source_target_pairs={{0,1},{1,0},{2,3},{3,2},{4,5},{5,4},{6,7},{7,6},{8,9},{9,8},{10,11... | collective-permute-start | bytes 147464 | tf_op jit(solution)/shard_map/ppermute | solution.py:592
  23.0 7.2 %collective-permute-start.6 = (f32[2,136,128]{2,1,0:T(8,128)S(1)}, f32[2,136,128]{2,1,0:T(8,128)S(1)}, u32[]{:S(2)}, u32[]{:S(2)}) collective-permute-start(f32[2,136,128]{2,1,0:T(8,128)S(1)} %get-tuple-element.88), channel_id=1, source_target_pairs={{0,7},{1,2},{2,1},{3,4},{4,3},{5,6},{6,5},{7,0},{8,15},{9,10},{10,... | collective-permute-start | bytes 417800 | tf_op jit(solution)/shard_map/ppermute | solution.py:592
  25.3 4.9 %collective-permute-start.7 = (f32[2,136,128]{2,1,0:T(8,128)S(1)}, f32[2,136,128]{2,1,0:T(8,128)S(1)}, u32[]{:S(2)}, u32[]{:S(2)}) collective-permute-start(f32[2,136,128]{2,1,0:T(8,128)S(1)} %get-tuple-element.89), channel_id=1, source_target_pairs={{0,1},{1,0},{2,3},{3,2},{4,5},{5,4},{6,7},{7,6},{8,9},{9,8},{10,11... | collective-permute-start | bytes 417800 | tf_op jit(solution)/shard_map/ppermute | solution.py:592
  30.6 7.1 %collective-permute-start.8 = (f32[2,136,128]{2,1,0:T(8,128)S(1)}, f32[2,136,128]{2,1,0:T(8,128)S(1)}, u32[]{:S(2)}, u32[]{:S(2)}) collective-permute-start(f32[2,136,128]{2,1,0:T(8,128)S(1)} %get-tuple-element.94), channel_id=1, source_target_pairs={{0,7},{1,2},{2,1},{3,4},{4,3},{5,6},{6,5},{7,0},{8,15},{9,10},{10,... | collective-permute-start | bytes 417800 | tf_op jit(solution)/shard_map/ppermute | solution.py:592
  32.0 5.6 %collective-permute-start.9 = (f32[2,136,128]{2,1,0:T(8,128)S(1)}, f32[2,136,128]{2,1,0:T(8,128)S(1)}, u32[]{:S(2)}, u32[]{:S(2)}) collective-permute-start(f32[2,136,128]{2,1,0:T(8,128)S(1)} %get-tuple-element.95), channel_id=1, source_target_pairs={{0,1},{1,0},{2,3},{3,2},{4,5},{5,4},{6,7},{7,6},{8,9},{9,8},{10,11... | collective-permute-start | bytes 417800 | tf_op jit(solution)/shard_map/ppermute | solution.py:592

commit v14 on v13

--- a/solution.py
+++ b/solution.py
@@ -128,7 +128,7 @@
 
 
 def all_rows(rows, cols, nz, adj, mob, mob_skip, chem, curve, swing, rate, before, pot, part, out,
-             grad):
+             grad, between=None):
     low, high = reach(cols)
     mask = face_mask(adj.shape[2], nz)
 
@@ -155,8 +155,10 @@
 
     for row in (0, rows + 1):
         pot[row] = jnp.zeros(pot.shape[1:], f32)
-    lax.fori_loop(0, rows, body, 0)
-    lax.fori_loop(0, rows, close, 0)
+    lax.fori_loop(0, rows, body, 0, unroll=2)
+    if between is not None:
+        between()
+    lax.fori_loop(0, rows, close, 0, unroll=4)
 
 
 def a_is_next(axis, first):
@@ -300,8 +302,8 @@
                      set_row(swing, row), at, size, mask)
         return 0
 
-    lax.fori_loop(1, rows + 1, mob_row, 0)
-    lax.fori_loop(1, rows + 1, mu_row, 0)
+    lax.fori_loop(1, rows + 1, mob_row, 0, unroll=4)
+    lax.fori_loop(1, rows + 1, mu_row, 0, unroll=2)
     all_rows(rows, cols, nz, adj, mob, 1, chem, curve, swing, rate, None, pot, part, out, grad)
 
 
@@ -433,7 +435,7 @@
                          set_row(swing.at[i], y), at, size, mask)
             return 0
 
-        lax.fori_loop(0, rows, row, 0)
+        lax.fori_loop(0, rows, row, 0, unroll=2)
 
 
 def prepare_kernel(steps, rows, cols, nz, back, conc_own, from_a, from_b, x_low, x_high,
@@ -460,37 +462,31 @@
     if ahead:
         put_ahead(ahead[0], conc_own, back + 1, x_low, x_high, places, rows, cols)
 
-    def rim_row(y, _):
+    for y in range(rows):
         for at in (low - 8, pad + cols):
             span = slice(at, at + 16)
             mob[depth + y, span, :] = mobility(conc[depth + y, span, :])
         for at in (low, pad + cols - 8):
             chem_row(row_of(conc, depth + y), set_row(chem, 1 + y), set_row(curve, 1 + y),
                      set_row(swing, 1 + y), at, 16, mask)
-        return 0
-
-    lax.fori_loop(0, rows, rim_row, 0)
     for y, beyond in ((0, -1), (rows - 1, rows)):
         inner = slice(pad + 8, pad + cols - 8)
         chem[1 + y, inner, :] = chem[1 + y, inner, :] - (time_step * grad_energy) * (
             conc[depth + beyond, inner, :]
         )
 
-    def far_row(s, _):
-        y = s * (rows + 1) - 1
+    for y in (-1, rows):
         for at, size in chunks(low - 8, high + 8):
             mob[depth + y, at : at + size, :] = mobility(conc[depth + y, at : at + size, :])
         for at, size in chunks(low, high):
             chem_row(row_of(conc, depth + y), set_row(chem, 1 + y), lambda *_: None,
                      lambda *_: None, at, size, mask)
-        return 0
-
-    lax.fori_loop(0, 2, far_row, 0)
 
 
 def next_interior(rows, cols, nz, final, mob, chem, curve, swing, rate, inner, outer, before, *rest):
     if final:
-        out, tiles, grad_out, adj, pot, part, grad = rest
+        out, tiles, grad_out, adj, pot, part, grad, turned, sem = rest
+        send = pltpu.make_async_copy(turned, grad_out, sem)
     else:
         edge_before, out, grad, adj, pot, part, sums = rest
         for y in range(rows):
@@ -505,13 +501,18 @@
         adj[1 + y] = outer[s, k]
     adj[0] = outer[0, 0]
     adj[1 + rows] = outer[1, 0]
+
+    def send_grad():
+        for y in range(rows):
+            turned[pl.ds(y, nz, stride=rows), :] = fold(grad[y, pad : pad + cols, :].T, nz)
+        send.start()
+
     all_rows(rows, cols, nz, adj, mob, depth, chem, curve, swing, rate, before, pot, part, out,
-             grad)
+             grad, send_grad if final else None)
     if final:
-        for y in range(rows):
-            grad_out[pl.ds(y, nz, stride=rows), :] = fold(grad[y, pad : pad + cols, :].T, nz)
         for y in range(depth, rows - depth):
             tiles[pl.ds(y, lanes, stride=rows), :] = out[y, pad : pad + cols, :].T
+        send.wait()
 
 
 def fold(value, nz):
@@ -568,7 +569,7 @@
         send_rows(result, ahead, rate, to_a, to_b, open_g, cols, nz)
 
 
-def call(kernel, outs, scratch, *operands, cost=0, far=False):
+def call(kernel, outs, scratch, *operands, cost=0, far=False, far_outs=()):
     if far:
         operands = [pltpu.with_memory_space_constraint(value, pltpu.HBM) for value in operands]
     space = pl.ANY if far else pltpu.VMEM
@@ -576,7 +577,10 @@
         kernel,
         out_shape=[jax.ShapeDtypeStruct(shape, f32) for shape in outs],
         in_specs=[pl.BlockSpec(memory_space=space)] * len(operands),
-        out_specs=[pl.BlockSpec(memory_space=pltpu.VMEM)] * len(outs),
+        out_specs=[
+            pl.BlockSpec(memory_space=pltpu.HBM if i in far_outs else pltpu.VMEM)
+            for i in range(len(outs))
+        ],
         scratch_shapes=[pltpu.VMEM(s, f32) if isinstance(s, tuple) else s for s in scratch],
         compiler_params=pltpu.CompilerParams(vmem_limit_bytes=vmem_limit),
         cost_estimate=pl.CostEstimate(
@@ -672,9 +676,10 @@
             inner, tiles, grad = call(
                 functools.partial(next_interior, rows, cols, nz, final),
                 [field(rows), (flat, cols), (nz * rows, cols)],
-                work,
+                work + [(nz * rows, cols), pltpu.SemaphoreType.DMA],
                 *fields, rate, inner, outer, *sums,
                 cost=3,
+                far_outs=(2,),
             )
             (adj,) = call(
                 functools.partial(next_boundary, rows, cols, nz, final),

time: 39 us -> 37.8 us (0.969)
  Pallas kernels: 23.2 us -> 16.1 us
  waiting for transfers between devices: 2.75 us -> 9.75 us
  starting transfers between devices: 12.1 us -> 11 us
    pallas_call x12, Pallas kernels: 23.2 us -> 16.1 us  [call(): pl.pallas_call(kernel, out_shape=[jax.ShapeDtypeStruct(shape, f32) for sh...]
    ppermute x5, waiting for transfers between devices: 1.37 us -> 7.65 us  [swap(): lax.ppermute(value_a, axis, pairs_a)]
    ppermute x5, starting transfers between devices: 5.85 us -> 4.73 us  [swap(): lax.ppermute(value_a, axis, pairs_a)]
    ppermute x5, waiting for transfers between devices: 1.38 us -> 2.1 us  [swap(): lax.ppermute(value_b, axis, pairs_b)]
  transfers between devices with their start and end apart: 10 -> 10, of which waited for: 3 -> 5; matrix products, arithmetic and copies ran while one was open for 0% -> 0% of each run, Pallas kernels for 47% -> 30%
where the time goes in v14:
time: 37.8 us; the launch traced here: 37.6 us
  Pallas kernels  16.1 us (43%)
  starting transfers between devices  11 us (29%)
  waiting for transfers between devices  9.75 us (26%)
  between operations  0.72 us (2%)
    pallas_call x12, Pallas kernels, call(): pl.pallas_call(kernel, out_shape=[jax.ShapeDtypeStruct(shape, f32) for sh...  16.1 us
    ppermute x5, waiting for transfers between devices, swap(): lax.ppermute(value_a, axis, pairs_a)  7.65 us
    ppermute x5, starting transfers between devices, swap(): lax.ppermute(value_b, axis, pairs_b)  6.28 us
    ppermute x5, starting transfers between devices, swap(): lax.ppermute(value_a, axis, pairs_a)  4.73 us
    ppermute x5, waiting for transfers between devices, swap(): lax.ppermute(value_b, axis, pairs_b)  2.1 us
  transfers between devices with their start and end apart: 10, of which 5 were waited for; matrix products, arithmetic and copies ran while one was open for 0% of the time, Pallas kernels for 30%

profile of v14, /device:TPU:0, one launch (start us, length us, event | category | flops | bytes accessed | tf_op | source)
XLA Modules:
  0.0 37.6 jit_solution(14980242868931480421)
XLA Ops:
  0.6 1.8 %shard_map.50 = (f32[3,1024,128]{2,1,0:T(8,128)S(1)}, f32[1024,128]{1,0:T(8,128)S(1)}, f32[512,128]{1,0:T(8,128)S(1)}, f32[1088,128]{1,0:T(8,128)S(1)}, f32[1088,128]{1,0:T(8,128)S(1)}) custom-call(f32[3,1024,128]{2,1,0:T(8,128)} %bitcast.5, f32[1024,128]{1,0:T(8,128)} %bitcast.6, f32[512,128]{1,0:T(8,128)} %bitcast.8), custom_call_target="tpu_custom_call" | custom-call | flops 2000000 | bytes 4000000 | tf_op jit(solution)/shard_map/pallas_call | solution.py:576
  2.4 0.5 %collective-permute-start = (f32[1088,128]{1,0:T(8,128)S(1)}, f32[1088,128]{1,0:T(8,128)S(1)}, u32[]{:S(2)}, u32[]{:S(2)}) collective-permute-start(f32[1088,128]{1,0:T(8,128)S(1)} %get-tuple-element.54), channel_id=1, source_target_pairs={{0,1},{1,0},{2,3},{3,2},{4,5},{5,4},{6,7},{7,6},{8,9},{9,8},{10,11... | collective-permute-start | bytes 1671176 | tf_op jit(solution)/shard_map/ppermute | solution.py:596
  2.9 4.7 %collective-permute-start.1 = (f32[1088,128]{1,0:T(8,128)S(1)}, f32[1088,128]{1,0:T(8,128)S(1)}, u32[]{:S(2)}, u32[]{:S(2)}) collective-permute-start(f32[1088,128]{1,0:T(8,128)S(1)} %get-tuple-element.55), channel_id=1, source_target_pairs={{0,7},{1,2},{2,1},{3,4},{4,3},{5,6},{6,5},{7,0},{8,15},{9,10},{10,... | collective-permute-start | bytes 1671176 | tf_op jit(solution)/shard_map/ppermute | solution.py:596
  7.6 0.7 %shard_map.51 = (f32[3,8,128,128]{3,2,1,0:T(8,128)S(1)}, f32[8,128,128]{2,1,0:T(8,128)S(1)}, f32[8,128,128]{2,1,0:T(8,128)S(1)}, f32[8,24,128]{2,1,0:T(8,128)S(1)}, f32[8,24,128]{2,1,0:T(8,128)S(1)}) custom-call(f32[3,1024,128]{2,1,0:T(8,128)S(1)} %get-tuple-element.50.conc_in, f32[1024,128]{1,0:T(8,128)S(1)} %get-tuple-element.51.adj_in, ...), custom_call_target="tpu_custom_call" | custom-call | flops 1000000 | bytes 2000000 | tf_op jit(solution)/shard_map/pallas_call | solution.py:576
  8.4 1.6 %collective-permute-start.2 = (f32[8,24,128]{2,1,0:T(8,128)S(1)}, f32[8,24,128]{2,1,0:T(8,128)S(1)}, u32[]{:S(2)}, u32[]{:S(2)}) collective-permute-start(f32[8,24,128]{2,1,0:T(8,128)S(1)} %get-tuple-element.56), channel_id=1, source_target_pairs={{0,8},{8,0},{16,24},{24,16},{1,9},{9,1},{17,25},{25,17},{2,10},{10... | collective-permute-start | bytes 294920 | tf_op jit(solution)/shard_map/ppermute | solution.py:596
  9.9 1.5 %collective-permute-start.3 = (f32[8,24,128]{2,1,0:T(8,128)S(1)}, f32[8,24,128]{2,1,0:T(8,128)S(1)}, u32[]{:S(2)}, u32[]{:S(2)}) collective-permute-start(f32[8,24,128]{2,1,0:T(8,128)S(1)} %get-tuple-element.57), channel_id=1, source_target_pairs={{0,24},{8,16},{16,8},{24,0},{1,25},{9,17},{17,9},{25,1},{2,26},{10... | collective-permute-start | bytes 294920 | tf_op jit(solution)/shard_map/ppermute | solution.py:596
  11.4 1.5 %shard_map.52 = (f32[2,8,160,128]{3,2,1,0:T(8,128)S(1)}, f32[2,8,160,128]{3,2,1,0:T(8,128)S(1)}, f32[2,8,160,128]{3,2,1,0:T(8,128)S(1)}, f32[2,8,160,128]{3,2,1,0:T(8,128)S(1)}) custom-call(f32[3,8,128,128]{3,2,1,0:T(8,128)S(1)} %get-tuple-element.53.conc_own), custom_call_target="tpu_custom_call" | custom-call | flops 2000000 | bytes 4000000 | tf_op jit(solution)/shard_map/pallas_call | solution.py:576
  13.0 0.4 %collective-permute-done.2.got_a = f32[8,24,128]{2,1,0:T(8,128)S(1)} collective-permute-done((f32[8,24,128]{2,1,0:T(8,128)S(1)}, f32[8,24,128]{2,1,0:T(8,128)S(1)}, u32[]{:S(2)}, u32[]{:S(2)}) %collective-permute-start.2) | collective-permute-done | bytes 98336 | tf_op jit(solution)/shard_map/ppermute | solution.py:596
  13.4 2.1 %collective-permute-done.3.got_b = f32[8,24,128]{2,1,0:T(8,128)S(1)} collective-permute-done((f32[8,24,128]{2,1,0:T(8,128)S(1)}, f32[8,24,128]{2,1,0:T(8,128)S(1)}, u32[]{:S(2)}, u32[]{:S(2)}) %collective-permute-start.3) | collective-permute-done | bytes 98336 | tf_op jit(solution)/shard_map/ppermute | solution.py:596
  15.5 0.1 collective-permute-start.4
  15.6 0.1 collective-permute-start.5
  15.7 3.2 %shard_map.55 = (f32[10,160,128]{2,1,0:T(8,128)S(1)}, f32[10,160,128]{2,1,0:T(8,128)S(1)}, f32[8,160,128]{2,1,0:T(8,128)S(1)}, f32[10,160,128]{2,1,0:T(8,128)S(1...) custom-call(f32[3,8,128,128]{3,2,1,0:T(8,128)S(1)} %get-tuple-elemen, ...), custom_call_target="tpu_custom_call" | custom-call | flops 3000000 | bytes 6000000 | tf_op jit(solution)/shard_map/pallas_call | solution.py:576
  18.9 2.6 %collective-permute-done.4.corner_b = f32[2,2,24,128]{3,2,1,0:T(8,128)S(1)} collective-permute-done((f32[2,2,24,128]{3,2,1,0:T(8,128)S(1)}, f32[2,2,24,128]{3,2,1,0:T(8,128)S(1)}, u32[]{:S(2)}, u32[]{:S(2)}) %collective-permute-start.4) | collective-permute-done | bytes 49184 | tf_op jit(solution)/shard_map/ppermute | solution.py:596
  21.5 0.0 collective-permute-done.5.corner_a
  21.5 0.0 collective-permute-done.from_a
  21.5 0.0 collective-permute-done.1.from_b
  21.5 1.5 %shard_map.57 = (f32[2,2,160,128]{3,2,1,0:T(8,128)S(1)}, f32[2,160,128]{2,1,0:T(8,128)S(1)}, f32[2,136,128]{2,1,0:T(8,128)S(1)}, f32[2,136,128]{2,1,0:T(8,128)S(1)}) custom-call(f32[10,160,128]{2,1,0:T(8,128)S(1)} %get-tuple-element.78.conc, f32[10,160,128]{2,1,0:T(8,128)S(1)} %get-tuple-element.79.adj, f32[8,160,128]{2,1,0:T(8,128)S(1)} %get-tuple-element.72.rate.rest_1_, ...), custom_call_target="tpu_custom_call" | custom-call | flops 2000000 | bytes 4000000 | tf_op jit(solution)/shard_map/pallas_call | solution.py:576
  23.0 1.5 %collective-permute-start.6 = (f32[2,136,128]{2,1,0:T(8,128)S(1)}, f32[2,136,128]{2,1,0:T(8,128)S(1)}, u32[]{:S(2)}, u32[]{:S(2)}) collective-permute-start(f32[2,136,128]{2,1,0:T(8,128)S(1)} %get-tuple-element.88), channel_id=1, source_target_pairs={{0,7},{1,2},{2,1},{3,4},{4,3},{5,6},{6,5},{7,0},{8,15},{9,10},{10,... | collective-permute-start | bytes 417800 | tf_op jit(solution)/shard_map/ppermute | solution.py:596
  24.5 0.0 collective-permute-start.7
  24.5 0.5 %shard_map.56 = (f32[12,160,128]{2,1,0:T(8,128)S(1)}, f32[10,160,128]{2,1,0:T(8,128)S(1)}, f32[10,160,128]{2,1,0:T(8,128)S(1)}, f32[10,160,128]{2,1,0:T(8,128)S(1)}, f32[2,2,160,128]{3,2,1,0:T(8,128)S(1)}) custom-call(f32[3,8,128,128]{3,2,1,0:T(8,128)S(1)} %get-tuple-element.53.conc_own, f32[1088,128]{1,0:T(8,128)S(1)} %collective-permute-done.from_a, ...), custom_call_target="tpu_custom_call" | custom-call | flops 2000000 | bytes 4000000 | tf_op jit(solution)/shard_map/pallas_call | solution.py:576
  25.0 2.3 %shard_map.58 = (f32[8,160,128]{2,1,0:T(8,128)S(1)}, f32[8,160,128]{2,1,0:T(8,128)S(1)}) custom-call(f32[12,160,128]{2,1,0:T(8,128)S(1)} %get-tuple-element.73.mob, f32[10,160,128]{2,1,0:T(8,128)S(1)} %get-tuple-element.74.chem, f32[10,160,128]{2,1,0:T(8,128)S(1)} %get-tuple-element.75.curve, f32[10,160,128]{2,1,0:T(8,128)S(1)} %get-tuple-element.76.swing, ...), custom_call_target="tpu_custom_call" | custom-call | flops 3000000 | bytes 6000000 | tf_op jit(solution)/shard_map/pallas_call | solution.py:576
  27.3 2.4 %collective-permute-done.6.from_a = f32[2,136,128]{2,1,0:T(8,128)S(1)} collective-permute-done((f32[2,136,128]{2,1,0:T(8,128)S(1)}, f32[2,136,128]{2,1,0:T(8,128)S(1)}, u32[]{:S(2)}, u32[]{:S(2)}) %collective-permute-start.6) | collective-permute-done | bytes 139296 | tf_op jit(solution)/shard_map/ppermute | solution.py:596
  29.8 0.0 collective-permute-done.7.from_b
  29.8 0.4 %shard_map.59 = (f32[2,2,160,128]{3,2,1,0:T(8,128)S(1)}, f32[2,136,128]{2,1,0:T(8,128)S(1)}, f32[2,136,128]{2,1,0:T(8,128)S(1)}) custom-call(f32[12,160,128]{2,1,0:T(8,128)S(1)} %get-tuple-element.73.mob, f32[10,160,128]{2,1,0:T(8,128)S(1)} %get-tuple-element.74.chem, f32[10,160,128]{2,1,0:T(8,128)S(1)} %get-tuple-element.75.curve, ...), custom_call_target="tpu_custom_call" | custom-call | flops 1000000 | bytes 2000000 | tf_op jit(solution)/shard_map/pallas_call | solution.py:576
  30.2 1.1 %collective-permute-start.8 = (f32[2,136,128]{2,1,0:T(8,128)S(1)}, f32[2,136,128]{2,1,0:T(8,128)S(1)}, u32[]{:S(2)}, u32[]{:S(2)}) collective-permute-start(f32[2,136,128]{2,1,0:T(8,128)S(1)} %get-tuple-element.94), channel_id=1, source_target_pairs={{0,7},{1,2},{2,1},{3,4},{4,3},{5,6},{6,5},{7,0},{8,15},{9,10},{10,... | collective-permute-start | bytes 417800 | tf_op jit(solution)/shard_map/ppermute | solution.py:596
  31.2 0.0 collective-permute-start.9
  31.3 0.4 %shard_map.54 = (f32[12,160,128]{2,1,0:T(8,128)S(1)}, f32[10,160,128]{2,1,0:T(8,128)S(1)}, f32[10,160,128]{2,1,0:T(8,128)S(1)}, f32[10,160,128]{2,1,0:T(8,128)S(1)}) custom-call(f32[3,8,128,128]{3,2,1,0:T(8,128)S(1)} %get-tuple-element.53.conc_own, f32[1088,128]{1,0:T(8,128)S(1)} %collective-permute-done.from_a, ...), custom_call_target="tpu_custom_call" | custom-call | flops 2000000 | bytes 4000000 | tf_op jit(solution)/shard_map/pallas_call | solution.py:576
  31.7 2.6 %shard_map.60 = (f32[8,160,128]{2,1,0:T(8,128)S(1)}, f32[1024,128]{1,0:T(8,128)S(1)}, f32[512,128]{1,0:T(8,128)}) custom-call(f32[12,160,128]{2,1,0:T(8,128)S(1)} %get-tuple-element.66.mob, f32[10,160,128]{2,1,0:T(8,128)S(1)} %get-tuple-element.67.chem, f32[10,160,128]{2,1,0:T(8,128)S(1)} %get-tuple-element.68.curve, ...), custom_call_target="tpu_custom_call" | custom-call | flops 3000000 | bytes 6000000 | tf_op jit(solution)/shard_map/pallas_call | solution.py:576
  34.3 2.2 %collective-permute-done.8.from_a = f32[2,136,128]{2,1,0:T(8,128)S(1)} collective-permute-done((f32[2,136,128]{2,1,0:T(8,128)S(1)}, f32[2,136,128]{2,1,0:T(8,128)S(1)}, u32[]{:S(2)}, u32[]{:S(2)}) %collective-permute-start.8) | collective-permute-done | bytes 139296 | tf_op jit(solution)/shard_map/ppermute | solution.py:596
  36.5 0.0 collective-permute-done.9.from_b
  36.5 1.1 %shard_map.61 = f32[1024,128]{1,0:T(8,128)} custom-call(f32[12,160,128]{2,1,0:T(8,128)S(1)} %get-tuple-element.66.mob, f32[10,160,128]{2,1,0:T(8,128)S(1)} %get-tuple-element.67.chem, f32[10,160,128]{2,1,0:T(8,128)S(1)} %get-tuple-element.68.curve, f32[10,160,128]{2,1,0:T(8,128)S(1)} %get-tuple-element.69.swing, ...), custom_call_target="tpu_custom_call" | custom-call | flops 1000000 | bytes 2000000 | tf_op jit(solution)/shard_map/pallas_call | solution.py:576
  (1 shorter events, 0.0 us)
Async XLA Ops:
  2.4 19.1 %collective-permute-start = (f32[1088,128]{1,0:T(8,128)S(1)}, f32[1088,128]{1,0:T(8,128)S(1)}, u32[]{:S(2)}, u32[]{:S(2)}) collective-permute-start(f32[1088,128]{1,0:T(8,128)S(1)} %get-tuple-element.54), channel_id=1, source_target_pairs={{0,1},{1,0},{2,3},{3,2},{4,5},{5,4},{6,7},{7,6},{8,9},{9,8},{10,11... | collective-permute-start | bytes 1671176 | tf_op jit(solution)/shard_map/ppermute | solution.py:596
  2.9 18.6 %collective-permute-start.1 = (f32[1088,128]{1,0:T(8,128)S(1)}, f32[1088,128]{1,0:T(8,128)S(1)}, u32[]{:S(2)}, u32[]{:S(2)}) collective-permute-start(f32[1088,128]{1,0:T(8,128)S(1)} %get-tuple-element.55), channel_id=1, source_target_pairs={{0,7},{1,2},{2,1},{3,4},{4,3},{5,6},{6,5},{7,0},{8,15},{9,10},{10,... | collective-permute-start | bytes 1671176 | tf_op jit(solution)/shard_map/ppermute | solution.py:596
  8.4 5.0 %collective-permute-start.2 = (f32[8,24,128]{2,1,0:T(8,128)S(1)}, f32[8,24,128]{2,1,0:T(8,128)S(1)}, u32[]{:S(2)}, u32[]{:S(2)}) collective-permute-start(f32[8,24,128]{2,1,0:T(8,128)S(1)} %get-tuple-element.56), channel_id=1, source_target_pairs={{0,8},{8,0},{16,24},{24,16},{1,9},{9,1},{17,25},{25,17},{2,10},{10... | collective-permute-start | bytes 294920 | tf_op jit(solution)/shard_map/ppermute | solution.py:596
  9.9 5.5 %collective-permute-start.3 = (f32[8,24,128]{2,1,0:T(8,128)S(1)}, f32[8,24,128]{2,1,0:T(8,128)S(1)}, u32[]{:S(2)}, u32[]{:S(2)}) collective-permute-start(f32[8,24,128]{2,1,0:T(8,128)S(1)} %get-tuple-element.57), channel_id=1, source_target_pairs={{0,24},{8,16},{16,8},{24,0},{1,25},{9,17},{17,9},{25,1},{2,26},{10... | collective-permute-start | bytes 294920 | tf_op jit(solution)/shard_map/ppermute | solution.py:596
  15.5 6.0 %collective-permute-start.4 = (f32[2,2,24,128]{3,2,1,0:T(8,128)S(1)}, f32[2,2,24,128]{3,2,1,0:T(8,128)S(1)}, u32[]{:S(2)}, u32[]{:S(2)}) collective-permute-start(f32[2,2,24,128]{3,2,1,0:T(8,128)S(1)} %get-tuple-element.61), channel_id=1, source_target_pairs={{0,7},{1,2},{2,1},{3,4},{4,3},{5,6},{6,5},{7,0},{8,15},{9,10},{10,... | collective-permute-start | bytes 147464 | tf_op jit(solution)/shard_map/ppermute | solution.py:596
  15.6 5.9 %collective-permute-start.5 = (f32[2,2,24,128]{3,2,1,0:T(8,128)S(1)}, f32[2,2,24,128]{3,2,1,0:T(8,128)S(1)}, u32[]{:S(2)}, u32[]{:S(2)}) collective-permute-start(f32[2,2,24,128]{3,2,1,0:T(8,128)S(1)} %get-tuple-element.62), channel_id=1, source_target_pairs={{0,1},{1,0},{2,3},{3,2},{4,5},{5,4},{6,7},{7,6},{8,9},{9,8},{10,11... | collective-permute-start | bytes 147464 | tf_op jit(solution)/shard_map/ppermute | solution.py:596
  23.0 6.7 %collective-permute-start.6 = (f32[2,136,128]{2,1,0:T(8,128)S(1)}, f32[2,136,128]{2,1,0:T(8,128)S(1)}, u32[]{:S(2)}, u32[]{:S(2)}) collective-permute-start(f32[2,136,128]{2,1,0:T(8,128)S(1)} %get-tuple-element.88), channel_id=1, source_target_pairs={{0,7},{1,2},{2,1},{3,4},{4,3},{5,6},{6,5},{7,0},{8,15},{9,10},{10,... | collective-permute-start | bytes 417800 | tf_op jit(solution)/shard_map/ppermute | solution.py:596
  24.5 5.3 %collective-permute-start.7 = (f32[2,136,128]{2,1,0:T(8,128)S(1)}, f32[2,136,128]{2,1,0:T(8,128)S(1)}, u32[]{:S(2)}, u32[]{:S(2)}) collective-permute-start(f32[2,136,128]{2,1,0:T(8,128)S(1)} %get-tuple-element.89), channel_id=1, source_target_pairs={{0,1},{1,0},{2,3},{3,2},{4,5},{5,4},{6,7},{7,6},{8,9},{9,8},{10,11... | collective-permute-start | bytes 417800 | tf_op jit(solution)/shard_map/ppermute | solution.py:596
  30.2 6.3 %collective-permute-start.8 = (f32[2,136,128]{2,1,0:T(8,128)S(1)}, f32[2,136,128]{2,1,0:T(8,128)S(1)}, u32[]{:S(2)}, u32[]{:S(2)}) collective-permute-start(f32[2,136,128]{2,1,0:T(8,128)S(1)} %get-tuple-element.94), channel_id=1, source_target_pairs={{0,7},{1,2},{2,1},{3,4},{4,3},{5,6},{6,5},{7,0},{8,15},{9,10},{10,... | collective-permute-start | bytes 417800 | tf_op jit(solution)/shard_map/ppermute | solution.py:596
  31.2 5.3 %collective-permute-start.9 = (f32[2,136,128]{2,1,0:T(8,128)S(1)}, f32[2,136,128]{2,1,0:T(8,128)S(1)}, u32[]{:S(2)}, u32[]{:S(2)}) collective-permute-start(f32[2,136,128]{2,1,0:T(8,128)S(1)} %get-tuple-element.95), channel_id=1, source_target_pairs={{0,1},{1,0},{2,3},{3,2},{4,5},{5,4},{6,7},{7,6},{8,9},{9,8},{10,11... | collective-permute-start | bytes 417800 | tf_op jit(solution)/shard_map/ppermute | solution.py:596

commit v15 on v14

--- a/solution.py
+++ b/solution.py
@@ -16,6 +16,7 @@
 pad = 16
 chunk = 72
 depth = 2
+early = 2
 x_first, main_first, round_first = 0, 0, 1
 vmem_limit = 20 * 1024 * 1024
 f32 = jnp.float32
@@ -186,28 +187,43 @@
     lanes = main_a.shape[1]
     half = cols // 2
     lower = lax.broadcasted_iota(jnp.int32, (half, lanes), 1) < nz
-    copies = [
-        pltpu.make_async_copy(adj_hbm, adj_in, sems.at[0]),
-        pltpu.make_async_copy(rate_hbm, rate_in, sems.at[1]),
-    ] + [
-        pltpu.make_async_copy(conc_hbm.at[steps - 1 - back], conc_in.at[back], sems.at[2 + back])
-        for back in range(steps)
+    fetches = [(adj_hbm, adj_in), (rate_hbm, rate_in)] + [
+        (conc_hbm.at[steps - 1 - back], conc_in.at[back]) for back in range(steps)
     ]
-    for copy in copies:
-        copy.start()
-    copies[0].wait()
+    copies = []
+    for i, (there, here) in enumerate(fetches):
+        part = here.shape[0] // 2
+        copies.append(
+            [
+                pltpu.make_async_copy(
+                    there.at[pl.ds(k * part, part)], here.at[pl.ds(k * part, part)], sems.at[i, k]
+                )
+                for k in range(2)
+            ]
+        )
+    for pair in copies:
+        for copy in pair:
+            copy.start()
+
+    def arrived(i):
+        for copy in copies[i]:
+            copy.wait()
+
+    arrived(0)
     for side, base in zip((main_a, main_b), bases(rows, main_first)):
         for at in range(depth):
             side[pl.ds(at * cols, cols), :] = adj_in[pl.ds(base + at, lanes, stride=rows), :].T
-    copies[1].wait()
+    arrived(1)
     for side, base in zip((main_a, main_b), bases(rows, main_first)):
         edge = jnp.where(base == 0, 0, rows - 1)
         rate = turned_rate(rate_in, edge, rows, nz, lanes)
-        side[pl.ds((1 + steps) * depth * cols, half), :] = jnp.where(
+        side[pl.ds((1 + early) * depth * cols, half), :] = jnp.where(
             lower, rate[:half], rate[half:]
         )
     for back in range(steps):
-        copies[2 + back].wait()
+        arrived(2 + back)
+        if back >= early:
+            continue
         for side, base in zip((main_a, main_b), bases(rows, main_first)):
             for at in range(depth):
                 side[pl.ds(((1 + back) * depth + at) * cols, cols), :] = conc_in[
@@ -346,7 +362,7 @@
     to_next = a_is_next("gy", main_first)
 
     def unpack(side):
-        packed = side[pl.ds((1 + steps) * depth * cols, half), :]
+        packed = side[pl.ds((1 + early) * depth * cols, half), :]
         turned = pltpu.roll(packed, lanes // 2, 1)
         return jnp.concatenate(
             [jnp.where(lower, packed, turned), jnp.where(lower, turned, packed)], axis=0
@@ -441,7 +457,7 @@
 def prepare_kernel(steps, rows, cols, nz, back, conc_own, from_a, from_b, x_low, x_high,
                    corner_b, corner_a, mob_core, chem_core, curve_core, swing_core,
                    mob, chem, curve, swing, *rest):
-    *ahead, conc = rest
+    *more, conc = rest
     places, _ = slots(steps)
     low, high = reach(cols)
     lanes = conc.shape[2]
@@ -456,11 +472,20 @@
         swing[1 + y, own, :] = swing_core[back - 1, y, own, :]
     for halo, corner, base in zip((from_a, from_b), (corner_a, corner_b), landings(rows, main_first)):
         for at in range(depth):
-            span = pl.ds(((1 + back) * depth + at) * cols, cols)
+            first = (1 + back) * depth if back < early else (back - early) * depth
+            span = pl.ds((first + at) * cols, cols)
             put_halo(conc, (base + at,), halo[span, :], at, place, cols, corner)
 
-    if ahead:
-        put_ahead(ahead[0], conc_own, back + 1, x_low, x_high, places, rows, cols)
+    if more:
+        ahead, late_a, late_b = more
+        put_ahead(ahead, conc_own, back + 1, x_low, x_high, places, rows, cols)
+        for side, base in zip((late_a, late_b), bases(rows, main_first)):
+            for after in range(early, steps):
+                for at in range(depth):
+                    span = pl.ds(((after - early) * depth + at) * cols, cols)
+                    side[span, :] = conc_own[after, base + at]
+            used = (steps - early) * depth * cols
+            side[used:, :] = jnp.zeros((side.shape[0] - used, lanes), f32)
 
     for y in range(rows):
         for at in (low - 8, pad + cols):
@@ -612,8 +637,8 @@
     raw = [(steps, flat, cols), (flat, cols), (nz * rows, cols)]
     conc_raw, adj_raw, rate_raw, main_a, main_b = call(
         functools.partial(edge_kernel, steps, rows, cols, nz),
-        raw + [((1 + steps) * depth * cols + cols // 2, lanes)] * 2,
-        [pltpu.SemaphoreType.DMA((2 + steps,))],
+        raw + [((1 + early) * depth * cols + cols // 2, lanes)] * 2,
+        [pltpu.SemaphoreType.DMA((2 + steps, 2))],
         saved_conc.reshape(raw[0]), adjoint_end.reshape(raw[1]), rate_field.reshape(raw[2]),
         cost=2,
         far=True,
@@ -660,17 +685,22 @@
         cost=2,
     )
     sums = (grad, edge_grad)
+    got = main_a, main_b
+    late = (max((steps - early) * depth * cols, 2 * (cols + 8) + 8), lanes)
     for back in range(1, steps):
         adj_a, adj_b = swap(to_a, to_b, "gy", round_first)
         final = back == steps - 1
         fields = call(
             functools.partial(prepare_kernel, steps, rows, cols, nz, back),
-            [field(rows + 2 * depth)] + [field(rows + 2)] * 3 + ([] if final else [both]),
+            [field(rows + 2 * depth)] + [field(rows + 2)] * 3
+            + ([] if final else [both, late, late]),
             [field(rows + 2 * depth)],
-            conc_own, main_a, main_b, x_low, x_high, corner_b, corner_a, *core,
+            conc_own, *got, x_low, x_high, corner_b, corner_a, *core,
             cost=2,
         )
-        fields, ahead = fields[:4], fields[4:]
+        fields, ahead, more = fields[:4], fields[4:5], fields[5:]
+        if not final:
+            got = swap(*more, "gy", main_first)
         work = [field(rows + 2)] * 2 + [field(rows)] * 2
         if final:
             inner, tiles, grad = call(

time: 37.8 us -> 37.5 us (level)
  waiting for transfers between devices: 9.75 us -> 5.48 us
  starting transfers between devices: 11 us -> 14.5 us
  Pallas kernels: 16.1 us -> 16.6 us
    ppermute x5 -> x6, waiting for transfers between devices: 7.65 us -> 3.09 us  [swap(): lax.ppermute(value_a, axis, pairs_a)]
    ppermute x5 -> x6, starting transfers between devices: 6.28 us -> 8.29 us  [swap(): lax.ppermute(value_b, axis, pairs_b)]
    ppermute x5 -> x6, starting transfers between devices: 4.73 us -> 6.23 us  [swap(): lax.ppermute(value_a, axis, pairs_a)]
    pallas_call x12, Pallas kernels: 16.1 us -> 16.6 us  [call(): pl.pallas_call(kernel, out_shape=[jax.ShapeDtypeStruct(shape, f32) for sh...]
    ppermute x5 -> x6, waiting for transfers between devices: 2.1 us -> 2.39 us  [swap(): lax.ppermute(value_b, axis, pairs_b)]
  transfers between devices with their start and end apart: 10 -> 12, of which waited for: 5 -> 5; matrix products, arithmetic and copies ran while one was open for 0% -> 0% of each run, Pallas kernels for 30% -> 33%
where the time goes in v15:
time: 37.5 us; the launch traced here: 37.4 us
  Pallas kernels  16.6 us (44%)
  starting transfers between devices  14.5 us (39%)
  waiting for transfers between devices  5.48 us (15%)
  between operations  0.74 us (2%)
    pallas_call x12, Pallas kernels, call(): pl.pallas_call(kernel, out_shape=[jax.ShapeDtypeStruct(shape, f32) for sh...  16.6 us
    ppermute x6, starting transfers between devices, swap(): lax.ppermute(value_b, axis, pairs_b)  8.29 us
    ppermute x6, starting transfers between devices, swap(): lax.ppermute(value_a, axis, pairs_a)  6.23 us
    ppermute x6, waiting for transfers between devices, swap(): lax.ppermute(value_a, axis, pairs_a)  3.09 us
    ppermute x6, waiting for transfers between devices, swap(): lax.ppermute(value_b, axis, pairs_b)  2.39 us
  transfers between devices with their start and end apart: 12, of which 5 were waited for; matrix products, arithmetic and copies ran while one was open for 0% of the time, Pallas kernels for 33%

profile of v15, /device:TPU:0, one launch (start us, length us, event | category | flops | bytes accessed | tf_op | source)
XLA Modules:
  0.0 37.4 jit_solution(12590754769712941018)
XLA Ops:
  0.6 1.7 %shard_map.50 = (f32[3,1024,128]{2,1,0:T(8,128)S(1)}, f32[1024,128]{1,0:T(8,128)S(1)}, f32[512,128]{1,0:T(8,128)S(1)}, f32[832,128]{1,0:T(8,128)S(1)}, f32[832,128]{1,0:T(8,128)S(1)}) custom-call(f32[3,1024,128]{2,1,0:T(8,128)} %bitcast.5, f32[1024,128]{1,0:T(8,128)} %bitcast.6, f32[512,128]{1,0:T(8,128)} %bitcast.8), custom_call_target="tpu_custom_call" | custom-call | flops 2000000 | bytes 4000000 | tf_op jit(solution)/shard_map/pallas_call | solution.py:601
  2.3 0.5 %collective-permute-start = (f32[832,128]{1,0:T(8,128)S(1)}, f32[832,128]{1,0:T(8,128)S(1)}, u32[]{:S(2)}, u32[]{:S(2)}) collective-permute-start(f32[832,128]{1,0:T(8,128)S(1)} %get-tuple-element.56), channel_id=1, source_target_pairs={{0,1},{1,0},{2,3},{3,2},{4,5},{5,4},{6,7},{7,6},{8,9},{9,8},{10,11... | collective-permute-start | bytes 1277960 | tf_op jit(solution)/shard_map/ppermute | solution.py:621
  2.8 4.7 %collective-permute-start.1 = (f32[832,128]{1,0:T(8,128)S(1)}, f32[832,128]{1,0:T(8,128)S(1)}, u32[]{:S(2)}, u32[]{:S(2)}) collective-permute-start(f32[832,128]{1,0:T(8,128)S(1)} %get-tuple-element.57), channel_id=1, source_target_pairs={{0,7},{1,2},{2,1},{3,4},{4,3},{5,6},{6,5},{7,0},{8,15},{9,10},{10,... | collective-permute-start | bytes 1277960 | tf_op jit(solution)/shard_map/ppermute | solution.py:621
  7.5 0.7 %shard_map.51 = (f32[3,8,128,128]{3,2,1,0:T(8,128)S(1)}, f32[8,128,128]{2,1,0:T(8,128)S(1)}, f32[8,128,128]{2,1,0:T(8,128)S(1)}, f32[8,24,128]{2,1,0:T(8,128)S(1)}, f32[8,24,128]{2,1,0:T(8,128)S(1)}) custom-call(f32[3,1024,128]{2,1,0:T(8,128)S(1)} %get-tuple-element.52.conc_in, f32[1024,128]{1,0:T(8,128)S(1)} %get-tuple-element.53.adj_in, ...), custom_call_target="tpu_custom_call" | custom-call | flops 1000000 | bytes 2000000 | tf_op jit(solution)/shard_map/pallas_call | solution.py:601
  8.3 1.6 %collective-permute-start.2 = (f32[8,24,128]{2,1,0:T(8,128)S(1)}, f32[8,24,128]{2,1,0:T(8,128)S(1)}, u32[]{:S(2)}, u32[]{:S(2)}) collective-permute-start(f32[8,24,128]{2,1,0:T(8,128)S(1)} %get-tuple-element.58), channel_id=1, source_target_pairs={{0,8},{8,0},{16,24},{24,16},{1,9},{9,1},{17,25},{25,17},{2,10},{10... | collective-permute-start | bytes 294920 | tf_op jit(solution)/shard_map/ppermute | solution.py:621
  9.8 1.5 %collective-permute-start.3 = (f32[8,24,128]{2,1,0:T(8,128)S(1)}, f32[8,24,128]{2,1,0:T(8,128)S(1)}, u32[]{:S(2)}, u32[]{:S(2)}) collective-permute-start(f32[8,24,128]{2,1,0:T(8,128)S(1)} %get-tuple-element.59), channel_id=1, source_target_pairs={{0,24},{8,16},{16,8},{24,0},{1,25},{9,17},{17,9},{25,1},{2,26},{10... | collective-permute-start | bytes 294920 | tf_op jit(solution)/shard_map/ppermute | solution.py:621
  11.3 1.5 %shard_map.52 = (f32[2,8,160,128]{3,2,1,0:T(8,128)S(1)}, f32[2,8,160,128]{3,2,1,0:T(8,128)S(1)}, f32[2,8,160,128]{3,2,1,0:T(8,128)S(1)}, f32[2,8,160,128]{3,2,1,0:T(8,128)S(1)}) custom-call(f32[3,8,128,128]{3,2,1,0:T(8,128)S(1)} %get-tuple-element.55.conc_own), custom_call_target="tpu_custom_call" | custom-call | flops 2000000 | bytes 4000000 | tf_op jit(solution)/shard_map/pallas_call | solution.py:601
  12.9 0.4 %collective-permute-done.2.got_a = f32[8,24,128]{2,1,0:T(8,128)S(1)} collective-permute-done((f32[8,24,128]{2,1,0:T(8,128)S(1)}, f32[8,24,128]{2,1,0:T(8,128)S(1)}, u32[]{:S(2)}, u32[]{:S(2)}) %collective-permute-start.2) | collective-permute-done | bytes 98336 | tf_op jit(solution)/shard_map/ppermute | solution.py:621
  13.3 2.1 %collective-permute-done.3.got_b = f32[8,24,128]{2,1,0:T(8,128)S(1)} collective-permute-done((f32[8,24,128]{2,1,0:T(8,128)S(1)}, f32[8,24,128]{2,1,0:T(8,128)S(1)}, u32[]{:S(2)}, u32[]{:S(2)}) %collective-permute-start.3) | collective-permute-done | bytes 98336 | tf_op jit(solution)/shard_map/ppermute | solution.py:621
  15.4 0.1 collective-permute-start.4
  15.5 0.1 collective-permute-start.5
  15.6 3.3 %shard_map.56 = (f32[10,160,128]{2,1,0:T(8,128)S(1)}, f32[10,160,128]{2,1,0:T(8,128)S(1)}, f32[8,160,128]{2,1,0:T(8,128)S(1)}, f32[10,160,128]{2,1,0:T(8,128)S(1...) custom-call(f32[3,8,128,128]{3,2,1,0:T(8,128)S(1)} %get-tuple-elemen, ...), custom_call_target="tpu_custom_call" | custom-call | flops 3000000 | bytes 6000000 | tf_op jit(solution)/shard_map/pallas_call | solution.py:601
  18.8 2.0 %collective-permute-done.4.corner_b = f32[2,2,24,128]{3,2,1,0:T(8,128)S(1)} collective-permute-done((f32[2,2,24,128]{3,2,1,0:T(8,128)S(1)}, f32[2,2,24,128]{3,2,1,0:T(8,128)S(1)}, u32[]{:S(2)}, u32[]{:S(2)}) %collective-permute-start.4) | collective-permute-done | bytes 49184 | tf_op jit(solution)/shard_map/ppermute | solution.py:621
  20.8 0.0 collective-permute-done.5.corner_a
  20.8 0.0 collective-permute-done.from_a
  20.8 0.0 collective-permute-done.1.from_b
  20.8 1.6 %shard_map.57 = (f32[2,2,160,128]{3,2,1,0:T(8,128)S(1)}, f32[2,160,128]{2,1,0:T(8,128)S(1)}, f32[2,136,128]{2,1,0:T(8,128)S(1)}, f32[2,136,128]{2,1,0:T(8,128)S(1)}) custom-call(f32[10,160,128]{2,1,0:T(8,128)S(1)} %get-tuple-element.82.conc, f32[10,160,128]{2,1,0:T(8,128)S(1)} %get-tuple-element.83.adj, f32[8,160,128]{2,1,0:T(8,128)S(1)} %get-tuple-element.76.rate.rest_1_, ...), custom_call_target="tpu_custom_call" | custom-call | flops 2000000 | bytes 4000000 | tf_op jit(solution)/shard_map/pallas_call | solution.py:601
  22.3 1.6 %collective-permute-start.8 = (f32[2,136,128]{2,1,0:T(8,128)S(1)}, f32[2,136,128]{2,1,0:T(8,128)S(1)}, u32[]{:S(2)}, u32[]{:S(2)}) collective-permute-start(f32[2,136,128]{2,1,0:T(8,128)S(1)} %get-tuple-element.92), channel_id=1, source_target_pairs={{0,7},{1,2},{2,1},{3,4},{4,3},{5,6},{6,5},{7,0},{8,15},{9,10},{10,... | collective-permute-start | bytes 417800 | tf_op jit(solution)/shard_map/ppermute | solution.py:621
  23.9 0.0 collective-permute-start.9
  23.9 0.5 %shard_map.54 = (f32[12,160,128]{2,1,0:T(8,128)S(1)}, f32[10,160,128]{2,1,0:T(8,128)S(1)}, f32[10,160,128]{2,1,0:T(8,128)S(1)}, f32[10,160,128]{2,1,0:T(8,128)S(...) custom-call(f32[3,8,128,128]{3,2,1,0:T(8,128)S(1)} %get-tuple-element.55.conc_own, ...), custom_call_target="tpu_custom_call" | custom-call | flops 2000000 | bytes 4000000 | tf_op jit(solution)/shard_map/pallas_call | solution.py:601
  24.5 0.6 %collective-permute-start.6 = (f32[280,128]{1,0:T(8,128)S(1)}, f32[280,128]{1,0:T(8,128)S(1)}, u32[]{:S(2)}, u32[]{:S(2)}) collective-permute-start(f32[280,128]{1,0:T(8,128)S(1)} %get-tuple-element.68), channel_id=1, source_target_pairs={{0,1},{1,0},{2,3},{3,2},{4,5},{5,4},{6,7},{7,6},{8,9},{9,8},{10,11... | collective-permute-start | bytes 430088 | tf_op jit(solution)/shard_map/ppermute | solution.py:621
  25.0 2.0 %collective-permute-start.7 = (f32[280,128]{1,0:T(8,128)S(1)}, f32[280,128]{1,0:T(8,128)S(1)}, u32[]{:S(2)}, u32[]{:S(2)}) collective-permute-start(f32[280,128]{1,0:T(8,128)S(1)} %get-tuple-element.69), channel_id=1, source_target_pairs={{0,7},{1,2},{2,1},{3,4},{4,3},{5,6},{6,5},{7,0},{8,15},{9,10},{10,... | collective-permute-start | bytes 430088 | tf_op jit(solution)/shard_map/ppermute | solution.py:621
  27.0 2.4 %shard_map.58 = (f32[8,160,128]{2,1,0:T(8,128)S(1)}, f32[8,160,128]{2,1,0:T(8,128)S(1)}) custom-call(f32[12,160,128]{2,1,0:T(8,128)S(1)} %get-tuple-element.77.mob, f32[10,160,128]{2,1,0:T(8,128)S(1)} %get-tuple-element.78.chem, f32[10,160,128]{2,1,0:T(8,128)S(1)} %get-tuple-element.79.curve, f32[10,160,128]{2,1,0:T(8,128)S(1)} %get-tuple-element.80.swing, ...), custom_call_target="tpu_custom_call" | custom-call | flops 3000000 | bytes 6000000 | tf_op jit(solution)/shard_map/pallas_call | solution.py:601
  29.4 0.0 collective-permute-done.8.from_a
  29.4 0.0 collective-permute-done.9.from_b
  29.4 0.4 %shard_map.59 = (f32[2,2,160,128]{3,2,1,0:T(8,128)S(1)}, f32[2,136,128]{2,1,0:T(8,128)S(1)}, f32[2,136,128]{2,1,0:T(8,128)S(1)}) custom-call(f32[12,160,128]{2,1,0:T(8,128)S(1)} %get-tuple-element.77.mob, f32[10,160,128]{2,1,0:T(8,128)S(1)} %get-tuple-element.78.chem, f32[10,160,128]{2,1,0:T(8,128)S(1)} %get-tuple-element.79.curve, ...), custom_call_target="tpu_custom_call" | custom-call | flops 1000000 | bytes 2000000 | tf_op jit(solution)/shard_map/pallas_call | solution.py:601
  29.9 1.9 %collective-permute-start.10 = (f32[2,136,128]{2,1,0:T(8,128)S(1)}, f32[2,136,128]{2,1,0:T(8,128)S(1)}, u32[]{:S(2)}, u32[]{:S(2)}) collective-permute-start(f32[2,136,128]{2,1,0:T(8,128)S(1)} %get-tuple-element.98), channel_id=1, source_target_pairs={{0,7},{1,2},{2,1},{3,4},{4,3},{5,6},{6,5},{7,0},{8,15},{9,10},{10,... | collective-permute-start | bytes 417800 | tf_op jit(solution)/shard_map/ppermute | solution.py:621
  31.8 0.0 collective-permute-start.11
  31.8 0.0 collective-permute-done.6.from_a
  31.8 0.3 collective-permute-done.7.from_b
  32.1 0.5 %shard_map.55 = (f32[12,160,128]{2,1,0:T(8,128)S(1)}, f32[10,160,128]{2,1,0:T(8,128)S(1)}, f32[10,160,128]{2,1,0:T(8,128)S(1)}, f32[10,160,128]{2,1,0:T(8,128)S(1)}) custom-call(f32[3,8,128,128]{3,2,1,0:T(8,128)S(1)} %get-tuple-element.55.conc_own, f32[280,128]{1,0:T(8,128)S(1)} %collective-permute-done.6.from_a, ...), custom_call_target="tpu_custom_call" | custom-call | flops 2000000 | bytes 4000000 | tf_op jit(solution)/shard_map/pallas_call | solution.py:601
  32.5 2.9 %shard_map.60 = (f32[8,160,128]{2,1,0:T(8,128)S(1)}, f32[1024,128]{1,0:T(8,128)S(1)}, f32[512,128]{1,0:T(8,128)}) custom-call(f32[12,160,128]{2,1,0:T(8,128)S(1)} %get-tuple-element.70.mob, f32[10,160,128]{2,1,0:T(8,128)S(1)} %get-tuple-element.71.chem, f32[10,160,128]{2,1,0:T(8,128)S(1)} %get-tuple-element.72.curve, ...), custom_call_target="tpu_custom_call" | custom-call | flops 3000000 | bytes 6000000 | tf_op jit(solution)/shard_map/pallas_call | solution.py:601
  35.5 0.7 %collective-permute-done.10.from_a = f32[2,136,128]{2,1,0:T(8,128)S(1)} collective-permute-done((f32[2,136,128]{2,1,0:T(8,128)S(1)}, f32[2,136,128]{2,1,0:T(8,128)S(1)}, u32[]{:S(2)}, u32[]{:S(2)}) %collective-permute-start.10) | collective-permute-done | bytes 139296 | tf_op jit(solution)/shard_map/ppermute | solution.py:621
  36.2 0.0 collective-permute-done.11.from_b
  36.2 1.2 %shard_map.61 = f32[1024,128]{1,0:T(8,128)} custom-call(f32[12,160,128]{2,1,0:T(8,128)S(1)} %get-tuple-element.70.mob, f32[10,160,128]{2,1,0:T(8,128)S(1)} %get-tuple-element.71.chem, f32[10,160,128]{2,1,0:T(8,128)S(1)} %get-tuple-element.72.curve, f32[10,160,128]{2,1,0:T(8,128)S(1)} %get-tuple-element.73.swing, ...), custom_call_target="tpu_custom_call" | custom-call | flops 1000000 | bytes 2000000 | tf_op jit(solution)/shard_map/pallas_call | solution.py:601
  (1 shorter events, 0.0 us)
Async XLA Ops:
  2.3 18.5 %collective-permute-start = (f32[832,128]{1,0:T(8,128)S(1)}, f32[832,128]{1,0:T(8,128)S(1)}, u32[]{:S(2)}, u32[]{:S(2)}) collective-permute-start(f32[832,128]{1,0:T(8,128)S(1)} %get-tuple-element.56), channel_id=1, source_target_pairs={{0,1},{1,0},{2,3},{3,2},{4,5},{5,4},{6,7},{7,6},{8,9},{9,8},{10,11... | collective-permute-start | bytes 1277960 | tf_op jit(solution)/shard_map/ppermute | solution.py:621
  2.8 18.0 %collective-permute-start.1 = (f32[832,128]{1,0:T(8,128)S(1)}, f32[832,128]{1,0:T(8,128)S(1)}, u32[]{:S(2)}, u32[]{:S(2)}) collective-permute-start(f32[832,128]{1,0:T(8,128)S(1)} %get-tuple-element.57), channel_id=1, source_target_pairs={{0,7},{1,2},{2,1},{3,4},{4,3},{5,6},{6,5},{7,0},{8,15},{9,10},{10,... | collective-permute-start | bytes 1277960 | tf_op jit(solution)/shard_map/ppermute | solution.py:621
  8.3 5.0 %collective-permute-start.2 = (f32[8,24,128]{2,1,0:T(8,128)S(1)}, f32[8,24,128]{2,1,0:T(8,128)S(1)}, u32[]{:S(2)}, u32[]{:S(2)}) collective-permute-start(f32[8,24,128]{2,1,0:T(8,128)S(1)} %get-tuple-element.58), channel_id=1, source_target_pairs={{0,8},{8,0},{16,24},{24,16},{1,9},{9,1},{17,25},{25,17},{2,10},{10... | collective-permute-start | bytes 294920 | tf_op jit(solution)/shard_map/ppermute | solution.py:621
  9.8 5.5 %collective-permute-start.3 = (f32[8,24,128]{2,1,0:T(8,128)S(1)}, f32[8,24,128]{2,1,0:T(8,128)S(1)}, u32[]{:S(2)}, u32[]{:S(2)}) collective-permute-start(f32[8,24,128]{2,1,0:T(8,128)S(1)} %get-tuple-element.59), channel_id=1, source_target_pairs={{0,24},{8,16},{16,8},{24,0},{1,25},{9,17},{17,9},{25,1},{2,26},{10... | collective-permute-start | bytes 294920 | tf_op jit(solution)/shard_map/ppermute | solution.py:621
  15.4 5.4 %collective-permute-start.4 = (f32[2,2,24,128]{3,2,1,0:T(8,128)S(1)}, f32[2,2,24,128]{3,2,1,0:T(8,128)S(1)}, u32[]{:S(2)}, u32[]{:S(2)}) collective-permute-start(f32[2,2,24,128]{3,2,1,0:T(8,128)S(1)} %get-tuple-element.63), channel_id=1, source_target_pairs={{0,7},{1,2},{2,1},{3,4},{4,3},{5,6},{6,5},{7,0},{8,15},{9,10},{10,... | collective-permute-start | bytes 147464 | tf_op jit(solution)/shard_map/ppermute | solution.py:621
  15.5 5.3 %collective-permute-start.5 = (f32[2,2,24,128]{3,2,1,0:T(8,128)S(1)}, f32[2,2,24,128]{3,2,1,0:T(8,128)S(1)}, u32[]{:S(2)}, u32[]{:S(2)}) collective-permute-start(f32[2,2,24,128]{3,2,1,0:T(8,128)S(1)} %get-tuple-element.64), channel_id=1, source_target_pairs={{0,1},{1,0},{2,3},{3,2},{4,5},{5,4},{6,7},{7,6},{8,9},{9,8},{10,11... | collective-permute-start | bytes 147464 | tf_op jit(solution)/shard_map/ppermute | solution.py:621
  22.3 7.1 %collective-permute-start.8 = (f32[2,136,128]{2,1,0:T(8,128)S(1)}, f32[2,136,128]{2,1,0:T(8,128)S(1)}, u32[]{:S(2)}, u32[]{:S(2)}) collective-permute-start(f32[2,136,128]{2,1,0:T(8,128)S(1)} %get-tuple-element.92), channel_id=1, source_target_pairs={{0,7},{1,2},{2,1},{3,4},{4,3},{5,6},{6,5},{7,0},{8,15},{9,10},{10,... | collective-permute-start | bytes 417800 | tf_op jit(solution)/shard_map/ppermute | solution.py:621
  23.9 5.5 %collective-permute-start.9 = (f32[2,136,128]{2,1,0:T(8,128)S(1)}, f32[2,136,128]{2,1,0:T(8,128)S(1)}, u32[]{:S(2)}, u32[]{:S(2)}) collective-permute-start(f32[2,136,128]{2,1,0:T(8,128)S(1)} %get-tuple-element.93), channel_id=1, source_target_pairs={{0,1},{1,0},{2,3},{3,2},{4,5},{5,4},{6,7},{7,6},{8,9},{9,8},{10,11... | collective-permute-start | bytes 417800 | tf_op jit(solution)/shard_map/ppermute | solution.py:621
  24.5 7.3 %collective-permute-start.6 = (f32[280,128]{1,0:T(8,128)S(1)}, f32[280,128]{1,0:T(8,128)S(1)}, u32[]{:S(2)}, u32[]{:S(2)}) collective-permute-start(f32[280,128]{1,0:T(8,128)S(1)} %get-tuple-element.68), channel_id=1, source_target_pairs={{0,1},{1,0},{2,3},{3,2},{4,5},{5,4},{6,7},{7,6},{8,9},{9,8},{10,11... | collective-permute-start | bytes 430088 | tf_op jit(solution)/shard_map/ppermute | solution.py:621
  25.0 7.0 %collective-permute-start.7 = (f32[280,128]{1,0:T(8,128)S(1)}, f32[280,128]{1,0:T(8,128)S(1)}, u32[]{:S(2)}, u32[]{:S(2)}) collective-permute-start(f32[280,128]{1,0:T(8,128)S(1)} %get-tuple-element.69), channel_id=1, source_target_pairs={{0,7},{1,2},{2,1},{3,4},{4,3},{5,6},{6,5},{7,0},{8,15},{9,10},{10,... | collective-permute-start | bytes 430088 | tf_op jit(solution)/shard_map/ppermute | solution.py:621
  29.9 6.3 %collective-permute-start.10 = (f32[2,136,128]{2,1,0:T(8,128)S(1)}, f32[2,136,128]{2,1,0:T(8,128)S(1)}, u32[]{:S(2)}, u32[]{:S(2)}) collective-permute-start(f32[2,136,128]{2,1,0:T(8,128)S(1)} %get-tuple-element.98), channel_id=1, source_target_pairs={{0,7},{1,2},{2,1},{3,4},{4,3},{5,6},{6,5},{7,0},{8,15},{9,10},{10,... | collective-permute-start | bytes 417800 | tf_op jit(solution)/shard_map/ppermute | solution.py:621
  31.8 4.4 %collective-permute-start.11 = (f32[2,136,128]{2,1,0:T(8,128)S(1)}, f32[2,136,128]{2,1,0:T(8,128)S(1)}, u32[]{:S(2)}, u32[]{:S(2)}) collective-permute-start(f32[2,136,128]{2,1,0:T(8,128)S(1)} %get-tuple-element.99), channel_id=1, source_target_pairs={{0,1},{1,0},{2,3},{3,2},{4,5},{5,4},{6,7},{7,6},{8,9},{9,8},{10,11... | collective-permute-start | bytes 417800 | tf_op jit(solution)/shard_map/ppermute | solution.py:621

commit v16 on v15

--- a/solution.py
+++ b/solution.py
@@ -156,10 +156,10 @@
 
     for row in (0, rows + 1):
         pot[row] = jnp.zeros(pot.shape[1:], f32)
-    lax.fori_loop(0, rows, body, 0, unroll=2)
+    lax.fori_loop(0, rows, body, 0, unroll=4)
     if between is not None:
         between()
-    lax.fori_loop(0, rows, close, 0, unroll=4)
+    lax.fori_loop(0, rows, close, 0, unroll=8)
 
 
 def a_is_next(axis, first):
@@ -318,8 +318,8 @@
                      set_row(swing, row), at, size, mask)
         return 0
 
-    lax.fori_loop(1, rows + 1, mob_row, 0, unroll=4)
-    lax.fori_loop(1, rows + 1, mu_row, 0, unroll=2)
+    lax.fori_loop(1, rows + 1, mob_row, 0, unroll=8)
+    lax.fori_loop(1, rows + 1, mu_row, 0, unroll=4)
     all_rows(rows, cols, nz, adj, mob, 1, chem, curve, swing, rate, None, pot, part, out, grad)
 
 
@@ -451,7 +451,7 @@
                          set_row(swing.at[i], y), at, size, mask)
             return 0
 
-        lax.fori_loop(0, rows, row, 0, unroll=2)
+        lax.fori_loop(0, rows, row, 0, unroll=4)
 
 
 def prepare_kernel(steps, rows, cols, nz, back, conc_own, from_a, from_b, x_low, x_high,

time: 37.5 us -> 39.3 us (1.048)
  Pallas kernels: 16.6 us -> 19.4 us
  waiting for transfers between devices: 5.48 us -> 4.07 us
  starting transfers between devices: 14.5 us -> 14.9 us
    pallas_call x12, Pallas kernels: 16.6 us -> 19.4 us  [call(): pl.pallas_call(kernel, out_shape=[jax.ShapeDtypeStruct(shape, f32) for sh...]
    ppermute x6, waiting for transfers between devices: 3.09 us -> 1.97 us  [swap(): lax.ppermute(value_a, axis, pairs_a)]
    ppermute x6, starting transfers between devices: 6.23 us -> 7.3 us  [swap(): lax.ppermute(value_a, axis, pairs_a)]
    ppermute x6, starting transfers between devices: 8.29 us -> 7.6 us  [swap(): lax.ppermute(value_b, axis, pairs_b)]
  transfers between devices with their start and end apart: 12 -> 12, of which waited for: 5 -> 3; matrix products, arithmetic and copies ran while one was open for 0% -> 0% of each run, Pallas kernels for 33% -> 38%
where the time goes in v16:
time: 39.3 us; the launch traced here: 39.1 us
  Pallas kernels  19.4 us (49%)
  starting transfers between devices  14.9 us (38%)
  waiting for transfers between devices  4.07 us (10%)
  between operations  0.75 us (2%)
    pallas_call x12, Pallas kernels, call(): pl.pallas_call(kernel, out_shape=[jax.ShapeDtypeStruct(shape, f32) for sh...  19.4 us
    ppermute x6, starting transfers between devices, swap(): lax.ppermute(value_b, axis, pairs_b)  7.6 us
    ppermute x6, starting transfers between devices, swap(): lax.ppermute(value_a, axis, pairs_a)  7.3 us
    ppermute x6, waiting for transfers between devices, swap(): lax.ppermute(value_b, axis, pairs_b)  2.1 us
    ppermute x6, waiting for transfers between devices, swap(): lax.ppermute(value_a, axis, pairs_a)  1.97 us
  transfers between devices with their start and end apart: 12, of which 3 were waited for; matrix products, arithmetic and copies ran while one was open for 0% of the time, Pallas kernels for 38%

profile of v16, /device:TPU:0, one launch (start us, length us, event | category | flops | bytes accessed | tf_op | source)
XLA Modules:
  0.0 39.1 jit_solution(7655222670383794319)
XLA Ops:
  0.6 1.7 %shard_map.50 = (f32[3,1024,128]{2,1,0:T(8,128)S(1)}, f32[1024,128]{1,0:T(8,128)S(1)}, f32[512,128]{1,0:T(8,128)S(1)}, f32[832,128]{1,0:T(8,128)S(1)}, f32[832,128]{1,0:T(8,128)S(1)}) custom-call(f32[3,1024,128]{2,1,0:T(8,128)} %bitcast.5, f32[1024,128]{1,0:T(8,128)} %bitcast.6, f32[512,128]{1,0:T(8,128)} %bitcast.8), custom_call_target="tpu_custom_call" | custom-call | flops 2000000 | bytes 4000000 | tf_op jit(solution)/shard_map/pallas_call | solution.py:601
  2.3 0.5 %collective-permute-start = (f32[832,128]{1,0:T(8,128)S(1)}, f32[832,128]{1,0:T(8,128)S(1)}, u32[]{:S(2)}, u32[]{:S(2)}) collective-permute-start(f32[832,128]{1,0:T(8,128)S(1)} %get-tuple-element.56), channel_id=1, source_target_pairs={{0,1},{1,0},{2,3},{3,2},{4,5},{5,4},{6,7},{7,6},{8,9},{9,8},{10,11... | collective-permute-start | bytes 1277960 | tf_op jit(solution)/shard_map/ppermute | solution.py:621
  2.8 4.7 %collective-permute-start.1 = (f32[832,128]{1,0:T(8,128)S(1)}, f32[832,128]{1,0:T(8,128)S(1)}, u32[]{:S(2)}, u32[]{:S(2)}) collective-permute-start(f32[832,128]{1,0:T(8,128)S(1)} %get-tuple-element.57), channel_id=1, source_target_pairs={{0,7},{1,2},{2,1},{3,4},{4,3},{5,6},{6,5},{7,0},{8,15},{9,10},{10,... | collective-permute-start | bytes 1277960 | tf_op jit(solution)/shard_map/ppermute | solution.py:621
  7.5 0.7 %shard_map.51 = (f32[3,8,128,128]{3,2,1,0:T(8,128)S(1)}, f32[8,128,128]{2,1,0:T(8,128)S(1)}, f32[8,128,128]{2,1,0:T(8,128)S(1)}, f32[8,24,128]{2,1,0:T(8,128)S(1)}, f32[8,24,128]{2,1,0:T(8,128)S(1)}) custom-call(f32[3,1024,128]{2,1,0:T(8,128)S(1)} %get-tuple-element.52.conc_in, f32[1024,128]{1,0:T(8,128)S(1)} %get-tuple-element.53.adj_in, ...), custom_call_target="tpu_custom_call" | custom-call | flops 1000000 | bytes 2000000 | tf_op jit(solution)/shard_map/pallas_call | solution.py:601
  8.3 1.6 %collective-permute-start.2 = (f32[8,24,128]{2,1,0:T(8,128)S(1)}, f32[8,24,128]{2,1,0:T(8,128)S(1)}, u32[]{:S(2)}, u32[]{:S(2)}) collective-permute-start(f32[8,24,128]{2,1,0:T(8,128)S(1)} %get-tuple-element.58), channel_id=1, source_target_pairs={{0,8},{8,0},{16,24},{24,16},{1,9},{9,1},{17,25},{25,17},{2,10},{10... | collective-permute-start | bytes 294920 | tf_op jit(solution)/shard_map/ppermute | solution.py:621
  9.8 1.5 %collective-permute-start.3 = (f32[8,24,128]{2,1,0:T(8,128)S(1)}, f32[8,24,128]{2,1,0:T(8,128)S(1)}, u32[]{:S(2)}, u32[]{:S(2)}) collective-permute-start(f32[8,24,128]{2,1,0:T(8,128)S(1)} %get-tuple-element.59), channel_id=1, source_target_pairs={{0,24},{8,16},{16,8},{24,0},{1,25},{9,17},{17,9},{25,1},{2,26},{10... | collective-permute-start | bytes 294920 | tf_op jit(solution)/shard_map/ppermute | solution.py:621
  11.3 1.2 %shard_map.52 = (f32[2,8,160,128]{3,2,1,0:T(8,128)S(1)}, f32[2,8,160,128]{3,2,1,0:T(8,128)S(1)}, f32[2,8,160,128]{3,2,1,0:T(8,128)S(1)}, f32[2,8,160,128]{3,2,1,0:T(8,128)S(1)}) custom-call(f32[3,8,128,128]{3,2,1,0:T(8,128)S(1)} %get-tuple-element.55.conc_own), custom_call_target="tpu_custom_call" | custom-call | flops 2000000 | bytes 4000000 | tf_op jit(solution)/shard_map/pallas_call | solution.py:601
  12.6 0.7 %collective-permute-done.2.got_a = f32[8,24,128]{2,1,0:T(8,128)S(1)} collective-permute-done((f32[8,24,128]{2,1,0:T(8,128)S(1)}, f32[8,24,128]{2,1,0:T(8,128)S(1)}, u32[]{:S(2)}, u32[]{:S(2)}) %collective-permute-start.2) | collective-permute-done | bytes 98336 | tf_op jit(solution)/shard_map/ppermute | solution.py:621
  13.3 2.1 %collective-permute-done.3.got_b = f32[8,24,128]{2,1,0:T(8,128)S(1)} collective-permute-done((f32[8,24,128]{2,1,0:T(8,128)S(1)}, f32[8,24,128]{2,1,0:T(8,128)S(1)}, u32[]{:S(2)}, u32[]{:S(2)}) %collective-permute-start.3) | collective-permute-done | bytes 98336 | tf_op jit(solution)/shard_map/ppermute | solution.py:621
  15.4 0.1 collective-permute-start.4
  15.5 0.1 collective-permute-start.5
  15.6 4.0 %shard_map.56 = (f32[10,160,128]{2,1,0:T(8,128)S(1)}, f32[10,160,128]{2,1,0:T(8,128)S(1)}, f32[8,160,128]{2,1,0:T(8,128)S(1)}, f32[10,160,128]{2,1,0:T(8,128)S(1...) custom-call(f32[3,8,128,128]{3,2,1,0:T(8,128)S(1)} %get-tuple-elemen, ...), custom_call_target="tpu_custom_call" | custom-call | flops 3000000 | bytes 6000000 | tf_op jit(solution)/shard_map/pallas_call | solution.py:601
  19.5 1.3 %collective-permute-done.4.corner_b = f32[2,2,24,128]{3,2,1,0:T(8,128)S(1)} collective-permute-done((f32[2,2,24,128]{3,2,1,0:T(8,128)S(1)}, f32[2,2,24,128]{3,2,1,0:T(8,128)S(1)}, u32[]{:S(2)}, u32[]{:S(2)}) %collective-permute-start.4) | collective-permute-done | bytes 49184 | tf_op jit(solution)/shard_map/ppermute | solution.py:621
  20.8 0.0 collective-permute-done.5.corner_a
  20.8 0.0 collective-permute-done.from_a
  20.8 0.0 collective-permute-done.1.from_b
  20.8 1.6 %shard_map.57 = (f32[2,2,160,128]{3,2,1,0:T(8,128)S(1)}, f32[2,160,128]{2,1,0:T(8,128)S(1)}, f32[2,136,128]{2,1,0:T(8,128)S(1)}, f32[2,136,128]{2,1,0:T(8,128)S(1)}) custom-call(f32[10,160,128]{2,1,0:T(8,128)S(1)} %get-tuple-element.82.conc, f32[10,160,128]{2,1,0:T(8,128)S(1)} %get-tuple-element.83.adj, f32[8,160,128]{2,1,0:T(8,128)S(1)} %get-tuple-element.76.rate.rest_1_, ...), custom_call_target="tpu_custom_call" | custom-call | flops 2000000 | bytes 4000000 | tf_op jit(solution)/shard_map/pallas_call | solution.py:601
  22.3 2.3 %collective-permute-start.8 = (f32[2,136,128]{2,1,0:T(8,128)S(1)}, f32[2,136,128]{2,1,0:T(8,128)S(1)}, u32[]{:S(2)}, u32[]{:S(2)}) collective-permute-start(f32[2,136,128]{2,1,0:T(8,128)S(1)} %get-tuple-element.92), channel_id=1, source_target_pairs={{0,7},{1,2},{2,1},{3,4},{4,3},{5,6},{6,5},{7,0},{8,15},{9,10},{10,... | collective-permute-start | bytes 417800 | tf_op jit(solution)/shard_map/ppermute | solution.py:621
  24.6 0.0 collective-permute-start.9
  24.6 0.5 %shard_map.54 = (f32[12,160,128]{2,1,0:T(8,128)S(1)}, f32[10,160,128]{2,1,0:T(8,128)S(1)}, f32[10,160,128]{2,1,0:T(8,128)S(1)}, f32[10,160,128]{2,1,0:T(8,128)S(...) custom-call(f32[3,8,128,128]{3,2,1,0:T(8,128)S(1)} %get-tuple-element.55.conc_own, ...), custom_call_target="tpu_custom_call" | custom-call | flops 2000000 | bytes 4000000 | tf_op jit(solution)/shard_map/pallas_call | solution.py:601
  25.2 0.6 %collective-permute-start.6 = (f32[280,128]{1,0:T(8,128)S(1)}, f32[280,128]{1,0:T(8,128)S(1)}, u32[]{:S(2)}, u32[]{:S(2)}) collective-permute-start(f32[280,128]{1,0:T(8,128)S(1)} %get-tuple-element.68), channel_id=1, source_target_pairs={{0,1},{1,0},{2,3},{3,2},{4,5},{5,4},{6,7},{7,6},{8,9},{9,8},{10,11... | collective-permute-start | bytes 430088 | tf_op jit(solution)/shard_map/ppermute | solution.py:621
  25.7 1.3 %collective-permute-start.7 = (f32[280,128]{1,0:T(8,128)S(1)}, f32[280,128]{1,0:T(8,128)S(1)}, u32[]{:S(2)}, u32[]{:S(2)}) collective-permute-start(f32[280,128]{1,0:T(8,128)S(1)} %get-tuple-element.69), channel_id=1, source_target_pairs={{0,7},{1,2},{2,1},{3,4},{4,3},{5,6},{6,5},{7,0},{8,15},{9,10},{10,... | collective-permute-start | bytes 430088 | tf_op jit(solution)/shard_map/ppermute | solution.py:621
  27.0 3.2 %shard_map.58 = (f32[8,160,128]{2,1,0:T(8,128)S(1)}, f32[8,160,128]{2,1,0:T(8,128)S(1)}) custom-call(f32[12,160,128]{2,1,0:T(8,128)S(1)} %get-tuple-element.77.mob, f32[10,160,128]{2,1,0:T(8,128)S(1)} %get-tuple-element.78.chem, f32[10,160,128]{2,1,0:T(8,128)S(1)} %get-tuple-element.79.curve, f32[10,160,128]{2,1,0:T(8,128)S(1)} %get-tuple-element.80.swing, ...), custom_call_target="tpu_custom_call" | custom-call | flops 3000000 | bytes 6000000 | tf_op jit(solution)/shard_map/pallas_call | solution.py:601
  30.2 0.0 collective-permute-done.8.from_a
  30.3 0.0 collective-permute-done.9.from_b
  30.3 0.4 %shard_map.59 = (f32[2,2,160,128]{3,2,1,0:T(8,128)S(1)}, f32[2,136,128]{2,1,0:T(8,128)S(1)}, f32[2,136,128]{2,1,0:T(8,128)S(1)}) custom-call(f32[12,160,128]{2,1,0:T(8,128)S(1)} %get-tuple-element.77.mob, f32[10,160,128]{2,1,0:T(8,128)S(1)} %get-tuple-element.78.chem, f32[10,160,128]{2,1,0:T(8,128)S(1)} %get-tuple-element.79.curve, ...), custom_call_target="tpu_custom_call" | custom-call | flops 1000000 | bytes 2000000 | tf_op jit(solution)/shard_map/pallas_call | solution.py:601
  30.7 2.3 %collective-permute-start.10 = (f32[2,136,128]{2,1,0:T(8,128)S(1)}, f32[2,136,128]{2,1,0:T(8,128)S(1)}, u32[]{:S(2)}, u32[]{:S(2)}) collective-permute-start(f32[2,136,128]{2,1,0:T(8,128)S(1)} %get-tuple-element.98), channel_id=1, source_target_pairs={{0,7},{1,2},{2,1},{3,4},{4,3},{5,6},{6,5},{7,0},{8,15},{9,10},{10,... | collective-permute-start | bytes 417800 | tf_op jit(solution)/shard_map/ppermute | solution.py:621
  33.0 0.0 collective-permute-start.11
  33.0 0.0 collective-permute-done.6.from_a
  33.0 0.0 collective-permute-done.7.from_b
  33.0 0.5 %shard_map.55 = (f32[12,160,128]{2,1,0:T(8,128)S(1)}, f32[10,160,128]{2,1,0:T(8,128)S(1)}, f32[10,160,128]{2,1,0:T(8,128)S(1)}, f32[10,160,128]{2,1,0:T(8,128)S(1)}) custom-call(f32[3,8,128,128]{3,2,1,0:T(8,128)S(1)} %get-tuple-element.55.conc_own, f32[280,128]{1,0:T(8,128)S(1)} %collective-permute-done.6.from_a, ...), custom_call_target="tpu_custom_call" | custom-call | flops 2000000 | bytes 4000000 | tf_op jit(solution)/shard_map/pallas_call | solution.py:601
  33.5 4.4 %shard_map.60 = (f32[8,160,128]{2,1,0:T(8,128)S(1)}, f32[1024,128]{1,0:T(8,128)S(1)}, f32[512,128]{1,0:T(8,128)}) custom-call(f32[12,160,128]{2,1,0:T(8,128)S(1)} %get-tuple-element.70.mob, f32[10,160,128]{2,1,0:T(8,128)S(1)} %get-tuple-element.71.chem, f32[10,160,128]{2,1,0:T(8,128)S(1)} %get-tuple-element.72.curve, ...), custom_call_target="tpu_custom_call" | custom-call | flops 3000000 | bytes 6000000 | tf_op jit(solution)/shard_map/pallas_call | solution.py:601
  37.9 0.0 collective-permute-done.10.from_a
  37.9 0.0 collective-permute-done.11.from_b
  37.9 1.2 %shard_map.61 = f32[1024,128]{1,0:T(8,128)} custom-call(f32[12,160,128]{2,1,0:T(8,128)S(1)} %get-tuple-element.70.mob, f32[10,160,128]{2,1,0:T(8,128)S(1)} %get-tuple-element.71.chem, f32[10,160,128]{2,1,0:T(8,128)S(1)} %get-tuple-element.72.curve, f32[10,160,128]{2,1,0:T(8,128)S(1)} %get-tuple-element.73.swing, ...), custom_call_target="tpu_custom_call" | custom-call | flops 1000000 | bytes 2000000 | tf_op jit(solution)/shard_map/pallas_call | solution.py:601
  (1 shorter events, 0.0 us)
Async XLA Ops:
  2.3 18.5 %collective-permute-start = (f32[832,128]{1,0:T(8,128)S(1)}, f32[832,128]{1,0:T(8,128)S(1)}, u32[]{:S(2)}, u32[]{:S(2)}) collective-permute-start(f32[832,128]{1,0:T(8,128)S(1)} %get-tuple-element.56), channel_id=1, source_target_pairs={{0,1},{1,0},{2,3},{3,2},{4,5},{5,4},{6,7},{7,6},{8,9},{9,8},{10,11... | collective-permute-start | bytes 1277960 | tf_op jit(solution)/shard_map/ppermute | solution.py:621
  2.8 18.0 %collective-permute-start.1 = (f32[832,128]{1,0:T(8,128)S(1)}, f32[832,128]{1,0:T(8,128)S(1)}, u32[]{:S(2)}, u32[]{:S(2)}) collective-permute-start(f32[832,128]{1,0:T(8,128)S(1)} %get-tuple-element.57), channel_id=1, source_target_pairs={{0,7},{1,2},{2,1},{3,4},{4,3},{5,6},{6,5},{7,0},{8,15},{9,10},{10,... | collective-permute-start | bytes 1277960 | tf_op jit(solution)/shard_map/ppermute | solution.py:621
  8.3 5.0 %collective-permute-start.2 = (f32[8,24,128]{2,1,0:T(8,128)S(1)}, f32[8,24,128]{2,1,0:T(8,128)S(1)}, u32[]{:S(2)}, u32[]{:S(2)}) collective-permute-start(f32[8,24,128]{2,1,0:T(8,128)S(1)} %get-tuple-element.58), channel_id=1, source_target_pairs={{0,8},{8,0},{16,24},{24,16},{1,9},{9,1},{17,25},{25,17},{2,10},{10... | collective-permute-start | bytes 294920 | tf_op jit(solution)/shard_map/ppermute | solution.py:621
  9.8 5.5 %collective-permute-start.3 = (f32[8,24,128]{2,1,0:T(8,128)S(1)}, f32[8,24,128]{2,1,0:T(8,128)S(1)}, u32[]{:S(2)}, u32[]{:S(2)}) collective-permute-start(f32[8,24,128]{2,1,0:T(8,128)S(1)} %get-tuple-element.59), channel_id=1, source_target_pairs={{0,24},{8,16},{16,8},{24,0},{1,25},{9,17},{17,9},{25,1},{2,26},{10... | collective-permute-start | bytes 294920 | tf_op jit(solution)/shard_map/ppermute | solution.py:621
  15.4 5.4 %collective-permute-start.4 = (f32[2,2,24,128]{3,2,1,0:T(8,128)S(1)}, f32[2,2,24,128]{3,2,1,0:T(8,128)S(1)}, u32[]{:S(2)}, u32[]{:S(2)}) collective-permute-start(f32[2,2,24,128]{3,2,1,0:T(8,128)S(1)} %get-tuple-element.63), channel_id=1, source_target_pairs={{0,7},{1,2},{2,1},{3,4},{4,3},{5,6},{6,5},{7,0},{8,15},{9,10},{10,... | collective-permute-start | bytes 147464 | tf_op jit(solution)/shard_map/ppermute | solution.py:621
  15.5 5.3 %collective-permute-start.5 = (f32[2,2,24,128]{3,2,1,0:T(8,128)S(1)}, f32[2,2,24,128]{3,2,1,0:T(8,128)S(1)}, u32[]{:S(2)}, u32[]{:S(2)}) collective-permute-start(f32[2,2,24,128]{3,2,1,0:T(8,128)S(1)} %get-tuple-element.64), channel_id=1, source_target_pairs={{0,1},{1,0},{2,3},{3,2},{4,5},{5,4},{6,7},{7,6},{8,9},{9,8},{10,11... | collective-permute-start | bytes 147464 | tf_op jit(solution)/shard_map/ppermute | solution.py:621
  22.3 7.9 %collective-permute-start.8 = (f32[2,136,128]{2,1,0:T(8,128)S(1)}, f32[2,136,128]{2,1,0:T(8,128)S(1)}, u32[]{:S(2)}, u32[]{:S(2)}) collective-permute-start(f32[2,136,128]{2,1,0:T(8,128)S(1)} %get-tuple-element.92), channel_id=1, source_target_pairs={{0,7},{1,2},{2,1},{3,4},{4,3},{5,6},{6,5},{7,0},{8,15},{9,10},{10,... | collective-permute-start | bytes 417800 | tf_op jit(solution)/shard_map/ppermute | solution.py:621
  24.6 5.6 %collective-permute-start.9 = (f32[2,136,128]{2,1,0:T(8,128)S(1)}, f32[2,136,128]{2,1,0:T(8,128)S(1)}, u32[]{:S(2)}, u32[]{:S(2)}) collective-permute-start(f32[2,136,128]{2,1,0:T(8,128)S(1)} %get-tuple-element.93), channel_id=1, source_target_pairs={{0,1},{1,0},{2,3},{3,2},{4,5},{5,4},{6,7},{7,6},{8,9},{9,8},{10,11... | collective-permute-start | bytes 417800 | tf_op jit(solution)/shard_map/ppermute | solution.py:621
  25.2 7.8 %collective-permute-start.6 = (f32[280,128]{1,0:T(8,128)S(1)}, f32[280,128]{1,0:T(8,128)S(1)}, u32[]{:S(2)}, u32[]{:S(2)}) collective-permute-start(f32[280,128]{1,0:T(8,128)S(1)} %get-tuple-element.68), channel_id=1, source_target_pairs={{0,1},{1,0},{2,3},{3,2},{4,5},{5,4},{6,7},{7,6},{8,9},{9,8},{10,11... | collective-permute-start | bytes 430088 | tf_op jit(solution)/shard_map/ppermute | solution.py:621
  25.7 7.2 %collective-permute-start.7 = (f32[280,128]{1,0:T(8,128)S(1)}, f32[280,128]{1,0:T(8,128)S(1)}, u32[]{:S(2)}, u32[]{:S(2)}) collective-permute-start(f32[280,128]{1,0:T(8,128)S(1)} %get-tuple-element.69), channel_id=1, source_target_pairs={{0,7},{1,2},{2,1},{3,4},{4,3},{5,6},{6,5},{7,0},{8,15},{9,10},{10,... | collective-permute-start | bytes 430088 | tf_op jit(solution)/shard_map/ppermute | solution.py:621
  30.7 7.2 %collective-permute-start.10 = (f32[2,136,128]{2,1,0:T(8,128)S(1)}, f32[2,136,128]{2,1,0:T(8,128)S(1)}, u32[]{:S(2)}, u32[]{:S(2)}) collective-permute-start(f32[2,136,128]{2,1,0:T(8,128)S(1)} %get-tuple-element.98), channel_id=1, source_target_pairs={{0,7},{1,2},{2,1},{3,4},{4,3},{5,6},{6,5},{7,0},{8,15},{9,10},{10,... | collective-permute-start | bytes 417800 | tf_op jit(solution)/shard_map/ppermute | solution.py:621
  33.0 5.0 %collective-permute-start.11 = (f32[2,136,128]{2,1,0:T(8,128)S(1)}, f32[2,136,128]{2,1,0:T(8,128)S(1)}, u32[]{:S(2)}, u32[]{:S(2)}) collective-permute-start(f32[2,136,128]{2,1,0:T(8,128)S(1)} %get-tuple-element.99), channel_id=1, source_target_pairs={{0,1},{1,0},{2,3},{3,2},{4,5},{5,4},{6,7},{7,6},{8,9},{9,8},{10,11... | collective-permute-start | bytes 417800 | tf_op jit(solution)/shard_map/ppermute | solution.py:621

commit v17 on v15

--- a/solution.py
+++ b/solution.py
@@ -381,7 +381,7 @@
                  places[steps + 1], cols, corner)
 
     share = time_step * grad_energy
-    for s in range(2):
+    def side_rows(s, _):
         y, y1 = s * (rows - 1), 1 + s * (rows - 3)
         for at, size in chunks(low - 8, high + 8):
             span = slice(at, at + size)
@@ -431,6 +431,9 @@
                 inside[y1, span, :] + swing[1 + y1, span, :] * inward - grad_energy * more
             )
             edge_grad[s, span, :] = grad[y, span, :] + less * a
+        return 0
+
+    lax.fori_loop(0, 2, side_rows, 0)
     send_rows(out, ahead, rate, to_a, to_b, open_g, cols, nz)
 
 
@@ -451,7 +454,7 @@
                          set_row(swing.at[i], y), at, size, mask)
             return 0
 
-        lax.fori_loop(0, rows, row, 0, unroll=2)
+        lax.fori_loop(0, rows, row, 0, unroll=4)
 
 
 def prepare_kernel(steps, rows, cols, nz, back, conc_own, from_a, from_b, x_low, x_high,

time: 37.5 us -> 37.1 us (0.989)
  Pallas kernels: 16.6 us -> 16 us
    pallas_call x12, Pallas kernels: 16.6 us -> 16 us  [call(): pl.pallas_call(kernel, out_shape=[jax.ShapeDtypeStruct(shape, f32) for sh...]
  transfers between devices with their start and end apart: 12 -> 12, of which waited for: 5 -> 5; matrix products, arithmetic and copies ran while one was open for 0% -> 0% of each run, Pallas kernels for 33% -> 32%
where the time goes in v17:
time: 37.1 us; the launch traced here: 37 us
  Pallas kernels  16 us (43%)
  starting transfers between devices  14.5 us (39%)
  waiting for transfers between devices  5.77 us (16%)
  between operations  0.74 us (2%)
    pallas_call x12, Pallas kernels, call(): pl.pallas_call(kernel, out_shape=[jax.ShapeDtypeStruct(shape, f32) for sh...  16 us
    ppermute x6, starting transfers between devices, swap(): lax.ppermute(value_b, axis, pairs_b)  8.3 us
    ppermute x6, starting transfers between devices, swap(): lax.ppermute(value_a, axis, pairs_a)  6.22 us
    ppermute x6, waiting for transfers between devices, swap(): lax.ppermute(value_a, axis, pairs_a)  3.37 us
    ppermute x6, waiting for transfers between devices, swap(): lax.ppermute(value_b, axis, pairs_b)  2.4 us
  transfers between devices with their start and end apart: 12, of which 5 were waited for; matrix products, arithmetic and copies ran while one was open for 0% of the time, Pallas kernels for 32%

profile of v17, /device:TPU:0, one launch (start us, length us, event | category | flops | bytes accessed | tf_op | source)
XLA Modules:
  0.0 37.0 jit_solution(2471742701339809058)
XLA Ops:
  0.6 1.7 %shard_map.50 = (f32[3,1024,128]{2,1,0:T(8,128)S(1)}, f32[1024,128]{1,0:T(8,128)S(1)}, f32[512,128]{1,0:T(8,128)S(1)}, f32[832,128]{1,0:T(8,128)S(1)}, f32[832,128]{1,0:T(8,128)S(1)}) custom-call(f32[3,1024,128]{2,1,0:T(8,128)} %bitcast.5, f32[1024,128]{1,0:T(8,128)} %bitcast.6, f32[512,128]{1,0:T(8,128)} %bitcast.8), custom_call_target="tpu_custom_call" | custom-call | flops 2000000 | bytes 4000000 | tf_op jit(solution)/shard_map/pallas_call | solution.py:604
  2.3 0.5 %collective-permute-start = (f32[832,128]{1,0:T(8,128)S(1)}, f32[832,128]{1,0:T(8,128)S(1)}, u32[]{:S(2)}, u32[]{:S(2)}) collective-permute-start(f32[832,128]{1,0:T(8,128)S(1)} %get-tuple-element.56), channel_id=1, source_target_pairs={{0,1},{1,0},{2,3},{3,2},{4,5},{5,4},{6,7},{7,6},{8,9},{9,8},{10,11... | collective-permute-start | bytes 1277960 | tf_op jit(solution)/shard_map/ppermute | solution.py:624
  2.8 4.7 %collective-permute-start.1 = (f32[832,128]{1,0:T(8,128)S(1)}, f32[832,128]{1,0:T(8,128)S(1)}, u32[]{:S(2)}, u32[]{:S(2)}) collective-permute-start(f32[832,128]{1,0:T(8,128)S(1)} %get-tuple-element.57), channel_id=1, source_target_pairs={{0,7},{1,2},{2,1},{3,4},{4,3},{5,6},{6,5},{7,0},{8,15},{9,10},{10,... | collective-permute-start | bytes 1277960 | tf_op jit(solution)/shard_map/ppermute | solution.py:624
  7.5 0.7 %shard_map.51 = (f32[3,8,128,128]{3,2,1,0:T(8,128)S(1)}, f32[8,128,128]{2,1,0:T(8,128)S(1)}, f32[8,128,128]{2,1,0:T(8,128)S(1)}, f32[8,24,128]{2,1,0:T(8,128)S(1)}, f32[8,24,128]{2,1,0:T(8,128)S(1)}) custom-call(f32[3,1024,128]{2,1,0:T(8,128)S(1)} %get-tuple-element.52.conc_in, f32[1024,128]{1,0:T(8,128)S(1)} %get-tuple-element.53.adj_in, ...), custom_call_target="tpu_custom_call" | custom-call | flops 1000000 | bytes 2000000 | tf_op jit(solution)/shard_map/pallas_call | solution.py:604
  8.3 1.6 %collective-permute-start.2 = (f32[8,24,128]{2,1,0:T(8,128)S(1)}, f32[8,24,128]{2,1,0:T(8,128)S(1)}, u32[]{:S(2)}, u32[]{:S(2)}) collective-permute-start(f32[8,24,128]{2,1,0:T(8,128)S(1)} %get-tuple-element.58), channel_id=1, source_target_pairs={{0,8},{8,0},{16,24},{24,16},{1,9},{9,1},{17,25},{25,17},{2,10},{10... | collective-permute-start | bytes 294920 | tf_op jit(solution)/shard_map/ppermute | solution.py:624
  9.8 1.5 %collective-permute-start.3 = (f32[8,24,128]{2,1,0:T(8,128)S(1)}, f32[8,24,128]{2,1,0:T(8,128)S(1)}, u32[]{:S(2)}, u32[]{:S(2)}) collective-permute-start(f32[8,24,128]{2,1,0:T(8,128)S(1)} %get-tuple-element.59), channel_id=1, source_target_pairs={{0,24},{8,16},{16,8},{24,0},{1,25},{9,17},{17,9},{25,1},{2,26},{10... | collective-permute-start | bytes 294920 | tf_op jit(solution)/shard_map/ppermute | solution.py:624
  11.3 1.2 %shard_map.52 = (f32[2,8,160,128]{3,2,1,0:T(8,128)S(1)}, f32[2,8,160,128]{3,2,1,0:T(8,128)S(1)}, f32[2,8,160,128]{3,2,1,0:T(8,128)S(1)}, f32[2,8,160,128]{3,2,1,0:T(8,128)S(1)}) custom-call(f32[3,8,128,128]{3,2,1,0:T(8,128)S(1)} %get-tuple-element.55.conc_own), custom_call_target="tpu_custom_call" | custom-call | flops 2000000 | bytes 4000000 | tf_op jit(solution)/shard_map/pallas_call | solution.py:604
  12.6 0.7 %collective-permute-done.2.got_a = f32[8,24,128]{2,1,0:T(8,128)S(1)} collective-permute-done((f32[8,24,128]{2,1,0:T(8,128)S(1)}, f32[8,24,128]{2,1,0:T(8,128)S(1)}, u32[]{:S(2)}, u32[]{:S(2)}) %collective-permute-start.2) | collective-permute-done | bytes 98336 | tf_op jit(solution)/shard_map/ppermute | solution.py:624
  13.3 2.1 %collective-permute-done.3.got_b = f32[8,24,128]{2,1,0:T(8,128)S(1)} collective-permute-done((f32[8,24,128]{2,1,0:T(8,128)S(1)}, f32[8,24,128]{2,1,0:T(8,128)S(1)}, u32[]{:S(2)}, u32[]{:S(2)}) %collective-permute-start.3) | collective-permute-done | bytes 98336 | tf_op jit(solution)/shard_map/ppermute | solution.py:624
  15.4 0.1 collective-permute-start.4
  15.5 0.1 collective-permute-start.5
  15.6 3.3 %shard_map.56 = (f32[10,160,128]{2,1,0:T(8,128)S(1)}, f32[10,160,128]{2,1,0:T(8,128)S(1)}, f32[8,160,128]{2,1,0:T(8,128)S(1)}, f32[10,160,128]{2,1,0:T(8,128)S(1...) custom-call(f32[3,8,128,128]{3,2,1,0:T(8,128)S(1)} %get-tuple-elemen, ...), custom_call_target="tpu_custom_call" | custom-call | flops 3000000 | bytes 6000000 | tf_op jit(solution)/shard_map/pallas_call | solution.py:604
  18.8 2.0 %collective-permute-done.4.corner_b = f32[2,2,24,128]{3,2,1,0:T(8,128)S(1)} collective-permute-done((f32[2,2,24,128]{3,2,1,0:T(8,128)S(1)}, f32[2,2,24,128]{3,2,1,0:T(8,128)S(1)}, u32[]{:S(2)}, u32[]{:S(2)}) %collective-permute-start.4) | collective-permute-done | bytes 49184 | tf_op jit(solution)/shard_map/ppermute | solution.py:624
  20.8 0.0 collective-permute-done.5.corner_a
  20.8 0.0 collective-permute-done.from_a
  20.8 0.0 collective-permute-done.1.from_b
  20.8 1.2 %shard_map.57 = (f32[2,2,160,128]{3,2,1,0:T(8,128)S(1)}, f32[2,160,128]{2,1,0:T(8,128)S(1)}, f32[2,136,128]{2,1,0:T(8,128)S(1)}, f32[2,136,128]{2,1,0:T(8,128)S(1)}) custom-call(f32[10,160,128]{2,1,0:T(8,128)S(1)} %get-tuple-element.82.conc, f32[10,160,128]{2,1,0:T(8,128)S(1)} %get-tuple-element.83.adj, f32[8,160,128]{2,1,0:T(8,128)S(1)} %get-tuple-element.76.rate.rest_1_, ...), custom_call_target="tpu_custom_call" | custom-call | flops 2000000 | bytes 4000000 | tf_op jit(solution)/shard_map/pallas_call | solution.py:604
  22.0 1.6 %collective-permute-start.8 = (f32[2,136,128]{2,1,0:T(8,128)S(1)}, f32[2,136,128]{2,1,0:T(8,128)S(1)}, u32[]{:S(2)}, u32[]{:S(2)}) collective-permute-start(f32[2,136,128]{2,1,0:T(8,128)S(1)} %get-tuple-element.92), channel_id=1, source_target_pairs={{0,7},{1,2},{2,1},{3,4},{4,3},{5,6},{6,5},{7,0},{8,15},{9,10},{10,... | collective-permute-start | bytes 417800 | tf_op jit(solution)/shard_map/ppermute | solution.py:624
  23.6 0.0 collective-permute-start.9
  23.6 0.5 %shard_map.54 = (f32[12,160,128]{2,1,0:T(8,128)S(1)}, f32[10,160,128]{2,1,0:T(8,128)S(1)}, f32[10,160,128]{2,1,0:T(8,128)S(1)}, f32[10,160,128]{2,1,0:T(8,128)S(...) custom-call(f32[3,8,128,128]{3,2,1,0:T(8,128)S(1)} %get-tuple-element.55.conc_own, ...), custom_call_target="tpu_custom_call" | custom-call | flops 2000000 | bytes 4000000 | tf_op jit(solution)/shard_map/pallas_call | solution.py:604
  24.1 0.6 %collective-permute-start.6 = (f32[280,128]{1,0:T(8,128)S(1)}, f32[280,128]{1,0:T(8,128)S(1)}, u32[]{:S(2)}, u32[]{:S(2)}) collective-permute-start(f32[280,128]{1,0:T(8,128)S(1)} %get-tuple-element.68), channel_id=1, source_target_pairs={{0,1},{1,0},{2,3},{3,2},{4,5},{5,4},{6,7},{7,6},{8,9},{9,8},{10,11... | collective-permute-start | bytes 430088 | tf_op jit(solution)/shard_map/ppermute | solution.py:624
  24.7 2.0 %collective-permute-start.7 = (f32[280,128]{1,0:T(8,128)S(1)}, f32[280,128]{1,0:T(8,128)S(1)}, u32[]{:S(2)}, u32[]{:S(2)}) collective-permute-start(f32[280,128]{1,0:T(8,128)S(1)} %get-tuple-element.69), channel_id=1, source_target_pairs={{0,7},{1,2},{2,1},{3,4},{4,3},{5,6},{6,5},{7,0},{8,15},{9,10},{10,... | collective-permute-start | bytes 430088 | tf_op jit(solution)/shard_map/ppermute | solution.py:624
  26.7 2.4 %shard_map.58 = (f32[8,160,128]{2,1,0:T(8,128)S(1)}, f32[8,160,128]{2,1,0:T(8,128)S(1)}) custom-call(f32[12,160,128]{2,1,0:T(8,128)S(1)} %get-tuple-element.77.mob, f32[10,160,128]{2,1,0:T(8,128)S(1)} %get-tuple-element.78.chem, f32[10,160,128]{2,1,0:T(8,128)S(1)} %get-tuple-element.79.curve, f32[10,160,128]{2,1,0:T(8,128)S(1)} %get-tuple-element.80.swing, ...), custom_call_target="tpu_custom_call" | custom-call | flops 3000000 | bytes 6000000 | tf_op jit(solution)/shard_map/pallas_call | solution.py:604
  29.0 0.0 collective-permute-done.8.from_a
  29.1 0.0 collective-permute-done.9.from_b
  29.1 0.4 %shard_map.59 = (f32[2,2,160,128]{3,2,1,0:T(8,128)S(1)}, f32[2,136,128]{2,1,0:T(8,128)S(1)}, f32[2,136,128]{2,1,0:T(8,128)S(1)}) custom-call(f32[12,160,128]{2,1,0:T(8,128)S(1)} %get-tuple-element.77.mob, f32[10,160,128]{2,1,0:T(8,128)S(1)} %get-tuple-element.78.chem, f32[10,160,128]{2,1,0:T(8,128)S(1)} %get-tuple-element.79.curve, ...), custom_call_target="tpu_custom_call" | custom-call | flops 1000000 | bytes 2000000 | tf_op jit(solution)/shard_map/pallas_call | solution.py:604
  29.5 1.9 %collective-permute-start.10 = (f32[2,136,128]{2,1,0:T(8,128)S(1)}, f32[2,136,128]{2,1,0:T(8,128)S(1)}, u32[]{:S(2)}, u32[]{:S(2)}) collective-permute-start(f32[2,136,128]{2,1,0:T(8,128)S(1)} %get-tuple-element.98), channel_id=1, source_target_pairs={{0,7},{1,2},{2,1},{3,4},{4,3},{5,6},{6,5},{7,0},{8,15},{9,10},{10,... | collective-permute-start | bytes 417800 | tf_op jit(solution)/shard_map/ppermute | solution.py:624
  31.4 0.0 collective-permute-start.11
  31.4 0.0 collective-permute-done.6.from_a
  31.4 0.3 collective-permute-done.7.from_b
  31.7 0.5 %shard_map.55 = (f32[12,160,128]{2,1,0:T(8,128)S(1)}, f32[10,160,128]{2,1,0:T(8,128)S(1)}, f32[10,160,128]{2,1,0:T(8,128)S(1)}, f32[10,160,128]{2,1,0:T(8,128)S(1)}) custom-call(f32[3,8,128,128]{3,2,1,0:T(8,128)S(1)} %get-tuple-element.55.conc_own, f32[280,128]{1,0:T(8,128)S(1)} %collective-permute-done.6.from_a, ...), custom_call_target="tpu_custom_call" | custom-call | flops 2000000 | bytes 4000000 | tf_op jit(solution)/shard_map/pallas_call | solution.py:604
  32.2 2.9 %shard_map.60 = (f32[8,160,128]{2,1,0:T(8,128)S(1)}, f32[1024,128]{1,0:T(8,128)S(1)}, f32[512,128]{1,0:T(8,128)}) custom-call(f32[12,160,128]{2,1,0:T(8,128)S(1)} %get-tuple-element.70.mob, f32[10,160,128]{2,1,0:T(8,128)S(1)} %get-tuple-element.71.chem, f32[10,160,128]{2,1,0:T(8,128)S(1)} %get-tuple-element.72.curve, ...), custom_call_target="tpu_custom_call" | custom-call | flops 3000000 | bytes 6000000 | tf_op jit(solution)/shard_map/pallas_call | solution.py:604
  35.1 0.7 %collective-permute-done.10.from_a = f32[2,136,128]{2,1,0:T(8,128)S(1)} collective-permute-done((f32[2,136,128]{2,1,0:T(8,128)S(1)}, f32[2,136,128]{2,1,0:T(8,128)S(1)}, u32[]{:S(2)}, u32[]{:S(2)}) %collective-permute-start.10) | collective-permute-done | bytes 139296 | tf_op jit(solution)/shard_map/ppermute | solution.py:624
  35.8 0.0 collective-permute-done.11.from_b
  35.8 1.2 %shard_map.61 = f32[1024,128]{1,0:T(8,128)} custom-call(f32[12,160,128]{2,1,0:T(8,128)S(1)} %get-tuple-element.70.mob, f32[10,160,128]{2,1,0:T(8,128)S(1)} %get-tuple-element.71.chem, f32[10,160,128]{2,1,0:T(8,128)S(1)} %get-tuple-element.72.curve, f32[10,160,128]{2,1,0:T(8,128)S(1)} %get-tuple-element.73.swing, ...), custom_call_target="tpu_custom_call" | custom-call | flops 1000000 | bytes 2000000 | tf_op jit(solution)/shard_map/pallas_call | solution.py:604
  (1 shorter events, 0.0 us)
Async XLA Ops:
  2.3 18.5 %collective-permute-start = (f32[832,128]{1,0:T(8,128)S(1)}, f32[832,128]{1,0:T(8,128)S(1)}, u32[]{:S(2)}, u32[]{:S(2)}) collective-permute-start(f32[832,128]{1,0:T(8,128)S(1)} %get-tuple-element.56), channel_id=1, source_target_pairs={{0,1},{1,0},{2,3},{3,2},{4,5},{5,4},{6,7},{7,6},{8,9},{9,8},{10,11... | collective-permute-start | bytes 1277960 | tf_op jit(solution)/shard_map/ppermute | solution.py:624
  2.8 18.0 %collective-permute-start.1 = (f32[832,128]{1,0:T(8,128)S(1)}, f32[832,128]{1,0:T(8,128)S(1)}, u32[]{:S(2)}, u32[]{:S(2)}) collective-permute-start(f32[832,128]{1,0:T(8,128)S(1)} %get-tuple-element.57), channel_id=1, source_target_pairs={{0,7},{1,2},{2,1},{3,4},{4,3},{5,6},{6,5},{7,0},{8,15},{9,10},{10,... | collective-permute-start | bytes 1277960 | tf_op jit(solution)/shard_map/ppermute | solution.py:624
  8.3 5.0 %collective-permute-start.2 = (f32[8,24,128]{2,1,0:T(8,128)S(1)}, f32[8,24,128]{2,1,0:T(8,128)S(1)}, u32[]{:S(2)}, u32[]{:S(2)}) collective-permute-start(f32[8,24,128]{2,1,0:T(8,128)S(1)} %get-tuple-element.58), channel_id=1, source_target_pairs={{0,8},{8,0},{16,24},{24,16},{1,9},{9,1},{17,25},{25,17},{2,10},{10... | collective-permute-start | bytes 294920 | tf_op jit(solution)/shard_map/ppermute | solution.py:624
  9.8 5.5 %collective-permute-start.3 = (f32[8,24,128]{2,1,0:T(8,128)S(1)}, f32[8,24,128]{2,1,0:T(8,128)S(1)}, u32[]{:S(2)}, u32[]{:S(2)}) collective-permute-start(f32[8,24,128]{2,1,0:T(8,128)S(1)} %get-tuple-element.59), channel_id=1, source_target_pairs={{0,24},{8,16},{16,8},{24,0},{1,25},{9,17},{17,9},{25,1},{2,26},{10... | collective-permute-start | bytes 294920 | tf_op jit(solution)/shard_map/ppermute | solution.py:624
  15.4 5.4 %collective-permute-start.4 = (f32[2,2,24,128]{3,2,1,0:T(8,128)S(1)}, f32[2,2,24,128]{3,2,1,0:T(8,128)S(1)}, u32[]{:S(2)}, u32[]{:S(2)}) collective-permute-start(f32[2,2,24,128]{3,2,1,0:T(8,128)S(1)} %get-tuple-element.63), channel_id=1, source_target_pairs={{0,7},{1,2},{2,1},{3,4},{4,3},{5,6},{6,5},{7,0},{8,15},{9,10},{10,... | collective-permute-start | bytes 147464 | tf_op jit(solution)/shard_map/ppermute | solution.py:624
  15.5 5.3 %collective-permute-start.5 = (f32[2,2,24,128]{3,2,1,0:T(8,128)S(1)}, f32[2,2,24,128]{3,2,1,0:T(8,128)S(1)}, u32[]{:S(2)}, u32[]{:S(2)}) collective-permute-start(f32[2,2,24,128]{3,2,1,0:T(8,128)S(1)} %get-tuple-element.64), channel_id=1, source_target_pairs={{0,1},{1,0},{2,3},{3,2},{4,5},{5,4},{6,7},{7,6},{8,9},{9,8},{10,11... | collective-permute-start | bytes 147464 | tf_op jit(solution)/shard_map/ppermute | solution.py:624
  22.0 7.1 %collective-permute-start.8 = (f32[2,136,128]{2,1,0:T(8,128)S(1)}, f32[2,136,128]{2,1,0:T(8,128)S(1)}, u32[]{:S(2)}, u32[]{:S(2)}) collective-permute-start(f32[2,136,128]{2,1,0:T(8,128)S(1)} %get-tuple-element.92), channel_id=1, source_target_pairs={{0,7},{1,2},{2,1},{3,4},{4,3},{5,6},{6,5},{7,0},{8,15},{9,10},{10,... | collective-permute-start | bytes 417800 | tf_op jit(solution)/shard_map/ppermute | solution.py:624
  23.6 5.5 %collective-permute-start.9 = (f32[2,136,128]{2,1,0:T(8,128)S(1)}, f32[2,136,128]{2,1,0:T(8,128)S(1)}, u32[]{:S(2)}, u32[]{:S(2)}) collective-permute-start(f32[2,136,128]{2,1,0:T(8,128)S(1)} %get-tuple-element.93), channel_id=1, source_target_pairs={{0,1},{1,0},{2,3},{3,2},{4,5},{5,4},{6,7},{7,6},{8,9},{9,8},{10,11... | collective-permute-start | bytes 417800 | tf_op jit(solution)/shard_map/ppermute | solution.py:624
  24.1 7.3 %collective-permute-start.6 = (f32[280,128]{1,0:T(8,128)S(1)}, f32[280,128]{1,0:T(8,128)S(1)}, u32[]{:S(2)}, u32[]{:S(2)}) collective-permute-start(f32[280,128]{1,0:T(8,128)S(1)} %get-tuple-element.68), channel_id=1, source_target_pairs={{0,1},{1,0},{2,3},{3,2},{4,5},{5,4},{6,7},{7,6},{8,9},{9,8},{10,11... | collective-permute-start | bytes 430088 | tf_op jit(solution)/shard_map/ppermute | solution.py:624
  24.7 7.0 %collective-permute-start.7 = (f32[280,128]{1,0:T(8,128)S(1)}, f32[280,128]{1,0:T(8,128)S(1)}, u32[]{:S(2)}, u32[]{:S(2)}) collective-permute-start(f32[280,128]{1,0:T(8,128)S(1)} %get-tuple-element.69), channel_id=1, source_target_pairs={{0,7},{1,2},{2,1},{3,4},{4,3},{5,6},{6,5},{7,0},{8,15},{9,10},{10,... | collective-permute-start | bytes 430088 | tf_op jit(solution)/shard_map/ppermute | solution.py:624
  29.5 6.3 %collective-permute-start.10 = (f32[2,136,128]{2,1,0:T(8,128)S(1)}, f32[2,136,128]{2,1,0:T(8,128)S(1)}, u32[]{:S(2)}, u32[]{:S(2)}) collective-permute-start(f32[2,136,128]{2,1,0:T(8,128)S(1)} %get-tuple-element.98), channel_id=1, source_target_pairs={{0,7},{1,2},{2,1},{3,4},{4,3},{5,6},{6,5},{7,0},{8,15},{9,10},{10,... | collective-permute-start | bytes 417800 | tf_op jit(solution)/shard_map/ppermute | solution.py:624
  31.4 4.4 %collective-permute-start.11 = (f32[2,136,128]{2,1,0:T(8,128)S(1)}, f32[2,136,128]{2,1,0:T(8,128)S(1)}, u32[]{:S(2)}, u32[]{:S(2)}) collective-permute-start(f32[2,136,128]{2,1,0:T(8,128)S(1)} %get-tuple-element.99), channel_id=1, source_target_pairs={{0,1},{1,0},{2,3},{3,2},{4,5},{5,4},{6,7},{7,6},{8,9},{9,8},{10,11... | collective-permute-start | bytes 417800 | tf_op jit(solution)/shard_map/ppermute | solution.py:624

commit v18 on v17

--- a/solution.py
+++ b/solution.py
@@ -249,7 +249,7 @@
         x_b[y, start : start + width, :] = jnp.where(next_x, first, last)
 
     used = sum(places[-1])
-    for y in range(rows):
+    def one_row(y, _):
         adj = adj_in[pl.ds(y, lanes, stride=rows), :].T
         adj_out[y] = adj
         to_x(y, adj, places[0])
@@ -263,6 +263,9 @@
             conc = conc_in[back, pl.ds(y, lanes, stride=rows), :].T
             conc_out[back, y] = conc
             to_x(y, conc, places[1 + back])
+        return 0
+
+    lax.fori_loop(0, rows, one_row, 0, unroll=2)
 
 
 def put_own(out, row, value, y, place, cols, x_low, x_high):
@@ -328,7 +331,7 @@
     first, last = sent(cols)
     rows, lanes = rate.shape[0], rate.shape[2]
     mask = face_mask(lanes, nz)
-    for s in range(2):
+    def side_rows(s, _):
         for at, size in chunks(low, high):
             a, _mu, flow, _pair = face_sums(
                 lambda dy, cut: out[s, dy, cut, :], lambda dy, cut: ahead[s, dy, cut, :], None,
@@ -337,6 +340,9 @@
             open_g[s, at - low : at - low + size, :] = (
                 flow - rate[s * (rows - 1), at : at + size, :] * a
             )
+        return 0
+
+    lax.fori_loop(0, 2, side_rows, 0)
     to_next = a_is_next("gy", round_first)
     for to, side in ((to_a, jnp.where(to_next, 1, 0)), (to_b, jnp.where(to_next, 0, 1))):
         to[0] = out[side, 0, first:last, :]
@@ -564,7 +570,7 @@
     for got, side in ((from_a, jnp.where(to_next, 1, 0)), (from_b, jnp.where(to_next, 0, 1))):
         for k in range(2):
             halo[side, k, first:last, :] = got[k]
-    for s in range(2):
+    def side_rows(s, _):
         y, beyond = s * (rows - 1), s * (rows + 1) - 1
         for at, size in chunks(low, high):
             span = slice(at, at + size)
@@ -589,6 +595,9 @@
                 - grad_energy * lap
             )
             result[s, 1, span, :] = inside[1 + s * (rows - 3), span, :] - grad_energy * more
+        return 0
+
+    lax.fori_loop(0, 2, side_rows, 0)
     if final:
         out[...] = tiles[...]
         for s, k, y in sides_of(rows):

time: 37.1 us -> 38 us (1.024)
  Pallas kernels: 16 us -> 16.8 us
    pallas_call x12, Pallas kernels: 16 us -> 16.8 us  [call(): pl.pallas_call(kernel, out_shape=[jax.ShapeDtypeStruct(shape, f32) for sh...]
  transfers between devices with their start and end apart: 12 -> 12, of which waited for: 5 -> 4; matrix products, arithmetic and copies ran while one was open for 0% -> 0% of each run, Pallas kernels for 32% -> 33%
where the time goes in v18:
time: 38 us; the launch traced here: 37.8 us
  Pallas kernels  16.8 us (44%)
  starting transfers between devices  14.5 us (38%)
  waiting for transfers between devices  5.77 us (15%)
  between operations  0.75 us (2%)
    pallas_call x12, Pallas kernels, call(): pl.pallas_call(kernel, out_shape=[jax.ShapeDtypeStruct(shape, f32) for sh...  16.8 us
    ppermute x6, starting transfers between devices, swap(): lax.ppermute(value_b, axis, pairs_b)  8.3 us
    ppermute x6, starting transfers between devices, swap(): lax.ppermute(value_a, axis, pairs_a)  6.22 us
    ppermute x6, waiting for transfers between devices, swap(): lax.ppermute(value_a, axis, pairs_a)  3.67 us
    ppermute x6, waiting for transfers between devices, swap(): lax.ppermute(value_b, axis, pairs_b)  2.1 us
  transfers between devices with their start and end apart: 12, of which 4 were waited for; matrix products, arithmetic and copies ran while one was open for 0% of the time, Pallas kernels for 33%

profile of v18, /device:TPU:0, one launch (start us, length us, event | category | flops | bytes accessed | tf_op | source)
XLA Modules:
  0.0 37.8 jit_solution(15122428646091916679)
XLA Ops:
  0.6 1.7 %shard_map.50 = (f32[3,1024,128]{2,1,0:T(8,128)S(1)}, f32[1024,128]{1,0:T(8,128)S(1)}, f32[512,128]{1,0:T(8,128)S(1)}, f32[832,128]{1,0:T(8,128)S(1)}, f32[832,128]{1,0:T(8,128)S(1)}) custom-call(f32[3,1024,128]{2,1,0:T(8,128)} %bitcast.5, f32[1024,128]{1,0:T(8,128)} %bitcast.6, f32[512,128]{1,0:T(8,128)} %bitcast.8), custom_call_target="tpu_custom_call" | custom-call | flops 2000000 | bytes 4000000 | tf_op jit(solution)/shard_map/pallas_call | solution.py:613
  2.3 0.5 %collective-permute-start = (f32[832,128]{1,0:T(8,128)S(1)}, f32[832,128]{1,0:T(8,128)S(1)}, u32[]{:S(2)}, u32[]{:S(2)}) collective-permute-start(f32[832,128]{1,0:T(8,128)S(1)} %get-tuple-element.56), channel_id=1, source_target_pairs={{0,1},{1,0},{2,3},{3,2},{4,5},{5,4},{6,7},{7,6},{8,9},{9,8},{10,11... | collective-permute-start | bytes 1277960 | tf_op jit(solution)/shard_map/ppermute | solution.py:633
  2.8 4.7 %collective-permute-start.1 = (f32[832,128]{1,0:T(8,128)S(1)}, f32[832,128]{1,0:T(8,128)S(1)}, u32[]{:S(2)}, u32[]{:S(2)}) collective-permute-start(f32[832,128]{1,0:T(8,128)S(1)} %get-tuple-element.57), channel_id=1, source_target_pairs={{0,7},{1,2},{2,1},{3,4},{4,3},{5,6},{6,5},{7,0},{8,15},{9,10},{10,... | collective-permute-start | bytes 1277960 | tf_op jit(solution)/shard_map/ppermute | solution.py:633
  7.5 1.0 %shard_map.51 = (f32[3,8,128,128]{3,2,1,0:T(8,128)S(1)}, f32[8,128,128]{2,1,0:T(8,128)S(1)}, f32[8,128,128]{2,1,0:T(8,128)S(1)}, f32[8,24,128]{2,1,0:T(8,128)S(1)}, f32[8,24,128]{2,1,0:T(8,128)S(1)}) custom-call(f32[3,1024,128]{2,1,0:T(8,128)S(1)} %get-tuple-element.52.conc_in, f32[1024,128]{1,0:T(8,128)S(1)} %get-tuple-element.53.adj_in, ...), custom_call_target="tpu_custom_call" | custom-call | flops 1000000 | bytes 2000000 | tf_op jit(solution)/shard_map/pallas_call | solution.py:613
  8.5 1.6 %collective-permute-start.2 = (f32[8,24,128]{2,1,0:T(8,128)S(1)}, f32[8,24,128]{2,1,0:T(8,128)S(1)}, u32[]{:S(2)}, u32[]{:S(2)}) collective-permute-start(f32[8,24,128]{2,1,0:T(8,128)S(1)} %get-tuple-element.58), channel_id=1, source_target_pairs={{0,8},{8,0},{16,24},{24,16},{1,9},{9,1},{17,25},{25,17},{2,10},{10... | collective-permute-start | bytes 294920 | tf_op jit(solution)/shard_map/ppermute | solution.py:633
  10.1 1.5 %collective-permute-start.3 = (f32[8,24,128]{2,1,0:T(8,128)S(1)}, f32[8,24,128]{2,1,0:T(8,128)S(1)}, u32[]{:S(2)}, u32[]{:S(2)}) collective-permute-start(f32[8,24,128]{2,1,0:T(8,128)S(1)} %get-tuple-element.59), channel_id=1, source_target_pairs={{0,24},{8,16},{16,8},{24,0},{1,25},{9,17},{17,9},{25,1},{2,26},{10... | collective-permute-start | bytes 294920 | tf_op jit(solution)/shard_map/ppermute | solution.py:633
  11.6 1.2 %shard_map.52 = (f32[2,8,160,128]{3,2,1,0:T(8,128)S(1)}, f32[2,8,160,128]{3,2,1,0:T(8,128)S(1)}, f32[2,8,160,128]{3,2,1,0:T(8,128)S(1)}, f32[2,8,160,128]{3,2,1,0:T(8,128)S(1)}) custom-call(f32[3,8,128,128]{3,2,1,0:T(8,128)S(1)} %get-tuple-element.55.conc_own), custom_call_target="tpu_custom_call" | custom-call | flops 2000000 | bytes 4000000 | tf_op jit(solution)/shard_map/pallas_call | solution.py:613
  12.8 0.7 %collective-permute-done.2.got_a = f32[8,24,128]{2,1,0:T(8,128)S(1)} collective-permute-done((f32[8,24,128]{2,1,0:T(8,128)S(1)}, f32[8,24,128]{2,1,0:T(8,128)S(1)}, u32[]{:S(2)}, u32[]{:S(2)}) %collective-permute-start.2) | collective-permute-done | bytes 98336 | tf_op jit(solution)/shard_map/ppermute | solution.py:633
  13.5 2.1 %collective-permute-done.3.got_b = f32[8,24,128]{2,1,0:T(8,128)S(1)} collective-permute-done((f32[8,24,128]{2,1,0:T(8,128)S(1)}, f32[8,24,128]{2,1,0:T(8,128)S(1)}, u32[]{:S(2)}, u32[]{:S(2)}) %collective-permute-start.3) | collective-permute-done | bytes 98336 | tf_op jit(solution)/shard_map/ppermute | solution.py:633
  15.6 0.1 collective-permute-start.4
  15.7 0.1 collective-permute-start.5
  15.8 3.3 %shard_map.56 = (f32[10,160,128]{2,1,0:T(8,128)S(1)}, f32[10,160,128]{2,1,0:T(8,128)S(1)}, f32[8,160,128]{2,1,0:T(8,128)S(1)}, f32[10,160,128]{2,1,0:T(8,128)S(1...) custom-call(f32[3,8,128,128]{3,2,1,0:T(8,128)S(1)} %get-tuple-elemen, ...), custom_call_target="tpu_custom_call" | custom-call | flops 3000000 | bytes 6000000 | tf_op jit(solution)/shard_map/pallas_call | solution.py:613
  19.0 2.0 %collective-permute-done.4.corner_b = f32[2,2,24,128]{3,2,1,0:T(8,128)S(1)} collective-permute-done((f32[2,2,24,128]{3,2,1,0:T(8,128)S(1)}, f32[2,2,24,128]{3,2,1,0:T(8,128)S(1)}, u32[]{:S(2)}, u32[]{:S(2)}) %collective-permute-start.4) | collective-permute-done | bytes 49184 | tf_op jit(solution)/shard_map/ppermute | solution.py:633
  21.0 0.0 collective-permute-done.5.corner_a
  21.0 0.0 collective-permute-done.from_a
  21.0 0.0 collective-permute-done.1.from_b
  21.0 1.3 %shard_map.57 = (f32[2,2,160,128]{3,2,1,0:T(8,128)S(1)}, f32[2,160,128]{2,1,0:T(8,128)S(1)}, f32[2,136,128]{2,1,0:T(8,128)S(1)}, f32[2,136,128]{2,1,0:T(8,128)S(1)}) custom-call(f32[10,160,128]{2,1,0:T(8,128)S(1)} %get-tuple-element.82.conc, f32[10,160,128]{2,1,0:T(8,128)S(1)} %get-tuple-element.83.adj, f32[8,160,128]{2,1,0:T(8,128)S(1)} %get-tuple-element.76.rate.rest_1_, ...), custom_call_target="tpu_custom_call" | custom-call | flops 2000000 | bytes 4000000 | tf_op jit(solution)/shard_map/pallas_call | solution.py:613
  22.3 1.6 %collective-permute-start.8 = (f32[2,136,128]{2,1,0:T(8,128)S(1)}, f32[2,136,128]{2,1,0:T(8,128)S(1)}, u32[]{:S(2)}, u32[]{:S(2)}) collective-permute-start(f32[2,136,128]{2,1,0:T(8,128)S(1)} %get-tuple-element.92), channel_id=1, source_target_pairs={{0,7},{1,2},{2,1},{3,4},{4,3},{5,6},{6,5},{7,0},{8,15},{9,10},{10,... | collective-permute-start | bytes 417800 | tf_op jit(solution)/shard_map/ppermute | solution.py:633
  23.9 0.0 collective-permute-start.9
  23.9 0.5 %shard_map.54 = (f32[12,160,128]{2,1,0:T(8,128)S(1)}, f32[10,160,128]{2,1,0:T(8,128)S(1)}, f32[10,160,128]{2,1,0:T(8,128)S(1)}, f32[10,160,128]{2,1,0:T(8,128)S(...) custom-call(f32[3,8,128,128]{3,2,1,0:T(8,128)S(1)} %get-tuple-element.55.conc_own, ...), custom_call_target="tpu_custom_call" | custom-call | flops 2000000 | bytes 4000000 | tf_op jit(solution)/shard_map/pallas_call | solution.py:613
  24.4 0.6 %collective-permute-start.6 = (f32[280,128]{1,0:T(8,128)S(1)}, f32[280,128]{1,0:T(8,128)S(1)}, u32[]{:S(2)}, u32[]{:S(2)}) collective-permute-start(f32[280,128]{1,0:T(8,128)S(1)} %get-tuple-element.68), channel_id=1, source_target_pairs={{0,1},{1,0},{2,3},{3,2},{4,5},{5,4},{6,7},{7,6},{8,9},{9,8},{10,11... | collective-permute-start | bytes 430088 | tf_op jit(solution)/shard_map/ppermute | solution.py:633
  25.0 2.0 %collective-permute-start.7 = (f32[280,128]{1,0:T(8,128)S(1)}, f32[280,128]{1,0:T(8,128)S(1)}, u32[]{:S(2)}, u32[]{:S(2)}) collective-permute-start(f32[280,128]{1,0:T(8,128)S(1)} %get-tuple-element.69), channel_id=1, source_target_pairs={{0,7},{1,2},{2,1},{3,4},{4,3},{5,6},{6,5},{7,0},{8,15},{9,10},{10,... | collective-permute-start | bytes 430088 | tf_op jit(solution)/shard_map/ppermute | solution.py:633
  27.0 2.4 %shard_map.58 = (f32[8,160,128]{2,1,0:T(8,128)S(1)}, f32[8,160,128]{2,1,0:T(8,128)S(1)}) custom-call(f32[12,160,128]{2,1,0:T(8,128)S(1)} %get-tuple-element.77.mob, f32[10,160,128]{2,1,0:T(8,128)S(1)} %get-tuple-element.78.chem, f32[10,160,128]{2,1,0:T(8,128)S(1)} %get-tuple-element.79.curve, f32[10,160,128]{2,1,0:T(8,128)S(1)} %get-tuple-element.80.swing, ...), custom_call_target="tpu_custom_call" | custom-call | flops 3000000 | bytes 6000000 | tf_op jit(solution)/shard_map/pallas_call | solution.py:613
  29.4 0.0 collective-permute-done.8.from_a
  29.4 0.0 collective-permute-done.9.from_b
  29.4 0.7 %shard_map.59 = (f32[2,2,160,128]{3,2,1,0:T(8,128)S(1)}, f32[2,136,128]{2,1,0:T(8,128)S(1)}, f32[2,136,128]{2,1,0:T(8,128)S(1)}) custom-call(f32[12,160,128]{2,1,0:T(8,128)S(1)} %get-tuple-element.77.mob, f32[10,160,128]{2,1,0:T(8,128)S(1)} %get-tuple-element.78.chem, f32[10,160,128]{2,1,0:T(8,128)S(1)} %get-tuple-element.79.curve, ...), custom_call_target="tpu_custom_call" | custom-call | flops 1000000 | bytes 2000000 | tf_op jit(solution)/shard_map/pallas_call | solution.py:613
  30.1 1.9 %collective-permute-start.10 = (f32[2,136,128]{2,1,0:T(8,128)S(1)}, f32[2,136,128]{2,1,0:T(8,128)S(1)}, u32[]{:S(2)}, u32[]{:S(2)}) collective-permute-start(f32[2,136,128]{2,1,0:T(8,128)S(1)} %get-tuple-element.98), channel_id=1, source_target_pairs={{0,7},{1,2},{2,1},{3,4},{4,3},{5,6},{6,5},{7,0},{8,15},{9,10},{10,... | collective-permute-start | bytes 417800 | tf_op jit(solution)/shard_map/ppermute | solution.py:633
  32.1 0.0 collective-permute-start.11
  32.1 0.0 collective-permute-done.6.from_a
  32.1 0.0 collective-permute-done.7.from_b
  32.1 0.5 %shard_map.55 = (f32[12,160,128]{2,1,0:T(8,128)S(1)}, f32[10,160,128]{2,1,0:T(8,128)S(1)}, f32[10,160,128]{2,1,0:T(8,128)S(1)}, f32[10,160,128]{2,1,0:T(8,128)S(1)}) custom-call(f32[3,8,128,128]{3,2,1,0:T(8,128)S(1)} %get-tuple-element.55.conc_own, f32[280,128]{1,0:T(8,128)S(1)} %collective-permute-done.6.from_a, ...), custom_call_target="tpu_custom_call" | custom-call | flops 2000000 | bytes 4000000 | tf_op jit(solution)/shard_map/pallas_call | solution.py:613
  32.5 2.9 %shard_map.60 = (f32[8,160,128]{2,1,0:T(8,128)S(1)}, f32[1024,128]{1,0:T(8,128)S(1)}, f32[512,128]{1,0:T(8,128)}) custom-call(f32[12,160,128]{2,1,0:T(8,128)S(1)} %get-tuple-element.70.mob, f32[10,160,128]{2,1,0:T(8,128)S(1)} %get-tuple-element.71.chem, f32[10,160,128]{2,1,0:T(8,128)S(1)} %get-tuple-element.72.curve, ...), custom_call_target="tpu_custom_call" | custom-call | flops 3000000 | bytes 6000000 | tf_op jit(solution)/shard_map/pallas_call | solution.py:613
  35.5 1.0 %collective-permute-done.10.from_a = f32[2,136,128]{2,1,0:T(8,128)S(1)} collective-permute-done((f32[2,136,128]{2,1,0:T(8,128)S(1)}, f32[2,136,128]{2,1,0:T(8,128)S(1)}, u32[]{:S(2)}, u32[]{:S(2)}) %collective-permute-start.10) | collective-permute-done | bytes 139296 | tf_op jit(solution)/shard_map/ppermute | solution.py:633
  36.5 0.0 collective-permute-done.11.from_b
  36.5 1.3 %shard_map.61 = f32[1024,128]{1,0:T(8,128)} custom-call(f32[12,160,128]{2,1,0:T(8,128)S(1)} %get-tuple-element.70.mob, f32[10,160,128]{2,1,0:T(8,128)S(1)} %get-tuple-element.71.chem, f32[10,160,128]{2,1,0:T(8,128)S(1)} %get-tuple-element.72.curve, f32[10,160,128]{2,1,0:T(8,128)S(1)} %get-tuple-element.73.swing, ...), custom_call_target="tpu_custom_call" | custom-call | flops 1000000 | bytes 2000000 | tf_op jit(solution)/shard_map/pallas_call | solution.py:613
  (1 shorter events, 0.0 us)
Async XLA Ops:
  2.3 18.7 %collective-permute-start = (f32[832,128]{1,0:T(8,128)S(1)}, f32[832,128]{1,0:T(8,128)S(1)}, u32[]{:S(2)}, u32[]{:S(2)}) collective-permute-start(f32[832,128]{1,0:T(8,128)S(1)} %get-tuple-element.56), channel_id=1, source_target_pairs={{0,1},{1,0},{2,3},{3,2},{4,5},{5,4},{6,7},{7,6},{8,9},{9,8},{10,11... | collective-permute-start | bytes 1277960 | tf_op jit(solution)/shard_map/ppermute | solution.py:633
  2.8 18.2 %collective-permute-start.1 = (f32[832,128]{1,0:T(8,128)S(1)}, f32[832,128]{1,0:T(8,128)S(1)}, u32[]{:S(2)}, u32[]{:S(2)}) collective-permute-start(f32[832,128]{1,0:T(8,128)S(1)} %get-tuple-element.57), channel_id=1, source_target_pairs={{0,7},{1,2},{2,1},{3,4},{4,3},{5,6},{6,5},{7,0},{8,15},{9,10},{10,... | collective-permute-start | bytes 1277960 | tf_op jit(solution)/shard_map/ppermute | solution.py:633
  8.5 5.0 %collective-permute-start.2 = (f32[8,24,128]{2,1,0:T(8,128)S(1)}, f32[8,24,128]{2,1,0:T(8,128)S(1)}, u32[]{:S(2)}, u32[]{:S(2)}) collective-permute-start(f32[8,24,128]{2,1,0:T(8,128)S(1)} %get-tuple-element.58), channel_id=1, source_target_pairs={{0,8},{8,0},{16,24},{24,16},{1,9},{9,1},{17,25},{25,17},{2,10},{10... | collective-permute-start | bytes 294920 | tf_op jit(solution)/shard_map/ppermute | solution.py:633
  10.1 5.5 %collective-permute-start.3 = (f32[8,24,128]{2,1,0:T(8,128)S(1)}, f32[8,24,128]{2,1,0:T(8,128)S(1)}, u32[]{:S(2)}, u32[]{:S(2)}) collective-permute-start(f32[8,24,128]{2,1,0:T(8,128)S(1)} %get-tuple-element.59), channel_id=1, source_target_pairs={{0,24},{8,16},{16,8},{24,0},{1,25},{9,17},{17,9},{25,1},{2,26},{10... | collective-permute-start | bytes 294920 | tf_op jit(solution)/shard_map/ppermute | solution.py:633
  15.6 5.4 %collective-permute-start.4 = (f32[2,2,24,128]{3,2,1,0:T(8,128)S(1)}, f32[2,2,24,128]{3,2,1,0:T(8,128)S(1)}, u32[]{:S(2)}, u32[]{:S(2)}) collective-permute-start(f32[2,2,24,128]{3,2,1,0:T(8,128)S(1)} %get-tuple-element.63), channel_id=1, source_target_pairs={{0,7},{1,2},{2,1},{3,4},{4,3},{5,6},{6,5},{7,0},{8,15},{9,10},{10,... | collective-permute-start | bytes 147464 | tf_op jit(solution)/shard_map/ppermute | solution.py:633
  15.7 5.3 %collective-permute-start.5 = (f32[2,2,24,128]{3,2,1,0:T(8,128)S(1)}, f32[2,2,24,128]{3,2,1,0:T(8,128)S(1)}, u32[]{:S(2)}, u32[]{:S(2)}) collective-permute-start(f32[2,2,24,128]{3,2,1,0:T(8,128)S(1)} %get-tuple-element.64), channel_id=1, source_target_pairs={{0,1},{1,0},{2,3},{3,2},{4,5},{5,4},{6,7},{7,6},{8,9},{9,8},{10,11... | collective-permute-start | bytes 147464 | tf_op jit(solution)/shard_map/ppermute | solution.py:633
  22.3 7.1 %collective-permute-start.8 = (f32[2,136,128]{2,1,0:T(8,128)S(1)}, f32[2,136,128]{2,1,0:T(8,128)S(1)}, u32[]{:S(2)}, u32[]{:S(2)}) collective-permute-start(f32[2,136,128]{2,1,0:T(8,128)S(1)} %get-tuple-element.92), channel_id=1, source_target_pairs={{0,7},{1,2},{2,1},{3,4},{4,3},{5,6},{6,5},{7,0},{8,15},{9,10},{10,... | collective-permute-start | bytes 417800 | tf_op jit(solution)/shard_map/ppermute | solution.py:633
  23.9 5.5 %collective-permute-start.9 = (f32[2,136,128]{2,1,0:T(8,128)S(1)}, f32[2,136,128]{2,1,0:T(8,128)S(1)}, u32[]{:S(2)}, u32[]{:S(2)}) collective-permute-start(f32[2,136,128]{2,1,0:T(8,128)S(1)} %get-tuple-element.93), channel_id=1, source_target_pairs={{0,1},{1,0},{2,3},{3,2},{4,5},{5,4},{6,7},{7,6},{8,9},{9,8},{10,11... | collective-permute-start | bytes 417800 | tf_op jit(solution)/shard_map/ppermute | solution.py:633
  24.4 7.6 %collective-permute-start.6 = (f32[280,128]{1,0:T(8,128)S(1)}, f32[280,128]{1,0:T(8,128)S(1)}, u32[]{:S(2)}, u32[]{:S(2)}) collective-permute-start(f32[280,128]{1,0:T(8,128)S(1)} %get-tuple-element.68), channel_id=1, source_target_pairs={{0,1},{1,0},{2,3},{3,2},{4,5},{5,4},{6,7},{7,6},{8,9},{9,8},{10,11... | collective-permute-start | bytes 430088 | tf_op jit(solution)/shard_map/ppermute | solution.py:633
  25.0 7.1 %collective-permute-start.7 = (f32[280,128]{1,0:T(8,128)S(1)}, f32[280,128]{1,0:T(8,128)S(1)}, u32[]{:S(2)}, u32[]{:S(2)}) collective-permute-start(f32[280,128]{1,0:T(8,128)S(1)} %get-tuple-element.69), channel_id=1, source_target_pairs={{0,7},{1,2},{2,1},{3,4},{4,3},{5,6},{6,5},{7,0},{8,15},{9,10},{10,... | collective-permute-start | bytes 430088 | tf_op jit(solution)/shard_map/ppermute | solution.py:633
  30.1 6.3 %collective-permute-start.10 = (f32[2,136,128]{2,1,0:T(8,128)S(1)}, f32[2,136,128]{2,1,0:T(8,128)S(1)}, u32[]{:S(2)}, u32[]{:S(2)}) collective-permute-start(f32[2,136,128]{2,1,0:T(8,128)S(1)} %get-tuple-element.98), channel_id=1, source_target_pairs={{0,7},{1,2},{2,1},{3,4},{4,3},{5,6},{6,5},{7,0},{8,15},{9,10},{10,... | collective-permute-start | bytes 417800 | tf_op jit(solution)/shard_map/ppermute | solution.py:633
  32.1 4.4 %collective-permute-start.11 = (f32[2,136,128]{2,1,0:T(8,128)S(1)}, f32[2,136,128]{2,1,0:T(8,128)S(1)}, u32[]{:S(2)}, u32[]{:S(2)}) collective-permute-start(f32[2,136,128]{2,1,0:T(8,128)S(1)} %get-tuple-element.99), channel_id=1, source_target_pairs={{0,1},{1,0},{2,3},{3,2},{4,5},{5,4},{6,7},{7,6},{8,9},{9,8},{10,11... | collective-permute-start | bytes 417800 | tf_op jit(solution)/shard_map/ppermute | solution.py:633

commit v19 on v17

--- a/solution.py
+++ b/solution.py
@@ -182,11 +182,14 @@
     return [(0, 0, 0), (0, 1, 1), (1, 0, rows - 1), (1, 1, rows - 2)]
 
 
-def edge_kernel(steps, rows, cols, nz, conc_hbm, adj_hbm, rate_hbm, conc_in, adj_in, rate_in,
-                main_a, main_b, sems):
-    lanes = main_a.shape[1]
+def pack_kernel(steps, rows, cols, nz, conc_hbm, adj_hbm, rate_hbm, conc_out, adj_out, rate_out,
+                main_a, main_b, x_a, x_b, conc_in, adj_in, rate_in, sems):
+    places, total = slots(steps)
+    lanes = adj_out.shape[2]
     half = cols // 2
     lower = lax.broadcasted_iota(jnp.int32, (half, lanes), 1) < nz
+    next_x = a_is_next("gx", x_first)
+    sides = list(zip((main_a, main_b), bases(rows, main_first)))
     fetches = [(adj_hbm, adj_in), (rate_hbm, rate_in)] + [
         (conc_hbm.at[steps - 1 - back], conc_in.at[back]) for back in range(steps)
     ]
@@ -209,39 +212,6 @@
         for copy in copies[i]:
             copy.wait()
 
-    arrived(0)
-    for side, base in zip((main_a, main_b), bases(rows, main_first)):
-        for at in range(depth):
-            side[pl.ds(at * cols, cols), :] = adj_in[pl.ds(base + at, lanes, stride=rows), :].T
-    arrived(1)
-    for side, base in zip((main_a, main_b), bases(rows, main_first)):
-        edge = jnp.where(base == 0, 0, rows - 1)
-        rate = turned_rate(rate_in, edge, rows, nz, lanes)
-        side[pl.ds((1 + early) * depth * cols, half), :] = jnp.where(
-            lower, rate[:half], rate[half:]
-        )
-    for back in range(steps):
-        arrived(2 + back)
-        if back >= early:
-            continue
-        for side, base in zip((main_a, main_b), bases(rows, main_first)):
-            for at in range(depth):
-                side[pl.ds(((1 + back) * depth + at) * cols, cols), :] = conc_in[
-                    back, pl.ds(base + at, lanes, stride=rows), :
-                ].T
-
-
-def turned_rate(rate, y, rows, nz, lanes):
-    value = time_step * rate[pl.ds(y, nz, stride=rows), :]
-    return jnp.concatenate([value] * (lanes // nz), axis=0).T
-
-
-def turn_kernel(steps, rows, cols, nz, conc_in, adj_in, rate_in, conc_out, adj_out, rate_out,
-                x_a, x_b):
-    places, total = slots(steps)
-    lanes = adj_out.shape[2]
-    next_x = a_is_next("gx", x_first)
-
     def to_x(y, value, place):
         start, width = place
         last, first = value[cols - width :, :], value[:width, :]
@@ -249,20 +219,44 @@
         x_b[y, start : start + width, :] = jnp.where(next_x, first, last)
 
     used = sum(places[-1])
+    arrived(0)
     for y in range(rows):
         adj = adj_in[pl.ds(y, lanes, stride=rows), :].T
         adj_out[y] = adj
         to_x(y, adj, places[0])
+    for side, base in sides:
+        for at in range(depth):
+            side[pl.ds(at * cols, cols), :] = adj_out[base + at]
+    arrived(1)
+    for y in range(rows):
         rate = turned_rate(rate_in, y, rows, nz, lanes)
         rate_out[y] = rate
         to_x(y, rate, places[steps + 1])
         if used < total:
             x_a[y, used:, :] = jnp.zeros((total - used, lanes), f32)
             x_b[y, used:, :] = jnp.zeros((total - used, lanes), f32)
-        for back in range(steps):
+    for side, base in sides:
+        edge = jnp.where(base == 0, 0, rows - 1)
+        side[pl.ds((1 + early) * depth * cols, half), :] = jnp.where(
+            lower, rate_out[edge, :half, :], rate_out[edge, half:, :]
+        )
+    for back in range(steps):
+        arrived(2 + back)
+        for y in range(rows):
             conc = conc_in[back, pl.ds(y, lanes, stride=rows), :].T
             conc_out[back, y] = conc
             to_x(y, conc, places[1 + back])
+        if back < early:
+            for side, base in sides:
+                for at in range(depth):
+                    side[pl.ds(((1 + back) * depth + at) * cols, cols), :] = conc_out[
+                        back, base + at
+                    ]
+
+
+def turned_rate(rate, y, rows, nz, lanes):
+    value = time_step * rate[pl.ds(y, nz, stride=rows), :]
+    return jnp.concatenate([value] * (lanes // nz), axis=0).T
 
 
 def put_own(out, row, value, y, place, cols, x_low, x_high):
@@ -638,23 +632,17 @@
     edge = (2, cols + 8, lanes)
     open_g = (2, cols + 16, lanes)
     raw = [(steps, flat, cols), (flat, cols), (nz * rows, cols)]
-    conc_raw, adj_raw, rate_raw, main_a, main_b = call(
-        functools.partial(edge_kernel, steps, rows, cols, nz),
-        raw + [((1 + early) * depth * cols + cols // 2, lanes)] * 2,
-        [pltpu.SemaphoreType.DMA((2 + steps, 2))],
+    conc_own, adj_own, rate_own, main_a, main_b, x_a, x_b = call(
+        functools.partial(pack_kernel, steps, rows, cols, nz),
+        [(steps, rows, cols, lanes), (rows, cols, lanes), (rows, cols, lanes)]
+        + [((1 + early) * depth * cols + cols // 2, lanes)] * 2
+        + [(rows, total, lanes)] * 2,
+        raw + [pltpu.SemaphoreType.DMA((2 + steps, 2))],
         saved_conc.reshape(raw[0]), adjoint_end.reshape(raw[1]), rate_field.reshape(raw[2]),
-        cost=2,
+        cost=3,
         far=True,
     )
     main_a, main_b = swap(main_a, main_b, "gy", main_first)
-    conc_own, adj_own, rate_own, x_a, x_b = call(
-        functools.partial(turn_kernel, steps, rows, cols, nz),
-        [(steps, rows, cols, lanes), (rows, cols, lanes), (rows, cols, lanes)]
-        + [(rows, total, lanes)] * 2,
-        [],
-        conc_raw, adj_raw, rate_raw,
-        cost=1,
-    )
     x_a, x_b = swap(x_a, x_b, "gx", x_first)
     whole = (steps - 1, rows, width, lanes)
     core = call(

time: 37.1 us -> 37 us (level)
    pallas_call x12 -> x11, Pallas kernels: 16 us -> 15.8 us  [call(): pl.pallas_call(kernel, out_shape=[jax.ShapeDtypeStruct(shape, f32) for sh...]
  transfers between devices with their start and end apart: 12 -> 12, of which waited for: 5 -> 5; matrix products, arithmetic and copies ran while one was open for 0% -> 0% of each run, Pallas kernels for 32% -> 30%
where the time goes in v19:
time: 37 us; the launch traced here: 36.8 us
  Pallas kernels  15.8 us (43%)
  starting transfers between devices  14.4 us (39%)
  waiting for transfers between devices  5.78 us (16%)
  between operations  0.73 us (2%)
    pallas_call x11, Pallas kernels, call(): pl.pallas_call(kernel, out_shape=[jax.ShapeDtypeStruct(shape, f32) for sh...  15.8 us
    ppermute x6, starting transfers between devices, swap(): lax.ppermute(value_b, axis, pairs_b)  8.29 us
    ppermute x6, starting transfers between devices, swap(): lax.ppermute(value_a, axis, pairs_a)  6.16 us
    ppermute x6, waiting for transfers between devices, swap(): lax.ppermute(value_a, axis, pairs_a)  3.37 us
    ppermute x6, waiting for transfers between devices, swap(): lax.ppermute(value_b, axis, pairs_b)  2.4 us
  transfers between devices with their start and end apart: 12, of which 5 were waited for; matrix products, arithmetic and copies ran while one was open for 0% of the time, Pallas kernels for 30%

profile of v19, /device:TPU:0, one launch (start us, length us, event | category | flops | bytes accessed | tf_op | source)
XLA Modules:
  0.0 36.8 jit_solution(11814431059329322802)
XLA Ops:
  0.6 2.3 %shard_map.50 = (f32[3,8,128,128]{3,2,1,0:T(8,128)S(1)}, f32[8,128,128]{2,1,0:T(8,128)S(1)}, f32[8,128,128]{2,1,0:T(8,128)S(1)}, f32[832,128]{1,0:T(8,128)S(1)},...) custom-call(f32[3,1024,128]{2,1,0:T(8,128)} %bitcast.5, f32[1024,128]{1,0:T(8,128)} %bitcast.6, ...), custom_call_target="tpu_custom_call" | custom-call | flops 3000000 | bytes 6000000 | tf_op jit(solution)/shard_map/pallas_call | solution.py:598
  2.9 0.5 %collective-permute-start = (f32[832,128]{1,0:T(8,128)S(1)}, f32[832,128]{1,0:T(8,128)S(1)}, u32[]{:S(2)}, u32[]{:S(2)}) collective-permute-start(f32[832,128]{1,0:T(8,128)S(1)} %get-tuple-element.50), channel_id=1, source_target_pairs={{0,1},{1,0},{2,3},{3,2},{4,5},{5,4},{6,7},{7,6},{8,9},{9,8},{10,11... | collective-permute-start | bytes 1277960 | tf_op jit(solution)/shard_map/ppermute | solution.py:618
  3.5 4.7 %collective-permute-start.1 = (f32[832,128]{1,0:T(8,128)S(1)}, f32[832,128]{1,0:T(8,128)S(1)}, u32[]{:S(2)}, u32[]{:S(2)}) collective-permute-start(f32[832,128]{1,0:T(8,128)S(1)} %get-tuple-element.51), channel_id=1, source_target_pairs={{0,7},{1,2},{2,1},{3,4},{4,3},{5,6},{6,5},{7,0},{8,15},{9,10},{10,... | collective-permute-start | bytes 1277960 | tf_op jit(solution)/shard_map/ppermute | solution.py:618
  8.2 1.5 %collective-permute-start.2 = (f32[8,24,128]{2,1,0:T(8,128)S(1)}, f32[8,24,128]{2,1,0:T(8,128)S(1)}, u32[]{:S(2)}, u32[]{:S(2)}) collective-permute-start(f32[8,24,128]{2,1,0:T(8,128)S(1)} %get-tuple-element.52), channel_id=1, source_target_pairs={{0,8},{8,0},{16,24},{24,16},{1,9},{9,1},{17,25},{25,17},{2,10},{10... | collective-permute-start | bytes 294920 | tf_op jit(solution)/shard_map/ppermute | solution.py:618
  9.7 1.5 %collective-permute-start.3 = (f32[8,24,128]{2,1,0:T(8,128)S(1)}, f32[8,24,128]{2,1,0:T(8,128)S(1)}, u32[]{:S(2)}, u32[]{:S(2)}) collective-permute-start(f32[8,24,128]{2,1,0:T(8,128)S(1)} %get-tuple-element.53), channel_id=1, source_target_pairs={{0,24},{8,16},{16,8},{24,0},{1,25},{9,17},{17,9},{25,1},{2,26},{10... | collective-permute-start | bytes 294920 | tf_op jit(solution)/shard_map/ppermute | solution.py:618
  11.2 1.2 %shard_map.51 = (f32[2,8,160,128]{3,2,1,0:T(8,128)S(1)}, f32[2,8,160,128]{3,2,1,0:T(8,128)S(1)}, f32[2,8,160,128]{3,2,1,0:T(8,128)S(1)}, f32[2,8,160,128]{3,2,1,0:T(8,128)S(1)}) custom-call(f32[3,8,128,128]{3,2,1,0:T(8,128)S(1)} %get-tuple-element.49.conc_own), custom_call_target="tpu_custom_call" | custom-call | flops 2000000 | bytes 4000000 | tf_op jit(solution)/shard_map/pallas_call | solution.py:598
  12.4 0.7 %collective-permute-done.2.got_a = f32[8,24,128]{2,1,0:T(8,128)S(1)} collective-permute-done((f32[8,24,128]{2,1,0:T(8,128)S(1)}, f32[8,24,128]{2,1,0:T(8,128)S(1)}, u32[]{:S(2)}, u32[]{:S(2)}) %collective-permute-start.2) | collective-permute-done | bytes 98336 | tf_op jit(solution)/shard_map/ppermute | solution.py:618
  13.1 2.1 %collective-permute-done.3.got_b = f32[8,24,128]{2,1,0:T(8,128)S(1)} collective-permute-done((f32[8,24,128]{2,1,0:T(8,128)S(1)}, f32[8,24,128]{2,1,0:T(8,128)S(1)}, u32[]{:S(2)}, u32[]{:S(2)}) %collective-permute-start.3) | collective-permute-done | bytes 98336 | tf_op jit(solution)/shard_map/ppermute | solution.py:618
  15.2 0.1 collective-permute-start.4
  15.3 0.1 collective-permute-start.5
  15.4 3.3 %shard_map.55 = (f32[10,160,128]{2,1,0:T(8,128)S(1)}, f32[10,160,128]{2,1,0:T(8,128)S(1)}, f32[8,160,128]{2,1,0:T(8,128)S(1)}, f32[10,160,128]{2,1,0:T(8,128)S(1...) custom-call(f32[3,8,128,128]{3,2,1,0:T(8,128)S(1)} %get-tuple-elemen, ...), custom_call_target="tpu_custom_call" | custom-call | flops 3000000 | bytes 6000000 | tf_op jit(solution)/shard_map/pallas_call | solution.py:598
  18.6 2.0 %collective-permute-done.4.corner_b = f32[2,2,24,128]{3,2,1,0:T(8,128)S(1)} collective-permute-done((f32[2,2,24,128]{3,2,1,0:T(8,128)S(1)}, f32[2,2,24,128]{3,2,1,0:T(8,128)S(1)}, u32[]{:S(2)}, u32[]{:S(2)}) %collective-permute-start.4) | collective-permute-done | bytes 49184 | tf_op jit(solution)/shard_map/ppermute | solution.py:618
  20.6 0.0 collective-permute-done.5.corner_a
  20.6 0.0 collective-permute-done.from_a
  20.6 0.0 collective-permute-done.1.from_b
  20.6 1.2 %shard_map.56 = (f32[2,2,160,128]{3,2,1,0:T(8,128)S(1)}, f32[2,160,128]{2,1,0:T(8,128)S(1)}, f32[2,136,128]{2,1,0:T(8,128)S(1)}, f32[2,136,128]{2,1,0:T(8,128)S(1)}) custom-call(f32[10,160,128]{2,1,0:T(8,128)S(1)} %get-tuple-element.76.conc, f32[10,160,128]{2,1,0:T(8,128)S(1)} %get-tuple-element.77.adj, f32[8,160,128]{2,1,0:T(8,128)S(1)} %get-tuple-element.70.rate.rest_1_, ...), custom_call_target="tpu_custom_call" | custom-call | flops 2000000 | bytes 4000000 | tf_op jit(solution)/shard_map/pallas_call | solution.py:598
  21.8 1.6 %collective-permute-start.8 = (f32[2,136,128]{2,1,0:T(8,128)S(1)}, f32[2,136,128]{2,1,0:T(8,128)S(1)}, u32[]{:S(2)}, u32[]{:S(2)}) collective-permute-start(f32[2,136,128]{2,1,0:T(8,128)S(1)} %get-tuple-element.86), channel_id=1, source_target_pairs={{0,7},{1,2},{2,1},{3,4},{4,3},{5,6},{6,5},{7,0},{8,15},{9,10},{10,... | collective-permute-start | bytes 417800 | tf_op jit(solution)/shard_map/ppermute | solution.py:618
  23.4 0.0 collective-permute-start.9
  23.4 0.5 %shard_map.53 = (f32[12,160,128]{2,1,0:T(8,128)S(1)}, f32[10,160,128]{2,1,0:T(8,128)S(1)}, f32[10,160,128]{2,1,0:T(8,128)S(1)}, f32[10,160,128]{2,1,0:T(8,128)S(...) custom-call(f32[3,8,128,128]{3,2,1,0:T(8,128)S(1)} %get-tuple-element.49.conc_own, ...), custom_call_target="tpu_custom_call" | custom-call | flops 2000000 | bytes 4000000 | tf_op jit(solution)/shard_map/pallas_call | solution.py:598
  23.9 0.6 %collective-permute-start.6 = (f32[280,128]{1,0:T(8,128)S(1)}, f32[280,128]{1,0:T(8,128)S(1)}, u32[]{:S(2)}, u32[]{:S(2)}) collective-permute-start(f32[280,128]{1,0:T(8,128)S(1)} %get-tuple-element.62), channel_id=1, source_target_pairs={{0,1},{1,0},{2,3},{3,2},{4,5},{5,4},{6,7},{7,6},{8,9},{9,8},{10,11... | collective-permute-start | bytes 430088 | tf_op jit(solution)/shard_map/ppermute | solution.py:618
  24.5 2.0 %collective-permute-start.7 = (f32[280,128]{1,0:T(8,128)S(1)}, f32[280,128]{1,0:T(8,128)S(1)}, u32[]{:S(2)}, u32[]{:S(2)}) collective-permute-start(f32[280,128]{1,0:T(8,128)S(1)} %get-tuple-element.63), channel_id=1, source_target_pairs={{0,7},{1,2},{2,1},{3,4},{4,3},{5,6},{6,5},{7,0},{8,15},{9,10},{10,... | collective-permute-start | bytes 430088 | tf_op jit(solution)/shard_map/ppermute | solution.py:618
  26.5 2.4 %shard_map.57 = (f32[8,160,128]{2,1,0:T(8,128)S(1)}, f32[8,160,128]{2,1,0:T(8,128)S(1)}) custom-call(f32[12,160,128]{2,1,0:T(8,128)S(1)} %get-tuple-element.71.mob, f32[10,160,128]{2,1,0:T(8,128)S(1)} %get-tuple-element.72.chem, f32[10,160,128]{2,1,0:T(8,128)S(1)} %get-tuple-element.73.curve, f32[10,160,128]{2,1,0:T(8,128)S(1)} %get-tuple-element.74.swing, ...), custom_call_target="tpu_custom_call" | custom-call | flops 3000000 | bytes 6000000 | tf_op jit(solution)/shard_map/pallas_call | solution.py:598
  28.9 0.0 collective-permute-done.8.from_a
  28.9 0.0 collective-permute-done.9.from_b
  28.9 0.4 %shard_map.58 = (f32[2,2,160,128]{3,2,1,0:T(8,128)S(1)}, f32[2,136,128]{2,1,0:T(8,128)S(1)}, f32[2,136,128]{2,1,0:T(8,128)S(1)}) custom-call(f32[12,160,128]{2,1,0:T(8,128)S(1)} %get-tuple-element.71.mob, f32[10,160,128]{2,1,0:T(8,128)S(1)} %get-tuple-element.72.chem, f32[10,160,128]{2,1,0:T(8,128)S(1)} %get-tuple-element.73.curve, ...), custom_call_target="tpu_custom_call" | custom-call | flops 1000000 | bytes 2000000 | tf_op jit(solution)/shard_map/pallas_call | solution.py:598
  29.3 1.9 %collective-permute-start.10 = (f32[2,136,128]{2,1,0:T(8,128)S(1)}, f32[2,136,128]{2,1,0:T(8,128)S(1)}, u32[]{:S(2)}, u32[]{:S(2)}) collective-permute-start(f32[2,136,128]{2,1,0:T(8,128)S(1)} %get-tuple-element.92), channel_id=1, source_target_pairs={{0,7},{1,2},{2,1},{3,4},{4,3},{5,6},{6,5},{7,0},{8,15},{9,10},{10,... | collective-permute-start | bytes 417800 | tf_op jit(solution)/shard_map/ppermute | solution.py:618
  31.2 0.0 collective-permute-start.11
  31.2 0.0 collective-permute-done.6.from_a
  31.2 0.3 collective-permute-done.7.from_b
  31.5 0.5 %shard_map.54 = (f32[12,160,128]{2,1,0:T(8,128)S(1)}, f32[10,160,128]{2,1,0:T(8,128)S(1)}, f32[10,160,128]{2,1,0:T(8,128)S(1)}, f32[10,160,128]{2,1,0:T(8,128)S(1)}) custom-call(f32[3,8,128,128]{3,2,1,0:T(8,128)S(1)} %get-tuple-element.49.conc_own, f32[280,128]{1,0:T(8,128)S(1)} %collective-permute-done.6.from_a, ...), custom_call_target="tpu_custom_call" | custom-call | flops 2000000 | bytes 4000000 | tf_op jit(solution)/shard_map/pallas_call | solution.py:598
  32.0 2.9 %shard_map.59 = (f32[8,160,128]{2,1,0:T(8,128)S(1)}, f32[1024,128]{1,0:T(8,128)S(1)}, f32[512,128]{1,0:T(8,128)}) custom-call(f32[12,160,128]{2,1,0:T(8,128)S(1)} %get-tuple-element.64.mob, f32[10,160,128]{2,1,0:T(8,128)S(1)} %get-tuple-element.65.chem, f32[10,160,128]{2,1,0:T(8,128)S(1)} %get-tuple-element.66.curve, ...), custom_call_target="tpu_custom_call" | custom-call | flops 3000000 | bytes 6000000 | tf_op jit(solution)/shard_map/pallas_call | solution.py:598
  34.9 0.7 %collective-permute-done.10.from_a = f32[2,136,128]{2,1,0:T(8,128)S(1)} collective-permute-done((f32[2,136,128]{2,1,0:T(8,128)S(1)}, f32[2,136,128]{2,1,0:T(8,128)S(1)}, u32[]{:S(2)}, u32[]{:S(2)}) %collective-permute-start.10) | collective-permute-done | bytes 139296 | tf_op jit(solution)/shard_map/ppermute | solution.py:618
  35.6 0.0 collective-permute-done.11.from_b
  35.6 1.2 %shard_map.60 = f32[1024,128]{1,0:T(8,128)} custom-call(f32[12,160,128]{2,1,0:T(8,128)S(1)} %get-tuple-element.64.mob, f32[10,160,128]{2,1,0:T(8,128)S(1)} %get-tuple-element.65.chem, f32[10,160,128]{2,1,0:T(8,128)S(1)} %get-tuple-element.66.curve, f32[10,160,128]{2,1,0:T(8,128)S(1)} %get-tuple-element.67.swing, ...), custom_call_target="tpu_custom_call" | custom-call | flops 1000000 | bytes 2000000 | tf_op jit(solution)/shard_map/pallas_call | solution.py:598
  (1 shorter events, 0.0 us)
Async XLA Ops:
  2.9 17.7 %collective-permute-start = (f32[832,128]{1,0:T(8,128)S(1)}, f32[832,128]{1,0:T(8,128)S(1)}, u32[]{:S(2)}, u32[]{:S(2)}) collective-permute-start(f32[832,128]{1,0:T(8,128)S(1)} %get-tuple-element.50), channel_id=1, source_target_pairs={{0,1},{1,0},{2,3},{3,2},{4,5},{5,4},{6,7},{7,6},{8,9},{9,8},{10,11... | collective-permute-start | bytes 1277960 | tf_op jit(solution)/shard_map/ppermute | solution.py:618
  3.5 17.1 %collective-permute-start.1 = (f32[832,128]{1,0:T(8,128)S(1)}, f32[832,128]{1,0:T(8,128)S(1)}, u32[]{:S(2)}, u32[]{:S(2)}) collective-permute-start(f32[832,128]{1,0:T(8,128)S(1)} %get-tuple-element.51), channel_id=1, source_target_pairs={{0,7},{1,2},{2,1},{3,4},{4,3},{5,6},{6,5},{7,0},{8,15},{9,10},{10,... | collective-permute-start | bytes 1277960 | tf_op jit(solution)/shard_map/ppermute | solution.py:618
  8.2 4.9 %collective-permute-start.2 = (f32[8,24,128]{2,1,0:T(8,128)S(1)}, f32[8,24,128]{2,1,0:T(8,128)S(1)}, u32[]{:S(2)}, u32[]{:S(2)}) collective-permute-start(f32[8,24,128]{2,1,0:T(8,128)S(1)} %get-tuple-element.52), channel_id=1, source_target_pairs={{0,8},{8,0},{16,24},{24,16},{1,9},{9,1},{17,25},{25,17},{2,10},{10... | collective-permute-start | bytes 294920 | tf_op jit(solution)/shard_map/ppermute | solution.py:618
  9.7 5.5 %collective-permute-start.3 = (f32[8,24,128]{2,1,0:T(8,128)S(1)}, f32[8,24,128]{2,1,0:T(8,128)S(1)}, u32[]{:S(2)}, u32[]{:S(2)}) collective-permute-start(f32[8,24,128]{2,1,0:T(8,128)S(1)} %get-tuple-element.53), channel_id=1, source_target_pairs={{0,24},{8,16},{16,8},{24,0},{1,25},{9,17},{17,9},{25,1},{2,26},{10... | collective-permute-start | bytes 294920 | tf_op jit(solution)/shard_map/ppermute | solution.py:618
  15.2 5.4 %collective-permute-start.4 = (f32[2,2,24,128]{3,2,1,0:T(8,128)S(1)}, f32[2,2,24,128]{3,2,1,0:T(8,128)S(1)}, u32[]{:S(2)}, u32[]{:S(2)}) collective-permute-start(f32[2,2,24,128]{3,2,1,0:T(8,128)S(1)} %get-tuple-element.57), channel_id=1, source_target_pairs={{0,7},{1,2},{2,1},{3,4},{4,3},{5,6},{6,5},{7,0},{8,15},{9,10},{10,... | collective-permute-start | bytes 147464 | tf_op jit(solution)/shard_map/ppermute | solution.py:618
  15.3 5.3 %collective-permute-start.5 = (f32[2,2,24,128]{3,2,1,0:T(8,128)S(1)}, f32[2,2,24,128]{3,2,1,0:T(8,128)S(1)}, u32[]{:S(2)}, u32[]{:S(2)}) collective-permute-start(f32[2,2,24,128]{3,2,1,0:T(8,128)S(1)} %get-tuple-element.58), channel_id=1, source_target_pairs={{0,1},{1,0},{2,3},{3,2},{4,5},{5,4},{6,7},{7,6},{8,9},{9,8},{10,11... | collective-permute-start | bytes 147464 | tf_op jit(solution)/shard_map/ppermute | solution.py:618
  21.8 7.1 %collective-permute-start.8 = (f32[2,136,128]{2,1,0:T(8,128)S(1)}, f32[2,136,128]{2,1,0:T(8,128)S(1)}, u32[]{:S(2)}, u32[]{:S(2)}) collective-permute-start(f32[2,136,128]{2,1,0:T(8,128)S(1)} %get-tuple-element.86), channel_id=1, source_target_pairs={{0,7},{1,2},{2,1},{3,4},{4,3},{5,6},{6,5},{7,0},{8,15},{9,10},{10,... | collective-permute-start | bytes 417800 | tf_op jit(solution)/shard_map/ppermute | solution.py:618
  23.4 5.5 %collective-permute-start.9 = (f32[2,136,128]{2,1,0:T(8,128)S(1)}, f32[2,136,128]{2,1,0:T(8,128)S(1)}, u32[]{:S(2)}, u32[]{:S(2)}) collective-permute-start(f32[2,136,128]{2,1,0:T(8,128)S(1)} %get-tuple-element.87), channel_id=1, source_target_pairs={{0,1},{1,0},{2,3},{3,2},{4,5},{5,4},{6,7},{7,6},{8,9},{9,8},{10,11... | collective-permute-start | bytes 417800 | tf_op jit(solution)/shard_map/ppermute | solution.py:618
  23.9 7.3 %collective-permute-start.6 = (f32[280,128]{1,0:T(8,128)S(1)}, f32[280,128]{1,0:T(8,128)S(1)}, u32[]{:S(2)}, u32[]{:S(2)}) collective-permute-start(f32[280,128]{1,0:T(8,128)S(1)} %get-tuple-element.62), channel_id=1, source_target_pairs={{0,1},{1,0},{2,3},{3,2},{4,5},{5,4},{6,7},{7,6},{8,9},{9,8},{10,11... | collective-permute-start | bytes 430088 | tf_op jit(solution)/shard_map/ppermute | solution.py:618
  24.5 7.0 %collective-permute-start.7 = (f32[280,128]{1,0:T(8,128)S(1)}, f32[280,128]{1,0:T(8,128)S(1)}, u32[]{:S(2)}, u32[]{:S(2)}) collective-permute-start(f32[280,128]{1,0:T(8,128)S(1)} %get-tuple-element.63), channel_id=1, source_target_pairs={{0,7},{1,2},{2,1},{3,4},{4,3},{5,6},{6,5},{7,0},{8,15},{9,10},{10,... | collective-permute-start | bytes 430088 | tf_op jit(solution)/shard_map/ppermute | solution.py:618
  29.3 6.3 %collective-permute-start.10 = (f32[2,136,128]{2,1,0:T(8,128)S(1)}, f32[2,136,128]{2,1,0:T(8,128)S(1)}, u32[]{:S(2)}, u32[]{:S(2)}) collective-permute-start(f32[2,136,128]{2,1,0:T(8,128)S(1)} %get-tuple-element.92), channel_id=1, source_target_pairs={{0,7},{1,2},{2,1},{3,4},{4,3},{5,6},{6,5},{7,0},{8,15},{9,10},{10,... | collective-permute-start | bytes 417800 | tf_op jit(solution)/shard_map/ppermute | solution.py:618
  31.2 4.4 %collective-permute-start.11 = (f32[2,136,128]{2,1,0:T(8,128)S(1)}, f32[2,136,128]{2,1,0:T(8,128)S(1)}, u32[]{:S(2)}, u32[]{:S(2)}) collective-permute-start(f32[2,136,128]{2,1,0:T(8,128)S(1)} %get-tuple-element.93), channel_id=1, source_target_pairs={{0,1},{1,0},{2,3},{3,2},{4,5},{5,4},{6,7},{7,6},{8,9},{9,8},{10,11... | collective-permute-start | bytes 417800 | tf_op jit(solution)/shard_map/ppermute | solution.py:618

commit v20 on v19

--- a/solution.py
+++ b/solution.py
@@ -467,7 +467,10 @@
         chem[1 + y, own, :] = chem_core[back - 1, y, own, :]
         curve[1 + y, own, :] = curve_core[back - 1, y, own, :]
         swing[1 + y, own, :] = swing_core[back - 1, y, own, :]
-    for halo, corner, base in zip((from_a, from_b), (corner_a, corner_b), landings(rows, main_first)):
+    first_swap, corners = main_first, (corner_a, corner_b)
+    if back >= early and round_first != main_first:
+        first_swap, corners = round_first, (corner_b, corner_a)
+    for halo, corner, base in zip((from_a, from_b), corners, landings(rows, first_swap)):
         for at in range(depth):
             first = (1 + back) * depth if back < early else (back - early) * depth
             span = pl.ds((first + at) * cols, cols)
@@ -476,7 +479,7 @@
     if more:
         ahead, late_a, late_b = more
         put_ahead(ahead, conc_own, back + 1, x_low, x_high, places, rows, cols)
-        for side, base in zip((late_a, late_b), bases(rows, main_first)):
+        for side, base in zip((late_a, late_b), bases(rows, round_first)):
             for after in range(early, steps):
                 for at in range(depth):
                     span = pl.ds(((after - early) * depth + at) * cols, cols)
@@ -691,7 +694,7 @@
         )
         fields, ahead, more = fields[:4], fields[4:5], fields[5:]
         if not final:
-            got = swap(*more, "gy", main_first)
+            got = swap(*more, "gy", round_first)
         work = [field(rows + 2)] * 2 + [field(rows)] * 2
         if final:
             inner, tiles, grad = call(

time: 37 us -> 36.8 us (level)
    ppermute x6, starting transfers between devices: 8.29 us -> 6.28 us  [swap(): lax.ppermute(value_b, axis, pairs_b)]
    ppermute x6, starting transfers between devices: 6.16 us -> 7.93 us  [swap(): lax.ppermute(value_a, axis, pairs_a)]
    ppermute x6, waiting for transfers between devices: 3.37 us -> 3.82 us  [swap(): lax.ppermute(value_a, axis, pairs_a)]
  transfers between devices with their start and end apart: 12 -> 12, of which waited for: 5 -> 6; matrix products, arithmetic and copies ran while one was open for 0% -> 0% of each run, Pallas kernels for 30% -> 31%
where the time goes in v20:
time: 36.8 us; the launch traced here: 36.7 us
  Pallas kernels  15.8 us (43%)
  starting transfers between devices  14.2 us (39%)
  waiting for transfers between devices  5.92 us (16%)
  between operations  0.72 us (2%)
    pallas_call x11, Pallas kernels, call(): pl.pallas_call(kernel, out_shape=[jax.ShapeDtypeStruct(shape, f32) for sh...  15.8 us
    ppermute x6, starting transfers between devices, swap(): lax.ppermute(value_a, axis, pairs_a)  7.93 us
    ppermute x6, starting transfers between devices, swap(): lax.ppermute(value_b, axis, pairs_b)  6.28 us
    ppermute x6, waiting for transfers between devices, swap(): lax.ppermute(value_a, axis, pairs_a)  3.82 us
    ppermute x6, waiting for transfers between devices, swap(): lax.ppermute(value_b, axis, pairs_b)  2.1 us
  transfers between devices with their start and end apart: 12, of which 6 were waited for; matrix products, arithmetic and copies ran while one was open for 0% of the time, Pallas kernels for 31%

profile of v20, /device:TPU:0, one launch (start us, length us, event | category | flops | bytes accessed | tf_op | source)
XLA Modules:
  0.0 36.7 jit_solution(5514580623406441607)
XLA Ops:
  0.6 2.3 %shard_map.50 = (f32[3,8,128,128]{3,2,1,0:T(8,128)S(1)}, f32[8,128,128]{2,1,0:T(8,128)S(1)}, f32[8,128,128]{2,1,0:T(8,128)S(1)}, f32[832,128]{1,0:T(8,128)S(1)},...) custom-call(f32[3,1024,128]{2,1,0:T(8,128)} %bitcast.5, f32[1024,128]{1,0:T(8,128)} %bitcast.6, ...), custom_call_target="tpu_custom_call" | custom-call | flops 3000000 | bytes 6000000 | tf_op jit(solution)/shard_map/pallas_call | solution.py:601
  2.9 0.5 %collective-permute-start = (f32[832,128]{1,0:T(8,128)S(1)}, f32[832,128]{1,0:T(8,128)S(1)}, u32[]{:S(2)}, u32[]{:S(2)}) collective-permute-start(f32[832,128]{1,0:T(8,128)S(1)} %get-tuple-element.50), channel_id=1, source_target_pairs={{0,1},{1,0},{2,3},{3,2},{4,5},{5,4},{6,7},{7,6},{8,9},{9,8},{10,11... | collective-permute-start | bytes 1277960 | tf_op jit(solution)/shard_map/ppermute | solution.py:621
  3.5 4.7 %collective-permute-start.1 = (f32[832,128]{1,0:T(8,128)S(1)}, f32[832,128]{1,0:T(8,128)S(1)}, u32[]{:S(2)}, u32[]{:S(2)}) collective-permute-start(f32[832,128]{1,0:T(8,128)S(1)} %get-tuple-element.51), channel_id=1, source_target_pairs={{0,7},{1,2},{2,1},{3,4},{4,3},{5,6},{6,5},{7,0},{8,15},{9,10},{10,... | collective-permute-start | bytes 1277960 | tf_op jit(solution)/shard_map/ppermute | solution.py:621
  8.2 1.5 %collective-permute-start.2 = (f32[8,24,128]{2,1,0:T(8,128)S(1)}, f32[8,24,128]{2,1,0:T(8,128)S(1)}, u32[]{:S(2)}, u32[]{:S(2)}) collective-permute-start(f32[8,24,128]{2,1,0:T(8,128)S(1)} %get-tuple-element.52), channel_id=1, source_target_pairs={{0,8},{8,0},{16,24},{24,16},{1,9},{9,1},{17,25},{25,17},{2,10},{10... | collective-permute-start | bytes 294920 | tf_op jit(solution)/shard_map/ppermute | solution.py:621
  9.7 1.5 %collective-permute-start.3 = (f32[8,24,128]{2,1,0:T(8,128)S(1)}, f32[8,24,128]{2,1,0:T(8,128)S(1)}, u32[]{:S(2)}, u32[]{:S(2)}) collective-permute-start(f32[8,24,128]{2,1,0:T(8,128)S(1)} %get-tuple-element.53), channel_id=1, source_target_pairs={{0,24},{8,16},{16,8},{24,0},{1,25},{9,17},{17,9},{25,1},{2,26},{10... | collective-permute-start | bytes 294920 | tf_op jit(solution)/shard_map/ppermute | solution.py:621
  11.2 1.2 %shard_map.51 = (f32[2,8,160,128]{3,2,1,0:T(8,128)S(1)}, f32[2,8,160,128]{3,2,1,0:T(8,128)S(1)}, f32[2,8,160,128]{3,2,1,0:T(8,128)S(1)}, f32[2,8,160,128]{3,2,1,0:T(8,128)S(1)}) custom-call(f32[3,8,128,128]{3,2,1,0:T(8,128)S(1)} %get-tuple-element.49.conc_own), custom_call_target="tpu_custom_call" | custom-call | flops 2000000 | bytes 4000000 | tf_op jit(solution)/shard_map/pallas_call | solution.py:601
  12.4 0.7 %collective-permute-done.2.got_a = f32[8,24,128]{2,1,0:T(8,128)S(1)} collective-permute-done((f32[8,24,128]{2,1,0:T(8,128)S(1)}, f32[8,24,128]{2,1,0:T(8,128)S(1)}, u32[]{:S(2)}, u32[]{:S(2)}) %collective-permute-start.2) | collective-permute-done | bytes 98336 | tf_op jit(solution)/shard_map/ppermute | solution.py:621
  13.1 2.1 %collective-permute-done.3.got_b = f32[8,24,128]{2,1,0:T(8,128)S(1)} collective-permute-done((f32[8,24,128]{2,1,0:T(8,128)S(1)}, f32[8,24,128]{2,1,0:T(8,128)S(1)}, u32[]{:S(2)}, u32[]{:S(2)}) %collective-permute-start.3) | collective-permute-done | bytes 98336 | tf_op jit(solution)/shard_map/ppermute | solution.py:621
  15.2 0.1 collective-permute-start.4
  15.3 0.1 collective-permute-start.5
  15.4 3.3 %shard_map.55 = (f32[10,160,128]{2,1,0:T(8,128)S(1)}, f32[10,160,128]{2,1,0:T(8,128)S(1)}, f32[8,160,128]{2,1,0:T(8,128)S(1)}, f32[10,160,128]{2,1,0:T(8,128)S(1...) custom-call(f32[3,8,128,128]{3,2,1,0:T(8,128)S(1)} %get-tuple-elemen, ...), custom_call_target="tpu_custom_call" | custom-call | flops 3000000 | bytes 6000000 | tf_op jit(solution)/shard_map/pallas_call | solution.py:601
  18.6 2.0 %collective-permute-done.4.corner_b = f32[2,2,24,128]{3,2,1,0:T(8,128)S(1)} collective-permute-done((f32[2,2,24,128]{3,2,1,0:T(8,128)S(1)}, f32[2,2,24,128]{3,2,1,0:T(8,128)S(1)}, u32[]{:S(2)}, u32[]{:S(2)}) %collective-permute-start.4) | collective-permute-done | bytes 49184 | tf_op jit(solution)/shard_map/ppermute | solution.py:621
  20.6 0.0 collective-permute-done.5.corner_a
  20.6 0.0 collective-permute-done.from_a
  20.6 0.0 collective-permute-done.1.from_b
  20.6 1.2 %shard_map.56 = (f32[2,2,160,128]{3,2,1,0:T(8,128)S(1)}, f32[2,160,128]{2,1,0:T(8,128)S(1)}, f32[2,136,128]{2,1,0:T(8,128)S(1)}, f32[2,136,128]{2,1,0:T(8,128)S(1)}) custom-call(f32[10,160,128]{2,1,0:T(8,128)S(1)} %get-tuple-element.76.conc, f32[10,160,128]{2,1,0:T(8,128)S(1)} %get-tuple-element.77.adj, f32[8,160,128]{2,1,0:T(8,128)S(1)} %get-tuple-element.70.rate.rest_1_, ...), custom_call_target="tpu_custom_call" | custom-call | flops 2000000 | bytes 4000000 | tf_op jit(solution)/shard_map/pallas_call | solution.py:601
  21.8 1.6 %collective-permute-start.8 = (f32[2,136,128]{2,1,0:T(8,128)S(1)}, f32[2,136,128]{2,1,0:T(8,128)S(1)}, u32[]{:S(2)}, u32[]{:S(2)}) collective-permute-start(f32[2,136,128]{2,1,0:T(8,128)S(1)} %get-tuple-element.86), channel_id=1, source_target_pairs={{0,7},{1,2},{2,1},{3,4},{4,3},{5,6},{6,5},{7,0},{8,15},{9,10},{10,... | collective-permute-start | bytes 417800 | tf_op jit(solution)/shard_map/ppermute | solution.py:621
  23.4 0.0 collective-permute-start.9
  23.4 0.5 %shard_map.53 = (f32[12,160,128]{2,1,0:T(8,128)S(1)}, f32[10,160,128]{2,1,0:T(8,128)S(1)}, f32[10,160,128]{2,1,0:T(8,128)S(1)}, f32[10,160,128]{2,1,0:T(8,128)S(...) custom-call(f32[3,8,128,128]{3,2,1,0:T(8,128)S(1)} %get-tuple-element.49.conc_own, ...), custom_call_target="tpu_custom_call" | custom-call | flops 2000000 | bytes 4000000 | tf_op jit(solution)/shard_map/pallas_call | solution.py:601
  23.9 2.1 %collective-permute-start.6 = (f32[280,128]{1,0:T(8,128)S(1)}, f32[280,128]{1,0:T(8,128)S(1)}, u32[]{:S(2)}, u32[]{:S(2)}) collective-permute-start(f32[280,128]{1,0:T(8,128)S(1)} %get-tuple-element.62), channel_id=1, source_target_pairs={{0,7},{1,2},{2,1},{3,4},{4,3},{5,6},{6,5},{7,0},{8,15},{9,10},{10,... | collective-permute-start | bytes 430088 | tf_op jit(solution)/shard_map/ppermute | solution.py:621
  26.0 0.0 collective-permute-start.7
  26.0 2.4 %shard_map.57 = (f32[8,160,128]{2,1,0:T(8,128)S(1)}, f32[8,160,128]{2,1,0:T(8,128)S(1)}) custom-call(f32[12,160,128]{2,1,0:T(8,128)S(1)} %get-tuple-element.71.mob, f32[10,160,128]{2,1,0:T(8,128)S(1)} %get-tuple-element.72.chem, f32[10,160,128]{2,1,0:T(8,128)S(1)} %get-tuple-element.73.curve, f32[10,160,128]{2,1,0:T(8,128)S(1)} %get-tuple-element.74.swing, ...), custom_call_target="tpu_custom_call" | custom-call | flops 3000000 | bytes 6000000 | tf_op jit(solution)/shard_map/pallas_call | solution.py:601
  28.4 0.4 collective-permute-done.8.from_a
  28.7 0.0 collective-permute-done.9.from_b
  28.7 0.4 %shard_map.58 = (f32[2,2,160,128]{3,2,1,0:T(8,128)S(1)}, f32[2,136,128]{2,1,0:T(8,128)S(1)}, f32[2,136,128]{2,1,0:T(8,128)S(1)}) custom-call(f32[12,160,128]{2,1,0:T(8,128)S(1)} %get-tuple-element.71.mob, f32[10,160,128]{2,1,0:T(8,128)S(1)} %get-tuple-element.72.chem, f32[10,160,128]{2,1,0:T(8,128)S(1)} %get-tuple-element.73.curve, ...), custom_call_target="tpu_custom_call" | custom-call | flops 1000000 | bytes 2000000 | tf_op jit(solution)/shard_map/pallas_call | solution.py:601
  29.1 2.2 %collective-permute-start.10 = (f32[2,136,128]{2,1,0:T(8,128)S(1)}, f32[2,136,128]{2,1,0:T(8,128)S(1)}, u32[]{:S(2)}, u32[]{:S(2)}) collective-permute-start(f32[2,136,128]{2,1,0:T(8,128)S(1)} %get-tuple-element.92), channel_id=1, source_target_pairs={{0,7},{1,2},{2,1},{3,4},{4,3},{5,6},{6,5},{7,0},{8,15},{9,10},{10,... | collective-permute-start | bytes 417800 | tf_op jit(solution)/shard_map/ppermute | solution.py:621
  31.3 0.0 collective-permute-start.11
  31.3 0.2 collective-permute-done.6.from_a
  31.5 0.0 collective-permute-done.7.from_b
  31.5 0.5 %shard_map.54 = (f32[12,160,128]{2,1,0:T(8,128)S(1)}, f32[10,160,128]{2,1,0:T(8,128)S(1)}, f32[10,160,128]{2,1,0:T(8,128)S(1)}, f32[10,160,128]{2,1,0:T(8,128)S(1)}) custom-call(f32[3,8,128,128]{3,2,1,0:T(8,128)S(1)} %get-tuple-element.49.conc_own, f32[280,128]{1,0:T(8,128)S(1)} %collective-permute-done.6.from_a, ...), custom_call_target="tpu_custom_call" | custom-call | flops 2000000 | bytes 4000000 | tf_op jit(solution)/shard_map/pallas_call | solution.py:601
  31.9 2.9 %shard_map.59 = (f32[8,160,128]{2,1,0:T(8,128)S(1)}, f32[1024,128]{1,0:T(8,128)S(1)}, f32[512,128]{1,0:T(8,128)}) custom-call(f32[12,160,128]{2,1,0:T(8,128)S(1)} %get-tuple-element.64.mob, f32[10,160,128]{2,1,0:T(8,128)S(1)} %get-tuple-element.65.chem, f32[10,160,128]{2,1,0:T(8,128)S(1)} %get-tuple-element.66.curve, ...), custom_call_target="tpu_custom_call" | custom-call | flops 3000000 | bytes 6000000 | tf_op jit(solution)/shard_map/pallas_call | solution.py:601
  34.9 0.7 %collective-permute-done.10.from_a = f32[2,136,128]{2,1,0:T(8,128)S(1)} collective-permute-done((f32[2,136,128]{2,1,0:T(8,128)S(1)}, f32[2,136,128]{2,1,0:T(8,128)S(1)}, u32[]{:S(2)}, u32[]{:S(2)}) %collective-permute-start.10) | collective-permute-done | bytes 139296 | tf_op jit(solution)/shard_map/ppermute | solution.py:621
  35.5 0.0 collective-permute-done.11.from_b
  35.5 1.2 %shard_map.60 = f32[1024,128]{1,0:T(8,128)} custom-call(f32[12,160,128]{2,1,0:T(8,128)S(1)} %get-tuple-element.64.mob, f32[10,160,128]{2,1,0:T(8,128)S(1)} %get-tuple-element.65.chem, f32[10,160,128]{2,1,0:T(8,128)S(1)} %get-tuple-element.66.curve, f32[10,160,128]{2,1,0:T(8,128)S(1)} %get-tuple-element.67.swing, ...), custom_call_target="tpu_custom_call" | custom-call | flops 1000000 | bytes 2000000 | tf_op jit(solution)/shard_map/pallas_call | solution.py:601
  (1 shorter events, 0.0 us)
Async XLA Ops:
  2.9 17.7 %collective-permute-start = (f32[832,128]{1,0:T(8,128)S(1)}, f32[832,128]{1,0:T(8,128)S(1)}, u32[]{:S(2)}, u32[]{:S(2)}) collective-permute-start(f32[832,128]{1,0:T(8,128)S(1)} %get-tuple-element.50), channel_id=1, source_target_pairs={{0,1},{1,0},{2,3},{3,2},{4,5},{5,4},{6,7},{7,6},{8,9},{9,8},{10,11... | collective-permute-start | bytes 1277960 | tf_op jit(solution)/shard_map/ppermute | solution.py:621
  3.5 17.1 %collective-permute-start.1 = (f32[832,128]{1,0:T(8,128)S(1)}, f32[832,128]{1,0:T(8,128)S(1)}, u32[]{:S(2)}, u32[]{:S(2)}) collective-permute-start(f32[832,128]{1,0:T(8,128)S(1)} %get-tuple-element.51), channel_id=1, source_target_pairs={{0,7},{1,2},{2,1},{3,4},{4,3},{5,6},{6,5},{7,0},{8,15},{9,10},{10,... | collective-permute-start | bytes 1277960 | tf_op jit(solution)/shard_map/ppermute | solution.py:621
  8.2 4.9 %collective-permute-start.2 = (f32[8,24,128]{2,1,0:T(8,128)S(1)}, f32[8,24,128]{2,1,0:T(8,128)S(1)}, u32[]{:S(2)}, u32[]{:S(2)}) collective-permute-start(f32[8,24,128]{2,1,0:T(8,128)S(1)} %get-tuple-element.52), channel_id=1, source_target_pairs={{0,8},{8,0},{16,24},{24,16},{1,9},{9,1},{17,25},{25,17},{2,10},{10... | collective-permute-start | bytes 294920 | tf_op jit(solution)/shard_map/ppermute | solution.py:621
  9.7 5.5 %collective-permute-start.3 = (f32[8,24,128]{2,1,0:T(8,128)S(1)}, f32[8,24,128]{2,1,0:T(8,128)S(1)}, u32[]{:S(2)}, u32[]{:S(2)}) collective-permute-start(f32[8,24,128]{2,1,0:T(8,128)S(1)} %get-tuple-element.53), channel_id=1, source_target_pairs={{0,24},{8,16},{16,8},{24,0},{1,25},{9,17},{17,9},{25,1},{2,26},{10... | collective-permute-start | bytes 294920 | tf_op jit(solution)/shard_map/ppermute | solution.py:621
  15.2 5.4 %collective-permute-start.4 = (f32[2,2,24,128]{3,2,1,0:T(8,128)S(1)}, f32[2,2,24,128]{3,2,1,0:T(8,128)S(1)}, u32[]{:S(2)}, u32[]{:S(2)}) collective-permute-start(f32[2,2,24,128]{3,2,1,0:T(8,128)S(1)} %get-tuple-element.57), channel_id=1, source_target_pairs={{0,7},{1,2},{2,1},{3,4},{4,3},{5,6},{6,5},{7,0},{8,15},{9,10},{10,... | collective-permute-start | bytes 147464 | tf_op jit(solution)/shard_map/ppermute | solution.py:621
  15.3 5.3 %collective-permute-start.5 = (f32[2,2,24,128]{3,2,1,0:T(8,128)S(1)}, f32[2,2,24,128]{3,2,1,0:T(8,128)S(1)}, u32[]{:S(2)}, u32[]{:S(2)}) collective-permute-start(f32[2,2,24,128]{3,2,1,0:T(8,128)S(1)} %get-tuple-element.58), channel_id=1, source_target_pairs={{0,1},{1,0},{2,3},{3,2},{4,5},{5,4},{6,7},{7,6},{8,9},{9,8},{10,11... | collective-permute-start | bytes 147464 | tf_op jit(solution)/shard_map/ppermute | solution.py:621
  21.8 6.9 %collective-permute-start.8 = (f32[2,136,128]{2,1,0:T(8,128)S(1)}, f32[2,136,128]{2,1,0:T(8,128)S(1)}, u32[]{:S(2)}, u32[]{:S(2)}) collective-permute-start(f32[2,136,128]{2,1,0:T(8,128)S(1)} %get-tuple-element.86), channel_id=1, source_target_pairs={{0,7},{1,2},{2,1},{3,4},{4,3},{5,6},{6,5},{7,0},{8,15},{9,10},{10,... | collective-permute-start | bytes 417800 | tf_op jit(solution)/shard_map/ppermute | solution.py:621
  23.4 5.3 %collective-permute-start.9 = (f32[2,136,128]{2,1,0:T(8,128)S(1)}, f32[2,136,128]{2,1,0:T(8,128)S(1)}, u32[]{:S(2)}, u32[]{:S(2)}) collective-permute-start(f32[2,136,128]{2,1,0:T(8,128)S(1)} %get-tuple-element.87), channel_id=1, source_target_pairs={{0,1},{1,0},{2,3},{3,2},{4,5},{5,4},{6,7},{7,6},{8,9},{9,8},{10,11... | collective-permute-start | bytes 417800 | tf_op jit(solution)/shard_map/ppermute | solution.py:621
  23.9 7.6 %collective-permute-start.6 = (f32[280,128]{1,0:T(8,128)S(1)}, f32[280,128]{1,0:T(8,128)S(1)}, u32[]{:S(2)}, u32[]{:S(2)}) collective-permute-start(f32[280,128]{1,0:T(8,128)S(1)} %get-tuple-element.62), channel_id=1, source_target_pairs={{0,7},{1,2},{2,1},{3,4},{4,3},{5,6},{6,5},{7,0},{8,15},{9,10},{10,... | collective-permute-start | bytes 430088 | tf_op jit(solution)/shard_map/ppermute | solution.py:621
  26.0 5.5 %collective-permute-start.7 = (f32[280,128]{1,0:T(8,128)S(1)}, f32[280,128]{1,0:T(8,128)S(1)}, u32[]{:S(2)}, u32[]{:S(2)}) collective-permute-start(f32[280,128]{1,0:T(8,128)S(1)} %get-tuple-element.63), channel_id=1, source_target_pairs={{0,1},{1,0},{2,3},{3,2},{4,5},{5,4},{6,7},{7,6},{8,9},{9,8},{10,11... | collective-permute-start | bytes 430088 | tf_op jit(solution)/shard_map/ppermute | solution.py:621
  29.1 6.4 %collective-permute-start.10 = (f32[2,136,128]{2,1,0:T(8,128)S(1)}, f32[2,136,128]{2,1,0:T(8,128)S(1)}, u32[]{:S(2)}, u32[]{:S(2)}) collective-permute-start(f32[2,136,128]{2,1,0:T(8,128)S(1)} %get-tuple-element.92), channel_id=1, source_target_pairs={{0,7},{1,2},{2,1},{3,4},{4,3},{5,6},{6,5},{7,0},{8,15},{9,10},{10,... | collective-permute-start | bytes 417800 | tf_op jit(solution)/shard_map/ppermute | solution.py:621
  31.3 4.2 %collective-permute-start.11 = (f32[2,136,128]{2,1,0:T(8,128)S(1)}, f32[2,136,128]{2,1,0:T(8,128)S(1)}, u32[]{:S(2)}, u32[]{:S(2)}) collective-permute-start(f32[2,136,128]{2,1,0:T(8,128)S(1)} %get-tuple-element.93), channel_id=1, source_target_pairs={{0,1},{1,0},{2,3},{3,2},{4,5},{5,4},{6,7},{7,6},{8,9},{9,8},{10,11... | collective-permute-start | bytes 417800 | tf_op jit(solution)/shard_map/ppermute | solution.py:621

commit v21 on v20

--- a/solution.py
+++ b/solution.py
@@ -159,7 +159,7 @@
     lax.fori_loop(0, rows, body, 0, unroll=2)
     if between is not None:
         between()
-    lax.fori_loop(0, rows, close, 0, unroll=4)
+    lax.fori_loop(0, rows, close, 0, unroll=2)
 
 
 def a_is_next(axis, first):

time: 36.8 us -> 37 us (level)
  Pallas kernels: 15.8 us -> 16.3 us
    pallas_call x11, Pallas kernels: 15.8 us -> 16.3 us  [call(): pl.pallas_call(kernel, out_shape=[jax.ShapeDtypeStruct(shape, f32) for sh...]
  transfers between devices with their start and end apart: 12 -> 12, of which waited for: 6 -> 6; matrix products, arithmetic and copies ran while one was open for 0% -> 0% of each run, Pallas kernels for 31% -> 32%
where the time goes in v21:
time: 37 us; the launch traced here: 36.8 us
  Pallas kernels  16.3 us (44%)
  starting transfers between devices  14.1 us (38%)
  waiting for transfers between devices  5.71 us (15%)
  between operations  0.72 us (2%)
    pallas_call x11, Pallas kernels, call(): pl.pallas_call(kernel, out_shape=[jax.ShapeDtypeStruct(shape, f32) for sh...  16.3 us
    ppermute x6, starting transfers between devices, swap(): lax.ppermute(value_a, axis, pairs_a)  7.87 us
    ppermute x6, starting transfers between devices, swap(): lax.ppermute(value_b, axis, pairs_b)  6.28 us
    ppermute x6, waiting for transfers between devices, swap(): lax.ppermute(value_a, axis, pairs_a)  3.61 us
    ppermute x6, waiting for transfers between devices, swap(): lax.ppermute(value_b, axis, pairs_b)  2.1 us
  transfers between devices with their start and end apart: 12, of which 6 were waited for; matrix products, arithmetic and copies ran while one was open for 0% of the time, Pallas kernels for 32%

profile of v21, /device:TPU:0, one launch (start us, length us, event | category | flops | bytes accessed | tf_op | source)
XLA Modules:
  0.0 36.8 jit_solution(6703783107035159201)
XLA Ops:
  0.6 2.3 %shard_map.50 = (f32[3,8,128,128]{3,2,1,0:T(8,128)S(1)}, f32[8,128,128]{2,1,0:T(8,128)S(1)}, f32[8,128,128]{2,1,0:T(8,128)S(1)}, f32[832,128]{1,0:T(8,128)S(1)},...) custom-call(f32[3,1024,128]{2,1,0:T(8,128)} %bitcast.5, f32[1024,128]{1,0:T(8,128)} %bitcast.6, ...), custom_call_target="tpu_custom_call" | custom-call | flops 3000000 | bytes 6000000 | tf_op jit(solution)/shard_map/pallas_call | solution.py:601
  2.9 0.5 %collective-permute-start = (f32[832,128]{1,0:T(8,128)S(1)}, f32[832,128]{1,0:T(8,128)S(1)}, u32[]{:S(2)}, u32[]{:S(2)}) collective-permute-start(f32[832,128]{1,0:T(8,128)S(1)} %get-tuple-element.50), channel_id=1, source_target_pairs={{0,1},{1,0},{2,3},{3,2},{4,5},{5,4},{6,7},{7,6},{8,9},{9,8},{10,11... | collective-permute-start | bytes 1277960 | tf_op jit(solution)/shard_map/ppermute | solution.py:621
  3.5 4.7 %collective-permute-start.1 = (f32[832,128]{1,0:T(8,128)S(1)}, f32[832,128]{1,0:T(8,128)S(1)}, u32[]{:S(2)}, u32[]{:S(2)}) collective-permute-start(f32[832,128]{1,0:T(8,128)S(1)} %get-tuple-element.51), channel_id=1, source_target_pairs={{0,7},{1,2},{2,1},{3,4},{4,3},{5,6},{6,5},{7,0},{8,15},{9,10},{10,... | collective-permute-start | bytes 1277960 | tf_op jit(solution)/shard_map/ppermute | solution.py:621
  8.2 1.5 %collective-permute-start.2 = (f32[8,24,128]{2,1,0:T(8,128)S(1)}, f32[8,24,128]{2,1,0:T(8,128)S(1)}, u32[]{:S(2)}, u32[]{:S(2)}) collective-permute-start(f32[8,24,128]{2,1,0:T(8,128)S(1)} %get-tuple-element.52), channel_id=1, source_target_pairs={{0,8},{8,0},{16,24},{24,16},{1,9},{9,1},{17,25},{25,17},{2,10},{10... | collective-permute-start | bytes 294920 | tf_op jit(solution)/shard_map/ppermute | solution.py:621
  9.7 1.5 %collective-permute-start.3 = (f32[8,24,128]{2,1,0:T(8,128)S(1)}, f32[8,24,128]{2,1,0:T(8,128)S(1)}, u32[]{:S(2)}, u32[]{:S(2)}) collective-permute-start(f32[8,24,128]{2,1,0:T(8,128)S(1)} %get-tuple-element.53), channel_id=1, source_target_pairs={{0,24},{8,16},{16,8},{24,0},{1,25},{9,17},{17,9},{25,1},{2,26},{10... | collective-permute-start | bytes 294920 | tf_op jit(solution)/shard_map/ppermute | solution.py:621
  11.2 1.2 %shard_map.51 = (f32[2,8,160,128]{3,2,1,0:T(8,128)S(1)}, f32[2,8,160,128]{3,2,1,0:T(8,128)S(1)}, f32[2,8,160,128]{3,2,1,0:T(8,128)S(1)}, f32[2,8,160,128]{3,2,1,0:T(8,128)S(1)}) custom-call(f32[3,8,128,128]{3,2,1,0:T(8,128)S(1)} %get-tuple-element.49.conc_own), custom_call_target="tpu_custom_call" | custom-call | flops 2000000 | bytes 4000000 | tf_op jit(solution)/shard_map/pallas_call | solution.py:601
  12.4 0.7 %collective-permute-done.2.got_a = f32[8,24,128]{2,1,0:T(8,128)S(1)} collective-permute-done((f32[8,24,128]{2,1,0:T(8,128)S(1)}, f32[8,24,128]{2,1,0:T(8,128)S(1)}, u32[]{:S(2)}, u32[]{:S(2)}) %collective-permute-start.2) | collective-permute-done | bytes 98336 | tf_op jit(solution)/shard_map/ppermute | solution.py:621
  13.1 2.1 %collective-permute-done.3.got_b = f32[8,24,128]{2,1,0:T(8,128)S(1)} collective-permute-done((f32[8,24,128]{2,1,0:T(8,128)S(1)}, f32[8,24,128]{2,1,0:T(8,128)S(1)}, u32[]{:S(2)}, u32[]{:S(2)}) %collective-permute-start.3) | collective-permute-done | bytes 98336 | tf_op jit(solution)/shard_map/ppermute | solution.py:621
  15.2 0.1 collective-permute-start.4
  15.3 0.1 collective-permute-start.5
  15.4 3.4 %shard_map.55 = (f32[10,160,128]{2,1,0:T(8,128)S(1)}, f32[10,160,128]{2,1,0:T(8,128)S(1)}, f32[8,160,128]{2,1,0:T(8,128)S(1)}, f32[10,160,128]{2,1,0:T(8,128)S(1...) custom-call(f32[3,8,128,128]{3,2,1,0:T(8,128)S(1)} %get-tuple-elemen, ...), custom_call_target="tpu_custom_call" | custom-call | flops 3000000 | bytes 6000000 | tf_op jit(solution)/shard_map/pallas_call | solution.py:601
  18.8 1.8 %collective-permute-done.4.corner_b = f32[2,2,24,128]{3,2,1,0:T(8,128)S(1)} collective-permute-done((f32[2,2,24,128]{3,2,1,0:T(8,128)S(1)}, f32[2,2,24,128]{3,2,1,0:T(8,128)S(1)}, u32[]{:S(2)}, u32[]{:S(2)}) %collective-permute-start.4) | collective-permute-done | bytes 49184 | tf_op jit(solution)/shard_map/ppermute | solution.py:621
  20.6 0.0 collective-permute-done.5.corner_a
  20.6 0.0 collective-permute-done.from_a
  20.6 0.0 collective-permute-done.1.from_b
  20.6 1.2 %shard_map.56 = (f32[2,2,160,128]{3,2,1,0:T(8,128)S(1)}, f32[2,160,128]{2,1,0:T(8,128)S(1)}, f32[2,136,128]{2,1,0:T(8,128)S(1)}, f32[2,136,128]{2,1,0:T(8,128)S(1)}) custom-call(f32[10,160,128]{2,1,0:T(8,128)S(1)} %get-tuple-element.76.conc, f32[10,160,128]{2,1,0:T(8,128)S(1)} %get-tuple-element.77.adj, f32[8,160,128]{2,1,0:T(8,128)S(1)} %get-tuple-element.70.rate.rest_1_, ...), custom_call_target="tpu_custom_call" | custom-call | flops 2000000 | bytes 4000000 | tf_op jit(solution)/shard_map/pallas_call | solution.py:601
  21.8 1.7 %collective-permute-start.8 = (f32[2,136,128]{2,1,0:T(8,128)S(1)}, f32[2,136,128]{2,1,0:T(8,128)S(1)}, u32[]{:S(2)}, u32[]{:S(2)}) collective-permute-start(f32[2,136,128]{2,1,0:T(8,128)S(1)} %get-tuple-element.86), channel_id=1, source_target_pairs={{0,7},{1,2},{2,1},{3,4},{4,3},{5,6},{6,5},{7,0},{8,15},{9,10},{10,... | collective-permute-start | bytes 417800 | tf_op jit(solution)/shard_map/ppermute | solution.py:621
  23.5 0.0 collective-permute-start.9
  23.5 0.5 %shard_map.53 = (f32[12,160,128]{2,1,0:T(8,128)S(1)}, f32[10,160,128]{2,1,0:T(8,128)S(1)}, f32[10,160,128]{2,1,0:T(8,128)S(1)}, f32[10,160,128]{2,1,0:T(8,128)S(...) custom-call(f32[3,8,128,128]{3,2,1,0:T(8,128)S(1)} %get-tuple-element.49.conc_own, ...), custom_call_target="tpu_custom_call" | custom-call | flops 2000000 | bytes 4000000 | tf_op jit(solution)/shard_map/pallas_call | solution.py:601
  24.0 1.9 %collective-permute-start.6 = (f32[280,128]{1,0:T(8,128)S(1)}, f32[280,128]{1,0:T(8,128)S(1)}, u32[]{:S(2)}, u32[]{:S(2)}) collective-permute-start(f32[280,128]{1,0:T(8,128)S(1)} %get-tuple-element.62), channel_id=1, source_target_pairs={{0,7},{1,2},{2,1},{3,4},{4,3},{5,6},{6,5},{7,0},{8,15},{9,10},{10,... | collective-permute-start | bytes 430088 | tf_op jit(solution)/shard_map/ppermute | solution.py:621
  26.0 0.0 collective-permute-start.7
  26.0 2.5 %shard_map.57 = (f32[8,160,128]{2,1,0:T(8,128)S(1)}, f32[8,160,128]{2,1,0:T(8,128)S(1)}) custom-call(f32[12,160,128]{2,1,0:T(8,128)S(1)} %get-tuple-element.71.mob, f32[10,160,128]{2,1,0:T(8,128)S(1)} %get-tuple-element.72.chem, f32[10,160,128]{2,1,0:T(8,128)S(1)} %get-tuple-element.73.curve, f32[10,160,128]{2,1,0:T(8,128)S(1)} %get-tuple-element.74.swing, ...), custom_call_target="tpu_custom_call" | custom-call | flops 3000000 | bytes 6000000 | tf_op jit(solution)/shard_map/pallas_call | solution.py:601
  28.5 0.4 %collective-permute-done.8.from_a = f32[2,136,128]{2,1,0:T(8,128)S(1)} collective-permute-done((f32[2,136,128]{2,1,0:T(8,128)S(1)}, f32[2,136,128]{2,1,0:T(8,128)S(1)}, u32[]{:S(2)}, u32[]{:S(2)}) %collective-permute-start.8) | collective-permute-done | bytes 139296 | tf_op jit(solution)/shard_map/ppermute | solution.py:621
  28.9 0.0 collective-permute-done.9.from_b
  28.9 0.4 %shard_map.58 = (f32[2,2,160,128]{3,2,1,0:T(8,128)S(1)}, f32[2,136,128]{2,1,0:T(8,128)S(1)}, f32[2,136,128]{2,1,0:T(8,128)S(1)}) custom-call(f32[12,160,128]{2,1,0:T(8,128)S(1)} %get-tuple-element.71.mob, f32[10,160,128]{2,1,0:T(8,128)S(1)} %get-tuple-element.72.chem, f32[10,160,128]{2,1,0:T(8,128)S(1)} %get-tuple-element.73.curve, ...), custom_call_target="tpu_custom_call" | custom-call | flops 1000000 | bytes 2000000 | tf_op jit(solution)/shard_map/pallas_call | solution.py:601
  29.3 2.1 %collective-permute-start.10 = (f32[2,136,128]{2,1,0:T(8,128)S(1)}, f32[2,136,128]{2,1,0:T(8,128)S(1)}, u32[]{:S(2)}, u32[]{:S(2)}) collective-permute-start(f32[2,136,128]{2,1,0:T(8,128)S(1)} %get-tuple-element.92), channel_id=1, source_target_pairs={{0,7},{1,2},{2,1},{3,4},{4,3},{5,6},{6,5},{7,0},{8,15},{9,10},{10,... | collective-permute-start | bytes 417800 | tf_op jit(solution)/shard_map/ppermute | solution.py:621
  31.4 0.0 collective-permute-start.11
  31.4 0.1 collective-permute-done.6.from_a
  31.6 0.0 collective-permute-done.7.from_b
  31.6 0.5 %shard_map.54 = (f32[12,160,128]{2,1,0:T(8,128)S(1)}, f32[10,160,128]{2,1,0:T(8,128)S(1)}, f32[10,160,128]{2,1,0:T(8,128)S(1)}, f32[10,160,128]{2,1,0:T(8,128)S(1)}) custom-call(f32[3,8,128,128]{3,2,1,0:T(8,128)S(1)} %get-tuple-element.49.conc_own, f32[280,128]{1,0:T(8,128)S(1)} %collective-permute-done.6.from_a, ...), custom_call_target="tpu_custom_call" | custom-call | flops 2000000 | bytes 4000000 | tf_op jit(solution)/shard_map/pallas_call | solution.py:601
  32.0 3.1 %shard_map.59 = (f32[8,160,128]{2,1,0:T(8,128)S(1)}, f32[1024,128]{1,0:T(8,128)S(1)}, f32[512,128]{1,0:T(8,128)}) custom-call(f32[12,160,128]{2,1,0:T(8,128)S(1)} %get-tuple-element.64.mob, f32[10,160,128]{2,1,0:T(8,128)S(1)} %get-tuple-element.65.chem, f32[10,160,128]{2,1,0:T(8,128)S(1)} %get-tuple-element.66.curve, ...), custom_call_target="tpu_custom_call" | custom-call | flops 3000000 | bytes 6000000 | tf_op jit(solution)/shard_map/pallas_call | solution.py:601
  35.1 0.6 %collective-permute-done.10.from_a = f32[2,136,128]{2,1,0:T(8,128)S(1)} collective-permute-done((f32[2,136,128]{2,1,0:T(8,128)S(1)}, f32[2,136,128]{2,1,0:T(8,128)S(1)}, u32[]{:S(2)}, u32[]{:S(2)}) %collective-permute-start.10) | collective-permute-done | bytes 139296 | tf_op jit(solution)/shard_map/ppermute | solution.py:621
  35.7 0.0 collective-permute-done.11.from_b
  35.7 1.2 %shard_map.60 = f32[1024,128]{1,0:T(8,128)} custom-call(f32[12,160,128]{2,1,0:T(8,128)S(1)} %get-tuple-element.64.mob, f32[10,160,128]{2,1,0:T(8,128)S(1)} %get-tuple-element.65.chem, f32[10,160,128]{2,1,0:T(8,128)S(1)} %get-tuple-element.66.curve, f32[10,160,128]{2,1,0:T(8,128)S(1)} %get-tuple-element.67.swing, ...), custom_call_target="tpu_custom_call" | custom-call | flops 1000000 | bytes 2000000 | tf_op jit(solution)/shard_map/pallas_call | solution.py:601
  (1 shorter events, 0.0 us)
Async XLA Ops:
  2.9 17.7 %collective-permute-start = (f32[832,128]{1,0:T(8,128)S(1)}, f32[832,128]{1,0:T(8,128)S(1)}, u32[]{:S(2)}, u32[]{:S(2)}) collective-permute-start(f32[832,128]{1,0:T(8,128)S(1)} %get-tuple-element.50), channel_id=1, source_target_pairs={{0,1},{1,0},{2,3},{3,2},{4,5},{5,4},{6,7},{7,6},{8,9},{9,8},{10,11... | collective-permute-start | bytes 1277960 | tf_op jit(solution)/shard_map/ppermute | solution.py:621
  3.5 17.1 %collective-permute-start.1 = (f32[832,128]{1,0:T(8,128)S(1)}, f32[832,128]{1,0:T(8,128)S(1)}, u32[]{:S(2)}, u32[]{:S(2)}) collective-permute-start(f32[832,128]{1,0:T(8,128)S(1)} %get-tuple-element.51), channel_id=1, source_target_pairs={{0,7},{1,2},{2,1},{3,4},{4,3},{5,6},{6,5},{7,0},{8,15},{9,10},{10,... | collective-permute-start | bytes 1277960 | tf_op jit(solution)/shard_map/ppermute | solution.py:621
  8.2 4.9 %collective-permute-start.2 = (f32[8,24,128]{2,1,0:T(8,128)S(1)}, f32[8,24,128]{2,1,0:T(8,128)S(1)}, u32[]{:S(2)}, u32[]{:S(2)}) collective-permute-start(f32[8,24,128]{2,1,0:T(8,128)S(1)} %get-tuple-element.52), channel_id=1, source_target_pairs={{0,8},{8,0},{16,24},{24,16},{1,9},{9,1},{17,25},{25,17},{2,10},{10... | collective-permute-start | bytes 294920 | tf_op jit(solution)/shard_map/ppermute | solution.py:621
  9.7 5.5 %collective-permute-start.3 = (f32[8,24,128]{2,1,0:T(8,128)S(1)}, f32[8,24,128]{2,1,0:T(8,128)S(1)}, u32[]{:S(2)}, u32[]{:S(2)}) collective-permute-start(f32[8,24,128]{2,1,0:T(8,128)S(1)} %get-tuple-element.53), channel_id=1, source_target_pairs={{0,24},{8,16},{16,8},{24,0},{1,25},{9,17},{17,9},{25,1},{2,26},{10... | collective-permute-start | bytes 294920 | tf_op jit(solution)/shard_map/ppermute | solution.py:621
  15.2 5.4 %collective-permute-start.4 = (f32[2,2,24,128]{3,2,1,0:T(8,128)S(1)}, f32[2,2,24,128]{3,2,1,0:T(8,128)S(1)}, u32[]{:S(2)}, u32[]{:S(2)}) collective-permute-start(f32[2,2,24,128]{3,2,1,0:T(8,128)S(1)} %get-tuple-element.57), channel_id=1, source_target_pairs={{0,7},{1,2},{2,1},{3,4},{4,3},{5,6},{6,5},{7,0},{8,15},{9,10},{10,... | collective-permute-start | bytes 147464 | tf_op jit(solution)/shard_map/ppermute | solution.py:621
  15.3 5.3 %collective-permute-start.5 = (f32[2,2,24,128]{3,2,1,0:T(8,128)S(1)}, f32[2,2,24,128]{3,2,1,0:T(8,128)S(1)}, u32[]{:S(2)}, u32[]{:S(2)}) collective-permute-start(f32[2,2,24,128]{3,2,1,0:T(8,128)S(1)} %get-tuple-element.58), channel_id=1, source_target_pairs={{0,1},{1,0},{2,3},{3,2},{4,5},{5,4},{6,7},{7,6},{8,9},{9,8},{10,11... | collective-permute-start | bytes 147464 | tf_op jit(solution)/shard_map/ppermute | solution.py:621
  21.8 7.1 %collective-permute-start.8 = (f32[2,136,128]{2,1,0:T(8,128)S(1)}, f32[2,136,128]{2,1,0:T(8,128)S(1)}, u32[]{:S(2)}, u32[]{:S(2)}) collective-permute-start(f32[2,136,128]{2,1,0:T(8,128)S(1)} %get-tuple-element.86), channel_id=1, source_target_pairs={{0,7},{1,2},{2,1},{3,4},{4,3},{5,6},{6,5},{7,0},{8,15},{9,10},{10,... | collective-permute-start | bytes 417800 | tf_op jit(solution)/shard_map/ppermute | solution.py:621
  23.5 5.4 %collective-permute-start.9 = (f32[2,136,128]{2,1,0:T(8,128)S(1)}, f32[2,136,128]{2,1,0:T(8,128)S(1)}, u32[]{:S(2)}, u32[]{:S(2)}) collective-permute-start(f32[2,136,128]{2,1,0:T(8,128)S(1)} %get-tuple-element.87), channel_id=1, source_target_pairs={{0,1},{1,0},{2,3},{3,2},{4,5},{5,4},{6,7},{7,6},{8,9},{9,8},{10,11... | collective-permute-start | bytes 417800 | tf_op jit(solution)/shard_map/ppermute | solution.py:621
  24.0 7.5 %collective-permute-start.6 = (f32[280,128]{1,0:T(8,128)S(1)}, f32[280,128]{1,0:T(8,128)S(1)}, u32[]{:S(2)}, u32[]{:S(2)}) collective-permute-start(f32[280,128]{1,0:T(8,128)S(1)} %get-tuple-element.62), channel_id=1, source_target_pairs={{0,7},{1,2},{2,1},{3,4},{4,3},{5,6},{6,5},{7,0},{8,15},{9,10},{10,... | collective-permute-start | bytes 430088 | tf_op jit(solution)/shard_map/ppermute | solution.py:621
  26.0 5.6 %collective-permute-start.7 = (f32[280,128]{1,0:T(8,128)S(1)}, f32[280,128]{1,0:T(8,128)S(1)}, u32[]{:S(2)}, u32[]{:S(2)}) collective-permute-start(f32[280,128]{1,0:T(8,128)S(1)} %get-tuple-element.63), channel_id=1, source_target_pairs={{0,1},{1,0},{2,3},{3,2},{4,5},{5,4},{6,7},{7,6},{8,9},{9,8},{10,11... | collective-permute-start | bytes 430088 | tf_op jit(solution)/shard_map/ppermute | solution.py:621
  29.3 6.3 %collective-permute-start.10 = (f32[2,136,128]{2,1,0:T(8,128)S(1)}, f32[2,136,128]{2,1,0:T(8,128)S(1)}, u32[]{:S(2)}, u32[]{:S(2)}) collective-permute-start(f32[2,136,128]{2,1,0:T(8,128)S(1)} %get-tuple-element.92), channel_id=1, source_target_pairs={{0,7},{1,2},{2,1},{3,4},{4,3},{5,6},{6,5},{7,0},{8,15},{9,10},{10,... | collective-permute-start | bytes 417800 | tf_op jit(solution)/shard_map/ppermute | solution.py:621
  31.4 4.2 %collective-permute-start.11 = (f32[2,136,128]{2,1,0:T(8,128)S(1)}, f32[2,136,128]{2,1,0:T(8,128)S(1)}, u32[]{:S(2)}, u32[]{:S(2)}) collective-permute-start(f32[2,136,128]{2,1,0:T(8,128)S(1)} %get-tuple-element.93), channel_id=1, source_target_pairs={{0,1},{1,0},{2,3},{3,2},{4,5},{5,4},{6,7},{7,6},{8,9},{9,8},{10,11... | collective-permute-start | bytes 417800 | tf_op jit(solution)/shard_map/ppermute | solution.py:621
